TPU v7x, 128 devices: a whole 4x4x4 slice. The times are simulated.
128 devices in a mesh: blk: 8 (over x_lo, y), feat: 16 (over x_hi, z, core).
Axes of the slice: x: 4 (x_hi: 2, x_lo: 2; x = x_hi * 2 + x_lo), y: 4, z: 4, core: 2. Of those that a mesh axis runs over, the one named last changes fastest.
Arguments:
- node_feats: bfloat16 [256, 65536], P('feat', 'blk'), may hold values from -6 to 6
- weight: bfloat16 [256, 256], P('feat'), may hold values from -0.375 to 0.375
- tiles: bfloat16 [512, 32, 128, 128], P('blk'), may hold values from -0.09375 to 0.09375
- block_cols: int32 [512, 32], P('blk'), may hold values from 0 to 511, all different within a row
- cotangent: bfloat16 [256, 65536], P('feat', 'blk'), may hold values from -6 to 6
Outputs:
- hidden: bfloat16 [256, 65536], P('feat', 'blk')
- weight_grad: float32 [256, 256], P('feat')
- feats_grad: bfloat16 [256, 65536], P('feat', 'blk')
Inputs may be any that keep to these rules, and one draw needn't show every extreme that they name: `block_cols`: within a block row the 32 source blocks differ; every source block is named by some block row.
All inputs are finite; a program needn't handle non-finite values.
Results may differ from a plain program's by a relative error of at most 0.02.
Values may be sent and summed in bfloat16 or wider, within the bound.
No kernel may reach another device: no remote copies, remote signals or barrier semaphores. Data moves between devices by JAX's collectives and lax.ppermute only.
A program may use at most 192 MiB of HBM per device.

v0:
```python
import jax
import jax.numpy as jnp
from jax import lax
from jax.sharding import PartitionSpec as P


def per_device(node_feats, weight, tiles, block_cols, cotangent):
    width_part, rows = node_feats.shape
    row_blocks, slots = block_cols.shape
    full_feats = lax.all_gather(node_feats, "blk", axis=1, tiled=True)
    all_blocks = full_feats.shape[1] // 128
    by_block = jnp.transpose(full_feats.reshape(width_part, all_blocks, 128), (1, 0, 2))
    by_block = by_block.reshape(all_blocks, width_part * 128)
    flat_cols = block_cols.reshape(-1)
    selector = (flat_cols[:, None] == jnp.arange(all_blocks, dtype=jnp.int32)[None, :]).astype(
        jnp.bfloat16
    )
    picked = jnp.dot(selector, by_block, preferred_element_type=jnp.float32).astype(jnp.bfloat16)
    picked = picked.reshape(row_blocks, slots, width_part, 128)
    aggregated = jnp.einsum("rpdk,rpjk->drj", picked, tiles, preferred_element_type=jnp.float32)
    aggregated = aggregated.reshape(width_part, rows).astype(jnp.bfloat16)
    full_weight = lax.all_gather(weight, "feat", axis=0, tiled=True)
    own_columns = lax.dynamic_slice_in_dim(
        full_weight, lax.axis_index("feat") * width_part, width_part, 1
    )
    pre = jnp.einsum(
        "ab,an->bn",
        own_columns,
        lax.all_gather(aggregated, "feat", axis=0, tiled=True),
        preferred_element_type=jnp.float32,
    )
    hidden = jax.nn.silu(pre).astype(jnp.bfloat16)
    sig = jax.nn.sigmoid(pre)
    pre_grad = (cotangent.astype(jnp.float32) * sig * (1.0 + pre * (1.0 - sig))).astype(
        jnp.bfloat16
    )
    full_grad = lax.all_gather(pre_grad, "feat", axis=0, tiled=True)
    local_wgrad = jnp.einsum("an,bn->ab", aggregated, full_grad, preferred_element_type=jnp.float32)
    weight_grad = lax.psum(local_wgrad, "blk")
    agg_grad = jnp.dot(weight, full_grad, preferred_element_type=jnp.float32).astype(jnp.bfloat16)
    grad_blocks = agg_grad.reshape(width_part, row_blocks, 128)
    contrib = jnp.einsum("drj,rpjk->rpdk", grad_blocks, tiles, preferred_element_type=jnp.float32)
    contrib = contrib.reshape(row_blocks * slots, width_part * 128)
    upper_part = contrib.astype(jnp.bfloat16)
    lower_part = (contrib - upper_part.astype(jnp.float32)).astype(jnp.bfloat16)
    summed_all = jnp.dot(selector.T, upper_part, preferred_element_type=jnp.float32)
    summed_all = summed_all + jnp.dot(selector.T, lower_part, preferred_element_type=jnp.float32)
    summed_all = summed_all.reshape(all_blocks, width_part, 128)
    summed = lax.psum_scatter(
        summed_all.astype(jnp.bfloat16), "blk", scatter_dimension=0, tiled=True
    ).astype(jnp.float32)
    feats_grad = jnp.transpose(summed, (1, 0, 2)).reshape(width_part, rows).astype(jnp.bfloat16)
    return (hidden, weight_grad, feats_grad)


def solution(mesh):
    placed = (
        P("feat", "blk"),
        P("feat", None),
        P("blk", None, None, None),
        P("blk", None),
        P("feat", "blk"),
    )
    return jax.shard_map(
        per_device,
        mesh=mesh,
        in_specs=placed,
        out_specs=(P("feat", "blk"), P("feat", None), P("feat", "blk")),
        check_vma=False,
    )
```

profile of v0, /device:TPU:0, one launch (start us, length us, event | category | flops | bytes accessed | tf_op | source)
XLA Modules:
  0.0 324.9 jit_solution(13033275174795730493)
XLA Ops:
  7.2 0.0 all-gather.4.cloned.1.call-start
  7.2 0.7 all-gather.4.cloned.1.call-update
  7.9 0.0 all-gather.6.cloned.1.call-start
  7.9 0.8 copy.14
  8.7 0.1 eq.15
  8.8 45.0 %all-gather.4.cloned.1.call-done = bf16[16,65536]{1,0:T(8,128)(2,1)} async-done(((bf16[16,8192]{1,0:T(8,128)(2,1)}), bf16[16,65536]{1,0:T(8,128)(2,1)}) %all-gather.4.cloned.1.call-update) | async-done | bytes 2097168 | tf_op jit(solution)/shard_map/all_gather | solution.py:10
  53.9 2.0 copy.25
  55.8 2.7 copy.15
  58.5 8.3 %convert_bitcast_fusion = bf16[256,8,16,128]{3,1,2,0:T(8,128)(2,1)} fusion(bf16[512,2048]{0,1:T(8,128)(2,1)} %bitcast.77, s32[2048]{0:T(1024)S(1)} %eq.15), kind=kOutput, calls=%fused_computation.8 | convolution fusion | flops 4300210176 | bytes 10493952 | tf_op jit(solution)/shard_map/dot_general | solution.py:18
  66.8 9.8 %copy.26 = bf16[256,8,16,128]{3,2,1,0:T(8,128)(2,1)} copy(bf16[256,8,16,128]{3,1,2,0:T(8,128)(2,1)} %convert_bitcast_fusion) | data formatting | bytes 16777216
  76.6 28.0 %fusion.20 = bf16[64,2,8,128]{3,2,1,0:T(8,128)(2,1)S(1)} fusion(bf16[64,32,128,128]{3,2,1,0:T(8,128)(2,1)} %param.7, bf16[64,32,16,128]{3,2,1,0:T(8,128)(2,1)} %bitcast.71), kind=kOutput, calls=%fused_computation.17 | convolution fusion | flops 1073872896 | bytes 75759616 | tf_op jit(solution)/shard_map/rpdk,rpjk->drj/dot_general | solution.py:20
  104.6 0.7 copy.45
  105.3 0.0 all-gather.6.cloned.1.call-update
  105.3 0.0 all-gather.8.cloned.1.call-start
  105.4 0.0 copy-done.1
  105.4 24.6 %all_gather.12 = bf16[256,256]{1,0:T(8,128)(2,1)S(1)} all-gather(bf16[16,256]{1,0:T(8,128)(2,1)S(1)} %copy-done.1), channel_id=1, replica_groups=mesh['blk'=8,'feat'=16] {'feat'}, dimensions={0}, use_global_device_ids=true | all-gather | bytes 139264 | tf_op jit(solution)/shard_map/all_gather | solution.py:22
  130.0 30.1 %all-gather.6.cloned.1.call-done = bf16[256,8192]{1,0:T(8,128)(2,1)} async-done(((bf16[16,8192]{1,0:T(8,128)(2,1)}), bf16[256,8192]{1,0:T(8,128)(2,1)}) %all-gather.6.cloned.1.call-update) | async-done | bytes 4194320 | tf_op jit(solution)/shard_map/all_gather | solution.py:29
  160.0 3.8 %multiply_convert_fusion = (bf16[16,8192]{1,0:T(8,128)(2,1)}, bf16[16,8192]{1,0:T(8,128)(2,1)}) fusion(bf16[16,8192]{1,0:T(8,128)(2,1)S(1)} %copy-done, bf16[256,8192]{1,0:T(8,128)(2,1)} %all-gather.6.cloned.1.call-done, bf16[256,256]{1,0:T(8,128)(2,1)S(1)} %all_gather.12, s32[]{:T(128)S(6)} %select_n.3), kind=kOutput, calls=%fused_computation.19 | convolution fusion | flops 68681728 | bytes 5046276 | tf_op jit(solution)/shard_map/ab,an->bn/dot_general | solution.py:26
  163.8 0.0 all-gather.8.cloned.1.call-update
  163.8 0.2 reduce-scatter.2.cloned.1.call-start
  164.1 53.1 %all-gather.8.cloned.1.call-done = bf16[256,8192]{1,0:T(8,128)(2,1)} async-done(((bf16[16,8192]{1,0:T(8,128)(2,1)}), bf16[256,8192]{1,0:T(8,128)(2,1)}) %all-gather.8.cloned.1.call-update) | async-done | bytes 4194320 | tf_op jit(solution)/shard_map/all_gather | solution.py:37
  217.2 2.8 fusion.23
  220.0 0.1 copy.27
  220.1 29.1 %fusion.24 = f32[64,16,32,128]{3,1,2,0:T(8,128)} fusion(bf16[64,32,128,128]{3,2,1,0:T(8,128)(2,1)} %param.7, bf16[16,64,128,1]{2,1,0,3:T(8,128)(2,1)S(1)} %bitcast.78), kind=kOutput, calls=%fused_computation.24 | convolution fusion | flops 1073741824 | bytes 84148224 | tf_op jit(solution)/shard_map/drj,rpjk->rpdk/dot_general | solution.py:42
  249.2 11.5 %fusion.1 = f32[512,2048]{1,0:T(8,128)S(1)} fusion(f32[256,8,16,128]{3,2,1,0:T(8,128)} %bitcast.72, s32[2048]{0:T(1024)S(1)} %eq.15), kind=kOutput, calls=%fused_computation.3 | convolution fusion | flops 4296015872 | bytes 20979712 | tf_op jit(solution)/shard_map/dot_general | solution.py:46
  260.7 13.6 %fusion.11 = bf16[64,8,16,128]{3,1,2,0:T(8,128)(2,1)S(1)} fusion(f32[512,2048]{1,0:T(8,128)S(1)} %fusion.1, f32[256,8,16,128]{3,2,1,0:T(8,128)} %bitcast.73, s32[2048]{0:T(1024)S(1)} %eq.15), kind=kOutput, calls=%fused_computation.14 | convolution fusion | flops 4314890240 | bytes 23076864 | tf_op jit(solution)/shard_map/dot_general | solution.py:47
  274.3 2.0 copy.29
  276.3 0.0 reduce-scatter.2.cloned.1.call-update
  276.3 3.4 %fusion.29 = f32[16,256]{1,0:T(8,128)S(1)} fusion(bf16[256,8192]{1,0:T(8,128)(2,1)} %all-gather.8.cloned.1.call-done, bf16[64,2,8,128]{3,2,1,0:T(8,128)(2,1)S(1)} %fusion.20), kind=kOutput, calls=%fused_computation.29 | convolution fusion | flops 67108864 | bytes 4472832 | tf_op jit(solution)/shard_map/an,bn->ab/dot_general | solution.py:38
  279.7 33.9 %psum.7 = f32[16,256]{1,0:T(8,128)} all-reduce(f32[16,256]{1,0:T(8,128)S(1)} %fusion.29), channel_id=1, replica_groups=mesh['blk'=8,'feat'=16] {'blk'}, use_global_device_ids=true, to_apply=%region_0.1 | all-reduce | flops 4096 | bytes 32768 | tf_op jit(solution)/shard_map/psum | solution.py:39
  313.6 3.1 reduce-scatter.2.cloned.1.call-done
  316.7 1.7 copy_bitcast_fusion
  (3 shorter events, 0.0 us)
Async XLA Ops:
  7.2 46.7 %all-gather.4.cloned.1.call-start = ((), (), s32[]{:S(2)}) async-start(), calls=%async_computation.1 | async-start | bytes 2359296 | tf_op jit(solution)/shard_map/all_gather | solution.py:10
  7.9 152.1 %all-gather.6.cloned.1.call-start = ((), (), s32[]{:S(2)}) async-start(), calls=%async_computation.2 | async-start | bytes 4456448 | tf_op jit(solution)/shard_map/all_gather | solution.py:29
  76.6 28.8 %copy-start.1 = (bf16[16,256]{1,0:T(8,128)(2,1)S(1)}, bf16[16,256]{1,0:T(8,128)(2,1)}, u32[]{:S(2)}) copy-start(bf16[16,256]{1,0:T(8,128)(2,1)} %param.6) | copy-start | bytes 24580
  76.6 83.5 %copy-start = (bf16[16,8192]{1,0:T(8,128)(2,1)S(1)}, bf16[16,8192]{1,0:T(8,128)(2,1)}, u32[]{:S(2)}) copy-start(bf16[16,8192]{1,0:T(8,128)(2,1)} %param.9) | copy-start | bytes 786436
  105.3 111.8 %all-gather.8.cloned.1.call-start = ((), (), s32[]{:S(2)}) async-start(), calls=%async_computation.3 | async-start | bytes 4456448 | tf_op jit(solution)/shard_map/all_gather | solution.py:37
  163.8 152.8 %reduce-scatter.2.cloned.1.call-start = ((), (), s32[]{:S(2)}) async-start(), calls=%async_computation.4 | async-start | bytes 2359296 | tf_op jit(solution)/shard_map/reduce_scatter | solution.py:49
Sparse Core Ops, SparseCore 0:
  9.6 44.1 all-gather.3
  105.5 54.5 all-gather.5
  164.0 53.1 all-gather.7
  276.4 40.2 reduce-scatter.1
where the time goes:
time: 325 us
  waiting for transfers between devices  132 us (41%)
  matrix products  101 us (31%)
  blocking collectives  58.5 us (18%)
  local copies, waits for them, and re-layouts  19.7 us (6%)
  between operations  13.8 us (4%)
    all_gather x1, waiting for transfers between devices, per_device(): full_grad = lax.all_gather(pre_grad, 'feat', axis=0, tiled=True)  53.1 us
    all_gather x1, waiting for transfers between devices, per_device(): full_feats = lax.all_gather(node_feats, 'blk', axis=1, tiled=True)  45 us
    psum x1, blocking collectives, per_device(): weight_grad = lax.psum(local_wgrad, 'blk')  33.9 us
    all_gather x1, waiting for transfers between devices, per_device(): lax.all_gather(aggregated, 'feat', axis=0, tiled=True)  30.1 us
    dot_general x1, matrix products, per_device(): jnp.einsum('drj,rpjk->rpdk', grad_blocks, tiles, preferred_element_type=j...  29.1 us
    dot_general x1, matrix products, per_device(): jnp.einsum('rpdk,rpjk->drj', picked, tiles, preferred_element_type=jnp.fl...  28 us
    all_gather x1, blocking collectives, per_device(): full_weight = lax.all_gather(weight, 'feat', axis=0, tiled=True)  24.6 us
    unnamed x9, local copies, waits for them, and re-layouts  14.6 us
  transfers between devices with their start and end apart: 4, of which 4 were waited for; matrix products, arithmetic and copies ran while one was open for 1% of the time, Pallas kernels for 0%

commit v1 on v0

v1 whole, which is shorter than its diff:
```python
import functools

import jax
import jax.numpy as jnp
from jax import lax
from jax.experimental import pallas as pl
from jax.experimental.pallas import tpu as pltpu
from jax.sharding import PartitionSpec as P

BF16 = jnp.bfloat16
F32 = jnp.float32
ANY = pl.BlockSpec(memory_space=pl.ANY)
VMEM = pl.BlockSpec(memory_space=pltpu.VMEM)
SMEM = pl.BlockSpec(memory_space=pltpu.SMEM)

STEPS = ((0, 0), (0, 1), (0, 3), (1, 0), (0, 2), (1, 1), (1, 3), (1, 2))
SLABS = 8
HALF = 16
PAIR = 32
LOCAL = 8192
NODES = 65536
SLOTS = 32
ROWS = 32


def _index(x, y):
    return x * 4 + y


def _from_step(step):
    dx, dy = step
    return [(_index(x ^ dx, (y + dy) % 4), _index(x, y)) for x in range(2) for y in range(4)]


def _to_step(step):
    return [(b, a) for a, b in _from_step(step)]


CORE_SWAP = [(f, f ^ 1) for f in range(16)]
SAME_CORE = [list(range(0, 16, 2)), list(range(1, 16, 2))]


def swap(a):
    return lax.ppermute(a, "feat", CORE_SWAP)


def load_kernel(info, tiles, out, sems):
    core = info[0]
    copies = []
    for g in range(8):
        copies.append(
            pltpu.make_async_copy(
                tiles.at[pl.ds(8 * g + 4 * core, 4)], out.at[pl.ds(4 * g, 4)], sems.at[g]
            )
        )
    for c in copies:
        c.start()
    for c in copies:
        c.wait()


def load_tiles(info, tiles):
    return pl.pallas_call(
        load_kernel,
        out_shape=pltpu.VMEM((ROWS, SLOTS, 128, 128), BF16),
        in_specs=[SMEM, ANY],
        out_specs=VMEM,
        scratch_shapes=[pltpu.SemaphoreType.DMA((8,))],
        compiler_params=pltpu.CompilerParams(vmem_limit_bytes=2 << 20),
        cost_estimate=pl.CostEstimate(flops=0, bytes_accessed=64 << 20, transcendentals=0),
        name="load_tiles",
    )(info, tiles)


def row_of(core, local):
    return 8 * (local // 4) + 4 * core + local % 4


def lanes_of(block):
    return pl.ds(pl.multiple_of(block * 128, 128), 128)


def forward_kernel(info, cols, tiles, *refs):
    pieces, (out, feats, sems) = refs[:16], refs[16:]
    core = info[0]
    copies = []
    for d in range(SLABS):
        lanes = pl.ds(pl.multiple_of(info[1 + d] * LOCAL, LOCAL), LOCAL)
        for h in range(2):
            copies.append(
                pltpu.make_async_copy(
                    pieces[2 * d + h], feats.at[pl.ds(HALF * h, HALF), lanes], sems.at[2 * d + h]
                )
            )
    for c in copies:
        c.start()
    for c in copies:
        c.wait()

    def row(local, carry):
        r = row_of(core, local)
        total = jnp.zeros((PAIR, 128), F32)
        for p in range(0, SLOTS, 2):
            picked = jnp.concatenate(
                [feats[:, lanes_of(cols[r, p + i])] for i in range(2)], axis=1
            )
            pair = jnp.concatenate([tiles[local, p + i] for i in range(2)], axis=1)
            total += lax.dot_general(
                picked, pair, (((1,), (1,)), ((), ())), preferred_element_type=F32
            )
        out[local // 4, :, lanes_of(local % 4)] = total.astype(BF16)
        return carry

    lax.fori_loop(0, ROWS, row, 0)


def forward(info, cols, tiles, pieces):
    return pl.pallas_call(
        forward_kernel,
        out_shape=jax.ShapeDtypeStruct((8, PAIR, 512), BF16),
        in_specs=[SMEM, SMEM, VMEM] + [ANY] * 16,
        out_specs=VMEM,
        scratch_shapes=[pltpu.VMEM((PAIR, NODES), BF16), pltpu.SemaphoreType.DMA((16,))],
        compiler_params=pltpu.CompilerParams(vmem_limit_bytes=12 << 20),
        cost_estimate=pl.CostEstimate(
            flops=8 * 2 * 1024 * 128 * 128 * 32, bytes_accessed=8 << 20, transcendentals=0
        ),
        name="forward",
    )(info, cols, tiles, *pieces)


def flip_halves(value, core):
    parts = []
    for g in range(8):
        a = value[PAIR * g : PAIR * g + HALF]
        b = value[PAIR * g + HALF : PAIR * (g + 1)]
        parts += [jnp.where(core == 1, b, a), jnp.where(core == 1, a, b)]
    return jnp.concatenate(parts, axis=0)


def dense_kernel(info, agg_ref, side_ref, grad_ref, tail_ref):
    core = info[0]
    agg = agg_ref[...]
    weight = flip_halves(side_ref[:, 512:], core)
    pre = lax.dot_general(weight, agg, (((0,), (0,)), ((), ())), preferred_element_type=F32)
    sig = 1.0 / (1.0 + jnp.exp(-pre))
    tail_ref[:, :512] = (pre * sig).astype(BF16)
    pre_grad = (side_ref[:, :512].astype(F32) * sig * (1.0 + pre * (1.0 - sig))).astype(BF16)
    grad_ref[...] = jnp.dot(weight, pre_grad, preferred_element_type=F32).astype(BF16)
    wgrad = lax.dot_general(agg, pre_grad, (((1,), (1,)), ((), ())), preferred_element_type=F32)
    tail_ref[:, 512:] = flip_halves(wgrad, core).astype(BF16)


def dense(info, agg, side):
    return pl.pallas_call(
        dense_kernel,
        out_shape=(
            jax.ShapeDtypeStruct((256, 512), BF16),
            jax.ShapeDtypeStruct((256, 768), BF16),
        ),
        in_specs=[SMEM, VMEM, VMEM],
        out_specs=(VMEM, VMEM),
        compiler_params=pltpu.CompilerParams(vmem_limit_bytes=8 << 20),
        cost_estimate=pl.CostEstimate(
            flops=3 * 2 * 256 * 256 * 512, bytes_accessed=2 << 20, transcendentals=256 * 512
        ),
        name="dense",
    )(info, agg, side)


def backward_kernel(info, cols, tiles, grad, *refs):
    outs, (total, staged, sems) = refs[:16], refs[16:]
    core = info[0]

    def clear(i, carry):
        total[:, pl.ds(pl.multiple_of(i * 2048, 2048), 2048)] = jnp.zeros((PAIR, 2048), F32)
        return carry

    lax.fori_loop(0, NODES // 2048, clear, 0)

    def row(local, carry):
        r = row_of(core, local)
        g = grad[local // 4, :, lanes_of(local % 4)]
        for first in range(0, SLOTS, 8):
            blocks = [lanes_of(cols[r, first + i]) for i in range(8)]
            terms = []
            for i in range(0, 8, 2):
                pair = jnp.concatenate([tiles[local, first + i + k] for k in range(2)], axis=1)
                both = jnp.dot(g, pair, preferred_element_type=F32)
                terms += [both[:, :128], both[:, 128:]]
            sums = [total[:, blocks[i]] + terms[i] for i in range(8)]
            for i in range(8):
                total[:, blocks[i]] = sums[i]
        return carry

    lax.fori_loop(0, ROWS, row, 0)

    copies = []
    for h in (1, 0):
        rows = pl.ds(HALF * h, HALF)
        for d in range(SLABS):
            base = info[1 + d] * LOCAL
            lanes = pl.ds(pl.multiple_of(base, LOCAL), LOCAL)
            staged[rows, lanes] = total[rows, lanes].astype(BF16)
            copy = pltpu.make_async_copy(
                staged.at[rows, lanes], outs[8 * h + d], sems.at[8 * h + d]
            )
            copy.start()
            copies.append(copy)
    for c in copies:
        c.wait()


def backward(info, cols, tiles, grad):
    return pl.pallas_call(
        backward_kernel,
        out_shape=[jax.ShapeDtypeStruct((HALF, LOCAL), BF16)] * 16,
        in_specs=[SMEM, SMEM, VMEM, VMEM],
        out_specs=[ANY] * 16,
        scratch_shapes=[
            pltpu.VMEM((PAIR, NODES), F32),
            pltpu.VMEM((PAIR, NODES), BF16),
            pltpu.SemaphoreType.DMA((16,)),
        ],
        compiler_params=pltpu.CompilerParams(vmem_limit_bytes=20 << 20),
        cost_estimate=pl.CostEstimate(
            flops=8 * 2 * 1024 * 128 * 128 * 32, bytes_accessed=8 << 20, transcendentals=0
        ),
        name="backward",
    )(info, cols, tiles, grad)


def per_device(node_feats, weight, tiles, block_cols, cotangent):
    core = lax.axis_index("feat") % 2
    slab = lax.axis_index("blk")
    x, y = slab // 4, slab % 4
    info = jnp.stack([core] + [(x ^ dx) * 4 + (y + dy) % 4 for dx, dy in STEPS]).astype(jnp.int32)

    blocks = [node_feats] + [
        lax.ppermute(node_feats, "blk", _from_step(step)) for step in STEPS[1:]
    ]
    pieces = []
    for block in blocks:
        pieces += [block, swap(block)]
    held = pltpu.with_memory_space_constraint(load_tiles(info, tiles), pltpu.VMEM)

    side = jnp.concatenate(
        [
            jnp.transpose(cotangent.reshape(HALF, 16, 512), (1, 0, 2)),
            jnp.broadcast_to(weight[None], (16, HALF, 256)),
        ],
        axis=2,
    )
    side = lax.all_to_all(side, "feat", 0, 0, tiled=True).reshape(256, 768)

    agg = forward(info, block_cols, held, pieces)
    agg = lax.all_to_all(agg, "feat", 0, 0, axis_index_groups=SAME_CORE, tiled=True)
    grad, tail = dense(info, agg.reshape(256, 512), side)
    grad = lax.all_to_all(
        grad.reshape(8, PAIR, 512), "feat", 0, 0, axis_index_groups=SAME_CORE, tiled=True
    )
    parts = backward(info, block_cols, held, grad)
    own, other = parts[:8], parts[8:]
    summed = [own[d].astype(F32) + swap(other[d]).astype(F32) for d in range(SLABS)]
    total = summed[0]
    for d in range(1, SLABS):
        total = total + lax.ppermute(summed[d].astype(BF16), "blk", _to_step(STEPS[d])).astype(F32)
    feats_grad = total.astype(BF16)

    tail = lax.all_to_all(tail.reshape(16, HALF, 768), "feat", 0, 0, tiled=True)
    hidden = jnp.transpose(tail[:, :, :512], (1, 0, 2)).reshape(HALF, LOCAL)
    wgrad = jnp.sum(tail[:, :, 512:].astype(F32), axis=0)
    wgrad = lax.all_to_all(
        jnp.broadcast_to(wgrad[None], (SLABS, HALF, 256)), "blk", 0, 0, tiled=True
    )
    weight_grad = jnp.sum(wgrad, axis=0)
    return hidden, weight_grad, feats_grad


def solution(mesh):
    placed = (
        P("feat", "blk"),
        P("feat", None),
        P("blk", None, None, None),
        P("blk", None),
        P("feat", "blk"),
    )
    return jax.shard_map(
        per_device,
        mesh=mesh,
        in_specs=placed,
        out_specs=(P("feat", "blk"), P("feat", None), P("feat", "blk")),
        check_vma=False,
    )
```

time: 325 us -> 186 us (0.57)
  matrix products: 101 us -> 0 us
  waiting for transfers between devices: 132 us -> 33.7 us
  starting transfers between devices: 0.34 us -> 45.2 us
  Pallas kernels: 0 us -> 42.7 us
  blocking collectives: 58.5 us -> 27.6 us
  between operations: 13.8 us -> 0.98 us
  local copies, waits for them, and re-layouts: 19.7 us -> 27.9 us
  other arithmetic: 0 us -> 6.29 us
    all_gather x3 -> x0, waiting for transfers between devices: 128 us -> none  [the longest x1 53.1 us: per_device(): full_grad = lax.all_gather(pre_grad, 'feat', axis=0, tiled=True)]
    dot_general x8 -> x0, matrix products: 101 us -> none  [the longest x1 29.1 us: per_device(): jnp.einsum('drj,rpjk->rpdk', grad_blocks, tiles, preferred_element_type=j...]
    pallas_call x0 -> x4, Pallas kernels: none -> 42.7 us  [the longest x1 17.2 us: forward(): pl.pallas_call(forward_kernel, out_shape=jax.ShapeDtypeStruct((8, PAIR, 5...]
    psum x1 -> x0, blocking collectives: 33.9 us -> none  [per_device(): weight_grad = lax.psum(local_wgrad, 'blk')]
    ppermute x0 -> x30, starting transfers between devices: none -> 29.8 us  [the longest x7 13.8 us: per_device(): lax.ppermute(node_feats, 'blk', _from_step(step))]
    ppermute x0 -> x30, waiting for transfers between devices: none -> 27.7 us  [the longest x7 24.1 us: per_device(): lax.ppermute(node_feats, 'blk', _from_step(step))]
    all_to_all x0 -> x2, blocking collectives: none -> 27.6 us  [the longest x1 15.8 us: per_device(): lax.all_to_all(agg, 'feat', 0, 0, axis_index_groups=SAME_CORE, tiled=True)]
    all_gather x1 -> x0, blocking collectives: 24.6 us -> none  [per_device(): full_weight = lax.all_gather(weight, 'feat', axis=0, tiled=True)]
  transfers between devices with their start and end apart: 4 -> 33, of which waited for: 4 -> 6; matrix products, arithmetic and copies ran while one was open for 1% -> 4% of each run, Pallas kernels for 0% -> 15%
where the time goes in v1:
time: 186 us; the launch traced here: 184 us
  starting transfers between devices  45.2 us (24%)
  Pallas kernels  42.7 us (23%)
  waiting for transfers between devices  33.7 us (18%)
  local copies, waits for them, and re-layouts  27.9 us (15%)
  blocking collectives  27.6 us (15%)
  other arithmetic  6.29 us (3%)
    unnamed x16, local copies, waits for them, and re-layouts  24.8 us
    ppermute x7, waiting for transfers between devices, per_device(): lax.ppermute(node_feats, 'blk', _from_step(step))  24.1 us
    pallas_call x1, Pallas kernels, forward(): pl.pallas_call(forward_kernel, out_shape=jax.ShapeDtypeStruct((8, PAIR, 5...  17.2 us
    all_to_all x1, blocking collectives, per_device(): lax.all_to_all(agg, 'feat', 0, 0, axis_index_groups=SAME_CORE, tiled=True)  15.8 us
    ppermute x7, starting transfers between devices, per_device(): lax.ppermute(node_feats, 'blk', _from_step(step))  13.8 us
    ppermute x7, starting transfers between devices, per_device(): lax.ppermute(summed[d].astype(BF16), 'blk', _to_step(STEPS[d])).astype(F32)  12.6 us
    pallas_call x1, Pallas kernels, backward(): pl.pallas_call(backward_kernel, out_shape=[jax.ShapeDtypeStruct((HALF, LO...  12.2 us
    all_to_all x1, blocking collectives, per_device(): lax.all_to_all(grad.reshape(8, PAIR, 512), 'feat', 0, 0, axis_index_group...  11.8 us
  transfers between devices with their start and end apart: 33, of which 6 were waited for; matrix products, arithmetic and copies ran while one was open for 4% of the time, Pallas kernels for 15%

profile of v1, /device:TPU:0, one launch (start us, length us, event | category | flops | bytes accessed | tf_op | source)
XLA Modules:
  0.0 184.3 jit_solution(3999524725884256440)
XLA Ops:
  0.7 3.2 %collective-permute-start.1 = (bf16[16,8192]{1,0:T(8,128)(2,1)}, bf16[16,8192]{1,0:T(8,128)(2,1)S(1)}, u32[]{:S(2)}, u32[]{:S(2)}) collective-permute-start(bf16[16,8192]{1,0:T(8,128)(2,1)} %refs_0_.1), channel_id=1, source_target_pairs={{16,0},{32,16},{48,32},{0,48},{80,64},{96,80},{112,96},{64,112},{1... | collective-permute-start | bytes 786440 | tf_op jit(solution)/shard_map/ppermute | solution.py:240
  3.9 1.5 collective-permute-start.5
  5.4 2.2 %collective-permute-start.7 = (bf16[16,8192]{1,0:T(8,128)(2,1)}, bf16[16,8192]{1,0:T(8,128)(2,1)S(1)}, u32[]{:S(2)}, u32[]{:S(2)}) collective-permute-start(bf16[16,8192]{1,0:T(8,128)(2,1)} %refs_0_.1), channel_id=1, source_target_pairs={{32,0},{48,16},{0,32},{16,48},{96,64},{112,80},{64,96},{80,112},{3... | collective-permute-start | bytes 786440 | tf_op jit(solution)/shard_map/ppermute | solution.py:240
  7.6 1.0 collective-permute-start.9
  8.6 13.0 %collective-permute-done.1.refs_2_ = bf16[16,8192]{1,0:T(8,128)(2,1)S(1)} collective-permute-done((bf16[16,8192]{1,0:T(8,128)(2,1)}, bf16[16,8192]{1,0:T(8,128)(2,1)S(1)}, u32[]{:S(2)}, u32[]{:S(2)}) %collective-permute-start.1) | collective-permute-done | bytes 262176 | tf_op jit(solution)/shard_map/ppermute | solution.py:240
  21.7 5.9 %collective-permute-start.13 = (bf16[16,8192]{1,0:T(8,128)(2,1)}, bf16[16,8192]{1,0:T(8,128)(2,1)S(1)}, u32[]{:S(2)}, u32[]{:S(2)}) collective-permute-start(bf16[16,8192]{1,0:T(8,128)(2,1)} %refs_0_.1), channel_id=1, source_target_pairs={{96,0},{112,16},{64,32},{80,48},{32,64},{48,80},{0,96},{16,112},{9... | collective-permute-start | bytes 786440 | tf_op jit(solution)/shard_map/ppermute | solution.py:240
  28.2 5.3 %collective-permute-done.11.refs_12_ = bf16[16,8192]{1,0:T(8,128)(2,1)S(1)} collective-permute-done((bf16[16,8192]{1,0:T(8,128)(2,1)}, bf16[16,8192]{1,0:T(8,128)(2,1)S(1)}, u32[]{:S(2)}, u32[]{:S(2)}) %collective-permute-start.11) | collective-permute-done | bytes 262176 | tf_op jit(solution)/shard_map/ppermute | solution.py:240
  33.5 5.7 %collective-permute-done.13.refs_14_ = bf16[16,8192]{1,0:T(8,128)(2,1)S(1)} collective-permute-done((bf16[16,8192]{1,0:T(8,128)(2,1)}, bf16[16,8192]{1,0:T(8,128)(2,1)S(1)}, u32[]{:S(2)}, u32[]{:S(2)}) %collective-permute-start.13) | collective-permute-done | bytes 262176 | tf_op jit(solution)/shard_map/ppermute | solution.py:240
  40.5 1.0 copy.19
  42.1 0.8 pad_maximum_fusion
  42.9 8.0 %all-to-all-start.1 = ((bf16[16,16,768]{2,1,0:T(8,128)(2,1)}), bf16[16,16,768]{2,1,0:T(8,128)(2,1)S(1)}, u32[]{:S(2)}, u32[]{:S(2)}) async-start(bf16[16,16,768]{2,1,0:T(8,128)(2,1)} %pad_maximum_fusion), calls=%async_computation.1 | async-start | bytes 786432 | tf_op jit(solution)/shard_map/all_to_all | solution.py:254
  51.0 0.8 copy.12.cols
  51.9 11.3 %load_tiles.1.tiles = bf16[32,32,128,128]{3,2,1,0:T(8,128)(2,1)S(1)} custom-call(s32[9]{0:T(128)S(1)} %stack.39.info, bf16[64,32,128,128]{3,2,1,0:T(8,128)(2,1)} %tiles.1), custom_call_target="tpu_custom_call" | custom-call | bytes 67108864 | tf_op jit(solution)/shard_map/load_tiles/pallas_call | solution.py:63
  64.0 0.9 copy-done.6
  64.9 17.2 %forward.1 = bf16[8,32,512]{2,1,0:T(8,128)(2,1)S(1)} custom-call(s32[9]{0:T(128)S(1)} %stack.39.info, s32[64,32]{1,0:T(8,128)S(1)} %copy.12.cols, bf16[32,32,128,128]{3,2,1,0:T(8,128)(2,1)S(1)} %load_tiles.1.tiles, bf16[16,8192]{1,0:T(8,128)(2,1)S(1)} %copy-done.2, bf16[16,8192]{1,0:T(8,128)(2,1)S(1)} %collective-permute-done.refs_1_, ...), custom_call_target="tpu_custom_call" | custom-call | flops 8589934592 | bytes 8388608 | tf_op jit(solution)/shard_map/forward/pallas_call | solution.py:118
  82.1 11.1 %copy-done = bf16[32,32,128,128]{3,2,1,0:T(8,128)(2,1)} copy-done((bf16[32,32,128,128]{3,2,1,0:T(8,128)(2,1)}, bf16[32,32,128,128]{3,2,1,0:T(8,128)(2,1)S(1)}, u32[]{:S(2)}) %copy-start) | copy-done | bytes 33554456
  93.2 15.8 %all_to_all.25 = bf16[8,32,512]{2,1,0:T(8,128)(2,1)S(1)} all-to-all(bf16[8,32,512]{2,1,0:T(8,128)(2,1)S(1)} %forward.1), channel_id=1, replica_groups={{0,2,4,6,8,10,12,14},{1,3,5,7,9,11,13,15},{16,18,20,22,24,26,28,30},{17..., dimensions={0} | all-to-all | bytes 524288 | tf_op jit(solution)/shard_map/all_to_all | solution.py:257
  109.0 2.0 %dense.1 = (bf16[256,512]{1,0:T(8,128)(2,1)S(1)}, bf16[256,768]{1,0:T(8,128)(2,1)}) custom-call(s32[9]{0:T(128)S(1)} %stack.39.info, bf16[256,512]{1,0:T(8,128)(2,1)S(1)} %bitcast.25, bf16[256,768]{1,0:T(8,128)(2,1)S(1)} %bitcast.24), custom_call_target="tpu_custom_call" | custom-call | flops 201326592 | bytes 2097152 | tf_op jit(solution)/shard_map/dense/pallas_call | solution.py:155
  111.0 11.8 %all_to_all.26.grad = bf16[8,32,512]{2,1,0:T(8,128)(2,1)} all-to-all(bf16[8,32,512]{2,1,0:T(8,128)(2,1)S(1)} %bitcast.26), channel_id=1, replica_groups={{0,2,4,6,8,10,12,14},{1,3,5,7,9,11,13,15},{16,18,20,22,24,26,28,30},{17..., dimensions={0} | all-to-all | bytes 524288 | tf_op jit(solution)/shard_map/all_to_all | solution.py:259
  122.7 10.5 %copy-done.1 = bf16[32,32,128,128]{3,2,1,0:T(8,128)(2,1)S(1)} copy-done((bf16[32,32,128,128]{3,2,1,0:T(8,128)(2,1)S(1)}, bf16[32,32,128,128]{3,2,1,0:T(8,128)(2,1)}, u32[]{:S(2)}) %copy-start.1) | copy-done | bytes 33554456
  133.3 12.2 %backward.1 = (bf16[16,8192]{1,0:T(8,128)(2,1)S(1)}, bf16[16,8192]{1,0:T(8,128)(2,1)S(1)}, bf16[16,8192]{1,0:T(8,128)(2,1)S(1)}, bf16[16,8192]{1,0:T(8,128)(2,1)...) custom-call(s32[9]{0:T(128)S(1)} %stack.39.info, ...), custom_call_target="tpu_custom_call" | custom-call | flops 8589934592 | bytes 8388608 | tf_op jit(solution)/shard_map/backward/pallas_call | solution.py:215
  145.6 3.6 %all-to-all-start.2 = ((bf16[16,16,768]{2,1,0:T(8,128)(2,1)}), bf16[16,16,768]{2,1,0:T(8,128)(2,1)S(1)}, u32[]{:S(2)}, u32[]{:S(2)}) async-start(bf16[16,16,768]{2,1,0:T(8,128)(2,1)} %bitcast.12), calls=%async_computation.2 | async-start | bytes 786432 | tf_op jit(solution)/shard_map/all_to_all | solution.py:270
  150.7 1.0 add_convert_fusion.1
  152.7 3.0 %collective-permute-start.27 = (bf16[16,8192]{1,0:T(8,128)(2,1)S(1)}, bf16[16,8192]{1,0:T(8,128)(2,1)S(1)}, u32[]{:S(2)}, u32[]{:S(2)}) collective-permute-start(bf16[16,8192]{1,0:T(8,128)(2,1)S(1)} %add_convert_fusion.2), channel_id=1, source_target_pairs={{0,112},{16,64},{32,80},{48,96},{64,48},{80,0},{96,16},{112,32},{1... | collective-permute-start | bytes 786440 | tf_op jit(solution)/shard_map/ppermute | solution.py:267
  156.7 3.5 %collective-permute-start.23 = (bf16[16,8192]{1,0:T(8,128)(2,1)S(1)}, bf16[16,8192]{1,0:T(8,128)(2,1)S(1)}, u32[]{:S(2)}, u32[]{:S(2)}) collective-permute-start(bf16[16,8192]{1,0:T(8,128)(2,1)S(1)} %add_convert_fusion.4), channel_id=1, source_target_pairs={{0,32},{16,48},{32,0},{48,16},{64,96},{80,112},{96,64},{112,80},{1... | collective-permute-start | bytes 786440 | tf_op jit(solution)/shard_map/ppermute | solution.py:267
  161.0 1.4 collective-permute-start.21
  162.4 1.8 collective-permute-done.29
  164.2 1.8 collective-permute-done.27
  166.0 4.5 %collective-permute-start.17 = (bf16[16,8192]{1,0:T(8,128)(2,1)}, bf16[16,8192]{1,0:T(8,128)(2,1)}, u32[]{:S(2)}, u32[]{:S(2)}) collective-permute-start(bf16[16,8192]{1,0:T(8,128)(2,1)} %add_convert_fusion.7), channel_id=1, source_target_pairs={{0,16},{16,32},{32,48},{48,0},{64,80},{80,96},{96,112},{112,64},{1... | collective-permute-start | bytes 786440 | tf_op jit(solution)/shard_map/ppermute | solution.py:267
  171.1 3.8 %all-to-all-start.3 = ((f32[8,16,256]{2,1,0:T(8,128)}), f32[8,16,256]{2,1,0:T(8,128)S(1)}, u32[]{:S(2)}, u32[]{:S(2)}) async-start(f32[8,16,256]{2,1,0:T(8,128)} %broadcast_in_dim.5), calls=%async_computation.3 | async-start | bytes 262144 | tf_op jit(solution)/shard_map/all_to_all | solution.py:273
  175.7 6.0 %all-to-all-done.3 = f32[8,16,256]{2,1,0:T(8,128)S(1)} async-done(((f32[8,16,256]{2,1,0:T(8,128)}), f32[8,16,256]{2,1,0:T(8,128)S(1)}, u32[]{:S(2)}, u32[]{:S(2)}) %all-to-all-start.3) | async-done | bytes 131104 | tf_op jit(solution)/shard_map/all_to_all | solution.py:273
  182.3 2.0 %add_convert_fusion = bf16[16,8192]{1,0:T(8,128)(2,1)} fusion(bf16[16,8192]{1,0:T(8,128)(2,1)S(1)} %collective-permute-done.29, bf16[16,8192]{1,0:T(8,128)(2,1)S(1)} %collective-permute-done.27, bf16[16,8192]{1,0:T(8,128)(2,1)S(1)} %collective-permute-done.25, bf16[16,8192]{1,0:T(8,128)(2,1)S(1)} %collective-permute-done.23, ...), kind=kLoop, calls=%fused_computation | loop fusion | flops 2359296 | bytes 2621440 | tf_op jit(solution)/shard_map/convert_element_type | solution.py:268
  (72 shorter events, 9.7 us)
Async XLA Ops:
  0.6 7.0 %collective-permute-start = (bf16[16,8192]{1,0:T(8,128)(2,1)}, bf16[16,8192]{1,0:T(8,128)(2,1)S(1)}, u32[]{:S(2)}, u32[]{:S(2)}) collective-permute-start(bf16[16,8192]{1,0:T(8,128)(2,1)} %refs_0_.1), channel_id=1, source_target_pairs={{0,1},{1,0},{2,3},{3,2},{4,5},{5,4},{6,7},{7,6},{8,9},{9,8},{10,11... | collective-permute-start | bytes 786440 | tf_op jit(solution)/shard_map/ppermute | solution.py:44
  0.7 20.9 %collective-permute-start.1 = (bf16[16,8192]{1,0:T(8,128)(2,1)}, bf16[16,8192]{1,0:T(8,128)(2,1)S(1)}, u32[]{:S(2)}, u32[]{:S(2)}) collective-permute-start(bf16[16,8192]{1,0:T(8,128)(2,1)} %refs_0_.1), channel_id=1, source_target_pairs={{16,0},{32,16},{48,32},{0,48},{80,64},{96,80},{112,96},{64,112},{1... | collective-permute-start | bytes 786440 | tf_op jit(solution)/shard_map/ppermute | solution.py:240
  3.9 17.8 %collective-permute-start.3 = (bf16[16,8192]{1,0:T(8,128)(2,1)}, bf16[16,8192]{1,0:T(8,128)(2,1)S(1)}, u32[]{:S(2)}, u32[]{:S(2)}) collective-permute-start(bf16[16,8192]{1,0:T(8,128)(2,1)} %refs_0_.1), channel_id=1, source_target_pairs={{48,0},{0,16},{16,32},{32,48},{112,64},{64,80},{80,96},{96,112},{4... | collective-permute-start | bytes 786440 | tf_op jit(solution)/shard_map/ppermute | solution.py:240
  3.9 23.7 %collective-permute-start.5 = (bf16[16,8192]{1,0:T(8,128)(2,1)}, bf16[16,8192]{1,0:T(8,128)(2,1)S(1)}, u32[]{:S(2)}, u32[]{:S(2)}) collective-permute-start(bf16[16,8192]{1,0:T(8,128)(2,1)} %refs_0_.1), channel_id=1, source_target_pairs={{64,0},{80,16},{96,32},{112,48},{0,64},{16,80},{32,96},{48,112},{6... | collective-permute-start | bytes 786440 | tf_op jit(solution)/shard_map/ppermute | solution.py:240
  5.4 22.2 %collective-permute-start.7 = (bf16[16,8192]{1,0:T(8,128)(2,1)}, bf16[16,8192]{1,0:T(8,128)(2,1)S(1)}, u32[]{:S(2)}, u32[]{:S(2)}) collective-permute-start(bf16[16,8192]{1,0:T(8,128)(2,1)} %refs_0_.1), channel_id=1, source_target_pairs={{32,0},{48,16},{0,32},{16,48},{96,64},{112,80},{64,96},{80,112},{3... | collective-permute-start | bytes 786440 | tf_op jit(solution)/shard_map/ppermute | solution.py:240
  7.6 20.5 %collective-permute-start.9 = (bf16[16,8192]{1,0:T(8,128)(2,1)}, bf16[16,8192]{1,0:T(8,128)(2,1)S(1)}, u32[]{:S(2)}, u32[]{:S(2)}) collective-permute-start(bf16[16,8192]{1,0:T(8,128)(2,1)} %refs_0_.1), channel_id=1, source_target_pairs={{80,0},{96,16},{112,32},{64,48},{16,64},{32,80},{48,96},{0,112},{8... | collective-permute-start | bytes 786440 | tf_op jit(solution)/shard_map/ppermute | solution.py:240
  21.7 11.9 %collective-permute-start.11 = (bf16[16,8192]{1,0:T(8,128)(2,1)}, bf16[16,8192]{1,0:T(8,128)(2,1)S(1)}, u32[]{:S(2)}, u32[]{:S(2)}) collective-permute-start(bf16[16,8192]{1,0:T(8,128)(2,1)} %refs_0_.1), channel_id=1, source_target_pairs={{112,0},{64,16},{80,32},{96,48},{48,64},{0,80},{16,96},{32,112},{1... | collective-permute-start | bytes 786440 | tf_op jit(solution)/shard_map/ppermute | solution.py:240
  21.7 17.6 %collective-permute-start.13 = (bf16[16,8192]{1,0:T(8,128)(2,1)}, bf16[16,8192]{1,0:T(8,128)(2,1)S(1)}, u32[]{:S(2)}, u32[]{:S(2)}) collective-permute-start(bf16[16,8192]{1,0:T(8,128)(2,1)} %refs_0_.1), channel_id=1, source_target_pairs={{96,0},{112,16},{64,32},{80,48},{32,64},{48,80},{0,96},{16,112},{9... | collective-permute-start | bytes 786440 | tf_op jit(solution)/shard_map/ppermute | solution.py:240
  27.6 11.7 %collective-permute-start.2 = (bf16[16,8192]{1,0:T(8,128)(2,1)S(1)}, bf16[16,8192]{1,0:T(8,128)(2,1)S(1)}, u32[]{:S(2)}, u32[]{:S(2)}) collective-permute-start(bf16[16,8192]{1,0:T(8,128)(2,1)S(1)} %collective-permute-done.1.refs_2_), channel_id=1, source_target_pairs={{0,1},{1,0},{2,3},{3,2},{4,5},{5,4},{6,7},{7,6},{8,9},{9,8},{10,11... | collective-permute-start | bytes 786440 | tf_op jit(solution)/shard_map/ppermute | solution.py:44
  27.6 12.2 %collective-permute-start.4 = (bf16[16,8192]{1,0:T(8,128)(2,1)S(1)}, bf16[16,8192]{1,0:T(8,128)(2,1)S(1)}, u32[]{:S(2)}, u32[]{:S(2)}) collective-permute-start(bf16[16,8192]{1,0:T(8,128)(2,1)S(1)} %collective-permute-done.3.refs_4_), channel_id=1, source_target_pairs={{0,1},{1,0},{2,3},{3,2},{4,5},{5,4},{6,7},{7,6},{8,9},{9,8},{10,11... | collective-permute-start | bytes 786440 | tf_op jit(solution)/shard_map/ppermute | solution.py:44
  28.1 35.1 %collective-permute-start.6 = (bf16[16,8192]{1,0:T(8,128)(2,1)S(1)}, bf16[16,8192]{1,0:T(8,128)(2,1)S(1)}, u32[]{:S(2)}, u32[]{:S(2)}) collective-permute-start(bf16[16,8192]{1,0:T(8,128)(2,1)S(1)} %collective-permute-done.5.refs_6_), channel_id=1, source_target_pairs={{0,1},{1,0},{2,3},{3,2},{4,5},{5,4},{6,7},{7,6},{8,9},{9,8},{10,11... | collective-permute-start | bytes 786440 | tf_op jit(solution)/shard_map/ppermute | solution.py:44
  33.5 30.4 %collective-permute-start.8 = (bf16[16,8192]{1,0:T(8,128)(2,1)S(1)}, bf16[16,8192]{1,0:T(8,128)(2,1)}, u32[]{:S(2)}, u32[]{:S(2)}) collective-permute-start(bf16[16,8192]{1,0:T(8,128)(2,1)S(1)} %collective-permute-done.7.refs_8_), channel_id=1, source_target_pairs={{0,1},{1,0},{2,3},{3,2},{4,5},{5,4},{6,7},{7,6},{8,9},{9,8},{10,11... | collective-permute-start | bytes 786440 | tf_op jit(solution)/shard_map/ppermute | solution.py:44
  39.2 24.7 %collective-permute-start.10 = (bf16[16,8192]{1,0:T(8,128)(2,1)S(1)}, bf16[16,8192]{1,0:T(8,128)(2,1)}, u32[]{:S(2)}, u32[]{:S(2)}) collective-permute-start(bf16[16,8192]{1,0:T(8,128)(2,1)S(1)} %collective-permute-done.9.refs_10_), channel_id=1, source_target_pairs={{0,1},{1,0},{2,3},{3,2},{4,5},{5,4},{6,7},{7,6},{8,9},{9,8},{10,11... | collective-permute-start | bytes 786440 | tf_op jit(solution)/shard_map/ppermute | solution.py:44
  39.2 24.7 %collective-permute-start.12 = (bf16[16,8192]{1,0:T(8,128)(2,1)S(1)}, bf16[16,8192]{1,0:T(8,128)(2,1)}, u32[]{:S(2)}, u32[]{:S(2)}) collective-permute-start(bf16[16,8192]{1,0:T(8,128)(2,1)S(1)} %collective-permute-done.11.refs_12_), channel_id=1, source_target_pairs={{0,1},{1,0},{2,3},{3,2},{4,5},{5,4},{6,7},{7,6},{8,9},{9,8},{10,11... | collective-permute-start | bytes 786440 | tf_op jit(solution)/shard_map/ppermute | solution.py:44
  40.5 23.5 %collective-permute-start.14 = (bf16[16,8192]{1,0:T(8,128)(2,1)S(1)}, bf16[16,8192]{1,0:T(8,128)(2,1)}, u32[]{:S(2)}, u32[]{:S(2)}) collective-permute-start(bf16[16,8192]{1,0:T(8,128)(2,1)S(1)} %collective-permute-done.13.refs_14_), channel_id=1, source_target_pairs={{0,1},{1,0},{2,3},{3,2},{4,5},{5,4},{6,7},{7,6},{8,9},{9,8},{10,11... | collective-permute-start | bytes 786440 | tf_op jit(solution)/shard_map/ppermute | solution.py:44
  42.9 50.2 %all-to-all-start.1 = ((bf16[16,16,768]{2,1,0:T(8,128)(2,1)}), bf16[16,16,768]{2,1,0:T(8,128)(2,1)S(1)}, u32[]{:S(2)}, u32[]{:S(2)}) async-start(bf16[16,16,768]{2,1,0:T(8,128)(2,1)} %pad_maximum_fusion), calls=%async_computation.1 | async-start | bytes 786432 | tf_op jit(solution)/shard_map/all_to_all | solution.py:254
  145.5 4.8 %collective-permute-start.28 = (bf16[16,8192]{1,0:T(8,128)(2,1)}, bf16[16,8192]{1,0:T(8,128)(2,1)S(1)}, u32[]{:S(2)}, u32[]{:S(2)}) collective-permute-start(bf16[16,8192]{1,0:T(8,128)(2,1)} %get-tuple-element.38), channel_id=1, source_target_pairs={{0,1},{1,0},{2,3},{3,2},{4,5},{5,4},{6,7},{7,6},{8,9},{9,8},{10,11... | collective-permute-start | bytes 786440 | tf_op jit(solution)/shard_map/ppermute | solution.py:44
  145.6 24.8 %all-to-all-start.2 = ((bf16[16,16,768]{2,1,0:T(8,128)(2,1)}), bf16[16,16,768]{2,1,0:T(8,128)(2,1)S(1)}, u32[]{:S(2)}, u32[]{:S(2)}) async-start(bf16[16,16,768]{2,1,0:T(8,128)(2,1)} %bitcast.12), calls=%async_computation.2 | async-start | bytes 786432 | tf_op jit(solution)/shard_map/all_to_all | solution.py:270
  149.2 2.5 %collective-permute-start.26 = (bf16[16,8192]{1,0:T(8,128)(2,1)}, bf16[16,8192]{1,0:T(8,128)(2,1)S(1)}, u32[]{:S(2)}, u32[]{:S(2)}) collective-permute-start(bf16[16,8192]{1,0:T(8,128)(2,1)} %get-tuple-element.36), channel_id=1, source_target_pairs={{0,1},{1,0},{2,3},{3,2},{4,5},{5,4},{6,7},{7,6},{8,9},{9,8},{10,11... | collective-permute-start | bytes 786440 | tf_op jit(solution)/shard_map/ppermute | solution.py:44
  149.8 2.7 %collective-permute-start.22 = (bf16[16,8192]{1,0:T(8,128)(2,1)}, bf16[16,8192]{1,0:T(8,128)(2,1)S(1)}, u32[]{:S(2)}, u32[]{:S(2)}) collective-permute-start(bf16[16,8192]{1,0:T(8,128)(2,1)} %get-tuple-element.32), channel_id=1, source_target_pairs={{0,1},{1,0},{2,3},{3,2},{4,5},{5,4},{6,7},{7,6},{8,9},{9,8},{10,11... | collective-permute-start | bytes 786440 | tf_op jit(solution)/shard_map/ppermute | solution.py:44
  150.2 2.5 %collective-permute-start.20 = (bf16[16,8192]{1,0:T(8,128)(2,1)}, bf16[16,8192]{1,0:T(8,128)(2,1)S(1)}, u32[]{:S(2)}, u32[]{:S(2)}) collective-permute-start(bf16[16,8192]{1,0:T(8,128)(2,1)} %get-tuple-element.30), channel_id=1, source_target_pairs={{0,1},{1,0},{2,3},{3,2},{4,5},{5,4},{6,7},{7,6},{8,9},{9,8},{10,11... | collective-permute-start | bytes 786440 | tf_op jit(solution)/shard_map/ppermute | solution.py:44
  150.3 5.5 %collective-permute-start.18 = (bf16[16,8192]{1,0:T(8,128)(2,1)}, bf16[16,8192]{1,0:T(8,128)(2,1)S(1)}, u32[]{:S(2)}, u32[]{:S(2)}) collective-permute-start(bf16[16,8192]{1,0:T(8,128)(2,1)} %get-tuple-element.28), channel_id=1, source_target_pairs={{0,1},{1,0},{2,3},{3,2},{4,5},{5,4},{6,7},{7,6},{8,9},{9,8},{10,11... | collective-permute-start | bytes 786440 | tf_op jit(solution)/shard_map/ppermute | solution.py:44
  151.7 5.0 %collective-permute-start.16 = (bf16[16,8192]{1,0:T(8,128)(2,1)}, bf16[16,8192]{1,0:T(8,128)(2,1)S(1)}, u32[]{:S(2)}, u32[]{:S(2)}) collective-permute-start(bf16[16,8192]{1,0:T(8,128)(2,1)} %get-tuple-element.26), channel_id=1, source_target_pairs={{0,1},{1,0},{2,3},{3,2},{4,5},{5,4},{6,7},{7,6},{8,9},{9,8},{10,11... | collective-permute-start | bytes 786440 | tf_op jit(solution)/shard_map/ppermute | solution.py:44
  152.0 9.0 %collective-permute-start.15 = (bf16[16,8192]{1,0:T(8,128)(2,1)}, bf16[16,8192]{1,0:T(8,128)(2,1)S(1)}, u32[]{:S(2)}, u32[]{:S(2)}) collective-permute-start(bf16[16,8192]{1,0:T(8,128)(2,1)} %get-tuple-element.24), channel_id=1, source_target_pairs={{0,1},{1,0},{2,3},{3,2},{4,5},{5,4},{6,7},{7,6},{8,9},{9,8},{10,11... | collective-permute-start | bytes 786440 | tf_op jit(solution)/shard_map/ppermute | solution.py:44
  152.5 11.7 %collective-permute-start.29 = (bf16[16,8192]{1,0:T(8,128)(2,1)S(1)}, bf16[16,8192]{1,0:T(8,128)(2,1)S(1)}, u32[]{:S(2)}, u32[]{:S(2)}) collective-permute-start(bf16[16,8192]{1,0:T(8,128)(2,1)S(1)} %add_convert_fusion.1), channel_id=1, source_target_pairs={{0,96},{16,112},{32,64},{48,80},{64,32},{80,48},{96,0},{112,16},{1... | collective-permute-start | bytes 786440 | tf_op jit(solution)/shard_map/ppermute | solution.py:267
  152.7 13.3 %collective-permute-start.27 = (bf16[16,8192]{1,0:T(8,128)(2,1)S(1)}, bf16[16,8192]{1,0:T(8,128)(2,1)S(1)}, u32[]{:S(2)}, u32[]{:S(2)}) collective-permute-start(bf16[16,8192]{1,0:T(8,128)(2,1)S(1)} %add_convert_fusion.2), channel_id=1, source_target_pairs={{0,112},{16,64},{32,80},{48,96},{64,48},{80,0},{96,16},{112,32},{1... | collective-permute-start | bytes 786440 | tf_op jit(solution)/shard_map/ppermute | solution.py:267
  155.8 26.4 %collective-permute-start.25 = (bf16[16,8192]{1,0:T(8,128)(2,1)S(1)}, bf16[16,8192]{1,0:T(8,128)(2,1)S(1)}, u32[]{:S(2)}, u32[]{:S(2)}) collective-permute-start(bf16[16,8192]{1,0:T(8,128)(2,1)S(1)} %add_convert_fusion.3), channel_id=1, source_target_pairs={{0,80},{16,96},{32,112},{48,64},{64,16},{80,32},{96,48},{112,0},{1... | collective-permute-start | bytes 786440 | tf_op jit(solution)/shard_map/ppermute | solution.py:267
  156.7 25.6 %collective-permute-start.23 = (bf16[16,8192]{1,0:T(8,128)(2,1)S(1)}, bf16[16,8192]{1,0:T(8,128)(2,1)S(1)}, u32[]{:S(2)}, u32[]{:S(2)}) collective-permute-start(bf16[16,8192]{1,0:T(8,128)(2,1)S(1)} %add_convert_fusion.4), channel_id=1, source_target_pairs={{0,32},{16,48},{32,0},{48,16},{64,96},{80,112},{96,64},{112,80},{1... | collective-permute-start | bytes 786440 | tf_op jit(solution)/shard_map/ppermute | solution.py:267
  161.0 21.3 %collective-permute-start.21 = (bf16[16,8192]{1,0:T(8,128)(2,1)S(1)}, bf16[16,8192]{1,0:T(8,128)(2,1)S(1)}, u32[]{:S(2)}, u32[]{:S(2)}) collective-permute-start(bf16[16,8192]{1,0:T(8,128)(2,1)S(1)} %add_convert_fusion.5), channel_id=1, source_target_pairs={{0,64},{16,80},{32,96},{48,112},{64,0},{80,16},{96,32},{112,48},{1... | collective-permute-start | bytes 786440 | tf_op jit(solution)/shard_map/ppermute | solution.py:267
  164.2 18.1 %collective-permute-start.19 = (bf16[16,8192]{1,0:T(8,128)(2,1)}, bf16[16,8192]{1,0:T(8,128)(2,1)}, u32[]{:S(2)}, u32[]{:S(2)}) collective-permute-start(bf16[16,8192]{1,0:T(8,128)(2,1)} %add_convert_fusion.6), channel_id=1, source_target_pairs={{0,48},{16,0},{32,16},{48,32},{64,112},{80,64},{96,80},{112,96},{1... | collective-permute-start | bytes 786440 | tf_op jit(solution)/shard_map/ppermute | solution.py:267
  166.0 16.3 %collective-permute-start.17 = (bf16[16,8192]{1,0:T(8,128)(2,1)}, bf16[16,8192]{1,0:T(8,128)(2,1)}, u32[]{:S(2)}, u32[]{:S(2)}) collective-permute-start(bf16[16,8192]{1,0:T(8,128)(2,1)} %add_convert_fusion.7), channel_id=1, source_target_pairs={{0,16},{16,32},{32,48},{48,0},{64,80},{80,96},{96,112},{112,64},{1... | collective-permute-start | bytes 786440 | tf_op jit(solution)/shard_map/ppermute | solution.py:267
  171.1 10.5 %all-to-all-start.3 = ((f32[8,16,256]{2,1,0:T(8,128)}), f32[8,16,256]{2,1,0:T(8,128)S(1)}, u32[]{:S(2)}, u32[]{:S(2)}) async-start(f32[8,16,256]{2,1,0:T(8,128)} %broadcast_in_dim.5), calls=%async_computation.3 | async-start | bytes 262144 | tf_op jit(solution)/shard_map/all_to_all | solution.py:273
  (8 other events, 101.6 us)

commit v2 on v1

v2 whole, which is shorter than its diff:
```python
import functools

import jax
import jax.numpy as jnp
from jax import lax
from jax.experimental import pallas as pl
from jax.experimental.pallas import tpu as pltpu
from jax.sharding import PartitionSpec as P

BF16 = jnp.bfloat16
F32 = jnp.float32
ANY = pl.BlockSpec(memory_space=pl.ANY)
VMEM = pl.BlockSpec(memory_space=pltpu.VMEM)
SMEM = pl.BlockSpec(memory_space=pltpu.SMEM)

STEPS = ((0, 0), (0, 1), (0, 3), (1, 0), (0, 2), (1, 1), (1, 3), (1, 2))
SLABS = 8
HALF = 16
PAIR = 32
LOCAL = 8192
NODES = 65536
SLOTS = 32
ROWS = 32
HELD = 16
RING = 6


def _index(x, y):
    return x * 4 + y


def _from_step(step):
    dx, dy = step
    return [(_index(x ^ dx, (y + dy) % 4), _index(x, y)) for x in range(2) for y in range(4)]


def _to_step(step):
    return [(b, a) for a, b in _from_step(step)]


CORE_SWAP = [(f, f ^ 1) for f in range(16)]
SAME_CORE = [list(range(0, 16, 2)), list(range(1, 16, 2))]


def swap(a):
    return lax.ppermute(a, "feat", CORE_SWAP)


def row_of(core, local):
    return 8 * (local // 4) + 4 * core + local % 4


def lanes_of(block):
    return pl.ds(pl.multiple_of(block * 128, 128), 128)


def prepare_kernel(info, first, second, ship, rest):
    core = info[0]
    low = jnp.where(core == 0, first[...], second[...])
    high = jnp.where(core == 0, second[...], first[...])
    both = jnp.concatenate([low, high], axis=0)
    tiles = []
    for m in range(16):
        stacked = jnp.concatenate(
            [both[:, 128 * q : 128 * (q + 1)] for q in range(4 * m, 4 * m + 4)], axis=0
        )
        tiles.append(stacked.T)
    for m in range(8):
        lanes = slice(128 * m, 128 * (m + 1))
        ship[:, lanes] = jnp.where(core == 0, tiles[m], tiles[8 + m])
        rest[:, lanes] = jnp.where(core == 0, tiles[8 + m], tiles[m])


def prepare(info, first, second):
    return pl.pallas_call(
        prepare_kernel,
        out_shape=[jax.ShapeDtypeStruct((128, 1024), BF16)] * 2,
        in_specs=[SMEM, VMEM, VMEM],
        out_specs=[VMEM, VMEM],
        compiler_params=pltpu.CompilerParams(vmem_limit_bytes=8 << 20),
        cost_estimate=pl.CostEstimate(flops=0, bytes_accessed=1 << 20, transcendentals=0),
        name="prepare",
    )(info, first, second)


def load_kernel(info, tiles, out, sems):
    core = info[0]
    copies = []
    for g in range(HELD // 4):
        copies.append(
            pltpu.make_async_copy(
                tiles.at[pl.ds(8 * g + 4 * core, 4)], out.at[pl.ds(4 * g, 4)], sems.at[g]
            )
        )
    for c in copies:
        c.start()
    for c in copies:
        c.wait()


def load_tiles(info, tiles):
    return pl.pallas_call(
        load_kernel,
        out_shape=pltpu.VMEM((HELD, SLOTS, 128, 128), BF16),
        in_specs=[SMEM, ANY],
        out_specs=VMEM,
        scratch_shapes=[pltpu.SemaphoreType.DMA((HELD // 4,))],
        compiler_params=pltpu.CompilerParams(vmem_limit_bytes=2 << 20),
        cost_estimate=pl.CostEstimate(flops=0, bytes_accessed=32 << 20, transcendentals=0),
        name="load_tiles",
    )(info, tiles)


class Stream:
    def __init__(self, core, tiles, ring, sems):
        self.core, self.tiles, self.ring, self.sems = core, tiles, ring, sems

    def copy(self, i):
        return pltpu.make_async_copy(
            self.tiles.at[row_of(self.core, HELD + i)],
            self.ring.at[lax.rem(i, RING)],
            self.sems.at[lax.rem(i, RING)],
        )

    def begin(self):
        for i in range(RING):
            self.copy(jnp.int32(i)).start()

    def next(self, i):
        @pl.when(i + RING < ROWS - HELD)
        def _():
            self.copy(i + RING).start()


def forward_kernel(info, cols, held, tiles, *refs):
    pieces, (out, feats, masks, ring, sems, ring_sems) = refs[:16], refs[16:]
    core = info[0]
    stream = Stream(core, tiles, ring, ring_sems)
    copies = []
    for d in range(SLABS):
        for h in range(2):
            half = jnp.where(core == h, 0, 1)
            at = pl.multiple_of(info[1 + d] * 2048 + half * 1024, 1024)
            copies.append(
                pltpu.make_async_copy(
                    pieces[2 * d + h], feats.at[:, pl.ds(at, 1024)], sems.at[2 * d + h]
                )
            )
    for c in copies:
        c.start()
    stream.begin()
    group = lax.broadcasted_iota(jnp.int32, (16, 128), 1) // PAIR
    for g in range(4):
        masks[g] = jnp.where(group == g, 1.0, 0.0).astype(BF16)
    for c in copies:
        c.wait()

    def picked(block):
        lanes = lanes_of(block // 4)
        mask = masks[lax.rem(block, 4)]
        return [feats[pl.ds(16 * i, 16), lanes] * mask for i in range(8)]

    def row(local, tile_of):
        r = row_of(core, local)
        total = jnp.zeros((128, 128), F32)
        for p in range(0, SLOTS, 2):
            right = jnp.concatenate(picked(cols[r, p]) + picked(cols[r, p + 1]), axis=0)
            left = jnp.concatenate([tile_of(p), tile_of(p + 1)], axis=1)
            total += jnp.dot(left, right, preferred_element_type=F32)
        turned = total.T
        folded = turned[0:32] + turned[32:64] + turned[64:96] + turned[96:128]
        out[local // 4, :, lanes_of(lax.rem(local, 4))] = folded.astype(BF16)

    def step(i, carry):
        stream.copy(i).wait()
        slot = lax.rem(i, RING)
        row(i, lambda p: held[i, p])
        row(HELD + i, lambda p: ring[slot, p])
        stream.next(i)
        return carry

    lax.fori_loop(0, HELD, step, 0)


def forward(info, cols, held, tiles, pieces):
    return pl.pallas_call(
        forward_kernel,
        out_shape=jax.ShapeDtypeStruct((8, PAIR, 512), BF16),
        in_specs=[SMEM, SMEM, VMEM, ANY] + [ANY] * 16,
        out_specs=VMEM,
        scratch_shapes=[
            pltpu.VMEM((128, NODES * PAIR // 128), BF16),
            pltpu.VMEM((4, 16, 128), BF16),
            pltpu.VMEM((RING, SLOTS, 128, 128), BF16),
            pltpu.SemaphoreType.DMA((16,)),
            pltpu.SemaphoreType.DMA((RING,)),
        ],
        compiler_params=pltpu.CompilerParams(vmem_limit_bytes=14 << 20),
        cost_estimate=pl.CostEstimate(
            flops=8 * 2 * 1024 * 128 * 128 * 32, bytes_accessed=8 << 20, transcendentals=0
        ),
        name="forward",
    )(info, cols, held, tiles, *pieces)


def dense_kernel(agg_ref, side_ref, grad_ref, tail_ref):
    agg = agg_ref[...]
    weight = side_ref[:, 512:]
    pre = lax.dot_general(weight, agg, (((0,), (0,)), ((), ())), preferred_element_type=F32)
    sig = 1.0 / (1.0 + jnp.exp(-pre))
    tail_ref[:, :512] = (pre * sig).astype(BF16)
    pre_grad = (side_ref[:, :512].astype(F32) * sig * (1.0 + pre * (1.0 - sig))).astype(BF16)
    grad_ref[...] = jnp.dot(weight, pre_grad, preferred_element_type=F32).astype(BF16)
    wgrad = lax.dot_general(agg, pre_grad, (((1,), (1,)), ((), ())), preferred_element_type=F32)
    tail_ref[:, 512:] = wgrad.astype(BF16)


def dense(agg, side):
    return pl.pallas_call(
        dense_kernel,
        out_shape=(
            jax.ShapeDtypeStruct((256, 512), BF16),
            jax.ShapeDtypeStruct((256, 768), BF16),
        ),
        in_specs=[VMEM, VMEM],
        out_specs=(VMEM, VMEM),
        compiler_params=pltpu.CompilerParams(vmem_limit_bytes=8 << 20),
        cost_estimate=pl.CostEstimate(
            flops=3 * 2 * 256 * 256 * 512, bytes_accessed=2 << 20, transcendentals=256 * 512
        ),
        name="dense",
    )(agg, side)


def backward_kernel(info, cols, held, tiles, grad, *refs):
    outs, (total, ring, ring_sems) = refs[:16], refs[16:]
    core = info[0]
    stream = Stream(core, tiles, ring, ring_sems)
    stream.begin()

    def clear(i, carry):
        total[:, pl.ds(pl.multiple_of(i * 2048, 2048), 2048)] = jnp.zeros((PAIR, 2048), F32)
        return carry

    lax.fori_loop(0, NODES // 2048, clear, 0)

    def row(local, tile_of):
        r = row_of(core, local)
        g = grad[local // 4, :, lanes_of(lax.rem(local, 4))]
        for first in range(0, SLOTS, 8):
            blocks = [lanes_of(cols[r, first + i]) for i in range(8)]
            terms = []
            for i in range(first, first + 8, 2):
                pair = jnp.concatenate([tile_of(i), tile_of(i + 1)], axis=1)
                both = jnp.dot(g, pair, preferred_element_type=F32)
                terms += [both[:, :128], both[:, 128:]]
            sums = [total[:, blocks[i]] + terms[i] for i in range(8)]
            for i in range(8):
                total[:, blocks[i]] = sums[i]

    def step(i, carry):
        stream.copy(i).wait()
        slot = lax.rem(i, RING)
        row(i, lambda p: held[i, p])
        row(HELD + i, lambda p: ring[slot, p])
        stream.next(i)
        return carry

    lax.fori_loop(0, HELD, step, 0)

    own = pl.ds(pl.multiple_of(HALF * core, HALF), HALF)
    other = pl.ds(pl.multiple_of(HALF * (1 - core), HALF), HALF)
    for d in range(SLABS):
        lanes = pl.ds(pl.multiple_of(info[1 + d] * LOCAL, LOCAL), LOCAL)
        outs[d][...] = total[own, lanes].astype(BF16)
        outs[8 + d][...] = total[other, lanes].astype(BF16)


def backward(info, cols, held, tiles, grad):
    return pl.pallas_call(
        backward_kernel,
        out_shape=[jax.ShapeDtypeStruct((HALF, LOCAL), BF16)] * 16,
        in_specs=[SMEM, SMEM, VMEM, ANY, VMEM],
        out_specs=[VMEM] * 16,
        scratch_shapes=[
            pltpu.VMEM((PAIR, NODES), F32),
            pltpu.VMEM((RING, SLOTS, 128, 128), BF16),
            pltpu.SemaphoreType.DMA((RING,)),
        ],
        compiler_params=pltpu.CompilerParams(vmem_limit_bytes=20 << 20),
        cost_estimate=pl.CostEstimate(
            flops=8 * 2 * 1024 * 128 * 128 * 32, bytes_accessed=8 << 20, transcendentals=0
        ),
        name="backward",
    )(info, cols, held, tiles, grad)


def per_device(node_feats, weight, tiles, block_cols, cotangent):
    core = lax.axis_index("feat") % 2
    slab = lax.axis_index("blk")
    x, y = slab // 4, slab % 4
    info = jnp.stack([core] + [(x ^ dx) * 4 + (y + dy) % 4 for dx, dy in STEPS]).astype(jnp.int32)

    ship, rest = prepare(info, node_feats, swap(node_feats))
    pieces = [ship, rest]
    for step in STEPS[1:]:
        block = lax.ppermute(ship, "blk", _from_step(step))
        pieces += [block, swap(block)]
    held = pltpu.with_memory_space_constraint(load_tiles(info, tiles), pltpu.VMEM)

    side = jnp.concatenate(
        [
            jnp.transpose(cotangent.reshape(HALF, 16, 512), (1, 0, 2)),
            jnp.broadcast_to(weight[None], (16, HALF, 256)),
        ],
        axis=2,
    )
    side = lax.all_to_all(side, "feat", 0, 0, tiled=True).reshape(256, 768)

    agg = forward(info, block_cols, held, tiles, pieces)
    agg = lax.all_to_all(agg, "feat", 0, 0, axis_index_groups=SAME_CORE, tiled=True)
    grad, tail = dense(agg.reshape(256, 512), side)
    grad = lax.all_to_all(
        grad.reshape(8, PAIR, 512), "feat", 0, 0, axis_index_groups=SAME_CORE, tiled=True
    )
    parts = backward(info, block_cols, held, tiles, grad)
    own, other = parts[:8], parts[8:]
    summed = [own[d].astype(F32) + swap(other[d]).astype(F32) for d in range(SLABS)]
    total = summed[0]
    for d in range(1, SLABS):
        total = total + lax.ppermute(summed[d].astype(BF16), "blk", _to_step(STEPS[d])).astype(F32)
    feats_grad = total.astype(BF16)

    tail = lax.all_to_all(tail.reshape(16, HALF, 768), "feat", 0, 0, tiled=True)
    hidden = jnp.transpose(tail[:, :, :512], (1, 0, 2)).reshape(HALF, LOCAL)
    wgrad = jnp.sum(tail[:, :, 512:].astype(F32), axis=0)
    wgrad = lax.all_to_all(
        jnp.broadcast_to(wgrad[None], (SLABS, HALF, 256)), "blk", 0, 0, tiled=True
    )
    weight_grad = jnp.sum(wgrad, axis=0)
    return hidden, weight_grad, feats_grad


def solution(mesh):
    placed = (
        P("feat", "blk"),
        P("feat", None),
        P("blk", None, None, None),
        P("blk", None),
        P("feat", "blk"),
    )
    return jax.shard_map(
        per_device,
        mesh=mesh,
        in_specs=placed,
        out_specs=(P("feat", "blk"), P("feat", None), P("feat", "blk")),
        check_vma=False,
    )
```

time: 186 us -> 176 us (0.946)
  local copies, waits for them, and re-layouts: 27.9 us -> 21.2 us
  Pallas kernels: 42.7 us -> 39.6 us
    unnamed x16 -> x22, local copies, waits for them, and re-layouts: 24.8 us -> 18 us
    pallas_call x1 -> x2, Pallas kernels: 11.3 us -> 7.18 us  [the longest x1 6.43 us: load_tiles(): pl.pallas_call(load_kernel, out_shape=pltpu.VMEM((HELD, SLOTS, 128, 128),...]
    pallas_call x1, Pallas kernels: 17.2 us -> 20.1 us  [forward(): pl.pallas_call(forward_kernel, out_shape=jax.ShapeDtypeStruct((8, PAIR, 5...]
  transfers between devices with their start and end apart: 33 -> 33, of which waited for: 6 -> 7; matrix products, arithmetic and copies ran while one was open for 4% -> 5% of each run, Pallas kernels for 15% -> 15%
where the time goes in v2:
time: 176 us; the launch traced here: 175 us
  starting transfers between devices  45.9 us (26%)
  Pallas kernels  39.6 us (22%)
  waiting for transfers between devices  33.6 us (19%)
  blocking collectives  27.3 us (16%)
  local copies, waits for them, and re-layouts  21.2 us (12%)
  other arithmetic  6.48 us (4%)
    ppermute x7, waiting for transfers between devices, per_device(): block = lax.ppermute(ship, 'blk', _from_step(step))  22.9 us
    pallas_call x1, Pallas kernels, forward(): pl.pallas_call(forward_kernel, out_shape=jax.ShapeDtypeStruct((8, PAIR, 5...  20.1 us
    unnamed x22, local copies, waits for them, and re-layouts  18 us
    all_to_all x1, blocking collectives, per_device(): lax.all_to_all(agg, 'feat', 0, 0, axis_index_groups=SAME_CORE, tiled=True)  15.9 us
    ppermute x7, starting transfers between devices, per_device(): block = lax.ppermute(ship, 'blk', _from_step(step))  13.9 us
    ppermute x7, starting transfers between devices, per_device(): lax.ppermute(summed[d].astype(BF16), 'blk', _to_step(STEPS[d])).astype(F32)  12.6 us
    all_to_all x1, blocking collectives, per_device(): lax.all_to_all(grad.reshape(8, PAIR, 512), 'feat', 0, 0, axis_index_group...  11.3 us
    pallas_call x1, Pallas kernels, backward(): pl.pallas_call(backward_kernel, out_shape=[jax.ShapeDtypeStruct((HALF, LO...  11 us
  transfers between devices with their start and end apart: 33, of which 7 were waited for; matrix products, arithmetic and copies ran while one was open for 5% of the time, Pallas kernels for 15%

profile of v2, /device:TPU:0, one launch (start us, length us, event | category | flops | bytes accessed | tf_op | source)
XLA Modules:
  0.0 175.0 jit_solution(4483538642416224232)
XLA Ops:
  0.9 1.6 collective-permute-done.second
  2.5 0.9 copy-done.6
  4.2 3.2 %collective-permute-start.1 = (bf16[128,1024]{1,0:T(8,128)(2,1)S(1)}, bf16[128,1024]{1,0:T(8,128)(2,1)S(1)}, u32[]{:S(2)}, u32[]{:S(2)}) collective-permute-start(bf16[128,1024]{1,0:T(8,128)(2,1)S(1)} %get-tuple-element.23.refs_0_), channel_id=1, source_target_pairs={{16,0},{32,16},{48,32},{0,48},{80,64},{96,80},{112,96},{64,112},{1... | collective-permute-start | bytes 786440 | tf_op jit(solution)/shard_map/ppermute | solution.py:307
  7.3 1.5 collective-permute-start.5
  8.8 2.2 %collective-permute-start.7 = (bf16[128,1024]{1,0:T(8,128)(2,1)S(1)}, bf16[128,1024]{1,0:T(8,128)(2,1)S(1)}, u32[]{:S(2)}, u32[]{:S(2)}) collective-permute-start(bf16[128,1024]{1,0:T(8,128)(2,1)S(1)} %get-tuple-element.23.refs_0_), channel_id=1, source_target_pairs={{32,0},{48,16},{0,32},{16,48},{96,64},{112,80},{64,96},{80,112},{3... | collective-permute-start | bytes 786440 | tf_op jit(solution)/shard_map/ppermute | solution.py:307
  11.0 1.0 collective-permute-start.9
  12.1 12.4 %collective-permute-done.1.refs_2_ = bf16[128,1024]{1,0:T(8,128)(2,1)S(1)} collective-permute-done((bf16[128,1024]{1,0:T(8,128)(2,1)S(1)}, bf16[128,1024]{1,0:T(8,128)(2,1)S(1)}, u32[]{:S(2)}, u32[]{:S(2)}) %collective-permute-start.1) | collective-permute-done | bytes 262176 | tf_op jit(solution)/shard_map/ppermute | solution.py:307
  24.5 6.0 %collective-permute-start.13 = (bf16[128,1024]{1,0:T(8,128)(2,1)S(1)}, bf16[128,1024]{1,0:T(8,128)(2,1)S(1)}, u32[]{:S(2)}, u32[]{:S(2)}) collective-permute-start(bf16[128,1024]{1,0:T(8,128)(2,1)S(1)} %get-tuple-element.23.refs_0_), channel_id=1, source_target_pairs={{96,0},{112,16},{64,32},{80,48},{32,64},{48,80},{0,96},{16,112},{9... | collective-permute-start | bytes 786440 | tf_op jit(solution)/shard_map/ppermute | solution.py:307
  31.1 5.2 %collective-permute-done.11.refs_12_ = bf16[128,1024]{1,0:T(8,128)(2,1)S(1)} collective-permute-done((bf16[128,1024]{1,0:T(8,128)(2,1)S(1)}, bf16[128,1024]{1,0:T(8,128)(2,1)S(1)}, u32[]{:S(2)}, u32[]{:S(2)}) %collective-permute-start.11) | collective-permute-done | bytes 262176 | tf_op jit(solution)/shard_map/ppermute | solution.py:307
  36.3 5.3 %collective-permute-done.13.refs_14_ = bf16[128,1024]{1,0:T(8,128)(2,1)S(1)} collective-permute-done((bf16[128,1024]{1,0:T(8,128)(2,1)S(1)}, bf16[128,1024]{1,0:T(8,128)(2,1)S(1)}, u32[]{:S(2)}, u32[]{:S(2)}) %collective-permute-start.13) | collective-permute-done | bytes 262176 | tf_op jit(solution)/shard_map/ppermute | solution.py:307
  42.8 1.0 copy.19
  45.3 8.0 %all-to-all-start.1 = ((bf16[16,16,768]{2,1,0:T(8,128)(2,1)}), bf16[16,16,768]{2,1,0:T(8,128)(2,1)S(1)}, u32[]{:S(2)}, u32[]{:S(2)}) async-start(bf16[16,16,768]{2,1,0:T(8,128)(2,1)} %pad_maximum_fusion), calls=%async_computation.1 | async-start | bytes 786432 | tf_op jit(solution)/shard_map/all_to_all | solution.py:318
  54.1 6.4 %load_tiles.1.held = bf16[16,32,128,128]{3,2,1,0:T(8,128)(2,1)S(1)} custom-call(s32[9]{0:T(128)S(1)} %stack.39.info, bf16[64,32,128,128]{3,2,1,0:T(8,128)(2,1)} %tiles.5), custom_call_target="tpu_custom_call" | custom-call | bytes 33554432 | tf_op jit(solution)/shard_map/load_tiles/pallas_call | solution.py:102
  62.2 20.1 %forward.1 = bf16[8,32,512]{2,1,0:T(8,128)(2,1)S(1)} custom-call(s32[9]{0:T(128)S(1)} %stack.39.info, s32[64,32]{1,0:T(8,128)S(1)} %copy.12.cols, bf16[16,32,128,128]{3,2,1,0:T(8,128)(2,1)S(1)} %load_tiles.1.held, bf16[64,32,128,128]{3,2,1,0:T(8,128)(2,1)} %tiles.5, bf16[128,1024]{1,0:T(8,128)(2,1)S(1)} %get-tuple-element.23.refs_0_, ...), custom_call_target="tpu_custom_call" | custom-call | flops 8589934592 | bytes 8388608 | tf_op jit(solution)/shard_map/forward/pallas_call | solution.py:186
  82.3 5.7 %copy-done = bf16[16,32,128,128]{3,2,1,0:T(8,128)(2,1)} copy-done((bf16[16,32,128,128]{3,2,1,0:T(8,128)(2,1)}, bf16[16,32,128,128]{3,2,1,0:T(8,128)(2,1)S(1)}, u32[]{:S(2)}) %copy-start) | copy-done | bytes 16777240
  88.0 15.9 %all_to_all.25 = bf16[8,32,512]{2,1,0:T(8,128)(2,1)S(1)} all-to-all(bf16[8,32,512]{2,1,0:T(8,128)(2,1)S(1)} %forward.1), channel_id=1, replica_groups={{0,2,4,6,8,10,12,14},{1,3,5,7,9,11,13,15},{16,18,20,22,24,26,28,30},{17..., dimensions={0} | all-to-all | bytes 524288 | tf_op jit(solution)/shard_map/all_to_all | solution.py:321
  104.0 1.4 dense.1
  105.4 11.3 %all_to_all.26.grad = bf16[8,32,512]{2,1,0:T(8,128)(2,1)S(1)} all-to-all(bf16[8,32,512]{2,1,0:T(8,128)(2,1)S(1)} %bitcast.26), channel_id=1, replica_groups={{0,2,4,6,8,10,12,14},{1,3,5,7,9,11,13,15},{16,18,20,22,24,26,28,30},{17..., dimensions={0} | all-to-all | bytes 524288 | tf_op jit(solution)/shard_map/all_to_all | solution.py:323
  116.7 5.8 %copy-done.1 = bf16[16,32,128,128]{3,2,1,0:T(8,128)(2,1)S(1)} copy-done((bf16[16,32,128,128]{3,2,1,0:T(8,128)(2,1)S(1)}, bf16[16,32,128,128]{3,2,1,0:T(8,128)(2,1)}, u32[]{:S(2)}) %copy-start.1) | copy-done | bytes 16777240
  122.4 11.0 %backward.1 = (bf16[16,8192]{1,0:T(8,128)(2,1)S(1)}, bf16[16,8192]{1,0:T(8,128)(2,1)S(1)}, bf16[16,8192]{1,0:T(8,128)(2,1)S(1)}, bf16[16,8192]{1,0:T(8,128)(2,1)...) custom-call(s32[9]{0:T(128)S(1)} %stack.39.info, ...), custom_call_target="tpu_custom_call" | custom-call | flops 8589934592 | bytes 8388608 | tf_op jit(solution)/shard_map/backward/pallas_call | solution.py:280
  134.9 4.2 %all-to-all-start.2 = ((bf16[16,16,768]{2,1,0:T(8,128)(2,1)}), bf16[16,16,768]{2,1,0:T(8,128)(2,1)}, u32[]{:S(2)}, u32[]{:S(2)}) async-start(bf16[16,16,768]{2,1,0:T(8,128)(2,1)} %bitcast.12), calls=%async_computation.2 | async-start | bytes 786432 | tf_op jit(solution)/shard_map/all_to_all | solution.py:334
  140.6 1.0 add_convert_fusion.1
  143.3 3.0 %collective-permute-start.27 = (bf16[16,8192]{1,0:T(8,128)(2,1)S(1)}, bf16[16,8192]{1,0:T(8,128)(2,1)S(1)}, u32[]{:S(2)}, u32[]{:S(2)}) collective-permute-start(bf16[16,8192]{1,0:T(8,128)(2,1)S(1)} %add_convert_fusion.2), channel_id=1, source_target_pairs={{0,112},{16,64},{32,80},{48,96},{64,48},{80,0},{96,16},{112,32},{1... | collective-permute-start | bytes 786440 | tf_op jit(solution)/shard_map/ppermute | solution.py:331
  146.5 3.5 %collective-permute-start.23 = (bf16[16,8192]{1,0:T(8,128)(2,1)}, bf16[16,8192]{1,0:T(8,128)(2,1)S(1)}, u32[]{:S(2)}, u32[]{:S(2)}) collective-permute-start(bf16[16,8192]{1,0:T(8,128)(2,1)} %add_convert_fusion.4), channel_id=1, source_target_pairs={{0,32},{16,48},{32,0},{48,16},{64,96},{80,112},{96,64},{112,80},{1... | collective-permute-start | bytes 786440 | tf_op jit(solution)/shard_map/ppermute | solution.py:331
  150.2 1.5 collective-permute-start.21
  151.7 2.4 %collective-permute-done.29 = bf16[16,8192]{1,0:T(8,128)(2,1)S(1)} collective-permute-done((bf16[16,8192]{1,0:T(8,128)(2,1)S(1)}, bf16[16,8192]{1,0:T(8,128)(2,1)S(1)}, u32[]{:S(2)}, u32[]{:S(2)}) %collective-permute-start.29) | collective-permute-done | bytes 262176 | tf_op jit(solution)/shard_map/ppermute | solution.py:331
  154.1 1.8 %collective-permute-done.27 = bf16[16,8192]{1,0:T(8,128)(2,1)S(1)} collective-permute-done((bf16[16,8192]{1,0:T(8,128)(2,1)S(1)}, bf16[16,8192]{1,0:T(8,128)(2,1)S(1)}, u32[]{:S(2)}, u32[]{:S(2)}) %collective-permute-start.27) | collective-permute-done | bytes 262176 | tf_op jit(solution)/shard_map/ppermute | solution.py:331
  155.9 4.4 %collective-permute-start.17 = (bf16[16,8192]{1,0:T(8,128)(2,1)S(1)}, bf16[16,8192]{1,0:T(8,128)(2,1)}, u32[]{:S(2)}, u32[]{:S(2)}) collective-permute-start(bf16[16,8192]{1,0:T(8,128)(2,1)S(1)} %add_convert_fusion.7), channel_id=1, source_target_pairs={{0,16},{16,32},{32,48},{48,0},{64,80},{80,96},{96,112},{112,64},{1... | collective-permute-start | bytes 786440 | tf_op jit(solution)/shard_map/ppermute | solution.py:331
  161.9 3.8 %all-to-all-start.3 = ((f32[8,16,256]{2,1,0:T(8,128)}), f32[8,16,256]{2,1,0:T(8,128)S(1)}, u32[]{:S(2)}, u32[]{:S(2)}) async-start(f32[8,16,256]{2,1,0:T(8,128)} %broadcast_in_dim.5), calls=%async_computation.3 | async-start | bytes 262144 | tf_op jit(solution)/shard_map/all_to_all | solution.py:337
  165.7 1.0 slice_bitcast_fusion
  167.4 4.9 %all-to-all-done.3 = f32[8,16,256]{2,1,0:T(8,128)S(1)} async-done(((f32[8,16,256]{2,1,0:T(8,128)}), f32[8,16,256]{2,1,0:T(8,128)S(1)}, u32[]{:S(2)}, u32[]{:S(2)}) %all-to-all-start.3) | async-done | bytes 131104 | tf_op jit(solution)/shard_map/all_to_all | solution.py:337
  173.0 2.0 %add_convert_fusion = bf16[16,8192]{1,0:T(8,128)(2,1)} fusion(bf16[16,8192]{1,0:T(8,128)(2,1)S(1)} %collective-permute-done.29, bf16[16,8192]{1,0:T(8,128)(2,1)S(1)} %collective-permute-done.27, bf16[16,8192]{1,0:T(8,128)(2,1)S(1)} %collective-permute-done.25, bf16[16,8192]{1,0:T(8,128)(2,1)S(1)} %collective-permute-done.23, ...), kind=kLoop, calls=%fused_computation | loop fusion | flops 2359296 | bytes 2621440 | tf_op jit(solution)/shard_map/convert_element_type | solution.py:332
  (79 shorter events, 14.5 us)
Async XLA Ops:
  4.2 20.3 %collective-permute-start.1 = (bf16[128,1024]{1,0:T(8,128)(2,1)S(1)}, bf16[128,1024]{1,0:T(8,128)(2,1)S(1)}, u32[]{:S(2)}, u32[]{:S(2)}) collective-permute-start(bf16[128,1024]{1,0:T(8,128)(2,1)S(1)} %get-tuple-element.23.refs_0_), channel_id=1, source_target_pairs={{16,0},{32,16},{48,32},{0,48},{80,64},{96,80},{112,96},{64,112},{1... | collective-permute-start | bytes 786440 | tf_op jit(solution)/shard_map/ppermute | solution.py:307
  7.3 17.1 %collective-permute-start.3 = (bf16[128,1024]{1,0:T(8,128)(2,1)S(1)}, bf16[128,1024]{1,0:T(8,128)(2,1)S(1)}, u32[]{:S(2)}, u32[]{:S(2)}) collective-permute-start(bf16[128,1024]{1,0:T(8,128)(2,1)S(1)} %get-tuple-element.23.refs_0_), channel_id=1, source_target_pairs={{48,0},{0,16},{16,32},{32,48},{112,64},{64,80},{80,96},{96,112},{4... | collective-permute-start | bytes 786440 | tf_op jit(solution)/shard_map/ppermute | solution.py:307
  7.3 23.2 %collective-permute-start.5 = (bf16[128,1024]{1,0:T(8,128)(2,1)S(1)}, bf16[128,1024]{1,0:T(8,128)(2,1)S(1)}, u32[]{:S(2)}, u32[]{:S(2)}) collective-permute-start(bf16[128,1024]{1,0:T(8,128)(2,1)S(1)} %get-tuple-element.23.refs_0_), channel_id=1, source_target_pairs={{64,0},{80,16},{96,32},{112,48},{0,64},{16,80},{32,96},{48,112},{6... | collective-permute-start | bytes 786440 | tf_op jit(solution)/shard_map/ppermute | solution.py:307
  8.8 21.7 %collective-permute-start.7 = (bf16[128,1024]{1,0:T(8,128)(2,1)S(1)}, bf16[128,1024]{1,0:T(8,128)(2,1)S(1)}, u32[]{:S(2)}, u32[]{:S(2)}) collective-permute-start(bf16[128,1024]{1,0:T(8,128)(2,1)S(1)} %get-tuple-element.23.refs_0_), channel_id=1, source_target_pairs={{32,0},{48,16},{0,32},{16,48},{96,64},{112,80},{64,96},{80,112},{3... | collective-permute-start | bytes 786440 | tf_op jit(solution)/shard_map/ppermute | solution.py:307
  11.0 20.0 %collective-permute-start.9 = (bf16[128,1024]{1,0:T(8,128)(2,1)S(1)}, bf16[128,1024]{1,0:T(8,128)(2,1)S(1)}, u32[]{:S(2)}, u32[]{:S(2)}) collective-permute-start(bf16[128,1024]{1,0:T(8,128)(2,1)S(1)} %get-tuple-element.23.refs_0_), channel_id=1, source_target_pairs={{80,0},{96,16},{112,32},{64,48},{16,64},{32,80},{48,96},{0,112},{8... | collective-permute-start | bytes 786440 | tf_op jit(solution)/shard_map/ppermute | solution.py:307
  24.5 11.8 %collective-permute-start.11 = (bf16[128,1024]{1,0:T(8,128)(2,1)S(1)}, bf16[128,1024]{1,0:T(8,128)(2,1)S(1)}, u32[]{:S(2)}, u32[]{:S(2)}) collective-permute-start(bf16[128,1024]{1,0:T(8,128)(2,1)S(1)} %get-tuple-element.23.refs_0_), channel_id=1, source_target_pairs={{112,0},{64,16},{80,32},{96,48},{48,64},{0,80},{16,96},{32,112},{1... | collective-permute-start | bytes 786440 | tf_op jit(solution)/shard_map/ppermute | solution.py:307
  24.5 17.1 %collective-permute-start.13 = (bf16[128,1024]{1,0:T(8,128)(2,1)S(1)}, bf16[128,1024]{1,0:T(8,128)(2,1)S(1)}, u32[]{:S(2)}, u32[]{:S(2)}) collective-permute-start(bf16[128,1024]{1,0:T(8,128)(2,1)S(1)} %get-tuple-element.23.refs_0_), channel_id=1, source_target_pairs={{96,0},{112,16},{64,32},{80,48},{32,64},{48,80},{0,96},{16,112},{9... | collective-permute-start | bytes 786440 | tf_op jit(solution)/shard_map/ppermute | solution.py:307
  30.5 11.1 %collective-permute-start.2 = (bf16[128,1024]{1,0:T(8,128)(2,1)S(1)}, bf16[128,1024]{1,0:T(8,128)(2,1)S(1)}, u32[]{:S(2)}, u32[]{:S(2)}) collective-permute-start(bf16[128,1024]{1,0:T(8,128)(2,1)S(1)} %collective-permute-done.1.refs_2_), channel_id=1, source_target_pairs={{0,1},{1,0},{2,3},{3,2},{4,5},{5,4},{6,7},{7,6},{8,9},{9,8},{10,11... | collective-permute-start | bytes 786440 | tf_op jit(solution)/shard_map/ppermute | solution.py:46
  30.5 11.6 %collective-permute-start.4 = (bf16[128,1024]{1,0:T(8,128)(2,1)S(1)}, bf16[128,1024]{1,0:T(8,128)(2,1)S(1)}, u32[]{:S(2)}, u32[]{:S(2)}) collective-permute-start(bf16[128,1024]{1,0:T(8,128)(2,1)S(1)} %collective-permute-done.3.refs_4_), channel_id=1, source_target_pairs={{0,1},{1,0},{2,3},{3,2},{4,5},{5,4},{6,7},{7,6},{8,9},{9,8},{10,11... | collective-permute-start | bytes 786440 | tf_op jit(solution)/shard_map/ppermute | solution.py:46
  31.0 29.5 %collective-permute-start.6 = (bf16[128,1024]{1,0:T(8,128)(2,1)S(1)}, bf16[128,1024]{1,0:T(8,128)(2,1)S(1)}, u32[]{:S(2)}, u32[]{:S(2)}) collective-permute-start(bf16[128,1024]{1,0:T(8,128)(2,1)S(1)} %collective-permute-done.5.refs_6_), channel_id=1, source_target_pairs={{0,1},{1,0},{2,3},{3,2},{4,5},{5,4},{6,7},{7,6},{8,9},{9,8},{10,11... | collective-permute-start | bytes 786440 | tf_op jit(solution)/shard_map/ppermute | solution.py:46
  36.3 25.0 %collective-permute-start.8 = (bf16[128,1024]{1,0:T(8,128)(2,1)S(1)}, bf16[128,1024]{1,0:T(8,128)(2,1)}, u32[]{:S(2)}, u32[]{:S(2)}) collective-permute-start(bf16[128,1024]{1,0:T(8,128)(2,1)S(1)} %collective-permute-done.7.refs_8_), channel_id=1, source_target_pairs={{0,1},{1,0},{2,3},{3,2},{4,5},{5,4},{6,7},{7,6},{8,9},{9,8},{10,11... | collective-permute-start | bytes 786440 | tf_op jit(solution)/shard_map/ppermute | solution.py:46
  41.6 19.6 %collective-permute-start.10 = (bf16[128,1024]{1,0:T(8,128)(2,1)S(1)}, bf16[128,1024]{1,0:T(8,128)(2,1)}, u32[]{:S(2)}, u32[]{:S(2)}) collective-permute-start(bf16[128,1024]{1,0:T(8,128)(2,1)S(1)} %collective-permute-done.9.refs_10_), channel_id=1, source_target_pairs={{0,1},{1,0},{2,3},{3,2},{4,5},{5,4},{6,7},{7,6},{8,9},{9,8},{10,11... | collective-permute-start | bytes 786440 | tf_op jit(solution)/shard_map/ppermute | solution.py:46
  41.6 19.6 %collective-permute-start.12 = (bf16[128,1024]{1,0:T(8,128)(2,1)S(1)}, bf16[128,1024]{1,0:T(8,128)(2,1)}, u32[]{:S(2)}, u32[]{:S(2)}) collective-permute-start(bf16[128,1024]{1,0:T(8,128)(2,1)S(1)} %collective-permute-done.11.refs_12_), channel_id=1, source_target_pairs={{0,1},{1,0},{2,3},{3,2},{4,5},{5,4},{6,7},{7,6},{8,9},{9,8},{10,11... | collective-permute-start | bytes 786440 | tf_op jit(solution)/shard_map/ppermute | solution.py:46
  42.8 18.4 %collective-permute-start.14 = (bf16[128,1024]{1,0:T(8,128)(2,1)S(1)}, bf16[128,1024]{1,0:T(8,128)(2,1)}, u32[]{:S(2)}, u32[]{:S(2)}) collective-permute-start(bf16[128,1024]{1,0:T(8,128)(2,1)S(1)} %collective-permute-done.13.refs_14_), channel_id=1, source_target_pairs={{0,1},{1,0},{2,3},{3,2},{4,5},{5,4},{6,7},{7,6},{8,9},{9,8},{10,11... | collective-permute-start | bytes 786440 | tf_op jit(solution)/shard_map/ppermute | solution.py:46
  45.3 42.8 %all-to-all-start.1 = ((bf16[16,16,768]{2,1,0:T(8,128)(2,1)}), bf16[16,16,768]{2,1,0:T(8,128)(2,1)S(1)}, u32[]{:S(2)}, u32[]{:S(2)}) async-start(bf16[16,16,768]{2,1,0:T(8,128)(2,1)} %pad_maximum_fusion), calls=%async_computation.1 | async-start | bytes 786432 | tf_op jit(solution)/shard_map/all_to_all | solution.py:318
  134.8 5.4 %collective-permute-start.28 = (bf16[16,8192]{1,0:T(8,128)(2,1)}, bf16[16,8192]{1,0:T(8,128)(2,1)}, u32[]{:S(2)}, u32[]{:S(2)}) collective-permute-start(bf16[16,8192]{1,0:T(8,128)(2,1)} %get-tuple-element.42), channel_id=1, source_target_pairs={{0,1},{1,0},{2,3},{3,2},{4,5},{5,4},{6,7},{7,6},{8,9},{9,8},{10,11... | collective-permute-start | bytes 786440 | tf_op jit(solution)/shard_map/ppermute | solution.py:46
  134.9 25.4 %all-to-all-start.2 = ((bf16[16,16,768]{2,1,0:T(8,128)(2,1)}), bf16[16,16,768]{2,1,0:T(8,128)(2,1)}, u32[]{:S(2)}, u32[]{:S(2)}) async-start(bf16[16,16,768]{2,1,0:T(8,128)(2,1)} %bitcast.12), calls=%async_computation.2 | async-start | bytes 786432 | tf_op jit(solution)/shard_map/all_to_all | solution.py:334
  139.1 2.5 %collective-permute-start.26 = (bf16[16,8192]{1,0:T(8,128)(2,1)}, bf16[16,8192]{1,0:T(8,128)(2,1)S(1)}, u32[]{:S(2)}, u32[]{:S(2)}) collective-permute-start(bf16[16,8192]{1,0:T(8,128)(2,1)} %copy-done.9), channel_id=1, source_target_pairs={{0,1},{1,0},{2,3},{3,2},{4,5},{5,4},{6,7},{7,6},{8,9},{9,8},{10,11... | collective-permute-start | bytes 786440 | tf_op jit(solution)/shard_map/ppermute | solution.py:46
  139.5 2.4 %collective-permute-start.24 = (bf16[16,8192]{1,0:T(8,128)(2,1)}, bf16[16,8192]{1,0:T(8,128)(2,1)S(1)}, u32[]{:S(2)}, u32[]{:S(2)}) collective-permute-start(bf16[16,8192]{1,0:T(8,128)(2,1)} %copy-done.8), channel_id=1, source_target_pairs={{0,1},{1,0},{2,3},{3,2},{4,5},{5,4},{6,7},{7,6},{8,9},{9,8},{10,11... | collective-permute-start | bytes 786440 | tf_op jit(solution)/shard_map/ppermute | solution.py:46
  139.7 2.7 %collective-permute-start.22 = (bf16[16,8192]{1,0:T(8,128)(2,1)}, bf16[16,8192]{1,0:T(8,128)(2,1)S(1)}, u32[]{:S(2)}, u32[]{:S(2)}) collective-permute-start(bf16[16,8192]{1,0:T(8,128)(2,1)} %copy-done.7), channel_id=1, source_target_pairs={{0,1},{1,0},{2,3},{3,2},{4,5},{5,4},{6,7},{7,6},{8,9},{9,8},{10,11... | collective-permute-start | bytes 786440 | tf_op jit(solution)/shard_map/ppermute | solution.py:46
  140.1 3.2 %collective-permute-start.20 = (bf16[16,8192]{1,0:T(8,128)(2,1)S(1)}, bf16[16,8192]{1,0:T(8,128)(2,1)S(1)}, u32[]{:S(2)}, u32[]{:S(2)}) collective-permute-start(bf16[16,8192]{1,0:T(8,128)(2,1)S(1)} %get-tuple-element.34), channel_id=1, source_target_pairs={{0,1},{1,0},{2,3},{3,2},{4,5},{5,4},{6,7},{7,6},{8,9},{9,8},{10,11... | collective-permute-start | bytes 786440 | tf_op jit(solution)/shard_map/ppermute | solution.py:46
  140.2 6.2 %collective-permute-start.18 = (bf16[16,8192]{1,0:T(8,128)(2,1)S(1)}, bf16[16,8192]{1,0:T(8,128)(2,1)S(1)}, u32[]{:S(2)}, u32[]{:S(2)}) collective-permute-start(bf16[16,8192]{1,0:T(8,128)(2,1)S(1)} %get-tuple-element.32), channel_id=1, source_target_pairs={{0,1},{1,0},{2,3},{3,2},{4,5},{5,4},{6,7},{7,6},{8,9},{9,8},{10,11... | collective-permute-start | bytes 786440 | tf_op jit(solution)/shard_map/ppermute | solution.py:46
  141.6 4.9 %collective-permute-start.16 = (bf16[16,8192]{1,0:T(8,128)(2,1)S(1)}, bf16[16,8192]{1,0:T(8,128)(2,1)S(1)}, u32[]{:S(2)}, u32[]{:S(2)}) collective-permute-start(bf16[16,8192]{1,0:T(8,128)(2,1)S(1)} %get-tuple-element.30), channel_id=1, source_target_pairs={{0,1},{1,0},{2,3},{3,2},{4,5},{5,4},{6,7},{7,6},{8,9},{9,8},{10,11... | collective-permute-start | bytes 786440 | tf_op jit(solution)/shard_map/ppermute | solution.py:46
  141.9 8.2 %collective-permute-start.15 = (bf16[16,8192]{1,0:T(8,128)(2,1)S(1)}, bf16[16,8192]{1,0:T(8,128)(2,1)S(1)}, u32[]{:S(2)}, u32[]{:S(2)}) collective-permute-start(bf16[16,8192]{1,0:T(8,128)(2,1)S(1)} %get-tuple-element.28), channel_id=1, source_target_pairs={{0,1},{1,0},{2,3},{3,2},{4,5},{5,4},{6,7},{7,6},{8,9},{9,8},{10,11... | collective-permute-start | bytes 786440 | tf_op jit(solution)/shard_map/ppermute | solution.py:46
  142.4 11.7 %collective-permute-start.29 = (bf16[16,8192]{1,0:T(8,128)(2,1)S(1)}, bf16[16,8192]{1,0:T(8,128)(2,1)S(1)}, u32[]{:S(2)}, u32[]{:S(2)}) collective-permute-start(bf16[16,8192]{1,0:T(8,128)(2,1)S(1)} %add_convert_fusion.1), channel_id=1, source_target_pairs={{0,96},{16,112},{32,64},{48,80},{64,32},{80,48},{96,0},{112,16},{1... | collective-permute-start | bytes 786440 | tf_op jit(solution)/shard_map/ppermute | solution.py:331
  143.3 12.6 %collective-permute-start.27 = (bf16[16,8192]{1,0:T(8,128)(2,1)S(1)}, bf16[16,8192]{1,0:T(8,128)(2,1)S(1)}, u32[]{:S(2)}, u32[]{:S(2)}) collective-permute-start(bf16[16,8192]{1,0:T(8,128)(2,1)S(1)} %add_convert_fusion.2), channel_id=1, source_target_pairs={{0,112},{16,64},{32,80},{48,96},{64,48},{80,0},{96,16},{112,32},{1... | collective-permute-start | bytes 786440 | tf_op jit(solution)/shard_map/ppermute | solution.py:331
  146.4 26.5 %collective-permute-start.25 = (bf16[16,8192]{1,0:T(8,128)(2,1)S(1)}, bf16[16,8192]{1,0:T(8,128)(2,1)S(1)}, u32[]{:S(2)}, u32[]{:S(2)}) collective-permute-start(bf16[16,8192]{1,0:T(8,128)(2,1)S(1)} %add_convert_fusion.3), channel_id=1, source_target_pairs={{0,80},{16,96},{32,112},{48,64},{64,16},{80,32},{96,48},{112,0},{1... | collective-permute-start | bytes 786440 | tf_op jit(solution)/shard_map/ppermute | solution.py:331
  146.5 26.4 %collective-permute-start.23 = (bf16[16,8192]{1,0:T(8,128)(2,1)}, bf16[16,8192]{1,0:T(8,128)(2,1)S(1)}, u32[]{:S(2)}, u32[]{:S(2)}) collective-permute-start(bf16[16,8192]{1,0:T(8,128)(2,1)} %add_convert_fusion.4), channel_id=1, source_target_pairs={{0,32},{16,48},{32,0},{48,16},{64,96},{80,112},{96,64},{112,80},{1... | collective-permute-start | bytes 786440 | tf_op jit(solution)/shard_map/ppermute | solution.py:331
  150.2 22.8 %collective-permute-start.21 = (bf16[16,8192]{1,0:T(8,128)(2,1)S(1)}, bf16[16,8192]{1,0:T(8,128)(2,1)S(1)}, u32[]{:S(2)}, u32[]{:S(2)}) collective-permute-start(bf16[16,8192]{1,0:T(8,128)(2,1)S(1)} %add_convert_fusion.5), channel_id=1, source_target_pairs={{0,64},{16,80},{32,96},{48,112},{64,0},{80,16},{96,32},{112,48},{1... | collective-permute-start | bytes 786440 | tf_op jit(solution)/shard_map/ppermute | solution.py:331
  154.1 18.8 %collective-permute-start.19 = (bf16[16,8192]{1,0:T(8,128)(2,1)S(1)}, bf16[16,8192]{1,0:T(8,128)(2,1)}, u32[]{:S(2)}, u32[]{:S(2)}) collective-permute-start(bf16[16,8192]{1,0:T(8,128)(2,1)S(1)} %add_convert_fusion.6), channel_id=1, source_target_pairs={{0,48},{16,0},{32,16},{48,32},{64,112},{80,64},{96,80},{112,96},{1... | collective-permute-start | bytes 786440 | tf_op jit(solution)/shard_map/ppermute | solution.py:331
  155.9 17.1 %collective-permute-start.17 = (bf16[16,8192]{1,0:T(8,128)(2,1)S(1)}, bf16[16,8192]{1,0:T(8,128)(2,1)}, u32[]{:S(2)}, u32[]{:S(2)}) collective-permute-start(bf16[16,8192]{1,0:T(8,128)(2,1)S(1)} %add_convert_fusion.7), channel_id=1, source_target_pairs={{0,16},{16,32},{32,48},{48,0},{64,80},{80,96},{96,112},{112,64},{1... | collective-permute-start | bytes 786440 | tf_op jit(solution)/shard_map/ppermute | solution.py:331
  161.9 10.4 %all-to-all-start.3 = ((f32[8,16,256]{2,1,0:T(8,128)}), f32[8,16,256]{2,1,0:T(8,128)S(1)}, u32[]{:S(2)}, u32[]{:S(2)}) async-start(f32[8,16,256]{2,1,0:T(8,128)} %broadcast_in_dim.5), calls=%async_computation.3 | async-start | bytes 262144 | tf_op jit(solution)/shard_map/all_to_all | solution.py:337
  (11 other events, 26.0 us)

commit v3 on v2

v3 whole, which is shorter than its diff:
```python
import functools

import jax
import jax.numpy as jnp
from jax import lax
from jax.experimental import pallas as pl
from jax.experimental.pallas import tpu as pltpu
from jax.sharding import PartitionSpec as P

BF16 = jnp.bfloat16
F32 = jnp.float32
ANY = pl.BlockSpec(memory_space=pl.ANY)
VMEM = pl.BlockSpec(memory_space=pltpu.VMEM)
SMEM = pl.BlockSpec(memory_space=pltpu.SMEM)

STEPS = ((0, 0), (0, 1), (0, 3), (1, 0), (0, 2), (1, 1), (1, 3), (1, 2))
UP, DOWN, ACROSS = (0, 1), (0, 3), (1, 0)
PIECES = tuple((d, 0, 8192) for d in range(7)) + ((7, 0, 4096), (7, 4096, 4096))
SLABS = 8
HALF = 16
PAIR = 32
LOCAL = 8192
NODES = 65536
SLOTS = 32
ROWS = 32
HELD = 16
RING = 16


def _index(x, y):
    return x * 4 + y


def _from_step(step):
    dx, dy = step
    return [(_index(x ^ dx, (y + dy) % 4), _index(x, y)) for x in range(2) for y in range(4)]


def _to_step(step):
    return [(b, a) for a, b in _from_step(step)]


CORE_SWAP = [(f, f ^ 1) for f in range(16)]
SAME_CORE = [list(range(0, 16, 2)), list(range(1, 16, 2))]


def swap(a):
    return lax.ppermute(a, "feat", CORE_SWAP)


def receive(a, step):
    return lax.ppermute(a, "blk", _from_step(step))


def send(a, step):
    return lax.ppermute(a, "blk", _to_step(step))


def after(a, *others):
    return lax.optimization_barrier((a, *others))[0]


def row_of(core, local):
    return 8 * (local // 4) + 4 * core + local % 4


def lanes_of(block):
    return pl.ds(pl.multiple_of(block * 128, 128), 128)


def load_kernel(info, tiles, out, token, sems):
    core = info[0]
    copies = []
    for g in range(HELD // 4):
        copies.append(
            pltpu.make_async_copy(
                tiles.at[pl.ds(8 * g + 4 * core, 4)], out.at[pl.ds(4 * g, 4)], sems.at[g]
            )
        )
    for c in copies:
        c.start()
    token[...] = jnp.zeros_like(token)
    for c in copies:
        c.wait()


def load_tiles(info, tiles):
    return pl.pallas_call(
        load_kernel,
        out_shape=(
            pltpu.VMEM((HELD, SLOTS, 128, 128), BF16),
            jax.ShapeDtypeStruct((8, 128), F32),
        ),
        in_specs=[SMEM, ANY],
        out_specs=(VMEM, VMEM),
        scratch_shapes=[pltpu.SemaphoreType.DMA((HELD // 4,))],
        compiler_params=pltpu.CompilerParams(vmem_limit_bytes=2 << 20),
        cost_estimate=pl.CostEstimate(flops=0, bytes_accessed=32 << 20, transcendentals=0),
        name="load_tiles",
    )(info, tiles)


WIDE = 1280


def unpack_kernel(info, message, mine, other, wgrad_mine, wgrad_other):
    core = info[0]
    own = pl.ds(pl.multiple_of(HALF * core, HALF), HALF)
    sibling = pl.ds(pl.multiple_of(HALF * (1 - core), HALF), HALF)
    for rows, nodes, wgrad in ((own, mine, wgrad_mine), (sibling, other, wgrad_other)):
        total = jnp.zeros((HALF, 256), F32)
        for g in range(8):
            nodes[:, 512 * g : 512 * (g + 1)] = message[g, rows, 512:1024]
            total += message[g, rows, 1024:].astype(F32)
        wgrad[...] = total


def unpack(info, message):
    return pl.pallas_call(
        unpack_kernel,
        out_shape=(
            jax.ShapeDtypeStruct((HALF, 4096), BF16),
            jax.ShapeDtypeStruct((HALF, 4096), BF16),
            jax.ShapeDtypeStruct((HALF, 256), F32),
            jax.ShapeDtypeStruct((HALF, 256), F32),
        ),
        in_specs=[SMEM, VMEM],
        out_specs=(VMEM,) * 4,
        compiler_params=pltpu.CompilerParams(vmem_limit_bytes=4 << 20),
        cost_estimate=pl.CostEstimate(flops=0, bytes_accessed=1 << 20, transcendentals=0),
        name="unpack",
    )(info, message)


def join_kernel(info, mine, received, hidden):
    core = info[0]
    for g in range(8):
        chunk = slice(512 * g, 512 * (g + 1))
        a, b = mine[:, chunk], received[:, chunk]
        hidden[:, 1024 * g : 1024 * g + 512] = jnp.where(core == 0, a, b)
        hidden[:, 1024 * g + 512 : 1024 * (g + 1)] = jnp.where(core == 0, b, a)


def join(info, mine, received):
    return pl.pallas_call(
        join_kernel,
        out_shape=jax.ShapeDtypeStruct((HALF, LOCAL), BF16),
        in_specs=[SMEM, VMEM, VMEM],
        out_specs=VMEM,
        compiler_params=pltpu.CompilerParams(vmem_limit_bytes=4 << 20),
        cost_estimate=pl.CostEstimate(flops=0, bytes_accessed=1 << 20, transcendentals=0),
        name="join",
    )(info, mine, received)


def forward_kernel(info, cols, held, tiles, *refs):
    pieces, sides, (out, feats, ring, sems, ring_sems) = refs[:18], refs[18:22], refs[22:]
    core = info[0]
    copies = []
    for i, (d, first, count) in enumerate(PIECES):
        at = pl.multiple_of(info[1 + d] * LOCAL + first, 4096)
        for h in range(2):
            rows = pl.ds(pl.multiple_of(jnp.where(core == h, 0, HALF), HALF), HALF)
            copies.append(
                pltpu.make_async_copy(
                    pieces[2 * i + h], feats.at[rows, pl.ds(at, count)], sems.at[2 * i + h]
                )
            )
    stream = [
        pltpu.make_async_copy(tiles.at[row_of(core, HELD + i)], ring.at[i], ring_sems.at[i])
        for i in range(ROWS - HELD)
    ]
    for c in copies + stream:
        c.start()
    for h in range(2):
        rows = pl.ds(pl.multiple_of(jnp.where(core == h, 0, HALF), HALF), HALF)
        cot, weight = sides[2 * h], sides[2 * h + 1]
        for g in range(8):
            nodes = pl.ds(pl.multiple_of(1024 * g + 512 * core, 512), 512)
            out[g, rows, 512:1024] = cot[:, nodes]
            out[g, rows, 1024:] = weight[...]
    for c in copies:
        c.wait()

    def four_rows(first, source, offset, sums):
        rows = [row_of(core, first + k) for k in range(4)]

        def push(unit, p, register):
            right = [
                jnp.concatenate([source[first - offset + k, p + e] for e in range(2)], axis=1)
                for k in (2 * unit, 2 * unit + 1)
            ]
            pltpu.matmul_push_rhs(
                jnp.concatenate(right, axis=0), register, unit, transpose=True
            )

        def multiply(unit, p, register):
            left = [
                jnp.concatenate([feats[:, lanes_of(cols[p + e, r])] for e in range(2)], axis=1)
                for r in rows[2 * unit : 2 * unit + 2]
            ]
            pltpu.matmul_acc_lhs(
                sums[unit], jnp.concatenate(left, axis=0), load_staged_rhs=register
            )

        for unit in range(2):
            push(unit, 0, 0)
        for p in range(0, SLOTS, 2):
            if p + 2 < SLOTS:
                for unit in range(2):
                    push(unit, p + 2, (p // 2 + 1) % 2)
            for unit in range(2):
                multiply(unit, p, (p // 2) % 2)
        for unit in range(2):
            got = pltpu.matmul_pop(sums[unit])
            for k in range(2):
                value = got[PAIR * k : PAIR * (k + 1), 128 * k : 128 * (k + 1)]
                j = 2 * unit + k
                out[first // 4, :, 128 * j : 128 * (j + 1)] = value.astype(BF16)

    def held_rows(i, carry):
        pl.run_scoped(
            lambda *sums: four_rows(4 * i, held, 0, sums),
            *[pltpu.ACC(unit)((2 * PAIR, 256), F32) for unit in range(2)],
        )
        return carry

    lax.fori_loop(0, HELD // 4, held_rows, 0)
    for c in stream:
        c.wait()

    def streamed_rows(i, carry):
        pl.run_scoped(
            lambda *sums: four_rows(HELD + 4 * i, ring, HELD, sums),
            *[pltpu.ACC(unit)((2 * PAIR, 256), F32) for unit in range(2)],
        )
        return carry

    lax.fori_loop(0, (ROWS - HELD) // 4, streamed_rows, 0)


def forward(info, cols, held, tiles, pieces, sides):
    return pl.pallas_call(
        forward_kernel,
        out_shape=jax.ShapeDtypeStruct((8, PAIR, WIDE), BF16),
        in_specs=[SMEM, SMEM, VMEM, ANY] + [ANY] * 18 + [VMEM] * 4,
        out_specs=VMEM,
        scratch_shapes=[
            pltpu.VMEM((PAIR, NODES), BF16),
            pltpu.VMEM((ROWS - HELD, SLOTS, 128, 128), BF16),
            pltpu.SemaphoreType.DMA((18,)),
            pltpu.SemaphoreType.DMA((ROWS - HELD,)),
        ],
        compiler_params=pltpu.CompilerParams(vmem_limit_bytes=24 << 20),
        cost_estimate=pl.CostEstimate(
            flops=8 * 2 * 1024 * 128 * 128 * 32, bytes_accessed=8 << 20, transcendentals=0
        ),
        name="forward",
    )(info, cols, held, tiles, *pieces, *sides)


def dense_kernel(message, out):
    agg = message[:, :512]
    weight = message[:, 1024:]
    pre = lax.dot_general(weight, agg, (((0,), (0,)), ((), ())), preferred_element_type=F32)
    sig = 1.0 / (1.0 + jnp.exp(-pre))
    out[:, 512:1024] = (pre * sig).astype(BF16)
    cot = message[:, 512:1024].astype(F32)
    pre_grad = (cot * sig * (1.0 + pre * (1.0 - sig))).astype(BF16)
    out[:, :512] = jnp.dot(weight, pre_grad, preferred_element_type=F32).astype(BF16)
    wgrad = lax.dot_general(agg, pre_grad, (((1,), (1,)), ((), ())), preferred_element_type=F32)
    out[:, 1024:] = wgrad.astype(BF16)


def dense(message):
    return pl.pallas_call(
        dense_kernel,
        out_shape=jax.ShapeDtypeStruct((256, WIDE), BF16),
        in_specs=[VMEM],
        out_specs=VMEM,
        compiler_params=pltpu.CompilerParams(vmem_limit_bytes=8 << 20),
        cost_estimate=pl.CostEstimate(
            flops=3 * 2 * 256 * 256 * 512, bytes_accessed=2 << 20, transcendentals=256 * 512
        ),
        name="dense",
    )(message)


def backward_kernel(info, cols, tiles, grad, *refs):
    outs, (total, ring, sems) = refs[:18], refs[18:]
    core = info[0]

    def copy(i):
        slot = lax.rem(i, RING)
        return pltpu.make_async_copy(tiles.at[row_of(core, i)], ring.at[slot], sems.at[slot])

    for i in range(RING):
        copy(jnp.int32(i)).start()

    def clear(i, carry):
        total[:, pl.ds(pl.multiple_of(i * 2048, 2048), 2048)] = jnp.zeros((PAIR, 2048), F32)
        return carry

    lax.fori_loop(0, NODES // 2048, clear, 0)

    def row(local):
        r = row_of(core, local)
        slot = lax.rem(local, RING)
        g = grad[local // 4, :, lanes_of(lax.rem(local, 4))]
        for first in range(0, SLOTS, 8):
            blocks = [lanes_of(cols[first + i, r]) for i in range(8)]
            terms = []
            for i in range(first, first + 8, 2):
                pair = jnp.concatenate([ring[slot, i], ring[slot, i + 1]], axis=1)
                both = jnp.dot(g, pair, preferred_element_type=F32)
                terms += [both[:, :128], both[:, 128:]]
            sums = [total[:, blocks[i]] + terms[i] for i in range(8)]
            for i in range(8):
                total[:, blocks[i]] = sums[i]

    def step(i, carry):
        for k in range(2):
            copy(2 * i + k).wait()
        for k in range(2):
            row(2 * i + k)

        @pl.when(2 * i + RING < ROWS)
        def _():
            for k in range(2):
                copy(2 * i + k + RING).start()

        return carry

    lax.fori_loop(0, ROWS // 2, step, 0)

    own = pl.ds(pl.multiple_of(HALF * core, HALF), HALF)
    other = pl.ds(pl.multiple_of(HALF * (1 - core), HALF), HALF)
    for i, (d, first, count) in enumerate(PIECES):
        lanes = pl.ds(pl.multiple_of(info[1 + d] * LOCAL + first, 4096), count)
        outs[i][...] = total[own, lanes].astype(BF16)
        outs[9 + i][...] = total[other, lanes].astype(BF16)


def backward(info, cols, tiles, grad):
    return pl.pallas_call(
        backward_kernel,
        out_shape=[jax.ShapeDtypeStruct((HALF, n), BF16) for _, _, n in PIECES] * 2,
        in_specs=[SMEM, SMEM, ANY, VMEM],
        out_specs=[VMEM] * 18,
        scratch_shapes=[
            pltpu.VMEM((PAIR, NODES), F32),
            pltpu.VMEM((RING, SLOTS, 128, 128), BF16),
            pltpu.SemaphoreType.DMA((RING,)),
        ],
        compiler_params=pltpu.CompilerParams(vmem_limit_bytes=32 << 20),
        cost_estimate=pl.CostEstimate(
            flops=8 * 2 * 1024 * 128 * 128 * 32, bytes_accessed=8 << 20, transcendentals=0
        ),
        name="backward",
    )(info, cols, tiles, grad)


def per_device(node_feats, weight, tiles, block_cols, cotangent):
    core = lax.axis_index("feat") % 2
    slab = lax.axis_index("blk")
    x, y = slab // 4, slab % 4
    info = jnp.stack([core] + [(x ^ dx) * 4 + (y + dy) % 4 for dx, dy in STEPS]).astype(jnp.int32)
    cols = block_cols.T

    up, down, across = (receive(node_feats, s) for s in (UP, DOWN, ACROSS))
    held, token = load_tiles(info, tiles)
    up2, across2 = after(up, token), after(across, token)
    far = receive(up2, UP)
    across_up = receive(up2, ACROSS)
    across_down = receive(across2, DOWN)
    corner = [receive(across_up[:, :4096], UP), receive(across_down[:, 4096:], DOWN)]
    pieces = []
    for block in (node_feats, up, down, across, far, across_up, across_down, *corner):
        pieces += [block, swap(block)]
    sides = [cotangent, weight, swap(cotangent), swap(weight)]
    held = pltpu.with_memory_space_constraint(held, pltpu.VMEM)

    message = forward(info, cols, held, tiles, pieces, sides)
    message = lax.all_to_all(message, "feat", 0, 0, axis_index_groups=SAME_CORE, tiled=True)
    message = dense(message.reshape(256, WIDE)).reshape(8, PAIR, WIDE)
    message = lax.all_to_all(message, "feat", 0, 0, axis_index_groups=SAME_CORE, tiled=True)
    parts = backward(info, cols, tiles, message)

    def mine(i):
        return parts[i].astype(F32) + swap(parts[9 + i]).astype(F32)

    def widen(a, low, high):
        return lax.pad(a, jnp.zeros((), a.dtype), ((0, 0, 0), (low, high, 0))).astype(F32)

    corner_up = send(mine(7).astype(BF16), UP)
    corner_down = send(mine(8).astype(BF16), DOWN)
    hidden, hidden_other, wgrad, wgrad_other = unpack(info, after(message, parts[0]))
    hidden = join(info, hidden, swap(hidden_other))
    wgrad = wgrad + swap(wgrad_other)
    wgrad = wgrad + receive(wgrad, ACROSS)
    across_up = (mine(5) + widen(corner_up, 0, 4096)).astype(BF16)
    across_down = (mine(6) + widen(corner_down, 4096, 0)).astype(BF16)
    across_up, across_down, wgrad, hidden = lax.optimization_barrier(
        (across_up, across_down, wgrad, hidden)
    )
    from_across = send(across_up, ACROSS)
    from_up = send(across_down, DOWN)
    from_down = send(mine(4).astype(BF16), UP)
    wgrad = wgrad + lax.ppermute(wgrad, "blk", [(b, b ^ 1) for b in range(8)])
    up = (mine(1) + from_across.astype(F32) + from_down.astype(F32)).astype(BF16)
    across = (mine(3) + from_up.astype(F32)).astype(BF16)
    up, across, down, wgrad = lax.optimization_barrier((up, across, mine(2).astype(BF16), wgrad))
    weight_grad = wgrad + lax.ppermute(wgrad, "blk", [(b, b ^ 2) for b in range(8)])
    last = [send(up, UP), send(down, DOWN), send(across, ACROSS)]
    total = mine(0)
    for a in last:
        total = total + a.astype(F32)
    return hidden, weight_grad, total.astype(BF16)


def solution(mesh):
    placed = (
        P("feat", "blk"),
        P("feat", None),
        P("blk", None, None, None),
        P("blk", None),
        P("feat", "blk"),
    )
    return jax.shard_map(
        per_device,
        mesh=mesh,
        in_specs=placed,
        out_specs=(P("feat", "blk"), P("feat", None), P("feat", "blk")),
        check_vma=False,
    )
```

time: 176 us -> 145 us (0.82)
  starting transfers between devices: 45.9 us -> 20.8 us
  local copies, waits for them, and re-layouts: 21.2 us -> 0.12 us
  waiting for transfers between devices: 33.6 us -> 50.3 us
  blocking collectives: 27.3 us -> 35.6 us
  Pallas kernels: 39.6 us -> 35.1 us
  other arithmetic: 6.48 us -> 2.08 us
    ppermute x14 -> x19, waiting for transfers between devices: 27.1 us -> 46.9 us  [the longest x9 22.2 us: receive(): return lax.ppermute(a, 'blk', _from_step(step))]
    unnamed x22 -> x8, local copies, waits for them, and re-layouts: 18 us -> 0.02 us
    all_to_all x3 -> x0, starting transfers between devices: 16 us -> none  [the longest x1 7.99 us: per_device(): side = lax.all_to_all(side, 'feat', 0, 0, tiled=True).reshape(256, 768)]
    ppermute x14 -> x19, starting transfers between devices: 26.5 us -> 16.8 us  [the longest x9 9.66 us: receive(): return lax.ppermute(a, 'blk', _from_step(step))]
    all_to_all x2, blocking collectives: 27.3 us -> 35.6 us  [per_device(): lax.all_to_all(message, 'feat', 0, 0, axis_index_groups=SAME_CORE, tiled=...]
    all_to_all x3 -> x0, waiting for transfers between devices: 4.9 us -> none  [the longest x1 4.89 us: per_device(): lax.all_to_all(jnp.broadcast_to(wgrad[None], (SLABS, HALF, 256)), 'blk',...]
    pallas_call x5 -> x6, Pallas kernels: 39.6 us -> 35.1 us  [the longest x1 13 us: forward(): pl.pallas_call(forward_kernel, out_shape=jax.ShapeDtypeStruct((8, PAIR, W...]
    convert_element_type x8 -> x9, other arithmetic: 4.18 us -> 1.46 us  [the longest x1 0.88 us: per_device(): return (hidden, weight_grad, total.astype(BF16))]
  transfers between devices with their start and end apart: 33 -> 41, of which waited for: 7 -> 15; matrix products, arithmetic and copies ran while one was open for 5% -> 1% of each run, Pallas kernels for 15% -> 6%
where the time goes in v3:
time: 145 us
  waiting for transfers between devices  50.3 us (35%)
  blocking collectives  35.6 us (25%)
  Pallas kernels  35.1 us (24%)
  starting transfers between devices  20.8 us (14%)
  other arithmetic  2.08 us (1%)
    all_to_all x2, blocking collectives, per_device(): lax.all_to_all(message, 'feat', 0, 0, axis_index_groups=SAME_CORE, tiled=...  35.6 us
    ppermute x9, waiting for transfers between devices, receive(): return lax.ppermute(a, 'blk', _from_step(step))  22.2 us
    ppermute x8, waiting for transfers between devices, send(): return lax.ppermute(a, 'blk', _to_step(step))  18.2 us
    pallas_call x1, Pallas kernels, forward(): pl.pallas_call(forward_kernel, out_shape=jax.ShapeDtypeStruct((8, PAIR, W...  13 us
    pallas_call x1, Pallas kernels, backward(): pl.pallas_call(backward_kernel, out_shape=[jax.ShapeDtypeStruct((HALF, n)...  12.6 us
    ppermute x9, starting transfers between devices, receive(): return lax.ppermute(a, 'blk', _from_step(step))  9.66 us
    pallas_call x1, Pallas kernels, load_tiles(): pl.pallas_call(load_kernel, out_shape=(pltpu.VMEM((HELD, SLOTS, 128, 128)...  7.03 us
    ppermute x8, starting transfers between devices, send(): return lax.ppermute(a, 'blk', _to_step(step))  6.34 us
  transfers between devices with their start and end apart: 41, of which 15 were waited for; matrix products, arithmetic and copies ran while one was open for 1% of the time, Pallas kernels for 6%

profile of v3, /device:TPU:0, one launch (start us, length us, event | category | flops | bytes accessed | tf_op | source)
XLA Modules:
  0.0 144.8 jit_solution(17148276946199687379)
XLA Ops:
  0.7 1.7 %collective-permute-start.5 = (bf16[16,8192]{1,0:T(8,128)(2,1)}, bf16[16,8192]{1,0:T(8,128)(2,1)S(1)}, u32[]{:S(2)}, u32[]{:S(2)}) collective-permute-start(bf16[16,8192]{1,0:T(8,128)(2,1)} %refs_0_.1), channel_id=1, source_target_pairs={{64,0},{80,16},{96,32},{112,48},{0,64},{16,80},{32,96},{48,112},{6... | collective-permute-start | bytes 786440 | tf_op jit(solution)/shard_map/ppermute | solution.py:52
  2.3 3.0 %collective-permute-start.1 = (bf16[16,8192]{1,0:T(8,128)(2,1)}, bf16[16,8192]{1,0:T(8,128)(2,1)S(1)}, u32[]{:S(2)}, u32[]{:S(2)}) collective-permute-start(bf16[16,8192]{1,0:T(8,128)(2,1)} %refs_0_.1), channel_id=1, source_target_pairs={{16,0},{32,16},{48,32},{0,48},{80,64},{96,80},{112,96},{64,112},{1... | collective-permute-start | bytes 786440 | tf_op jit(solution)/shard_map/ppermute | solution.py:52
  5.4 7.0 %load_tiles.1 = (bf16[16,32,128,128]{3,2,1,0:T(8,128)(2,1)S(1)}, f32[8,128]{1,0:T(8,128)}) custom-call(s32[9]{0:T(128)S(1)} %stack.39.info, bf16[64,32,128,128]{3,2,1,0:T(8,128)(2,1)} %tiles.5), custom_call_target="tpu_custom_call" | custom-call | bytes 33554432 | tf_op jit(solution)/shard_map/load_tiles/pallas_call | solution.py:88
  12.5 0.6 collective-permute-start.9
  13.1 0.6 collective-permute-start.11
  13.7 1.2 collective-permute-done.18.refs_21_
  15.6 5.7 %collective-permute-done.9.refs_10_ = bf16[16,8192]{1,0:T(8,128)(2,1)S(1)} collective-permute-done((bf16[16,8192]{1,0:T(8,128)(2,1)S(1)}, bf16[16,8192]{1,0:T(8,128)(2,1)S(1)}, u32[]{:S(2)}, u32[]{:S(2)}) %collective-permute-start.9) | collective-permute-done | bytes 262176 | tf_op jit(solution)/shard_map/ppermute | solution.py:52
  21.3 3.2 %collective-permute-start.7 = (bf16[16,8192]{1,0:T(8,128)(2,1)S(1)}, bf16[16,8192]{1,0:T(8,128)(2,1)S(1)}, u32[]{:S(2)}, u32[]{:S(2)}) collective-permute-start(bf16[16,8192]{1,0:T(8,128)(2,1)S(1)} %collective-permute-done.1.refs_2_), channel_id=1, source_target_pairs={{16,0},{32,16},{48,32},{0,48},{80,64},{96,80},{112,96},{64,112},{1... | collective-permute-start | bytes 786440 | tf_op jit(solution)/shard_map/ppermute | solution.py:52
  25.4 5.8 %collective-permute-done.7.refs_8_ = bf16[16,8192]{1,0:T(8,128)(2,1)S(1)} collective-permute-done((bf16[16,8192]{1,0:T(8,128)(2,1)S(1)}, bf16[16,8192]{1,0:T(8,128)(2,1)S(1)}, u32[]{:S(2)}, u32[]{:S(2)}) %collective-permute-start.7) | collective-permute-done | bytes 262176 | tf_op jit(solution)/shard_map/ppermute | solution.py:52
  31.3 1.5 %collective-permute-done.13.refs_14_ = bf16[16,4096]{1,0:T(8,128)(2,1)S(1)} collective-permute-done((bf16[16,4096]{1,0:T(8,128)(2,1)S(1)}, bf16[16,4096]{1,0:T(8,128)(2,1)S(1)}, u32[]{:S(2)}, u32[]{:S(2)}) %collective-permute-start.13) | collective-permute-done | bytes 131104 | tf_op jit(solution)/shard_map/ppermute | solution.py:52
  32.8 6.3 %collective-permute-done.15.refs_16_ = bf16[16,4096]{1,0:T(8,128)(2,1)S(1)} collective-permute-done((bf16[16,4096]{1,0:T(8,128)(2,1)S(1)}, bf16[16,4096]{1,0:T(8,128)(2,1)S(1)}, u32[]{:S(2)}, u32[]{:S(2)}) %collective-permute-start.15) | collective-permute-done | bytes 131104 | tf_op jit(solution)/shard_map/ppermute | solution.py:52
  39.1 1.3 collective-permute-done.16.refs_17_
  40.5 13.0 %forward.1 = bf16[8,32,1280]{2,1,0:T(8,128)(2,1)S(1)} custom-call(s32[9]{0:T(128)S(1)} %stack.39.info, s32[32,64]{1,0:T(8,128)S(1)} %bitcast.14, bf16[16,32,128,128]{3,2,1,0:T(8,128)(2,1)S(1)} %get-tuple-element.38.held, bf16[64,32,128,128]{3,2,1,0:T(8,128)(2,1)} %tiles.5, bf16[16,8192]{1,0:T(8,128)(2,1)S(1)} %copy-done, ...), custom_call_target="tpu_custom_call" | custom-call | flops 8589934592 | bytes 8388608 | tf_op jit(solution)/shard_map/forward/pallas_call | solution.py:243
  53.5 20.6 %all_to_all.10 = bf16[8,32,1280]{2,1,0:T(8,128)(2,1)S(1)} all-to-all(bf16[8,32,1280]{2,1,0:T(8,128)(2,1)S(1)} %forward.1), channel_id=1, replica_groups={{0,2,4,6,8,10,12,14},{1,3,5,7,9,11,13,15},{16,18,20,22,24,26,28,30},{17..., dimensions={0} | all-to-all | bytes 1310720 | tf_op jit(solution)/shard_map/all_to_all | solution.py:384
  74.1 0.6 dense.1
  74.7 15.0 %all_to_all.11.grad.message = bf16[8,32,1280]{2,1,0:T(8,128)(2,1)S(1)} all-to-all(bf16[8,32,1280]{2,1,0:T(8,128)(2,1)S(1)} %bitcast.13), channel_id=1, replica_groups={{0,2,4,6,8,10,12,14},{1,3,5,7,9,11,13,15},{16,18,20,22,24,26,28,30},{17..., dimensions={0} | all-to-all | bytes 1310720 | tf_op jit(solution)/shard_map/all_to_all | solution.py:386
  89.7 12.6 %backward.1 = (bf16[16,8192]{1,0:T(8,128)(2,1)S(1)}, bf16[16,8192]{1,0:T(8,128)(2,1)S(1)}, bf16[16,8192]{1,0:T(8,128)(2,1)S(1)}, bf16[16,8192]{1,0:T(8,128)(2,1)...) custom-call(s32[9]{0:T(128)S(1)} %stack.39.info, ...), custom_call_target="tpu_custom_call" | custom-call | flops 8589934592 | bytes 8388608 | tf_op jit(solution)/shard_map/backward/pallas_call | solution.py:345
  102.4 0.6 unpack.1
  103.6 0.8 collective-permute-done.25
  105.4 2.8 %collective-permute-done.26 = f32[16,256]{1,0:T(8,128)S(1)} collective-permute-done((f32[16,256]{1,0:T(8,128)S(1)}, f32[16,256]{1,0:T(8,128)S(1)}, u32[]{:S(2)}, u32[]{:S(2)}) %collective-permute-start.26) | collective-permute-done | bytes 16416 | tf_op jit(solution)/shard_map/ppermute | solution.py:52
  109.5 1.3 join.1
  111.0 6.5 %collective-permute-done.21 = bf16[16,4096]{1,0:T(8,128)(2,1)S(1)} collective-permute-done((bf16[16,4096]{1,0:T(8,128)(2,1)S(1)}, bf16[16,4096]{1,0:T(8,128)(2,1)S(1)}, u32[]{:S(2)}, u32[]{:S(2)}) %collective-permute-start.21) | collective-permute-done | bytes 131104 | tf_op jit(solution)/shard_map/ppermute | solution.py:56
  118.1 4.2 %collective-permute-done.24 = bf16[16,4096]{1,0:T(8,128)(2,1)S(1)} collective-permute-done((bf16[16,4096]{1,0:T(8,128)(2,1)S(1)}, bf16[16,4096]{1,0:T(8,128)(2,1)S(1)}, u32[]{:S(2)}, u32[]{:S(2)}) %collective-permute-start.24) | collective-permute-done | bytes 131104 | tf_op jit(solution)/shard_map/ppermute | solution.py:56
  122.6 1.8 %collective-permute-start.33 = (bf16[16,8192]{1,0:T(8,128)(2,1)S(1)}, bf16[16,8192]{1,0:T(8,128)(2,1)S(1)}, u32[]{:S(2)}, u32[]{:S(2)}) collective-permute-start(bf16[16,8192]{1,0:T(8,128)(2,1)S(1)} %add_convert_fusion.5), channel_id=1, source_target_pairs={{0,48},{16,0},{32,16},{48,32},{64,112},{80,64},{96,80},{112,96},{1... | collective-permute-start | bytes 786440 | tf_op jit(solution)/shard_map/ppermute | solution.py:56
  124.5 1.9 %collective-permute-done.35 = f32[16,256]{1,0:T(8,128)S(1)} collective-permute-done((f32[16,256]{1,0:T(8,128)S(1)}, f32[16,256]{1,0:T(8,128)S(1)}, u32[]{:S(2)}, u32[]{:S(2)}) %collective-permute-start.35) | collective-permute-done | bytes 16416 | tf_op jit(solution)/shard_map/ppermute | solution.py:409
  126.8 2.4 %collective-permute-done.33 = bf16[16,8192]{1,0:T(8,128)(2,1)S(1)} collective-permute-done((bf16[16,8192]{1,0:T(8,128)(2,1)S(1)}, bf16[16,8192]{1,0:T(8,128)(2,1)S(1)}, u32[]{:S(2)}, u32[]{:S(2)}) %collective-permute-start.33) | collective-permute-done | bytes 262176 | tf_op jit(solution)/shard_map/ppermute | solution.py:56
  129.2 4.9 %collective-permute-done.31 = bf16[16,8192]{1,0:T(8,128)(2,1)S(1)} collective-permute-done((bf16[16,8192]{1,0:T(8,128)(2,1)S(1)}, bf16[16,8192]{1,0:T(8,128)(2,1)S(1)}, u32[]{:S(2)}, u32[]{:S(2)}) %collective-permute-start.31) | collective-permute-done | bytes 262176 | tf_op jit(solution)/shard_map/ppermute | solution.py:56
  134.4 3.2 %collective-permute-start.39 = (bf16[16,8192]{1,0:T(8,128)(2,1)S(1)}, bf16[16,8192]{1,0:T(8,128)(2,1)S(1)}, u32[]{:S(2)}, u32[]{:S(2)}) collective-permute-start(bf16[16,8192]{1,0:T(8,128)(2,1)S(1)} %add_convert_fusion.1), channel_id=1, source_target_pairs={{0,48},{16,0},{32,16},{48,32},{64,112},{80,64},{96,80},{112,96},{1... | collective-permute-start | bytes 786440 | tf_op jit(solution)/shard_map/ppermute | solution.py:56
  137.8 0.7 collective-permute-start.36
  138.5 4.6 %collective-permute-done.36 = f32[16,256]{1,0:T(8,128)S(1)} collective-permute-done((f32[16,256]{1,0:T(8,128)S(1)}, f32[16,256]{1,0:T(8,128)S(1)}, u32[]{:S(2)}, u32[]{:S(2)}) %collective-permute-start.36) | collective-permute-done | bytes 16416 | tf_op jit(solution)/shard_map/ppermute | solution.py:413
  143.1 0.6 add.160
  144.0 0.9 add_convert_fusion
  (82 shorter events, 7.0 us)
Async XLA Ops:
  0.7 11.8 %collective-permute-start.5 = (bf16[16,8192]{1,0:T(8,128)(2,1)}, bf16[16,8192]{1,0:T(8,128)(2,1)S(1)}, u32[]{:S(2)}, u32[]{:S(2)}) collective-permute-start(bf16[16,8192]{1,0:T(8,128)(2,1)} %refs_0_.1), channel_id=1, source_target_pairs={{64,0},{80,16},{96,32},{112,48},{0,64},{16,80},{32,96},{48,112},{6... | collective-permute-start | bytes 786440 | tf_op jit(solution)/shard_map/ppermute | solution.py:52
  2.3 10.2 %collective-permute-start.1 = (bf16[16,8192]{1,0:T(8,128)(2,1)}, bf16[16,8192]{1,0:T(8,128)(2,1)S(1)}, u32[]{:S(2)}, u32[]{:S(2)}) collective-permute-start(bf16[16,8192]{1,0:T(8,128)(2,1)} %refs_0_.1), channel_id=1, source_target_pairs={{16,0},{32,16},{48,32},{0,48},{80,64},{96,80},{112,96},{64,112},{1... | collective-permute-start | bytes 786440 | tf_op jit(solution)/shard_map/ppermute | solution.py:52
  5.3 9.7 %collective-permute-start.3 = (bf16[16,8192]{1,0:T(8,128)(2,1)}, bf16[16,8192]{1,0:T(8,128)(2,1)S(1)}, u32[]{:S(2)}, u32[]{:S(2)}) collective-permute-start(bf16[16,8192]{1,0:T(8,128)(2,1)} %refs_0_.1), channel_id=1, source_target_pairs={{48,0},{0,16},{16,32},{32,48},{112,64},{64,80},{80,96},{96,112},{4... | collective-permute-start | bytes 786440 | tf_op jit(solution)/shard_map/ppermute | solution.py:52
  5.3 10.0 %collective-permute-start.17 = (bf16[16,8192]{1,0:T(8,128)(2,1)}, bf16[16,8192]{1,0:T(8,128)(2,1)S(1)}, u32[]{:S(2)}, u32[]{:S(2)}) collective-permute-start(bf16[16,8192]{1,0:T(8,128)(2,1)} %refs_18_.1), channel_id=1, source_target_pairs={{0,1},{1,0},{2,3},{3,2},{4,5},{5,4},{6,7},{7,6},{8,9},{9,8},{10,11... | collective-permute-start | bytes 786440 | tf_op jit(solution)/shard_map/ppermute | solution.py:48
  12.5 8.8 %collective-permute-start.9 = (bf16[16,8192]{1,0:T(8,128)(2,1)S(1)}, bf16[16,8192]{1,0:T(8,128)(2,1)S(1)}, u32[]{:S(2)}, u32[]{:S(2)}) collective-permute-start(bf16[16,8192]{1,0:T(8,128)(2,1)S(1)} %collective-permute-done.1.refs_2_), channel_id=1, source_target_pairs={{64,0},{80,16},{96,32},{112,48},{0,64},{16,80},{32,96},{48,112},{6... | collective-permute-start | bytes 786440 | tf_op jit(solution)/shard_map/ppermute | solution.py:52
  13.1 11.4 %collective-permute-start.11 = (bf16[16,8192]{1,0:T(8,128)(2,1)S(1)}, bf16[16,8192]{1,0:T(8,128)(2,1)S(1)}, u32[]{:S(2)}, u32[]{:S(2)}) collective-permute-start(bf16[16,8192]{1,0:T(8,128)(2,1)S(1)} %collective-permute-done.5.refs_6_), channel_id=1, source_target_pairs={{48,0},{0,16},{16,32},{32,48},{112,64},{64,80},{80,96},{96,112},{4... | collective-permute-start | bytes 786440 | tf_op jit(solution)/shard_map/ppermute | solution.py:52
  14.9 9.7 %collective-permute-start = (bf16[16,8192]{1,0:T(8,128)(2,1)S(1)}, bf16[16,8192]{1,0:T(8,128)(2,1)S(1)}, u32[]{:S(2)}, u32[]{:S(2)}) collective-permute-start(bf16[16,8192]{1,0:T(8,128)(2,1)S(1)} %copy-done), channel_id=1, source_target_pairs={{0,1},{1,0},{2,3},{3,2},{4,5},{5,4},{6,7},{7,6},{8,9},{9,8},{10,11... | collective-permute-start | bytes 786440 | tf_op jit(solution)/shard_map/ppermute | solution.py:48
  15.0 9.9 %collective-permute-start.4 = (bf16[16,8192]{1,0:T(8,128)(2,1)S(1)}, bf16[16,8192]{1,0:T(8,128)(2,1)S(1)}, u32[]{:S(2)}, u32[]{:S(2)}) collective-permute-start(bf16[16,8192]{1,0:T(8,128)(2,1)S(1)} %collective-permute-done.3.refs_4_), channel_id=1, source_target_pairs={{0,1},{1,0},{2,3},{3,2},{4,5},{5,4},{6,7},{7,6},{8,9},{9,8},{10,11... | collective-permute-start | bytes 786440 | tf_op jit(solution)/shard_map/ppermute | solution.py:48
  15.4 9.9 %collective-permute-start.2 = (bf16[16,8192]{1,0:T(8,128)(2,1)S(1)}, bf16[16,8192]{1,0:T(8,128)(2,1)S(1)}, u32[]{:S(2)}, u32[]{:S(2)}) collective-permute-start(bf16[16,8192]{1,0:T(8,128)(2,1)S(1)} %collective-permute-done.1.refs_2_), channel_id=1, source_target_pairs={{0,1},{1,0},{2,3},{3,2},{4,5},{5,4},{6,7},{7,6},{8,9},{9,8},{10,11... | collective-permute-start | bytes 786440 | tf_op jit(solution)/shard_map/ppermute | solution.py:48
  21.3 10.0 %collective-permute-start.7 = (bf16[16,8192]{1,0:T(8,128)(2,1)S(1)}, bf16[16,8192]{1,0:T(8,128)(2,1)S(1)}, u32[]{:S(2)}, u32[]{:S(2)}) collective-permute-start(bf16[16,8192]{1,0:T(8,128)(2,1)S(1)} %collective-permute-done.1.refs_2_), channel_id=1, source_target_pairs={{16,0},{32,16},{48,32},{0,48},{80,64},{96,80},{112,96},{64,112},{1... | collective-permute-start | bytes 786440 | tf_op jit(solution)/shard_map/ppermute | solution.py:52
  24.5 6.7 %collective-permute-start.6 = (bf16[16,8192]{1,0:T(8,128)(2,1)S(1)}, bf16[16,8192]{1,0:T(8,128)(2,1)S(1)}, u32[]{:S(2)}, u32[]{:S(2)}) collective-permute-start(bf16[16,8192]{1,0:T(8,128)(2,1)S(1)} %collective-permute-done.5.refs_6_), channel_id=1, source_target_pairs={{0,1},{1,0},{2,3},{3,2},{4,5},{5,4},{6,7},{7,6},{8,9},{9,8},{10,11... | collective-permute-start | bytes 786440 | tf_op jit(solution)/shard_map/ppermute | solution.py:48
  24.6 8.2 %collective-permute-start.13 = (bf16[16,4096]{1,0:T(8,128)(2,1)S(1)}, bf16[16,4096]{1,0:T(8,128)(2,1)S(1)}, u32[]{:S(2)}, u32[]{:S(2)}) collective-permute-start(bf16[16,4096]{1,0:T(8,128)(2,1)S(1)} %slice.8), channel_id=1, source_target_pairs={{16,0},{32,16},{48,32},{0,48},{80,64},{96,80},{112,96},{64,112},{1... | collective-permute-start | bytes 393224 | tf_op jit(solution)/shard_map/ppermute | solution.py:52
  24.9 14.2 %collective-permute-start.10 = (bf16[16,8192]{1,0:T(8,128)(2,1)S(1)}, bf16[16,8192]{1,0:T(8,128)(2,1)S(1)}, u32[]{:S(2)}, u32[]{:S(2)}) collective-permute-start(bf16[16,8192]{1,0:T(8,128)(2,1)S(1)} %collective-permute-done.9.refs_10_), channel_id=1, source_target_pairs={{0,1},{1,0},{2,3},{3,2},{4,5},{5,4},{6,7},{7,6},{8,9},{9,8},{10,11... | collective-permute-start | bytes 786440 | tf_op jit(solution)/shard_map/ppermute | solution.py:48
  25.2 13.9 %collective-permute-start.12 = (bf16[16,8192]{1,0:T(8,128)(2,1)S(1)}, bf16[16,8192]{1,0:T(8,128)(2,1)S(1)}, u32[]{:S(2)}, u32[]{:S(2)}) collective-permute-start(bf16[16,8192]{1,0:T(8,128)(2,1)S(1)} %collective-permute-done.11.refs_12_), channel_id=1, source_target_pairs={{0,1},{1,0},{2,3},{3,2},{4,5},{5,4},{6,7},{7,6},{8,9},{9,8},{10,11... | collective-permute-start | bytes 786440 | tf_op jit(solution)/shard_map/ppermute | solution.py:48
  31.2 7.9 %collective-permute-start.8 = (bf16[16,8192]{1,0:T(8,128)(2,1)S(1)}, bf16[16,8192]{1,0:T(8,128)(2,1)S(1)}, u32[]{:S(2)}, u32[]{:S(2)}) collective-permute-start(bf16[16,8192]{1,0:T(8,128)(2,1)S(1)} %collective-permute-done.7.refs_8_), channel_id=1, source_target_pairs={{0,1},{1,0},{2,3},{3,2},{4,5},{5,4},{6,7},{7,6},{8,9},{9,8},{10,11... | collective-permute-start | bytes 786440 | tf_op jit(solution)/shard_map/ppermute | solution.py:48
  31.3 7.9 %collective-permute-start.15 = (bf16[16,4096]{1,0:T(8,128)(2,1)S(1)}, bf16[16,4096]{1,0:T(8,128)(2,1)S(1)}, u32[]{:S(2)}, u32[]{:S(2)}) collective-permute-start(bf16[16,4096]{1,0:T(8,128)(2,1)S(1)} %slice.9), channel_id=1, source_target_pairs={{48,0},{0,16},{16,32},{32,48},{112,64},{64,80},{80,96},{96,112},{4... | collective-permute-start | bytes 393224 | tf_op jit(solution)/shard_map/ppermute | solution.py:52
  32.8 6.4 %collective-permute-start.14 = (bf16[16,4096]{1,0:T(8,128)(2,1)S(1)}, bf16[16,4096]{1,0:T(8,128)(2,1)S(1)}, u32[]{:S(2)}, u32[]{:S(2)}) collective-permute-start(bf16[16,4096]{1,0:T(8,128)(2,1)S(1)} %collective-permute-done.13.refs_14_), channel_id=1, source_target_pairs={{0,1},{1,0},{2,3},{3,2},{4,5},{5,4},{6,7},{7,6},{8,9},{9,8},{10,11... | collective-permute-start | bytes 393224 | tf_op jit(solution)/shard_map/ppermute | solution.py:48
  102.3 5.9 %collective-permute-start.20 = (bf16[16,4096]{1,0:T(8,128)(2,1)S(1)}, bf16[16,4096]{1,0:T(8,128)(2,1)S(1)}, u32[]{:S(2)}, u32[]{:S(2)}) collective-permute-start(bf16[16,4096]{1,0:T(8,128)(2,1)S(1)} %get-tuple-element.45), channel_id=1, source_target_pairs={{0,1},{1,0},{2,3},{3,2},{4,5},{5,4},{6,7},{7,6},{8,9},{9,8},{10,11... | collective-permute-start | bytes 393224 | tf_op jit(solution)/shard_map/ppermute | solution.py:48
  105.2 5.7 %collective-permute-start.19 = (bf16[16,8192]{1,0:T(8,128)(2,1)S(1)}, bf16[16,8192]{1,0:T(8,128)(2,1)S(1)}, u32[]{:S(2)}, u32[]{:S(2)}) collective-permute-start(bf16[16,8192]{1,0:T(8,128)(2,1)S(1)} %get-tuple-element.43), channel_id=1, source_target_pairs={{0,1},{1,0},{2,3},{3,2},{4,5},{5,4},{6,7},{7,6},{8,9},{9,8},{10,11... | collective-permute-start | bytes 786440 | tf_op jit(solution)/shard_map/ppermute | solution.py:48
  108.2 9.9 %collective-permute-start.22 = (bf16[16,8192]{1,0:T(8,128)(2,1)S(1)}, bf16[16,8192]{1,0:T(8,128)(2,1)S(1)}, u32[]{:S(2)}, u32[]{:S(2)}) collective-permute-start(bf16[16,8192]{1,0:T(8,128)(2,1)S(1)} %get-tuple-element.47), channel_id=1, source_target_pairs={{0,1},{1,0},{2,3},{3,2},{4,5},{5,4},{6,7},{7,6},{8,9},{9,8},{10,11... | collective-permute-start | bytes 786440 | tf_op jit(solution)/shard_map/ppermute | solution.py:48
  108.2 21.1 %collective-permute-start.28 = (bf16[16,8192]{1,0:T(8,128)(2,1)S(1)}, bf16[16,8192]{1,0:T(8,128)(2,1)S(1)}, u32[]{:S(2)}, u32[]{:S(2)}) collective-permute-start(bf16[16,8192]{1,0:T(8,128)(2,1)S(1)} %get-tuple-element.58), channel_id=1, source_target_pairs={{0,1},{1,0},{2,3},{3,2},{4,5},{5,4},{6,7},{7,6},{8,9},{9,8},{10,11... | collective-permute-start | bytes 786440 | tf_op jit(solution)/shard_map/ppermute | solution.py:48
  108.9 17.5 %collective-permute-start.32 = (bf16[16,8192]{1,0:T(8,128)(2,1)S(1)}, bf16[16,8192]{1,0:T(8,128)(2,1)S(1)}, u32[]{:S(2)}, u32[]{:S(2)}) collective-permute-start(bf16[16,8192]{1,0:T(8,128)(2,1)S(1)} %get-tuple-element.63), channel_id=1, source_target_pairs={{0,1},{1,0},{2,3},{3,2},{4,5},{5,4},{6,7},{7,6},{8,9},{9,8},{10,11... | collective-permute-start | bytes 786440 | tf_op jit(solution)/shard_map/ppermute | solution.py:48
  110.8 6.6 %collective-permute-start.21 = (bf16[16,4096]{1,0:T(8,128)(2,1)S(1)}, bf16[16,4096]{1,0:T(8,128)(2,1)S(1)}, u32[]{:S(2)}, u32[]{:S(2)}) collective-permute-start(bf16[16,4096]{1,0:T(8,128)(2,1)S(1)} %add_convert_fusion.8), channel_id=1, source_target_pairs={{0,16},{16,32},{32,48},{48,0},{64,80},{80,96},{96,112},{112,64},{1... | collective-permute-start | bytes 393224 | tf_op jit(solution)/shard_map/ppermute | solution.py:56
  110.9 11.7 %collective-permute-start.34 = (bf16[16,8192]{1,0:T(8,128)(2,1)S(1)}, bf16[16,8192]{1,0:T(8,128)(2,1)S(1)}, u32[]{:S(2)}, u32[]{:S(2)}) collective-permute-start(bf16[16,8192]{1,0:T(8,128)(2,1)S(1)} %get-tuple-element.66), channel_id=1, source_target_pairs={{0,1},{1,0},{2,3},{3,2},{4,5},{5,4},{6,7},{7,6},{8,9},{9,8},{10,11... | collective-permute-start | bytes 786440 | tf_op jit(solution)/shard_map/ppermute | solution.py:48
  118.1 25.6 %collective-permute-start.37 = (bf16[16,8192]{1,0:T(8,128)(2,1)S(1)}, bf16[16,8192]{1,0:T(8,128)(2,1)S(1)}, u32[]{:S(2)}, u32[]{:S(2)}) collective-permute-start(bf16[16,8192]{1,0:T(8,128)(2,1)S(1)} %get-tuple-element.69), channel_id=1, source_target_pairs={{0,1},{1,0},{2,3},{3,2},{4,5},{5,4},{6,7},{7,6},{8,9},{9,8},{10,11... | collective-permute-start | bytes 786440 | tf_op jit(solution)/shard_map/ppermute | solution.py:48
  122.6 6.6 %collective-permute-start.33 = (bf16[16,8192]{1,0:T(8,128)(2,1)S(1)}, bf16[16,8192]{1,0:T(8,128)(2,1)S(1)}, u32[]{:S(2)}, u32[]{:S(2)}) collective-permute-start(bf16[16,8192]{1,0:T(8,128)(2,1)S(1)} %add_convert_fusion.5), channel_id=1, source_target_pairs={{0,48},{16,0},{32,16},{48,32},{64,112},{80,64},{96,80},{112,96},{1... | collective-permute-start | bytes 786440 | tf_op jit(solution)/shard_map/ppermute | solution.py:56
  126.3 7.8 %collective-permute-start.31 = (bf16[16,8192]{1,0:T(8,128)(2,1)S(1)}, bf16[16,8192]{1,0:T(8,128)(2,1)S(1)}, u32[]{:S(2)}, u32[]{:S(2)}) collective-permute-start(bf16[16,8192]{1,0:T(8,128)(2,1)S(1)} %add_convert_fusion.4), channel_id=1, source_target_pairs={{0,16},{16,32},{32,48},{48,0},{64,80},{80,96},{96,112},{112,64},{1... | collective-permute-start | bytes 786440 | tf_op jit(solution)/shard_map/ppermute | solution.py:56
  126.5 7.7 %collective-permute-start.29 = (bf16[16,8192]{1,0:T(8,128)(2,1)S(1)}, bf16[16,8192]{1,0:T(8,128)(2,1)S(1)}, u32[]{:S(2)}, u32[]{:S(2)}) collective-permute-start(bf16[16,8192]{1,0:T(8,128)(2,1)S(1)} %add_convert_fusion.6), channel_id=1, source_target_pairs={{0,64},{16,80},{32,96},{48,112},{64,0},{80,16},{96,32},{112,48},{1... | collective-permute-start | bytes 786440 | tf_op jit(solution)/shard_map/ppermute | solution.py:56
  134.3 9.4 %collective-permute-start.38 = (bf16[16,8192]{1,0:T(8,128)(2,1)S(1)}, bf16[16,8192]{1,0:T(8,128)(2,1)S(1)}, u32[]{:S(2)}, u32[]{:S(2)}) collective-permute-start(bf16[16,8192]{1,0:T(8,128)(2,1)S(1)} %add_convert_fusion.3), channel_id=1, source_target_pairs={{0,16},{16,32},{32,48},{48,0},{64,80},{80,96},{96,112},{112,64},{1... | collective-permute-start | bytes 786440 | tf_op jit(solution)/shard_map/ppermute | solution.py:56
  134.4 9.3 %collective-permute-start.39 = (bf16[16,8192]{1,0:T(8,128)(2,1)S(1)}, bf16[16,8192]{1,0:T(8,128)(2,1)S(1)}, u32[]{:S(2)}, u32[]{:S(2)}) collective-permute-start(bf16[16,8192]{1,0:T(8,128)(2,1)S(1)} %add_convert_fusion.1), channel_id=1, source_target_pairs={{0,48},{16,0},{32,16},{48,32},{64,112},{80,64},{96,80},{112,96},{1... | collective-permute-start | bytes 786440 | tf_op jit(solution)/shard_map/ppermute | solution.py:56
  137.6 6.4 %collective-permute-start.40 = (bf16[16,8192]{1,0:T(8,128)(2,1)S(1)}, bf16[16,8192]{1,0:T(8,128)(2,1)S(1)}, u32[]{:S(2)}, u32[]{:S(2)}) collective-permute-start(bf16[16,8192]{1,0:T(8,128)(2,1)S(1)} %add_convert_fusion.2), channel_id=1, source_target_pairs={{0,64},{16,80},{32,96},{48,112},{64,0},{80,16},{96,32},{112,48},{1... | collective-permute-start | bytes 786440 | tf_op jit(solution)/shard_map/ppermute | solution.py:56
  137.8 5.2 %collective-permute-start.36 = (f32[16,256]{1,0:T(8,128)S(1)}, f32[16,256]{1,0:T(8,128)S(1)}, u32[]{:S(2)}, u32[]{:S(2)}) collective-permute-start(f32[16,256]{1,0:T(8,128)S(1)} %add.159), channel_id=1, source_target_pairs={{0,32},{16,48},{32,0},{48,16},{64,96},{80,112},{96,64},{112,80},{1... | collective-permute-start | bytes 49160 | tf_op jit(solution)/shard_map/ppermute | solution.py:413
  (13 other events, 133.6 us)

commit v4 on v3

--- a/solution.py
+++ b/solution.py
@@ -15,6 +15,7 @@
 
 STEPS = ((0, 0), (0, 1), (0, 3), (1, 0), (0, 2), (1, 1), (1, 3), (1, 2))
 UP, DOWN, ACROSS = (0, 1), (0, 3), (1, 0)
+GROUPS = ((7,), (5, 6, 4), (1, 3, 2, 0))
 PIECES = tuple((d, 0, 8192) for d in range(7)) + ((7, 0, 4096), (7, 4096, 4096))
 SLABS = 8
 HALF = 16
@@ -68,13 +69,15 @@
     return pl.ds(pl.multiple_of(block * 128, 128), 128)
 
 
-def load_kernel(info, tiles, out, token, sems):
+def load_kernel(first, info, tiles, out, token, sems):
     core = info[0]
     copies = []
     for g in range(HELD // 4):
         copies.append(
             pltpu.make_async_copy(
-                tiles.at[pl.ds(8 * g + 4 * core, 4)], out.at[pl.ds(4 * g, 4)], sems.at[g]
+                tiles.at[pl.ds(8 * (first + g) + 4 * core, 4)],
+                out.at[pl.ds(4 * g, 4)],
+                sems.at[g],
             )
         )
     for c in copies:
@@ -84,9 +87,9 @@
         c.wait()
 
 
-def load_tiles(info, tiles):
-    return pl.pallas_call(
-        load_kernel,
+def load_tiles(info, tiles, first):
+    held, token = pl.pallas_call(
+        functools.partial(load_kernel, first),
         out_shape=(
             pltpu.VMEM((HELD, SLOTS, 128, 128), BF16),
             jax.ShapeDtypeStruct((8, 128), F32),
@@ -98,6 +101,7 @@
         cost_estimate=pl.CostEstimate(flops=0, bytes_accessed=32 << 20, transcendentals=0),
         name="load_tiles",
     )(info, tiles)
+    return pltpu.with_memory_space_constraint(held, pltpu.VMEM), token
 
 
 WIDE = 1280
@@ -153,8 +157,8 @@
     )(info, mine, received)
 
 
-def forward_kernel(info, cols, held, tiles, *refs):
-    pieces, sides, (out, feats, ring, sems, ring_sems) = refs[:18], refs[18:22], refs[22:]
+def forward_kernel(info, cols, low_tiles, high_tiles, *refs):
+    pieces, sides, (out, feats, sems) = refs[:18], refs[18:22], refs[22:]
     core = info[0]
     copies = []
     for i, (d, first, count) in enumerate(PIECES):
@@ -166,11 +170,7 @@
                     pieces[2 * i + h], feats.at[rows, pl.ds(at, count)], sems.at[2 * i + h]
                 )
             )
-    stream = [
-        pltpu.make_async_copy(tiles.at[row_of(core, HELD + i)], ring.at[i], ring_sems.at[i])
-        for i in range(ROWS - HELD)
-    ]
-    for c in copies + stream:
+    for c in copies:
         c.start()
     for h in range(2):
         rows = pl.ds(pl.multiple_of(jnp.where(core == h, 0, HALF), HALF), HALF)
@@ -218,45 +218,34 @@
                 j = 2 * unit + k
                 out[first // 4, :, 128 * j : 128 * (j + 1)] = value.astype(BF16)
 
-    def held_rows(i, carry):
-        pl.run_scoped(
-            lambda *sums: four_rows(4 * i, held, 0, sums),
-            *[pltpu.ACC(unit)((2 * PAIR, 256), F32) for unit in range(2)],
-        )
-        return carry
-
-    lax.fori_loop(0, HELD // 4, held_rows, 0)
-    for c in stream:
-        c.wait()
-
-    def streamed_rows(i, carry):
-        pl.run_scoped(
-            lambda *sums: four_rows(HELD + 4 * i, ring, HELD, sums),
-            *[pltpu.ACC(unit)((2 * PAIR, 256), F32) for unit in range(2)],
-        )
-        return carry
-
-    lax.fori_loop(0, (ROWS - HELD) // 4, streamed_rows, 0)
-
-
-def forward(info, cols, held, tiles, pieces, sides):
+    for source, offset in ((low_tiles, 0), (high_tiles, HELD)):
+
+        def step(i, carry, source=source, offset=offset):
+            pl.run_scoped(
+                lambda *sums: four_rows(offset + 4 * i, source, offset, sums),
+                *[pltpu.ACC(unit)((2 * PAIR, 256), F32) for unit in range(2)],
+            )
+            return carry
+
+        lax.fori_loop(0, HELD // 4, step, 0)
+
+
+def forward(info, cols, held, pieces, sides):
     return pl.pallas_call(
         forward_kernel,
         out_shape=jax.ShapeDtypeStruct((8, PAIR, WIDE), BF16),
-        in_specs=[SMEM, SMEM, VMEM, ANY] + [ANY] * 18 + [VMEM] * 4,
+        in_specs=[SMEM, SMEM, VMEM, VMEM] + [ANY] * 18 + [VMEM] * 4,
         out_specs=VMEM,
         scratch_shapes=[
             pltpu.VMEM((PAIR, NODES), BF16),
-            pltpu.VMEM((ROWS - HELD, SLOTS, 128, 128), BF16),
             pltpu.SemaphoreType.DMA((18,)),
-            pltpu.SemaphoreType.DMA((ROWS - HELD,)),
         ],
-        compiler_params=pltpu.CompilerParams(vmem_limit_bytes=24 << 20),
+        compiler_params=pltpu.CompilerParams(vmem_limit_bytes=8 << 20),
         cost_estimate=pl.CostEstimate(
             flops=8 * 2 * 1024 * 128 * 128 * 32, bytes_accessed=8 << 20, transcendentals=0
         ),
         name="forward",
-    )(info, cols, held, tiles, *pieces, *sides)
+    )(info, cols, *held, *pieces, *sides)
 
 
 def dense_kernel(message, out):
@@ -287,7 +276,7 @@
 
 
 def backward_kernel(info, cols, tiles, grad, *refs):
-    outs, (total, ring, sems) = refs[:18], refs[18:]
+    outs, (total, ring, sems) = refs[:6], refs[6:]
     core = info[0]
 
     def copy(i):
@@ -335,18 +324,20 @@
 
     own = pl.ds(pl.multiple_of(HALF * core, HALF), HALF)
     other = pl.ds(pl.multiple_of(HALF * (1 - core), HALF), HALF)
-    for i, (d, first, count) in enumerate(PIECES):
-        lanes = pl.ds(pl.multiple_of(info[1 + d] * LOCAL + first, 4096), count)
-        outs[i][...] = total[own, lanes].astype(BF16)
-        outs[9 + i][...] = total[other, lanes].astype(BF16)
+    for phase, group in enumerate(GROUPS):
+        for i, d in enumerate(group):
+            lanes = pl.ds(pl.multiple_of(info[1 + d] * LOCAL, LOCAL), LOCAL)
+            place = slice(LOCAL * i, LOCAL * (i + 1))
+            outs[phase][:, place] = total[own, lanes].astype(BF16)
+            outs[3 + phase][:, place] = total[other, lanes].astype(BF16)
 
 
 def backward(info, cols, tiles, grad):
     return pl.pallas_call(
         backward_kernel,
-        out_shape=[jax.ShapeDtypeStruct((HALF, n), BF16) for _, _, n in PIECES] * 2,
+        out_shape=[jax.ShapeDtypeStruct((HALF, LOCAL * len(g)), BF16) for g in GROUPS] * 2,
         in_specs=[SMEM, SMEM, ANY, VMEM],
-        out_specs=[VMEM] * 18,
+        out_specs=[VMEM] * 6,
         scratch_shapes=[
             pltpu.VMEM((PAIR, NODES), F32),
             pltpu.VMEM((RING, SLOTS, 128, 128), BF16),
@@ -360,6 +351,69 @@
     )(info, cols, tiles, grad)
 
 
+def cut_kernel(across_up, across_down, far, token, up_half, down_half):
+    up_half[...] = across_up[:, :4096]
+    down_half[...] = across_down[:, 4096:]
+
+
+def cut(across_up, across_down, far, token):
+    return pl.pallas_call(
+        cut_kernel,
+        out_shape=[jax.ShapeDtypeStruct((HALF, 4096), BF16)] * 2,
+        in_specs=[VMEM, VMEM, ANY, ANY],
+        out_specs=[VMEM] * 2,
+        compiler_params=pltpu.CompilerParams(vmem_limit_bytes=4 << 20),
+        cost_estimate=pl.CostEstimate(flops=0, bytes_accessed=1 << 19, transcendentals=0),
+        name="cut",
+    )(across_up, across_down, far, token)
+
+
+def sum_call(kernel, shapes, args, name):
+    return pl.pallas_call(
+        kernel,
+        out_shape=[jax.ShapeDtypeStruct(s, t) for s, t in shapes],
+        in_specs=[VMEM] * len(args),
+        out_specs=[VMEM] * len(shapes),
+        compiler_params=pltpu.CompilerParams(vmem_limit_bytes=8 << 20),
+        cost_estimate=pl.CostEstimate(flops=0, bytes_accessed=2 << 20, transcendentals=0),
+        name=name,
+    )(*args)
+
+
+def corner_kernel(own, other, low, high):
+    total = own[...].astype(F32) + other[...].astype(F32)
+    low[...] = total[:, :4096].astype(BF16)
+    high[...] = total[:, 4096:].astype(BF16)
+
+
+def middle_kernel(own, other, low, high, across_up, across_down, far):
+    def mine(i, first, count):
+        lanes = slice(LOCAL * i + first, LOCAL * i + first + count)
+        return own[:, lanes].astype(F32) + other[:, lanes].astype(F32)
+
+    across_up[:, :4096] = (mine(0, 0, 4096) + low[...].astype(F32)).astype(BF16)
+    across_up[:, 4096:] = mine(0, 4096, 4096).astype(BF16)
+    across_down[:, :4096] = mine(1, 0, 4096).astype(BF16)
+    across_down[:, 4096:] = (mine(1, 4096, 4096) + high[...].astype(F32)).astype(BF16)
+    far[...] = mine(2, 0, LOCAL).astype(BF16)
+
+
+def near_kernel(own, other, from_across, from_up, from_down, up, across, down, base):
+    def mine(i):
+        lanes = slice(LOCAL * i, LOCAL * (i + 1))
+        return own[:, lanes].astype(F32) + other[:, lanes].astype(F32)
+
+    up[...] = (mine(0) + from_across[...].astype(F32) + from_down[...].astype(F32)).astype(BF16)
+    across[...] = (mine(1) + from_up[...].astype(F32)).astype(BF16)
+    down[...] = mine(2).astype(BF16)
+    base[...] = mine(3)
+
+
+def last_kernel(base, a, b, c, out):
+    total = base[...] + a[...].astype(F32) + b[...].astype(F32) + c[...].astype(F32)
+    out[...] = total.astype(BF16)
+
+
 def per_device(node_feats, weight, tiles, block_cols, cotangent):
     core = lax.axis_index("feat") % 2
     slab = lax.axis_index("blk")
@@ -368,54 +422,56 @@
     cols = block_cols.T
 
     up, down, across = (receive(node_feats, s) for s in (UP, DOWN, ACROSS))
-    held, token = load_tiles(info, tiles)
-    up2, across2 = after(up, token), after(across, token)
+    low_tiles, token = load_tiles(info, tiles, 0)
+    feats_swapped, cot_swapped = swap(node_feats), swap(cotangent)
+    up2, across2 = after(up, token, feats_swapped, cot_swapped), after(across, token, down)
     far = receive(up2, UP)
     across_up = receive(up2, ACROSS)
     across_down = receive(across2, DOWN)
-    corner = [receive(across_up[:, :4096], UP), receive(across_down[:, 4096:], DOWN)]
-    pieces = []
-    for block in (node_feats, up, down, across, far, across_up, across_down, *corner):
+    high_tiles, token = load_tiles(info, after(tiles, up2, across2), HELD // 4)
+    weight_swapped = swap(after(weight, up2))
+    up_half, down_half = cut(across_up, across_down, far, token)
+    corner = [receive(up_half, UP), receive(down_half, DOWN)]
+    pieces = [node_feats, feats_swapped]
+    for block in (up, down, across, far, across_up, across_down):
+        pieces += [block, swap(after(block, up_half, down_half))]
+    for block in corner:
         pieces += [block, swap(block)]
-    sides = [cotangent, weight, swap(cotangent), swap(weight)]
-    held = pltpu.with_memory_space_constraint(held, pltpu.VMEM)
-
-    message = forward(info, cols, held, tiles, pieces, sides)
+    sides = [cotangent, weight, cot_swapped, weight_swapped]
+
+    message = forward(info, cols, (low_tiles, high_tiles), pieces, sides)
     message = lax.all_to_all(message, "feat", 0, 0, axis_index_groups=SAME_CORE, tiled=True)
     message = dense(message.reshape(256, WIDE)).reshape(8, PAIR, WIDE)
     message = lax.all_to_all(message, "feat", 0, 0, axis_index_groups=SAME_CORE, tiled=True)
-    parts = backward(info, cols, tiles, message)
-
-    def mine(i):
-        return parts[i].astype(F32) + swap(parts[9 + i]).astype(F32)
-
-    def widen(a, low, high):
-        return lax.pad(a, jnp.zeros((), a.dtype), ((0, 0, 0), (low, high, 0))).astype(F32)
-
-    corner_up = send(mine(7).astype(BF16), UP)
-    corner_down = send(mine(8).astype(BF16), DOWN)
-    hidden, hidden_other, wgrad, wgrad_other = unpack(info, after(message, parts[0]))
+
+    own_a, own_b, own_c, other_a, other_b, other_c = backward(info, cols, tiles, message)
+    half, whole = ((HALF, 4096), BF16), ((HALF, LOCAL), BF16)
+    low, high = sum_call(corner_kernel, [half] * 2, (own_a, swap(other_a)), "sum_corner")
+    corner_up, corner_down = send(low, UP), send(high, DOWN)
+    hidden, hidden_other, wgrad, wgrad_other = unpack(info, after(message, low, high))
+    across_up, across_down, far = sum_call(
+        middle_kernel, [whole] * 3, (own_b, swap(other_b), corner_up, corner_down), "sum_middle"
+    )
+    from_across = send(across_up, ACROSS)
+    from_up = send(across_down, DOWN)
+    from_down = send(far, UP)
+    hidden_other, wgrad_other = after(hidden_other, far), after(wgrad_other, far)
     hidden = join(info, hidden, swap(hidden_other))
     wgrad = wgrad + swap(wgrad_other)
     wgrad = wgrad + receive(wgrad, ACROSS)
-    across_up = (mine(5) + widen(corner_up, 0, 4096)).astype(BF16)
-    across_down = (mine(6) + widen(corner_down, 4096, 0)).astype(BF16)
-    across_up, across_down, wgrad, hidden = lax.optimization_barrier(
-        (across_up, across_down, wgrad, hidden)
+    wgrad = wgrad + lax.ppermute(wgrad, "blk", [(b, b ^ 1) for b in range(8)])
+    from_across, wgrad, hidden = lax.optimization_barrier((from_across, wgrad, hidden))
+    up, across, down, base = sum_call(
+        near_kernel,
+        [whole] * 3 + [((HALF, LOCAL), F32)],
+        (own_c, swap(other_c), from_across, from_up, from_down),
+        "sum_near",
     )
-    from_across = send(across_up, ACROSS)
-    from_up = send(across_down, DOWN)
-    from_down = send(mine(4).astype(BF16), UP)
-    wgrad = wgrad + lax.ppermute(wgrad, "blk", [(b, b ^ 1) for b in range(8)])
-    up = (mine(1) + from_across.astype(F32) + from_down.astype(F32)).astype(BF16)
-    across = (mine(3) + from_up.astype(F32)).astype(BF16)
-    up, across, down, wgrad = lax.optimization_barrier((up, across, mine(2).astype(BF16), wgrad))
+    last = [send(up, UP), send(across, ACROSS), send(down, DOWN)]
+    wgrad = after(wgrad, down)
     weight_grad = wgrad + lax.ppermute(wgrad, "blk", [(b, b ^ 2) for b in range(8)])
-    last = [send(up, UP), send(down, DOWN), send(across, ACROSS)]
-    total = mine(0)
-    for a in last:
-        total = total + a.astype(F32)
-    return hidden, weight_grad, total.astype(BF16)
+    (feats_grad,) = sum_call(last_kernel, [whole], (base, *last), "sum_last")
+    return hidden, weight_grad, feats_grad
 
 
 def solution(mesh):

time: 145 us -> 139 us (0.959)
  waiting for transfers between devices: 50.3 us -> 29.2 us
  starting transfers between devices: 20.8 us -> 28.7 us
  Pallas kernels: 35.1 us -> 42.5 us
  other arithmetic: 2.08 us -> 0.62 us
    ppermute x8, waiting for transfers between devices: 18.2 us -> 3.53 us  [send(): return lax.ppermute(a, 'blk', _to_step(step))]
    ppermute x9, waiting for transfers between devices: 22.2 us -> 9.38 us  [receive(): return lax.ppermute(a, 'blk', _from_step(step))]
    pallas_call x2 -> x8, Pallas kernels: 19.6 us -> 27.5 us  [the longest x2 13.5 us: load_tiles(): pl.pallas_call(functools.partial(load_kernel, first), out_shape=(pltpu.VM...]
    ppermute x8, starting transfers between devices: 6.34 us -> 11.9 us  [send(): return lax.ppermute(a, 'blk', _to_step(step))]
    ppermute x22 -> x16, waiting for transfers between devices: 3.37 us -> 7.34 us  [swap(): return lax.ppermute(a, 'feat', CORE_SWAP)]
    ppermute x9, starting transfers between devices: 9.66 us -> 12 us  [receive(): return lax.ppermute(a, 'blk', _from_step(step))]
    ppermute x1, waiting for transfers between devices: 1.87 us -> 3.73 us  [per_device(): wgrad = wgrad + lax.ppermute(wgrad, 'blk', [(b, b ^ 1) for b in range(8)])]
    convert_element_type x9 -> x0, other arithmetic: 1.46 us -> none  [the longest x1 0.88 us: per_device(): return (hidden, weight_grad, total.astype(BF16))]
  transfers between devices with their start and end apart: 41 -> 35, of which waited for: 15 -> 15; matrix products, arithmetic and copies ran while one was open for 1% -> 1% of each run, Pallas kernels for 6% -> 11%
where the time goes in v4:
time: 139 us; the launch traced here: 138 us
  Pallas kernels  42.5 us (31%)
  blocking collectives  35.9 us (26%)
  waiting for transfers between devices  29.2 us (21%)
  starting transfers between devices  28.7 us (21%)
    all_to_all x2, blocking collectives, per_device(): lax.all_to_all(message, 'feat', 0, 0, axis_index_groups=SAME_CORE, tiled=...  35.9 us
    pallas_call x2, Pallas kernels, load_tiles(): pl.pallas_call(functools.partial(load_kernel, first), out_shape=(pltpu.VM...  13.5 us
    pallas_call x1, Pallas kernels, backward(): pl.pallas_call(backward_kernel, out_shape=[jax.ShapeDtypeStruct((HALF, LO...  12.6 us
    pallas_call x1, Pallas kernels, forward(): pl.pallas_call(forward_kernel, out_shape=jax.ShapeDtypeStruct((8, PAIR, W...  12.5 us
    ppermute x9, starting transfers between devices, receive(): return lax.ppermute(a, 'blk', _from_step(step))  12 us
    ppermute x8, starting transfers between devices, send(): return lax.ppermute(a, 'blk', _to_step(step))  11.9 us
    ppermute x9, waiting for transfers between devices, receive(): return lax.ppermute(a, 'blk', _from_step(step))  9.38 us
    ppermute x16, waiting for transfers between devices, swap(): return lax.ppermute(a, 'feat', CORE_SWAP)  7.34 us
  transfers between devices with their start and end apart: 35, of which 15 were waited for; matrix products, arithmetic and copies ran while one was open for 1% of the time, Pallas kernels for 11%

profile of v4, /device:TPU:0, one launch (start us, length us, event | category | flops | bytes accessed | tf_op | source)
XLA Modules:
  0.0 137.9 jit_solution(2719879000690176245)
XLA Ops:
  1.2 3.1 %collective-permute-start = (bf16[16,8192]{1,0:T(8,128)(2,1)}, bf16[16,8192]{1,0:T(8,128)(2,1)S(1)}, u32[]{:S(2)}, u32[]{:S(2)}) collective-permute-start(bf16[16,8192]{1,0:T(8,128)(2,1)} %refs_0_.1), channel_id=1, source_target_pairs={{16,0},{32,16},{48,32},{0,48},{80,64},{96,80},{112,96},{64,112},{1... | collective-permute-start | bytes 786440 | tf_op jit(solution)/shard_map/ppermute | solution.py:53
  4.3 1.5 %collective-permute-start.3 = (bf16[16,8192]{1,0:T(8,128)(2,1)}, bf16[16,8192]{1,0:T(8,128)(2,1)S(1)}, u32[]{:S(2)}, u32[]{:S(2)}) collective-permute-start(bf16[16,8192]{1,0:T(8,128)(2,1)} %refs_0_.1), channel_id=1, source_target_pairs={{64,0},{80,16},{96,32},{112,48},{0,64},{16,80},{32,96},{48,112},{6... | collective-permute-start | bytes 786440 | tf_op jit(solution)/shard_map/ppermute | solution.py:53
  5.9 7.0 %load_tiles.2 = (bf16[16,32,128,128]{3,2,1,0:T(8,128)(2,1)S(1)}, f32[8,128]{1,0:T(8,128)}) custom-call(s32[9]{0:T(128)S(1)} %stack.39.info, bf16[64,32,128,128]{3,2,1,0:T(8,128)(2,1)} %tiles.4), custom_call_target="tpu_custom_call" | custom-call | bytes 33554432 | tf_op jit(solution)/shard_map/load_tiles/pallas_call | solution.py:91
  13.0 3.3 %collective-permute-start.7 = (bf16[16,8192]{1,0:T(8,128)(2,1)S(1)}, bf16[16,8192]{1,0:T(8,128)(2,1)S(1)}, u32[]{:S(2)}, u32[]{:S(2)}) collective-permute-start(bf16[16,8192]{1,0:T(8,128)(2,1)S(1)} %collective-permute-done.refs_2_), channel_id=1, source_target_pairs={{16,0},{32,16},{48,32},{0,48},{80,64},{96,80},{112,96},{64,112},{1... | collective-permute-start | bytes 786440 | tf_op jit(solution)/shard_map/ppermute | solution.py:53
  16.9 6.4 %load_tiles.3 = (bf16[16,32,128,128]{3,2,1,0:T(8,128)(2,1)S(1)}, f32[8,128]{1,0:T(8,128)S(1)}) custom-call(s32[9]{0:T(128)S(1)} %stack.39.info, bf16[64,32,128,128]{3,2,1,0:T(8,128)(2,1)} %tiles.4), custom_call_target="tpu_custom_call" | custom-call | bytes 33554432 | tf_op jit(solution)/shard_map/load_tiles/pallas_call | solution.py:91
  23.5 1.5 %collective-permute-done.6.across_down.refs_12_ = bf16[16,8192]{1,0:T(8,128)(2,1)S(1)} collective-permute-done((bf16[16,8192]{1,0:T(8,128)(2,1)S(1)}, bf16[16,8192]{1,0:T(8,128)(2,1)S(1)}, u32[]{:S(2)}, u32[]{:S(2)}) %collective-permute-start.6) | collective-permute-done | bytes 262176 | tf_op jit(solution)/shard_map/ppermute | solution.py:53
  25.6 1.6 %collective-permute-start.14 = (bf16[16,4096]{1,0:T(8,128)(2,1)S(1)}, bf16[16,4096]{1,0:T(8,128)(2,1)S(1)}, u32[]{:S(2)}, u32[]{:S(2)}) collective-permute-start(bf16[16,4096]{1,0:T(8,128)(2,1)S(1)} %get-tuple-element.52), channel_id=1, source_target_pairs={{16,0},{32,16},{48,32},{0,48},{80,64},{96,80},{112,96},{64,112},{1... | collective-permute-start | bytes 393224 | tf_op jit(solution)/shard_map/ppermute | solution.py:53
  28.1 3.0 %collective-permute-done.14.refs_14_ = bf16[16,4096]{1,0:T(8,128)(2,1)S(1)} collective-permute-done((bf16[16,4096]{1,0:T(8,128)(2,1)S(1)}, bf16[16,4096]{1,0:T(8,128)(2,1)S(1)}, u32[]{:S(2)}, u32[]{:S(2)}) %collective-permute-start.14) | collective-permute-done | bytes 131104 | tf_op jit(solution)/shard_map/ppermute | solution.py:53
  31.1 2.5 %collective-permute-done.16.refs_16_ = bf16[16,4096]{1,0:T(8,128)(2,1)S(1)} collective-permute-done((bf16[16,4096]{1,0:T(8,128)(2,1)S(1)}, bf16[16,4096]{1,0:T(8,128)(2,1)S(1)}, u32[]{:S(2)}, u32[]{:S(2)}) %collective-permute-start.16) | collective-permute-done | bytes 131104 | tf_op jit(solution)/shard_map/ppermute | solution.py:53
  35.9 12.5 %forward.1 = bf16[8,32,1280]{2,1,0:T(8,128)(2,1)S(1)} custom-call(s32[9]{0:T(128)S(1)} %stack.39.info, s32[32,64]{1,0:T(8,128)S(1)} %bitcast.14, bf16[16,32,128,128]{3,2,1,0:T(8,128)(2,1)S(1)} %get-tuple-element.45.low_tiles, bf16[16,32,128,128]{3,2,1,0:T(8,128)(2,1)S(1)} %get-tuple-element.50.high_tiles, bf16[16,8192]{1,0:T(8,128)(2,1)S(1)} %copy-done, ...), custom_call_target="tpu_custom_call" | custom-call | flops 8589934592 | bytes 8388608 | tf_op jit(solution)/shard_map/forward/pallas_call | solution.py:234
  48.5 20.9 %all_to_all.10 = bf16[8,32,1280]{2,1,0:T(8,128)(2,1)S(1)} all-to-all(bf16[8,32,1280]{2,1,0:T(8,128)(2,1)S(1)} %forward.1), channel_id=1, replica_groups={{0,2,4,6,8,10,12,14},{1,3,5,7,9,11,13,15},{16,18,20,22,24,26,28,30},{17..., dimensions={0} | all-to-all | bytes 1310720 | tf_op jit(solution)/shard_map/all_to_all | solution.py:443
  69.3 0.6 dense.1
  70.0 15.0 %all_to_all.11.grad.message = bf16[8,32,1280]{2,1,0:T(8,128)(2,1)S(1)} all-to-all(bf16[8,32,1280]{2,1,0:T(8,128)(2,1)S(1)} %bitcast.13), channel_id=1, replica_groups={{0,2,4,6,8,10,12,14},{1,3,5,7,9,11,13,15},{16,18,20,22,24,26,28,30},{17..., dimensions={0} | all-to-all | bytes 1310720 | tf_op jit(solution)/shard_map/all_to_all | solution.py:445
  85.0 12.6 %backward.1 = (bf16[16,8192]{1,0:T(8,128)(2,1)S(1)}, bf16[16,24576]{1,0:T(8,128)(2,1)S(1)}, bf16[16,32768]{1,0:T(8,128)(2,1)S(1)}, bf16[16,8192]{1,0:T(8,128)(2,...) custom-call(s32[9]{0:T(128)S(1)} %stack.39.info, s32[32,64]{1,0:T(8,128)S(1)} %bitcast.15, ...), custom_call_target="tpu_custom_call" | custom-call | flops 8589934592 | bytes 8388608 | tf_op jit(solution)/shard_map/backward/pallas_call | solution.py:336
  98.3 3.6 %collective-permute-done.20.other = bf16[16,8192]{1,0:T(8,128)(2,1)S(1)} collective-permute-done((bf16[16,8192]{1,0:T(8,128)(2,1)S(1)}, bf16[16,8192]{1,0:T(8,128)(2,1)S(1)}, u32[]{:S(2)}, u32[]{:S(2)}) %collective-permute-start.20) | collective-permute-done | bytes 262176 | tf_op jit(solution)/shard_map/ppermute | solution.py:49
  102.0 3.2 %collective-permute-start.22 = (bf16[16,4096]{1,0:T(8,128)(2,1)S(1)}, bf16[16,4096]{1,0:T(8,128)(2,1)S(1)}, u32[]{:S(2)}, u32[]{:S(2)}) collective-permute-start(bf16[16,4096]{1,0:T(8,128)(2,1)S(1)} %get-tuple-element.66), channel_id=1, source_target_pairs={{0,48},{16,0},{32,16},{48,32},{64,112},{80,64},{96,80},{112,96},{1... | collective-permute-start | bytes 393224 | tf_op jit(solution)/shard_map/ppermute | solution.py:57
  105.2 3.5 %collective-permute-done.21.low = bf16[16,4096]{1,0:T(8,128)(2,1)S(1)} collective-permute-done((bf16[16,4096]{1,0:T(8,128)(2,1)S(1)}, bf16[16,4096]{1,0:T(8,128)(2,1)S(1)}, u32[]{:S(2)}, u32[]{:S(2)}) %collective-permute-start.21) | collective-permute-done | bytes 131104 | tf_op jit(solution)/shard_map/ppermute | solution.py:57
  109.0 0.8 collective-permute-start.23
  109.7 3.0 %collective-permute-start.29 = (bf16[16,8192]{1,0:T(8,128)(2,1)S(1)}, bf16[16,8192]{1,0:T(8,128)(2,1)S(1)}, u32[]{:S(2)}, u32[]{:S(2)}) collective-permute-start(bf16[16,8192]{1,0:T(8,128)(2,1)S(1)} %get-tuple-element.81), channel_id=1, source_target_pairs={{0,48},{16,0},{32,16},{48,32},{64,112},{80,64},{96,80},{112,96},{1... | collective-permute-start | bytes 786440 | tf_op jit(solution)/shard_map/ppermute | solution.py:57
  112.7 0.6 unpack.1
  113.4 1.2 collective-permute-done.24
  114.5 1.5 %collective-permute-start.25 = (f32[16,256]{1,0:T(8,128)S(1)}, f32[16,256]{1,0:T(8,128)S(1)}, u32[]{:S(2)}, u32[]{:S(2)}) collective-permute-start(f32[16,256]{1,0:T(8,128)S(1)} %add.89), channel_id=1, source_target_pairs={{64,0},{80,16},{96,32},{112,48},{0,64},{16,80},{32,96},{48,112},{6... | collective-permute-start | bytes 49160 | tf_op jit(solution)/shard_map/ppermute | solution.py:53
  116.0 2.2 %collective-permute-done.25 = f32[16,256]{1,0:T(8,128)S(1)} collective-permute-done((f32[16,256]{1,0:T(8,128)S(1)}, f32[16,256]{1,0:T(8,128)S(1)}, u32[]{:S(2)}, u32[]{:S(2)}) %collective-permute-start.25) | collective-permute-done | bytes 16416 | tf_op jit(solution)/shard_map/ppermute | solution.py:53
  118.3 3.7 %collective-permute-done.26 = f32[16,256]{1,0:T(8,128)S(1)} collective-permute-done((f32[16,256]{1,0:T(8,128)S(1)}, f32[16,256]{1,0:T(8,128)S(1)}, u32[]{:S(2)}, u32[]{:S(2)}) %collective-permute-start.26) | collective-permute-done | bytes 16416 | tf_op jit(solution)/shard_map/ppermute | solution.py:462
  122.0 1.3 collective-permute-done.27.received
  123.4 1.3 join.1
  125.1 1.6 %collective-permute-start.33 = (bf16[16,8192]{1,0:T(8,128)(2,1)S(1)}, bf16[16,8192]{1,0:T(8,128)(2,1)S(1)}, u32[]{:S(2)}, u32[]{:S(2)}) collective-permute-start(bf16[16,8192]{1,0:T(8,128)(2,1)S(1)} %get-tuple-element.86), channel_id=1, source_target_pairs={{0,64},{16,80},{32,96},{48,112},{64,0},{80,16},{96,32},{112,48},{1... | collective-permute-start | bytes 786440 | tf_op jit(solution)/shard_map/ppermute | solution.py:57
  126.7 3.2 %collective-permute-start.34 = (bf16[16,8192]{1,0:T(8,128)(2,1)S(1)}, bf16[16,8192]{1,0:T(8,128)(2,1)S(1)}, u32[]{:S(2)}, u32[]{:S(2)}) collective-permute-start(bf16[16,8192]{1,0:T(8,128)(2,1)S(1)} %get-tuple-element.82), channel_id=1, source_target_pairs={{0,48},{16,0},{32,16},{48,32},{64,112},{80,64},{96,80},{112,96},{1... | collective-permute-start | bytes 786440 | tf_op jit(solution)/shard_map/ppermute | solution.py:57
  129.9 1.4 collective-permute-start.31
  131.3 5.2 %collective-permute-done.31 = f32[16,256]{1,0:T(8,128)S(1)} collective-permute-done((f32[16,256]{1,0:T(8,128)S(1)}, f32[16,256]{1,0:T(8,128)S(1)}, u32[]{:S(2)}, u32[]{:S(2)}) %collective-permute-start.31) | collective-permute-done | bytes 16416 | tf_op jit(solution)/shard_map/ppermute | solution.py:472
  136.5 0.6 add.92
  137.1 0.8 sum_last.1
  (65 shorter events, 6.8 us)
Async XLA Ops:
  0.6 12.4 %collective-permute-start.2 = (bf16[16,8192]{1,0:T(8,128)(2,1)}, bf16[16,8192]{1,0:T(8,128)(2,1)S(1)}, u32[]{:S(2)}, u32[]{:S(2)}) collective-permute-start(bf16[16,8192]{1,0:T(8,128)(2,1)} %refs_18_.1), channel_id=1, source_target_pairs={{0,1},{1,0},{2,3},{3,2},{4,5},{5,4},{6,7},{7,6},{8,9},{9,8},{10,11... | collective-permute-start | bytes 786440 | tf_op jit(solution)/shard_map/ppermute | solution.py:49
  0.7 12.3 %collective-permute-start.1 = (bf16[16,8192]{1,0:T(8,128)(2,1)}, bf16[16,8192]{1,0:T(8,128)(2,1)S(1)}, u32[]{:S(2)}, u32[]{:S(2)}) collective-permute-start(bf16[16,8192]{1,0:T(8,128)(2,1)} %refs_0_.1), channel_id=1, source_target_pairs={{0,1},{1,0},{2,3},{3,2},{4,5},{5,4},{6,7},{7,6},{8,9},{9,8},{10,11... | collective-permute-start | bytes 786440 | tf_op jit(solution)/shard_map/ppermute | solution.py:49
  1.2 11.8 %collective-permute-start = (bf16[16,8192]{1,0:T(8,128)(2,1)}, bf16[16,8192]{1,0:T(8,128)(2,1)S(1)}, u32[]{:S(2)}, u32[]{:S(2)}) collective-permute-start(bf16[16,8192]{1,0:T(8,128)(2,1)} %refs_0_.1), channel_id=1, source_target_pairs={{16,0},{32,16},{48,32},{0,48},{80,64},{96,80},{112,96},{64,112},{1... | collective-permute-start | bytes 786440 | tf_op jit(solution)/shard_map/ppermute | solution.py:53
  4.3 12.5 %collective-permute-start.3 = (bf16[16,8192]{1,0:T(8,128)(2,1)}, bf16[16,8192]{1,0:T(8,128)(2,1)S(1)}, u32[]{:S(2)}, u32[]{:S(2)}) collective-permute-start(bf16[16,8192]{1,0:T(8,128)(2,1)} %refs_0_.1), channel_id=1, source_target_pairs={{64,0},{80,16},{96,32},{112,48},{0,64},{16,80},{32,96},{48,112},{6... | collective-permute-start | bytes 786440 | tf_op jit(solution)/shard_map/ppermute | solution.py:53
  5.8 11.0 %collective-permute-start.4 = (bf16[16,8192]{1,0:T(8,128)(2,1)}, bf16[16,8192]{1,0:T(8,128)(2,1)S(1)}, u32[]{:S(2)}, u32[]{:S(2)}) collective-permute-start(bf16[16,8192]{1,0:T(8,128)(2,1)} %refs_0_.1), channel_id=1, source_target_pairs={{48,0},{0,16},{16,32},{32,48},{112,64},{64,80},{80,96},{96,112},{4... | collective-permute-start | bytes 786440 | tf_op jit(solution)/shard_map/ppermute | solution.py:53
  13.0 10.3 %collective-permute-start.7 = (bf16[16,8192]{1,0:T(8,128)(2,1)S(1)}, bf16[16,8192]{1,0:T(8,128)(2,1)S(1)}, u32[]{:S(2)}, u32[]{:S(2)}) collective-permute-start(bf16[16,8192]{1,0:T(8,128)(2,1)S(1)} %collective-permute-done.refs_2_), channel_id=1, source_target_pairs={{16,0},{32,16},{48,32},{0,48},{80,64},{96,80},{112,96},{64,112},{1... | collective-permute-start | bytes 786440 | tf_op jit(solution)/shard_map/ppermute | solution.py:53
  16.3 7.2 %collective-permute-start.5 = (bf16[16,8192]{1,0:T(8,128)(2,1)S(1)}, bf16[16,8192]{1,0:T(8,128)(2,1)S(1)}, u32[]{:S(2)}, u32[]{:S(2)}) collective-permute-start(bf16[16,8192]{1,0:T(8,128)(2,1)S(1)} %collective-permute-done.refs_2_), channel_id=1, source_target_pairs={{64,0},{80,16},{96,32},{112,48},{0,64},{16,80},{32,96},{48,112},{6... | collective-permute-start | bytes 786440 | tf_op jit(solution)/shard_map/ppermute | solution.py:53
  16.9 8.1 %collective-permute-start.6 = (bf16[16,8192]{1,0:T(8,128)(2,1)S(1)}, bf16[16,8192]{1,0:T(8,128)(2,1)S(1)}, u32[]{:S(2)}, u32[]{:S(2)}) collective-permute-start(bf16[16,8192]{1,0:T(8,128)(2,1)S(1)} %collective-permute-done.3.refs_6_), channel_id=1, source_target_pairs={{48,0},{0,16},{16,32},{32,48},{112,64},{64,80},{80,96},{96,112},{4... | collective-permute-start | bytes 786440 | tf_op jit(solution)/shard_map/ppermute | solution.py:53
  25.0 8.6 %collective-permute-start.8 = (bf16[16,8192]{1,0:T(8,128)(2,1)S(1)}, bf16[16,8192]{1,0:T(8,128)(2,1)S(1)}, u32[]{:S(2)}, u32[]{:S(2)}) collective-permute-start(bf16[16,8192]{1,0:T(8,128)(2,1)S(1)} %collective-permute-done.refs_2_), channel_id=1, source_target_pairs={{0,1},{1,0},{2,3},{3,2},{4,5},{5,4},{6,7},{7,6},{8,9},{9,8},{10,11... | collective-permute-start | bytes 786440 | tf_op jit(solution)/shard_map/ppermute | solution.py:49
  25.1 2.5 %collective-permute-start.18 = (bf16[16,256]{1,0:T(8,128)(2,1)S(1)}, bf16[16,256]{1,0:T(8,128)(2,1)S(1)}, u32[]{:S(2)}, u32[]{:S(2)}) collective-permute-start(bf16[16,256]{1,0:T(8,128)(2,1)S(1)} %copy-done.3), channel_id=1, source_target_pairs={{0,1},{1,0},{2,3},{3,2},{4,5},{5,4},{6,7},{7,6},{8,9},{9,8},{10,11... | collective-permute-start | bytes 24584 | tf_op jit(solution)/shard_map/ppermute | solution.py:49
  25.6 5.5 %collective-permute-start.14 = (bf16[16,4096]{1,0:T(8,128)(2,1)S(1)}, bf16[16,4096]{1,0:T(8,128)(2,1)S(1)}, u32[]{:S(2)}, u32[]{:S(2)}) collective-permute-start(bf16[16,4096]{1,0:T(8,128)(2,1)S(1)} %get-tuple-element.52), channel_id=1, source_target_pairs={{16,0},{32,16},{48,32},{0,48},{80,64},{96,80},{112,96},{64,112},{1... | collective-permute-start | bytes 393224 | tf_op jit(solution)/shard_map/ppermute | solution.py:53
  27.2 6.4 %collective-permute-start.16 = (bf16[16,4096]{1,0:T(8,128)(2,1)S(1)}, bf16[16,4096]{1,0:T(8,128)(2,1)S(1)}, u32[]{:S(2)}, u32[]{:S(2)}) collective-permute-start(bf16[16,4096]{1,0:T(8,128)(2,1)S(1)} %get-tuple-element.53), channel_id=1, source_target_pairs={{48,0},{0,16},{16,32},{32,48},{112,64},{64,80},{80,96},{96,112},{4... | collective-permute-start | bytes 393224 | tf_op jit(solution)/shard_map/ppermute | solution.py:53
  27.6 6.5 %collective-permute-start.9 = (bf16[16,8192]{1,0:T(8,128)(2,1)S(1)}, bf16[16,8192]{1,0:T(8,128)(2,1)S(1)}, u32[]{:S(2)}, u32[]{:S(2)}) collective-permute-start(bf16[16,8192]{1,0:T(8,128)(2,1)S(1)} %collective-permute-done.4.refs_4_), channel_id=1, source_target_pairs={{0,1},{1,0},{2,3},{3,2},{4,5},{5,4},{6,7},{7,6},{8,9},{9,8},{10,11... | collective-permute-start | bytes 786440 | tf_op jit(solution)/shard_map/ppermute | solution.py:49
  27.6 6.6 %collective-permute-start.10 = (bf16[16,8192]{1,0:T(8,128)(2,1)S(1)}, bf16[16,8192]{1,0:T(8,128)(2,1)S(1)}, u32[]{:S(2)}, u32[]{:S(2)}) collective-permute-start(bf16[16,8192]{1,0:T(8,128)(2,1)S(1)} %collective-permute-done.3.refs_6_), channel_id=1, source_target_pairs={{0,1},{1,0},{2,3},{3,2},{4,5},{5,4},{6,7},{7,6},{8,9},{9,8},{10,11... | collective-permute-start | bytes 786440 | tf_op jit(solution)/shard_map/ppermute | solution.py:49
  31.1 3.6 %collective-permute-start.11 = (bf16[16,8192]{1,0:T(8,128)(2,1)S(1)}, bf16[16,8192]{1,0:T(8,128)(2,1)S(1)}, u32[]{:S(2)}, u32[]{:S(2)}) collective-permute-start(bf16[16,8192]{1,0:T(8,128)(2,1)S(1)} %collective-permute-done.7.far.refs_8_), channel_id=1, source_target_pairs={{0,1},{1,0},{2,3},{3,2},{4,5},{5,4},{6,7},{7,6},{8,9},{9,8},{10,11... | collective-permute-start | bytes 786440 | tf_op jit(solution)/shard_map/ppermute | solution.py:49
  33.6 1.9 %collective-permute-start.13 = (bf16[16,8192]{1,0:T(8,128)(2,1)S(1)}, bf16[16,8192]{1,0:T(8,128)(2,1)S(1)}, u32[]{:S(2)}, u32[]{:S(2)}) collective-permute-start(bf16[16,8192]{1,0:T(8,128)(2,1)S(1)} %collective-permute-done.6.across_down.refs_12_), channel_id=1, source_target_pairs={{0,1},{1,0},{2,3},{3,2},{4,5},{5,4},{6,7},{7,6},{8,9},{9,8},{10,11... | collective-permute-start | bytes 786440 | tf_op jit(solution)/shard_map/ppermute | solution.py:49
  34.1 1.6 %collective-permute-start.15 = (bf16[16,4096]{1,0:T(8,128)(2,1)S(1)}, bf16[16,4096]{1,0:T(8,128)(2,1)S(1)}, u32[]{:S(2)}, u32[]{:S(2)}) collective-permute-start(bf16[16,4096]{1,0:T(8,128)(2,1)S(1)} %collective-permute-done.14.refs_14_), channel_id=1, source_target_pairs={{0,1},{1,0},{2,3},{3,2},{4,5},{5,4},{6,7},{7,6},{8,9},{9,8},{10,11... | collective-permute-start | bytes 393224 | tf_op jit(solution)/shard_map/ppermute | solution.py:49
  34.2 1.7 %collective-permute-start.17 = (bf16[16,4096]{1,0:T(8,128)(2,1)S(1)}, bf16[16,4096]{1,0:T(8,128)(2,1)S(1)}, u32[]{:S(2)}, u32[]{:S(2)}) collective-permute-start(bf16[16,4096]{1,0:T(8,128)(2,1)S(1)} %collective-permute-done.16.refs_16_), channel_id=1, source_target_pairs={{0,1},{1,0},{2,3},{3,2},{4,5},{5,4},{6,7},{7,6},{8,9},{9,8},{10,11... | collective-permute-start | bytes 393224 | tf_op jit(solution)/shard_map/ppermute | solution.py:49
  97.6 11.1 %collective-permute-start.19 = (bf16[16,24576]{1,0:T(8,128)(2,1)S(1)}, bf16[16,24576]{1,0:T(8,128)(2,1)S(1)}, u32[]{:S(2)}, u32[]{:S(2)}) collective-permute-start(bf16[16,24576]{1,0:T(8,128)(2,1)S(1)} %get-tuple-element.62), channel_id=1, source_target_pairs={{0,1},{1,0},{2,3},{3,2},{4,5},{5,4},{6,7},{7,6},{8,9},{9,8},{10,11... | collective-permute-start | bytes 2359304 | tf_op jit(solution)/shard_map/ppermute | solution.py:49
  97.7 27.0 %collective-permute-start.28 = (bf16[16,32768]{1,0:T(8,128)(2,1)S(1)}, bf16[16,32768]{1,0:T(8,128)(2,1)S(1)}, u32[]{:S(2)}, u32[]{:S(2)}) collective-permute-start(bf16[16,32768]{1,0:T(8,128)(2,1)S(1)} %get-tuple-element.79), channel_id=1, source_target_pairs={{0,1},{1,0},{2,3},{3,2},{4,5},{5,4},{6,7},{7,6},{8,9},{9,8},{10,11... | collective-permute-start | bytes 3145736 | tf_op jit(solution)/shard_map/ppermute | solution.py:49
  98.2 3.6 %collective-permute-start.20 = (bf16[16,8192]{1,0:T(8,128)(2,1)S(1)}, bf16[16,8192]{1,0:T(8,128)(2,1)S(1)}, u32[]{:S(2)}, u32[]{:S(2)}) collective-permute-start(bf16[16,8192]{1,0:T(8,128)(2,1)S(1)} %get-tuple-element.64), channel_id=1, source_target_pairs={{0,1},{1,0},{2,3},{3,2},{4,5},{5,4},{6,7},{7,6},{8,9},{9,8},{10,11... | collective-permute-start | bytes 786440 | tf_op jit(solution)/shard_map/ppermute | solution.py:49
  101.9 6.8 %collective-permute-start.21 = (bf16[16,4096]{1,0:T(8,128)(2,1)S(1)}, bf16[16,4096]{1,0:T(8,128)(2,1)S(1)}, u32[]{:S(2)}, u32[]{:S(2)}) collective-permute-start(bf16[16,4096]{1,0:T(8,128)(2,1)S(1)} %get-tuple-element.65), channel_id=1, source_target_pairs={{0,16},{16,32},{32,48},{48,0},{64,80},{80,96},{96,112},{112,64},{1... | collective-permute-start | bytes 393224 | tf_op jit(solution)/shard_map/ppermute | solution.py:57
  102.0 6.7 %collective-permute-start.22 = (bf16[16,4096]{1,0:T(8,128)(2,1)S(1)}, bf16[16,4096]{1,0:T(8,128)(2,1)S(1)}, u32[]{:S(2)}, u32[]{:S(2)}) collective-permute-start(bf16[16,4096]{1,0:T(8,128)(2,1)S(1)} %get-tuple-element.66), channel_id=1, source_target_pairs={{0,48},{16,0},{32,16},{48,32},{64,112},{80,64},{96,80},{112,96},{1... | collective-permute-start | bytes 393224 | tf_op jit(solution)/shard_map/ppermute | solution.py:57
  109.0 15.7 %collective-permute-start.23 = (bf16[16,8192]{1,0:T(8,128)(2,1)S(1)}, bf16[16,8192]{1,0:T(8,128)(2,1)S(1)}, u32[]{:S(2)}, u32[]{:S(2)}) collective-permute-start(bf16[16,8192]{1,0:T(8,128)(2,1)S(1)} %get-tuple-element.67), channel_id=1, source_target_pairs={{0,64},{16,80},{32,96},{48,112},{64,0},{80,16},{96,32},{112,48},{1... | collective-permute-start | bytes 786440 | tf_op jit(solution)/shard_map/ppermute | solution.py:57
  109.7 14.9 %collective-permute-start.29 = (bf16[16,8192]{1,0:T(8,128)(2,1)S(1)}, bf16[16,8192]{1,0:T(8,128)(2,1)S(1)}, u32[]{:S(2)}, u32[]{:S(2)}) collective-permute-start(bf16[16,8192]{1,0:T(8,128)(2,1)S(1)} %get-tuple-element.81), channel_id=1, source_target_pairs={{0,48},{16,0},{32,16},{48,32},{64,112},{80,64},{96,80},{112,96},{1... | collective-permute-start | bytes 786440 | tf_op jit(solution)/shard_map/ppermute | solution.py:57
  112.7 12.0 %collective-permute-start.30 = (bf16[16,8192]{1,0:T(8,128)(2,1)S(1)}, bf16[16,8192]{1,0:T(8,128)(2,1)S(1)}, u32[]{:S(2)}, u32[]{:S(2)}) collective-permute-start(bf16[16,8192]{1,0:T(8,128)(2,1)S(1)} %get-tuple-element.71), channel_id=1, source_target_pairs={{0,16},{16,32},{32,48},{48,0},{64,80},{80,96},{96,112},{112,64},{1... | collective-permute-start | bytes 786440 | tf_op jit(solution)/shard_map/ppermute | solution.py:57
  114.5 3.7 %collective-permute-start.25 = (f32[16,256]{1,0:T(8,128)S(1)}, f32[16,256]{1,0:T(8,128)S(1)}, u32[]{:S(2)}, u32[]{:S(2)}) collective-permute-start(f32[16,256]{1,0:T(8,128)S(1)} %add.89), channel_id=1, source_target_pairs={{64,0},{80,16},{96,32},{112,48},{0,64},{16,80},{32,96},{48,112},{6... | collective-permute-start | bytes 49160 | tf_op jit(solution)/shard_map/ppermute | solution.py:53
  118.3 3.7 %collective-permute-start.26 = (f32[16,256]{1,0:T(8,128)S(1)}, f32[16,256]{1,0:T(8,128)S(1)}, u32[]{:S(2)}, u32[]{:S(2)}) collective-permute-start(f32[16,256]{1,0:T(8,128)S(1)} %add.90), channel_id=1, source_target_pairs={{0,16},{16,0},{32,48},{48,32},{64,80},{80,64},{96,112},{112,96},{1... | collective-permute-start | bytes 49160 | tf_op jit(solution)/shard_map/ppermute | solution.py:462
  125.0 12.1 %collective-permute-start.32 = (bf16[16,8192]{1,0:T(8,128)(2,1)S(1)}, bf16[16,8192]{1,0:T(8,128)(2,1)S(1)}, u32[]{:S(2)}, u32[]{:S(2)}) collective-permute-start(bf16[16,8192]{1,0:T(8,128)(2,1)S(1)} %get-tuple-element.85), channel_id=1, source_target_pairs={{0,16},{16,32},{32,48},{48,0},{64,80},{80,96},{96,112},{112,64},{1... | collective-permute-start | bytes 786440 | tf_op jit(solution)/shard_map/ppermute | solution.py:57
  125.1 12.0 %collective-permute-start.33 = (bf16[16,8192]{1,0:T(8,128)(2,1)S(1)}, bf16[16,8192]{1,0:T(8,128)(2,1)S(1)}, u32[]{:S(2)}, u32[]{:S(2)}) collective-permute-start(bf16[16,8192]{1,0:T(8,128)(2,1)S(1)} %get-tuple-element.86), channel_id=1, source_target_pairs={{0,64},{16,80},{32,96},{48,112},{64,0},{80,16},{96,32},{112,48},{1... | collective-permute-start | bytes 786440 | tf_op jit(solution)/shard_map/ppermute | solution.py:57
  126.7 10.4 %collective-permute-start.34 = (bf16[16,8192]{1,0:T(8,128)(2,1)S(1)}, bf16[16,8192]{1,0:T(8,128)(2,1)S(1)}, u32[]{:S(2)}, u32[]{:S(2)}) collective-permute-start(bf16[16,8192]{1,0:T(8,128)(2,1)S(1)} %get-tuple-element.82), channel_id=1, source_target_pairs={{0,48},{16,0},{32,16},{48,32},{64,112},{80,64},{96,80},{112,96},{1... | collective-permute-start | bytes 786440 | tf_op jit(solution)/shard_map/ppermute | solution.py:57
  129.9 6.5 %collective-permute-start.31 = (f32[16,256]{1,0:T(8,128)S(1)}, f32[16,256]{1,0:T(8,128)S(1)}, u32[]{:S(2)}, u32[]{:S(2)}) collective-permute-start(f32[16,256]{1,0:T(8,128)S(1)} %add.91), channel_id=1, source_target_pairs={{0,32},{16,48},{32,0},{48,16},{64,96},{80,112},{96,64},{112,80},{1... | collective-permute-start | bytes 49160 | tf_op jit(solution)/shard_map/ppermute | solution.py:472
  (7 other events, 85.2 us)

commit v5 on v4

--- a/solution.py
+++ b/solution.py
@@ -368,16 +368,19 @@
     )(across_up, across_down, far, token)
 
 
-def sum_call(kernel, shapes, args, name):
-    return pl.pallas_call(
-        kernel,
+def sum_call(kernel, shapes, args, name, before=()):
+    def body(*refs):
+        kernel(*refs[: len(args)], *refs[len(args) + len(before) :])
+
+    return pl.pallas_call(
+        body,
         out_shape=[jax.ShapeDtypeStruct(s, t) for s, t in shapes],
-        in_specs=[VMEM] * len(args),
+        in_specs=[VMEM] * len(args) + [ANY] * len(before),
         out_specs=[VMEM] * len(shapes),
         compiler_params=pltpu.CompilerParams(vmem_limit_bytes=8 << 20),
         cost_estimate=pl.CostEstimate(flops=0, bytes_accessed=2 << 20, transcendentals=0),
         name=name,
-    )(*args)
+    )(*args, *before)
 
 
 def corner_kernel(own, other, low, high):
@@ -449,27 +452,31 @@
     low, high = sum_call(corner_kernel, [half] * 2, (own_a, swap(other_a)), "sum_corner")
     corner_up, corner_down = send(low, UP), send(high, DOWN)
     hidden, hidden_other, wgrad, wgrad_other = unpack(info, after(message, low, high))
+    wgrad_other, hidden_other = swap(wgrad_other), swap(hidden_other)
     across_up, across_down, far = sum_call(
-        middle_kernel, [whole] * 3, (own_b, swap(other_b), corner_up, corner_down), "sum_middle"
+        middle_kernel,
+        [whole] * 3,
+        (own_b, swap(after(other_b, low, high)), corner_up, corner_down),
+        "sum_middle",
+        before=(wgrad_other, hidden_other),
     )
     from_across = send(across_up, ACROSS)
     from_up = send(across_down, DOWN)
     from_down = send(far, UP)
-    hidden_other, wgrad_other = after(hidden_other, far), after(wgrad_other, far)
-    hidden = join(info, hidden, swap(hidden_other))
-    wgrad = wgrad + swap(wgrad_other)
+    wgrad = wgrad + after(wgrad_other, far)
     wgrad = wgrad + receive(wgrad, ACROSS)
-    wgrad = wgrad + lax.ppermute(wgrad, "blk", [(b, b ^ 1) for b in range(8)])
-    from_across, wgrad, hidden = lax.optimization_barrier((from_across, wgrad, hidden))
     up, across, down, base = sum_call(
         near_kernel,
         [whole] * 3 + [((HALF, LOCAL), F32)],
-        (own_c, swap(other_c), from_across, from_up, from_down),
+        (own_c, swap(after(other_c, far)), from_across, from_up, from_down),
         "sum_near",
+        before=(wgrad,),
     )
     last = [send(up, UP), send(across, ACROSS), send(down, DOWN)]
     wgrad = after(wgrad, down)
+    wgrad = wgrad + lax.ppermute(wgrad, "blk", [(b, b ^ 1) for b in range(8)])
     weight_grad = wgrad + lax.ppermute(wgrad, "blk", [(b, b ^ 2) for b in range(8)])
+    hidden = join(info, after(hidden, down), hidden_other)
     (feats_grad,) = sum_call(last_kernel, [whole], (base, *last), "sum_last")
     return hidden, weight_grad, feats_grad
 

time: 139 us -> 137 us (0.986)
  waiting for transfers between devices: 29.2 us -> 26.6 us
    ppermute x1, waiting for transfers between devices: 5.17 us -> 1.25 us  [per_device(): lax.ppermute(wgrad, 'blk', [(b, b ^ 2) for b in range(8)])]
    ppermute x16, waiting for transfers between devices: 7.34 us -> 3.98 us  [swap(): return lax.ppermute(a, 'feat', CORE_SWAP)]
    ppermute x8, waiting for transfers between devices: 3.53 us -> 6.16 us  [send(): return lax.ppermute(a, 'blk', _to_step(step))]
    ppermute x9, waiting for transfers between devices: 9.38 us -> 11.1 us  [receive(): return lax.ppermute(a, 'blk', _from_step(step))]
  transfers between devices with their start and end apart: 35 -> 35, of which waited for: 15 -> 16; matrix products, arithmetic and copies ran while one was open for 1% -> 1% of each run, Pallas kernels for 11% -> 11%
where the time goes in v5:
time: 137 us; the launch traced here: 136 us
  Pallas kernels  42.5 us (31%)
  blocking collectives  35.9 us (26%)
  starting transfers between devices  29.8 us (22%)
  waiting for transfers between devices  26.6 us (19%)
    all_to_all x2, blocking collectives, per_device(): lax.all_to_all(message, 'feat', 0, 0, axis_index_groups=SAME_CORE, tiled=...  35.9 us
    pallas_call x2, Pallas kernels, load_tiles(): pl.pallas_call(functools.partial(load_kernel, first), out_shape=(pltpu.VM...  13.5 us
    pallas_call x1, Pallas kernels, backward(): pl.pallas_call(backward_kernel, out_shape=[jax.ShapeDtypeStruct((HALF, LO...  12.6 us
    pallas_call x1, Pallas kernels, forward(): pl.pallas_call(forward_kernel, out_shape=jax.ShapeDtypeStruct((8, PAIR, W...  12.5 us
    ppermute x9, starting transfers between devices, receive(): return lax.ppermute(a, 'blk', _from_step(step))  12 us
    ppermute x8, starting transfers between devices, send(): return lax.ppermute(a, 'blk', _to_step(step))  11.6 us
    ppermute x9, waiting for transfers between devices, receive(): return lax.ppermute(a, 'blk', _from_step(step))  11.1 us
    ppermute x8, waiting for transfers between devices, send(): return lax.ppermute(a, 'blk', _to_step(step))  6.16 us
  transfers between devices with their start and end apart: 35, of which 16 were waited for; matrix products, arithmetic and copies ran while one was open for 1% of the time, Pallas kernels for 11%

profile of v5, /device:TPU:0, one launch (start us, length us, event | category | flops | bytes accessed | tf_op | source)
XLA Modules:
  0.0 136.5 jit_solution(18362524967042022692)
XLA Ops:
  1.2 3.1 %collective-permute-start = (bf16[16,8192]{1,0:T(8,128)(2,1)}, bf16[16,8192]{1,0:T(8,128)(2,1)S(1)}, u32[]{:S(2)}, u32[]{:S(2)}) collective-permute-start(bf16[16,8192]{1,0:T(8,128)(2,1)} %refs_0_.1), channel_id=1, source_target_pairs={{16,0},{32,16},{48,32},{0,48},{80,64},{96,80},{112,96},{64,112},{1... | collective-permute-start | bytes 786440 | tf_op jit(solution)/shard_map/ppermute | solution.py:53
  4.3 1.5 %collective-permute-start.3 = (bf16[16,8192]{1,0:T(8,128)(2,1)}, bf16[16,8192]{1,0:T(8,128)(2,1)S(1)}, u32[]{:S(2)}, u32[]{:S(2)}) collective-permute-start(bf16[16,8192]{1,0:T(8,128)(2,1)} %refs_0_.1), channel_id=1, source_target_pairs={{64,0},{80,16},{96,32},{112,48},{0,64},{16,80},{32,96},{48,112},{6... | collective-permute-start | bytes 786440 | tf_op jit(solution)/shard_map/ppermute | solution.py:53
  5.9 7.0 %load_tiles.2 = (bf16[16,32,128,128]{3,2,1,0:T(8,128)(2,1)S(1)}, f32[8,128]{1,0:T(8,128)}) custom-call(s32[9]{0:T(128)S(1)} %stack.39.info, bf16[64,32,128,128]{3,2,1,0:T(8,128)(2,1)} %tiles.4), custom_call_target="tpu_custom_call" | custom-call | bytes 33554432 | tf_op jit(solution)/shard_map/load_tiles/pallas_call | solution.py:91
  13.0 3.3 %collective-permute-start.7 = (bf16[16,8192]{1,0:T(8,128)(2,1)S(1)}, bf16[16,8192]{1,0:T(8,128)(2,1)S(1)}, u32[]{:S(2)}, u32[]{:S(2)}) collective-permute-start(bf16[16,8192]{1,0:T(8,128)(2,1)S(1)} %collective-permute-done.refs_2_), channel_id=1, source_target_pairs={{16,0},{32,16},{48,32},{0,48},{80,64},{96,80},{112,96},{64,112},{1... | collective-permute-start | bytes 786440 | tf_op jit(solution)/shard_map/ppermute | solution.py:53
  16.9 6.4 %load_tiles.3 = (bf16[16,32,128,128]{3,2,1,0:T(8,128)(2,1)S(1)}, f32[8,128]{1,0:T(8,128)S(1)}) custom-call(s32[9]{0:T(128)S(1)} %stack.39.info, bf16[64,32,128,128]{3,2,1,0:T(8,128)(2,1)} %tiles.4), custom_call_target="tpu_custom_call" | custom-call | bytes 33554432 | tf_op jit(solution)/shard_map/load_tiles/pallas_call | solution.py:91
  23.5 1.5 %collective-permute-done.6.across_down.refs_12_ = bf16[16,8192]{1,0:T(8,128)(2,1)S(1)} collective-permute-done((bf16[16,8192]{1,0:T(8,128)(2,1)S(1)}, bf16[16,8192]{1,0:T(8,128)(2,1)S(1)}, u32[]{:S(2)}, u32[]{:S(2)}) %collective-permute-start.6) | collective-permute-done | bytes 262176 | tf_op jit(solution)/shard_map/ppermute | solution.py:53
  25.6 1.6 %collective-permute-start.14 = (bf16[16,4096]{1,0:T(8,128)(2,1)S(1)}, bf16[16,4096]{1,0:T(8,128)(2,1)S(1)}, u32[]{:S(2)}, u32[]{:S(2)}) collective-permute-start(bf16[16,4096]{1,0:T(8,128)(2,1)S(1)} %get-tuple-element.51), channel_id=1, source_target_pairs={{16,0},{32,16},{48,32},{0,48},{80,64},{96,80},{112,96},{64,112},{1... | collective-permute-start | bytes 393224 | tf_op jit(solution)/shard_map/ppermute | solution.py:53
  28.1 3.0 %collective-permute-done.14.refs_14_ = bf16[16,4096]{1,0:T(8,128)(2,1)S(1)} collective-permute-done((bf16[16,4096]{1,0:T(8,128)(2,1)S(1)}, bf16[16,4096]{1,0:T(8,128)(2,1)S(1)}, u32[]{:S(2)}, u32[]{:S(2)}) %collective-permute-start.14) | collective-permute-done | bytes 131104 | tf_op jit(solution)/shard_map/ppermute | solution.py:53
  31.1 2.5 %collective-permute-done.16.refs_16_ = bf16[16,4096]{1,0:T(8,128)(2,1)S(1)} collective-permute-done((bf16[16,4096]{1,0:T(8,128)(2,1)S(1)}, bf16[16,4096]{1,0:T(8,128)(2,1)S(1)}, u32[]{:S(2)}, u32[]{:S(2)}) %collective-permute-start.16) | collective-permute-done | bytes 131104 | tf_op jit(solution)/shard_map/ppermute | solution.py:53
  35.9 12.5 %forward.1 = bf16[8,32,1280]{2,1,0:T(8,128)(2,1)S(1)} custom-call(s32[9]{0:T(128)S(1)} %stack.39.info, s32[32,64]{1,0:T(8,128)S(1)} %bitcast.14, bf16[16,32,128,128]{3,2,1,0:T(8,128)(2,1)S(1)} %get-tuple-element.44.low_tiles, bf16[16,32,128,128]{3,2,1,0:T(8,128)(2,1)S(1)} %get-tuple-element.49.high_tiles, bf16[16,8192]{1,0:T(8,128)(2,1)S(1)} %copy-done, ...), custom_call_target="tpu_custom_call" | custom-call | flops 8589934592 | bytes 8388608 | tf_op jit(solution)/shard_map/forward/pallas_call | solution.py:234
  48.5 20.9 %all_to_all.10 = bf16[8,32,1280]{2,1,0:T(8,128)(2,1)S(1)} all-to-all(bf16[8,32,1280]{2,1,0:T(8,128)(2,1)S(1)} %forward.1), channel_id=1, replica_groups={{0,2,4,6,8,10,12,14},{1,3,5,7,9,11,13,15},{16,18,20,22,24,26,28,30},{17..., dimensions={0} | all-to-all | bytes 1310720 | tf_op jit(solution)/shard_map/all_to_all | solution.py:446
  69.3 0.6 dense.1
  70.0 15.0 %all_to_all.11.grad.message = bf16[8,32,1280]{2,1,0:T(8,128)(2,1)S(1)} all-to-all(bf16[8,32,1280]{2,1,0:T(8,128)(2,1)S(1)} %bitcast.13), channel_id=1, replica_groups={{0,2,4,6,8,10,12,14},{1,3,5,7,9,11,13,15},{16,18,20,22,24,26,28,30},{17..., dimensions={0} | all-to-all | bytes 1310720 | tf_op jit(solution)/shard_map/all_to_all | solution.py:448
  85.0 12.6 %backward.1 = (bf16[16,8192]{1,0:T(8,128)(2,1)S(1)}, bf16[16,24576]{1,0:T(8,128)(2,1)S(1)}, bf16[16,32768]{1,0:T(8,128)(2,1)S(1)}, bf16[16,8192]{1,0:T(8,128)(2,...) custom-call(s32[9]{0:T(128)S(1)} %stack.39.info, s32[32,64]{1,0:T(8,128)S(1)} %bitcast.15, ...), custom_call_target="tpu_custom_call" | custom-call | flops 8589934592 | bytes 8388608 | tf_op jit(solution)/shard_map/backward/pallas_call | solution.py:336
  97.7 1.5 %collective-permute-done.19.refs_1_ = bf16[16,8192]{1,0:T(8,128)(2,1)S(1)} collective-permute-done((bf16[16,8192]{1,0:T(8,128)(2,1)S(1)}, bf16[16,8192]{1,0:T(8,128)(2,1)S(1)}, u32[]{:S(2)}, u32[]{:S(2)}) %collective-permute-start.19) | collective-permute-done | bytes 262176 | tf_op jit(solution)/shard_map/ppermute | solution.py:49
  99.5 0.6 unpack.1
  100.5 3.2 %collective-permute-start.22 = (bf16[16,4096]{1,0:T(8,128)(2,1)S(1)}, bf16[16,4096]{1,0:T(8,128)(2,1)S(1)}, u32[]{:S(2)}, u32[]{:S(2)}) collective-permute-start(bf16[16,4096]{1,0:T(8,128)(2,1)S(1)} %get-tuple-element.63), channel_id=1, source_target_pairs={{0,48},{16,0},{32,16},{48,32},{64,112},{80,64},{96,80},{112,96},{1... | collective-permute-start | bytes 393224 | tf_op jit(solution)/shard_map/ppermute | solution.py:57
  103.8 1.2 collective-permute-done.23.refs_4_
  105.0 2.3 %collective-permute-done.21.refs_2_ = bf16[16,4096]{1,0:T(8,128)(2,1)S(1)} collective-permute-done((bf16[16,4096]{1,0:T(8,128)(2,1)S(1)}, bf16[16,4096]{1,0:T(8,128)(2,1)S(1)}, u32[]{:S(2)}, u32[]{:S(2)}) %collective-permute-start.21) | collective-permute-done | bytes 131104 | tf_op jit(solution)/shard_map/ppermute | solution.py:57
  107.6 0.7 collective-permute-start.26
  108.3 3.0 %collective-permute-start.27 = (bf16[16,8192]{1,0:T(8,128)(2,1)S(1)}, bf16[16,8192]{1,0:T(8,128)(2,1)S(1)}, u32[]{:S(2)}, u32[]{:S(2)}) collective-permute-start(bf16[16,8192]{1,0:T(8,128)(2,1)S(1)} %get-tuple-element.76), channel_id=1, source_target_pairs={{0,48},{16,0},{32,16},{48,32},{64,112},{80,64},{96,80},{112,96},{1... | collective-permute-start | bytes 786440 | tf_op jit(solution)/shard_map/ppermute | solution.py:57
  111.2 1.5 %collective-permute-start.29 = (f32[16,256]{1,0:T(8,128)S(1)}, f32[16,256]{1,0:T(8,128)S(1)}, u32[]{:S(2)}, u32[]{:S(2)}) collective-permute-start(f32[16,256]{1,0:T(8,128)S(1)} %add.89), channel_id=1, source_target_pairs={{64,0},{80,16},{96,32},{112,48},{0,64},{16,80},{32,96},{48,112},{6... | collective-permute-start | bytes 49160 | tf_op jit(solution)/shard_map/ppermute | solution.py:53
  112.7 3.9 %collective-permute-done.29 = f32[16,256]{1,0:T(8,128)S(1)} collective-permute-done((f32[16,256]{1,0:T(8,128)S(1)}, f32[16,256]{1,0:T(8,128)S(1)}, u32[]{:S(2)}, u32[]{:S(2)}) %collective-permute-start.29) | collective-permute-done | bytes 16416 | tf_op jit(solution)/shard_map/ppermute | solution.py:53
  117.1 3.4 %collective-permute-done.28.refs_4_ = bf16[16,8192]{1,0:T(8,128)(2,1)S(1)} collective-permute-done((bf16[16,8192]{1,0:T(8,128)(2,1)S(1)}, bf16[16,8192]{1,0:T(8,128)(2,1)S(1)}, u32[]{:S(2)}, u32[]{:S(2)}) %collective-permute-start.28) | collective-permute-done | bytes 262176 | tf_op jit(solution)/shard_map/ppermute | solution.py:57
  120.9 1.5 %collective-permute-start.33 = (bf16[16,8192]{1,0:T(8,128)(2,1)S(1)}, bf16[16,8192]{1,0:T(8,128)(2,1)S(1)}, u32[]{:S(2)}, u32[]{:S(2)}) collective-permute-start(bf16[16,8192]{1,0:T(8,128)(2,1)S(1)} %get-tuple-element.84), channel_id=1, source_target_pairs={{0,64},{16,80},{32,96},{48,112},{64,0},{80,16},{96,32},{112,48},{1... | collective-permute-start | bytes 786440 | tf_op jit(solution)/shard_map/ppermute | solution.py:57
  122.5 3.1 %collective-permute-start.34 = (bf16[16,8192]{1,0:T(8,128)(2,1)S(1)}, bf16[16,8192]{1,0:T(8,128)(2,1)S(1)}, u32[]{:S(2)}, u32[]{:S(2)}) collective-permute-start(bf16[16,8192]{1,0:T(8,128)(2,1)S(1)} %get-tuple-element.79), channel_id=1, source_target_pairs={{0,48},{16,0},{32,16},{48,32},{64,112},{80,64},{96,80},{112,96},{1... | collective-permute-start | bytes 786440 | tf_op jit(solution)/shard_map/ppermute | solution.py:57
  125.6 4.2 %collective-permute-done.30 = f32[16,256]{1,0:T(8,128)S(1)} collective-permute-done((f32[16,256]{1,0:T(8,128)S(1)}, f32[16,256]{1,0:T(8,128)S(1)}, u32[]{:S(2)}, u32[]{:S(2)}) %collective-permute-start.30) | collective-permute-done | bytes 16416 | tf_op jit(solution)/shard_map/ppermute | solution.py:477
  129.8 2.7 %collective-permute-start.31 = (f32[16,256]{1,0:T(8,128)S(1)}, f32[16,256]{1,0:T(8,128)S(1)}, u32[]{:S(2)}, u32[]{:S(2)}) collective-permute-start(f32[16,256]{1,0:T(8,128)S(1)} %add.91), channel_id=1, source_target_pairs={{0,32},{16,48},{32,0},{48,16},{64,96},{80,112},{96,64},{112,80},{1... | collective-permute-start | bytes 49160 | tf_op jit(solution)/shard_map/ppermute | solution.py:478
  132.5 1.3 join.1
  133.8 1.3 collective-permute-done.31
  135.0 0.6 add.92
  135.6 0.8 sum_last.1
  (65 shorter events, 7.2 us)
Async XLA Ops:
  0.6 12.4 %collective-permute-start.2 = (bf16[16,8192]{1,0:T(8,128)(2,1)}, bf16[16,8192]{1,0:T(8,128)(2,1)S(1)}, u32[]{:S(2)}, u32[]{:S(2)}) collective-permute-start(bf16[16,8192]{1,0:T(8,128)(2,1)} %refs_18_.1), channel_id=1, source_target_pairs={{0,1},{1,0},{2,3},{3,2},{4,5},{5,4},{6,7},{7,6},{8,9},{9,8},{10,11... | collective-permute-start | bytes 786440 | tf_op jit(solution)/shard_map/ppermute | solution.py:49
  0.7 12.3 %collective-permute-start.1 = (bf16[16,8192]{1,0:T(8,128)(2,1)}, bf16[16,8192]{1,0:T(8,128)(2,1)S(1)}, u32[]{:S(2)}, u32[]{:S(2)}) collective-permute-start(bf16[16,8192]{1,0:T(8,128)(2,1)} %refs_0_.1), channel_id=1, source_target_pairs={{0,1},{1,0},{2,3},{3,2},{4,5},{5,4},{6,7},{7,6},{8,9},{9,8},{10,11... | collective-permute-start | bytes 786440 | tf_op jit(solution)/shard_map/ppermute | solution.py:49
  1.2 11.8 %collective-permute-start = (bf16[16,8192]{1,0:T(8,128)(2,1)}, bf16[16,8192]{1,0:T(8,128)(2,1)S(1)}, u32[]{:S(2)}, u32[]{:S(2)}) collective-permute-start(bf16[16,8192]{1,0:T(8,128)(2,1)} %refs_0_.1), channel_id=1, source_target_pairs={{16,0},{32,16},{48,32},{0,48},{80,64},{96,80},{112,96},{64,112},{1... | collective-permute-start | bytes 786440 | tf_op jit(solution)/shard_map/ppermute | solution.py:53
  4.3 12.5 %collective-permute-start.3 = (bf16[16,8192]{1,0:T(8,128)(2,1)}, bf16[16,8192]{1,0:T(8,128)(2,1)S(1)}, u32[]{:S(2)}, u32[]{:S(2)}) collective-permute-start(bf16[16,8192]{1,0:T(8,128)(2,1)} %refs_0_.1), channel_id=1, source_target_pairs={{64,0},{80,16},{96,32},{112,48},{0,64},{16,80},{32,96},{48,112},{6... | collective-permute-start | bytes 786440 | tf_op jit(solution)/shard_map/ppermute | solution.py:53
  5.8 11.0 %collective-permute-start.4 = (bf16[16,8192]{1,0:T(8,128)(2,1)}, bf16[16,8192]{1,0:T(8,128)(2,1)S(1)}, u32[]{:S(2)}, u32[]{:S(2)}) collective-permute-start(bf16[16,8192]{1,0:T(8,128)(2,1)} %refs_0_.1), channel_id=1, source_target_pairs={{48,0},{0,16},{16,32},{32,48},{112,64},{64,80},{80,96},{96,112},{4... | collective-permute-start | bytes 786440 | tf_op jit(solution)/shard_map/ppermute | solution.py:53
  13.0 10.3 %collective-permute-start.7 = (bf16[16,8192]{1,0:T(8,128)(2,1)S(1)}, bf16[16,8192]{1,0:T(8,128)(2,1)S(1)}, u32[]{:S(2)}, u32[]{:S(2)}) collective-permute-start(bf16[16,8192]{1,0:T(8,128)(2,1)S(1)} %collective-permute-done.refs_2_), channel_id=1, source_target_pairs={{16,0},{32,16},{48,32},{0,48},{80,64},{96,80},{112,96},{64,112},{1... | collective-permute-start | bytes 786440 | tf_op jit(solution)/shard_map/ppermute | solution.py:53
  16.3 7.2 %collective-permute-start.5 = (bf16[16,8192]{1,0:T(8,128)(2,1)S(1)}, bf16[16,8192]{1,0:T(8,128)(2,1)S(1)}, u32[]{:S(2)}, u32[]{:S(2)}) collective-permute-start(bf16[16,8192]{1,0:T(8,128)(2,1)S(1)} %collective-permute-done.refs_2_), channel_id=1, source_target_pairs={{64,0},{80,16},{96,32},{112,48},{0,64},{16,80},{32,96},{48,112},{6... | collective-permute-start | bytes 786440 | tf_op jit(solution)/shard_map/ppermute | solution.py:53
  16.9 8.1 %collective-permute-start.6 = (bf16[16,8192]{1,0:T(8,128)(2,1)S(1)}, bf16[16,8192]{1,0:T(8,128)(2,1)S(1)}, u32[]{:S(2)}, u32[]{:S(2)}) collective-permute-start(bf16[16,8192]{1,0:T(8,128)(2,1)S(1)} %collective-permute-done.3.refs_6_), channel_id=1, source_target_pairs={{48,0},{0,16},{16,32},{32,48},{112,64},{64,80},{80,96},{96,112},{4... | collective-permute-start | bytes 786440 | tf_op jit(solution)/shard_map/ppermute | solution.py:53
  25.0 8.6 %collective-permute-start.8 = (bf16[16,8192]{1,0:T(8,128)(2,1)S(1)}, bf16[16,8192]{1,0:T(8,128)(2,1)S(1)}, u32[]{:S(2)}, u32[]{:S(2)}) collective-permute-start(bf16[16,8192]{1,0:T(8,128)(2,1)S(1)} %collective-permute-done.refs_2_), channel_id=1, source_target_pairs={{0,1},{1,0},{2,3},{3,2},{4,5},{5,4},{6,7},{7,6},{8,9},{9,8},{10,11... | collective-permute-start | bytes 786440 | tf_op jit(solution)/shard_map/ppermute | solution.py:49
  25.1 2.5 %collective-permute-start.18 = (bf16[16,256]{1,0:T(8,128)(2,1)S(1)}, bf16[16,256]{1,0:T(8,128)(2,1)S(1)}, u32[]{:S(2)}, u32[]{:S(2)}) collective-permute-start(bf16[16,256]{1,0:T(8,128)(2,1)S(1)} %copy-done.3), channel_id=1, source_target_pairs={{0,1},{1,0},{2,3},{3,2},{4,5},{5,4},{6,7},{7,6},{8,9},{9,8},{10,11... | collective-permute-start | bytes 24584 | tf_op jit(solution)/shard_map/ppermute | solution.py:49
  25.6 5.5 %collective-permute-start.14 = (bf16[16,4096]{1,0:T(8,128)(2,1)S(1)}, bf16[16,4096]{1,0:T(8,128)(2,1)S(1)}, u32[]{:S(2)}, u32[]{:S(2)}) collective-permute-start(bf16[16,4096]{1,0:T(8,128)(2,1)S(1)} %get-tuple-element.51), channel_id=1, source_target_pairs={{16,0},{32,16},{48,32},{0,48},{80,64},{96,80},{112,96},{64,112},{1... | collective-permute-start | bytes 393224 | tf_op jit(solution)/shard_map/ppermute | solution.py:53
  27.2 6.4 %collective-permute-start.16 = (bf16[16,4096]{1,0:T(8,128)(2,1)S(1)}, bf16[16,4096]{1,0:T(8,128)(2,1)S(1)}, u32[]{:S(2)}, u32[]{:S(2)}) collective-permute-start(bf16[16,4096]{1,0:T(8,128)(2,1)S(1)} %get-tuple-element.52), channel_id=1, source_target_pairs={{48,0},{0,16},{16,32},{32,48},{112,64},{64,80},{80,96},{96,112},{4... | collective-permute-start | bytes 393224 | tf_op jit(solution)/shard_map/ppermute | solution.py:53
  27.6 6.5 %collective-permute-start.9 = (bf16[16,8192]{1,0:T(8,128)(2,1)S(1)}, bf16[16,8192]{1,0:T(8,128)(2,1)S(1)}, u32[]{:S(2)}, u32[]{:S(2)}) collective-permute-start(bf16[16,8192]{1,0:T(8,128)(2,1)S(1)} %collective-permute-done.4.refs_4_), channel_id=1, source_target_pairs={{0,1},{1,0},{2,3},{3,2},{4,5},{5,4},{6,7},{7,6},{8,9},{9,8},{10,11... | collective-permute-start | bytes 786440 | tf_op jit(solution)/shard_map/ppermute | solution.py:49
  27.6 6.6 %collective-permute-start.10 = (bf16[16,8192]{1,0:T(8,128)(2,1)S(1)}, bf16[16,8192]{1,0:T(8,128)(2,1)S(1)}, u32[]{:S(2)}, u32[]{:S(2)}) collective-permute-start(bf16[16,8192]{1,0:T(8,128)(2,1)S(1)} %collective-permute-done.3.refs_6_), channel_id=1, source_target_pairs={{0,1},{1,0},{2,3},{3,2},{4,5},{5,4},{6,7},{7,6},{8,9},{9,8},{10,11... | collective-permute-start | bytes 786440 | tf_op jit(solution)/shard_map/ppermute | solution.py:49
  31.1 3.6 %collective-permute-start.11 = (bf16[16,8192]{1,0:T(8,128)(2,1)S(1)}, bf16[16,8192]{1,0:T(8,128)(2,1)S(1)}, u32[]{:S(2)}, u32[]{:S(2)}) collective-permute-start(bf16[16,8192]{1,0:T(8,128)(2,1)S(1)} %collective-permute-done.7.far.refs_8_), channel_id=1, source_target_pairs={{0,1},{1,0},{2,3},{3,2},{4,5},{5,4},{6,7},{7,6},{8,9},{9,8},{10,11... | collective-permute-start | bytes 786440 | tf_op jit(solution)/shard_map/ppermute | solution.py:49
  33.6 1.9 %collective-permute-start.13 = (bf16[16,8192]{1,0:T(8,128)(2,1)S(1)}, bf16[16,8192]{1,0:T(8,128)(2,1)S(1)}, u32[]{:S(2)}, u32[]{:S(2)}) collective-permute-start(bf16[16,8192]{1,0:T(8,128)(2,1)S(1)} %collective-permute-done.6.across_down.refs_12_), channel_id=1, source_target_pairs={{0,1},{1,0},{2,3},{3,2},{4,5},{5,4},{6,7},{7,6},{8,9},{9,8},{10,11... | collective-permute-start | bytes 786440 | tf_op jit(solution)/shard_map/ppermute | solution.py:49
  34.2 1.7 %collective-permute-start.17 = (bf16[16,4096]{1,0:T(8,128)(2,1)S(1)}, bf16[16,4096]{1,0:T(8,128)(2,1)S(1)}, u32[]{:S(2)}, u32[]{:S(2)}) collective-permute-start(bf16[16,4096]{1,0:T(8,128)(2,1)S(1)} %collective-permute-done.16.refs_16_), channel_id=1, source_target_pairs={{0,1},{1,0},{2,3},{3,2},{4,5},{5,4},{6,7},{7,6},{8,9},{9,8},{10,11... | collective-permute-start | bytes 393224 | tf_op jit(solution)/shard_map/ppermute | solution.py:49
  97.6 1.6 %collective-permute-start.19 = (bf16[16,8192]{1,0:T(8,128)(2,1)S(1)}, bf16[16,8192]{1,0:T(8,128)(2,1)S(1)}, u32[]{:S(2)}, u32[]{:S(2)}) collective-permute-start(bf16[16,8192]{1,0:T(8,128)(2,1)S(1)} %get-tuple-element.61), channel_id=1, source_target_pairs={{0,1},{1,0},{2,3},{3,2},{4,5},{5,4},{6,7},{7,6},{8,9},{9,8},{10,11... | collective-permute-start | bytes 786440 | tf_op jit(solution)/shard_map/ppermute | solution.py:49
  99.3 8.0 %collective-permute-start.20 = (bf16[16,24576]{1,0:T(8,128)(2,1)S(1)}, bf16[16,24576]{1,0:T(8,128)(2,1)S(1)}, u32[]{:S(2)}, u32[]{:S(2)}) collective-permute-start(bf16[16,24576]{1,0:T(8,128)(2,1)S(1)} %get-tuple-element.70), channel_id=1, source_target_pairs={{0,1},{1,0},{2,3},{3,2},{4,5},{5,4},{6,7},{7,6},{8,9},{9,8},{10,11... | collective-permute-start | bytes 2359304 | tf_op jit(solution)/shard_map/ppermute | solution.py:49
  100.1 4.9 %collective-permute-start.24 = (bf16[16,4096]{1,0:T(8,128)(2,1)S(1)}, bf16[16,4096]{1,0:T(8,128)(2,1)S(1)}, u32[]{:S(2)}, u32[]{:S(2)}) collective-permute-start(bf16[16,4096]{1,0:T(8,128)(2,1)S(1)} %get-tuple-element.72), channel_id=1, source_target_pairs={{0,1},{1,0},{2,3},{3,2},{4,5},{5,4},{6,7},{7,6},{8,9},{9,8},{10,11... | collective-permute-start | bytes 393224 | tf_op jit(solution)/shard_map/ppermute | solution.py:49
  100.5 6.7 %collective-permute-start.21 = (bf16[16,4096]{1,0:T(8,128)(2,1)S(1)}, bf16[16,4096]{1,0:T(8,128)(2,1)S(1)}, u32[]{:S(2)}, u32[]{:S(2)}) collective-permute-start(bf16[16,4096]{1,0:T(8,128)(2,1)S(1)} %get-tuple-element.62), channel_id=1, source_target_pairs={{0,16},{16,32},{32,48},{48,0},{64,80},{80,96},{96,112},{112,64},{1... | collective-permute-start | bytes 393224 | tf_op jit(solution)/shard_map/ppermute | solution.py:57
  100.5 6.7 %collective-permute-start.22 = (bf16[16,4096]{1,0:T(8,128)(2,1)S(1)}, bf16[16,4096]{1,0:T(8,128)(2,1)S(1)}, u32[]{:S(2)}, u32[]{:S(2)}) collective-permute-start(bf16[16,4096]{1,0:T(8,128)(2,1)S(1)} %get-tuple-element.63), channel_id=1, source_target_pairs={{0,48},{16,0},{32,16},{48,32},{64,112},{80,64},{96,80},{112,96},{1... | collective-permute-start | bytes 393224 | tf_op jit(solution)/shard_map/ppermute | solution.py:57
  107.5 13.0 %collective-permute-start.25 = (bf16[16,32768]{1,0:T(8,128)(2,1)S(1)}, bf16[16,32768]{1,0:T(8,128)(2,1)S(1)}, u32[]{:S(2)}, u32[]{:S(2)}) collective-permute-start(bf16[16,32768]{1,0:T(8,128)(2,1)S(1)} %get-tuple-element.74), channel_id=1, source_target_pairs={{0,1},{1,0},{2,3},{3,2},{4,5},{5,4},{6,7},{7,6},{8,9},{9,8},{10,11... | collective-permute-start | bytes 3145736 | tf_op jit(solution)/shard_map/ppermute | solution.py:49
  107.6 9.1 %collective-permute-start.26 = (bf16[16,8192]{1,0:T(8,128)(2,1)S(1)}, bf16[16,8192]{1,0:T(8,128)(2,1)S(1)}, u32[]{:S(2)}, u32[]{:S(2)}) collective-permute-start(bf16[16,8192]{1,0:T(8,128)(2,1)S(1)} %get-tuple-element.75), channel_id=1, source_target_pairs={{0,64},{16,80},{32,96},{48,112},{64,0},{80,16},{96,32},{112,48},{1... | collective-permute-start | bytes 786440 | tf_op jit(solution)/shard_map/ppermute | solution.py:57
  108.3 8.8 %collective-permute-start.27 = (bf16[16,8192]{1,0:T(8,128)(2,1)S(1)}, bf16[16,8192]{1,0:T(8,128)(2,1)S(1)}, u32[]{:S(2)}, u32[]{:S(2)}) collective-permute-start(bf16[16,8192]{1,0:T(8,128)(2,1)S(1)} %get-tuple-element.76), channel_id=1, source_target_pairs={{0,48},{16,0},{32,16},{48,32},{64,112},{80,64},{96,80},{112,96},{1... | collective-permute-start | bytes 786440 | tf_op jit(solution)/shard_map/ppermute | solution.py:57
  111.2 9.3 %collective-permute-start.28 = (bf16[16,8192]{1,0:T(8,128)(2,1)S(1)}, bf16[16,8192]{1,0:T(8,128)(2,1)S(1)}, u32[]{:S(2)}, u32[]{:S(2)}) collective-permute-start(bf16[16,8192]{1,0:T(8,128)(2,1)S(1)} %get-tuple-element.73), channel_id=1, source_target_pairs={{0,16},{16,32},{32,48},{48,0},{64,80},{80,96},{96,112},{112,64},{1... | collective-permute-start | bytes 786440 | tf_op jit(solution)/shard_map/ppermute | solution.py:57
  111.2 5.4 %collective-permute-start.29 = (f32[16,256]{1,0:T(8,128)S(1)}, f32[16,256]{1,0:T(8,128)S(1)}, u32[]{:S(2)}, u32[]{:S(2)}) collective-permute-start(f32[16,256]{1,0:T(8,128)S(1)} %add.89), channel_id=1, source_target_pairs={{64,0},{80,16},{96,32},{112,48},{0,64},{16,80},{32,96},{48,112},{6... | collective-permute-start | bytes 49160 | tf_op jit(solution)/shard_map/ppermute | solution.py:53
  120.9 14.8 %collective-permute-start.32 = (bf16[16,8192]{1,0:T(8,128)(2,1)S(1)}, bf16[16,8192]{1,0:T(8,128)(2,1)S(1)}, u32[]{:S(2)}, u32[]{:S(2)}) collective-permute-start(bf16[16,8192]{1,0:T(8,128)(2,1)S(1)} %get-tuple-element.83), channel_id=1, source_target_pairs={{0,16},{16,32},{32,48},{48,0},{64,80},{80,96},{96,112},{112,64},{1... | collective-permute-start | bytes 786440 | tf_op jit(solution)/shard_map/ppermute | solution.py:57
  120.9 14.7 %collective-permute-start.33 = (bf16[16,8192]{1,0:T(8,128)(2,1)S(1)}, bf16[16,8192]{1,0:T(8,128)(2,1)S(1)}, u32[]{:S(2)}, u32[]{:S(2)}) collective-permute-start(bf16[16,8192]{1,0:T(8,128)(2,1)S(1)} %get-tuple-element.84), channel_id=1, source_target_pairs={{0,64},{16,80},{32,96},{48,112},{64,0},{80,16},{96,32},{112,48},{1... | collective-permute-start | bytes 786440 | tf_op jit(solution)/shard_map/ppermute | solution.py:57
  122.5 13.2 %collective-permute-start.34 = (bf16[16,8192]{1,0:T(8,128)(2,1)S(1)}, bf16[16,8192]{1,0:T(8,128)(2,1)S(1)}, u32[]{:S(2)}, u32[]{:S(2)}) collective-permute-start(bf16[16,8192]{1,0:T(8,128)(2,1)S(1)} %get-tuple-element.79), channel_id=1, source_target_pairs={{0,48},{16,0},{32,16},{48,32},{64,112},{80,64},{96,80},{112,96},{1... | collective-permute-start | bytes 786440 | tf_op jit(solution)/shard_map/ppermute | solution.py:57
  125.6 4.2 %collective-permute-start.30 = (f32[16,256]{1,0:T(8,128)S(1)}, f32[16,256]{1,0:T(8,128)S(1)}, u32[]{:S(2)}, u32[]{:S(2)}) collective-permute-start(f32[16,256]{1,0:T(8,128)S(1)} %add.90.refs_5_), channel_id=1, source_target_pairs={{0,16},{16,0},{32,48},{48,32},{64,80},{80,64},{96,112},{112,96},{1... | collective-permute-start | bytes 49160 | tf_op jit(solution)/shard_map/ppermute | solution.py:477
  129.8 5.2 %collective-permute-start.31 = (f32[16,256]{1,0:T(8,128)S(1)}, f32[16,256]{1,0:T(8,128)S(1)}, u32[]{:S(2)}, u32[]{:S(2)}) collective-permute-start(f32[16,256]{1,0:T(8,128)S(1)} %add.91), channel_id=1, source_target_pairs={{0,32},{16,48},{32,0},{48,16},{64,96},{80,112},{96,64},{112,80},{1... | collective-permute-start | bytes 49160 | tf_op jit(solution)/shard_map/ppermute | solution.py:478
  (7 other events, 85.3 us)

commit v6 on v5

v6 whole, which is shorter than its diff:
```python
import functools

import jax
import jax.numpy as jnp
from jax import lax
from jax.experimental import pallas as pl
from jax.experimental.pallas import tpu as pltpu
from jax.sharding import PartitionSpec as P

BF16 = jnp.bfloat16
F32 = jnp.float32
ANY = pl.BlockSpec(memory_space=pl.ANY)
VMEM = pl.BlockSpec(memory_space=pltpu.VMEM)
SMEM = pl.BlockSpec(memory_space=pltpu.SMEM)

STEPS = ((0, 0), (0, 1), (0, 3), (1, 0), (0, 2), (1, 1), (1, 3), (1, 2))
UP, DOWN, ACROSS = (0, 1), (0, 3), (1, 0)
GROUPS = ((7,), (5, 6, 4), (1, 3, 2, 0))
SLABS = 8
HALF = 16
PAIR = 32
LOCAL = 8192
NODES = 65536
SLOTS = 32
ROWS = 32
CHUNK = 32
RING = 4
LIST = 1152


def _index(x, y):
    return x * 4 + y


def _from_step(step):
    dx, dy = step
    return [(_index(x ^ dx, (y + dy) % 4), _index(x, y)) for x in range(2) for y in range(4)]


def _to_step(step):
    return [(b, a) for a, b in _from_step(step)]


CORE_SWAP = [(f, f ^ 1) for f in range(16)]
SAME_CORE = [list(range(0, 16, 2)), list(range(1, 16, 2))]


def swap(a):
    return lax.ppermute(a, "feat", CORE_SWAP)


def receive(a, step):
    return lax.ppermute(a, "blk", _from_step(step))


def send(a, step):
    return lax.ppermute(a, "blk", _to_step(step))


def after(a, *others):
    return lax.optimization_barrier((a, *others))[0]


def row_of(core, local):
    return 8 * (local // 4) + 4 * core + local % 4


def lanes_of(block):
    return pl.ds(pl.multiple_of(block * 128, 128), 128)


def list_kernel(info, cols, first, second, third, counts, place):
    core = info[0]
    lists = (first, second, third)
    for group, members in enumerate(GROUPS):
        for i, d in enumerate(members):
            place[info[1 + d]] = (group << 16) + 64 * i

    def row(local, ends):
        r = row_of(core, local)
        for p in range(SLOTS):
            block = cols[p, r]
            entry = place[block // 64]
            group = entry // 65536
            value = local * 65536 + p * 256 + lax.rem(entry, 65536) + lax.rem(block, 64)
            for i in range(3):
                lists[i][ends[i]] = value
            ends = tuple(e + (group == i).astype(jnp.int32) for i, e in enumerate(ends))
        return ends

    ends = lax.fori_loop(0, ROWS, row, (jnp.int32(0),) * 3)
    for i in range(3):
        counts[i] = ends[i]

        def pad(k, carry, i=i):
            lists[i][ends[i] + k] = jnp.int32(ROWS * 65536)
            return carry

        lax.fori_loop(0, CHUNK, pad, 0)


def make_lists(info, cols):
    *lists, counts = pl.pallas_call(
        list_kernel,
        out_shape=[jax.ShapeDtypeStruct((LIST,), jnp.int32)] * 3
        + [jax.ShapeDtypeStruct((3,), jnp.int32)],
        in_specs=[SMEM, SMEM],
        out_specs=[SMEM] * 4,
        scratch_shapes=[pltpu.SMEM((8,), jnp.int32)],
        cost_estimate=pl.CostEstimate(flops=0, bytes_accessed=24 << 20, transcendentals=0),
        name="lists",
    )(info, cols)
    return lists, counts


def each_chunk(core, entries, count, tiles, ring, sems, work):
    chunks = (count + CHUNK - 1) // CHUNK

    def fetch(i):
        slot = lax.rem(i, RING)
        for t in range(CHUNK):
            entry = entries[i * CHUNK + t]
            local = jnp.minimum(entry // 65536, ROWS - 1)
            p = lax.rem(entry // 256, 256)
            pltpu.make_async_copy(
                tiles.at[row_of(core, local), p], ring.at[slot, t], sems.at[slot]
            ).start()

    def fetch_if(i):
        @pl.when(i < chunks)
        def _():
            fetch(i)

    lax.fori_loop(0, RING - 1, lambda i, c: (fetch_if(i), c)[1], 0)

    def step(i, carry):
        fetch_if(i + RING - 1)
        slot = lax.rem(i, RING)
        pltpu.make_async_copy(ring.at[slot], ring.at[slot], sems.at[slot]).wait()
        work(i, slot)
        return carry

    lax.fori_loop(0, chunks, step, 0)


RING_SCRATCH = [
    pltpu.VMEM((RING, CHUNK, 128, 128), BF16),
    pltpu.SemaphoreType.DMA((RING,)),
]


WIDE = 1280


def unpack_kernel(info, message, mine, other, wgrad_mine, wgrad_other):
    core = info[0]
    own = pl.ds(pl.multiple_of(HALF * core, HALF), HALF)
    sibling = pl.ds(pl.multiple_of(HALF * (1 - core), HALF), HALF)
    for rows, nodes, wgrad in ((own, mine, wgrad_mine), (sibling, other, wgrad_other)):
        total = jnp.zeros((HALF, 256), F32)
        for g in range(8):
            nodes[:, 512 * g : 512 * (g + 1)] = message[g, rows, 512:1024]
            total += message[g, rows, 1024:].astype(F32)
        wgrad[...] = total


def unpack(info, message):
    return pl.pallas_call(
        unpack_kernel,
        out_shape=(
            jax.ShapeDtypeStruct((HALF, 4096), BF16),
            jax.ShapeDtypeStruct((HALF, 4096), BF16),
            jax.ShapeDtypeStruct((HALF, 256), F32),
            jax.ShapeDtypeStruct((HALF, 256), F32),
        ),
        in_specs=[SMEM, VMEM],
        out_specs=(VMEM,) * 4,
        compiler_params=pltpu.CompilerParams(vmem_limit_bytes=4 << 20),
        cost_estimate=pl.CostEstimate(flops=0, bytes_accessed=1 << 20, transcendentals=0),
        name="unpack",
    )(info, message)


def join_kernel(info, mine, received, hidden):
    core = info[0]
    for g in range(8):
        chunk = slice(512 * g, 512 * (g + 1))
        a, b = mine[:, chunk], received[:, chunk]
        hidden[:, 1024 * g : 1024 * g + 512] = jnp.where(core == 0, a, b)
        hidden[:, 1024 * g + 512 : 1024 * (g + 1)] = jnp.where(core == 0, b, a)


def join(info, mine, received):
    return pl.pallas_call(
        join_kernel,
        out_shape=jax.ShapeDtypeStruct((HALF, LOCAL), BF16),
        in_specs=[SMEM, VMEM, VMEM],
        out_specs=VMEM,
        compiler_params=pltpu.CompilerParams(vmem_limit_bytes=4 << 20),
        cost_estimate=pl.CostEstimate(flops=0, bytes_accessed=1 << 20, transcendentals=0),
        name="join",
    )(info, mine, received)


def forward_kernel(group, places, info, entries, counts, tiles, *refs):
    pieces, refs = refs[: 2 * len(places)], refs[2 * len(places) :]
    if group < 2:
        before, refs = refs[0], refs[1:]
    if group == 0:
        sides, refs = refs[:4], refs[4:]
    if group == 0:
        out, total, feats, sems, ring, ring_sems = refs
    else:
        total, feats, sems, ring, ring_sems = refs
    core = info[0]
    copies = []
    for i, (first, nodes) in enumerate(places):
        for h in range(2):
            rows = pl.ds(pl.multiple_of(jnp.where(core == h, 0, HALF), HALF), HALF)
            copies.append(
                pltpu.make_async_copy(
                    pieces[2 * i + h], feats.at[rows, pl.ds(first, nodes)], sems.at[2 * i + h]
                )
            )
    for c in copies:
        c.start()
    if group == 2:
        total[...] = jnp.zeros_like(total)
    else:
        total[...] = before[...]
    if group == 0:
        for h in range(2):
            rows = pl.ds(pl.multiple_of(jnp.where(core == h, 0, HALF), HALF), HALF)
            cot, weight = sides[2 * h], sides[2 * h + 1]
            for g in range(8):
                nodes = pl.ds(pl.multiple_of(1024 * g + 512 * core, 512), 512)
                out[g, rows, 512:1024] = cot[:, nodes]
                out[g, rows, 1024:] = weight[...]
    for c in copies:
        c.wait()

    def work(i, slot):
        for t in range(CHUNK):
            entry = entries[i * CHUNK + t]
            local = entry // 65536
            left = feats[:, lanes_of(lax.rem(entry, 256))]
            total[local] += lax.dot_general(
                left, ring[slot, t], (((1,), (1,)), ((), ())), preferred_element_type=F32
            )

    each_chunk(core, entries, counts[group], tiles, ring, ring_sems, work)
    if group == 0:
        for g in range(8):
            for i in range(4):
                out[g, :, 128 * i : 128 * (i + 1)] = total[4 * g + i].astype(BF16)


def forward(group, info, entries, counts, tiles, pieces, before=None, sides=()):
    widths = [p.shape[1] for p in pieces[::2]]
    places = tuple((sum(widths[:i]), n) for i, n in enumerate(widths))
    total = (ROWS + 1, PAIR, 128)
    args = [info, entries, counts, tiles, *pieces]
    specs = [SMEM, SMEM, SMEM, ANY] + [ANY] * len(pieces)
    if before is not None:
        args.append(before)
        specs.append(VMEM)
    args += sides
    specs += [VMEM] * len(sides)
    scratch = [
        pltpu.VMEM((PAIR, sum(widths)), BF16),
        pltpu.SemaphoreType.DMA((len(pieces),)),
        *RING_SCRATCH,
    ]
    if group == 0:
        out = jax.ShapeDtypeStruct((8, PAIR, WIDE), BF16)
        scratch = [pltpu.VMEM(total, F32)] + scratch
    else:
        out = jax.ShapeDtypeStruct(total, F32)
    return pl.pallas_call(
        functools.partial(forward_kernel, group, places),
        out_shape=out,
        in_specs=specs,
        out_specs=VMEM,
        scratch_shapes=scratch,
        compiler_params=pltpu.CompilerParams(vmem_limit_bytes=16 << 20),
        cost_estimate=pl.CostEstimate(flops=1 << 20, bytes_accessed=1 << 20, transcendentals=0),
        name="forward_" + ("corner", "middle", "near")[group],
    )(*args)


def dense_kernel(message, out):
    agg = message[:, :512]
    weight = message[:, 1024:]
    pre = lax.dot_general(weight, agg, (((0,), (0,)), ((), ())), preferred_element_type=F32)
    sig = 1.0 / (1.0 + jnp.exp(-pre))
    out[:, 512:1024] = (pre * sig).astype(BF16)
    cot = message[:, 512:1024].astype(F32)
    pre_grad = (cot * sig * (1.0 + pre * (1.0 - sig))).astype(BF16)
    out[:, :512] = jnp.dot(weight, pre_grad, preferred_element_type=F32).astype(BF16)
    wgrad = lax.dot_general(agg, pre_grad, (((1,), (1,)), ((), ())), preferred_element_type=F32)
    out[:, 1024:] = wgrad.astype(BF16)


def dense(message):
    return pl.pallas_call(
        dense_kernel,
        out_shape=jax.ShapeDtypeStruct((256, WIDE), BF16),
        in_specs=[VMEM],
        out_specs=VMEM,
        compiler_params=pltpu.CompilerParams(vmem_limit_bytes=8 << 20),
        cost_estimate=pl.CostEstimate(
            flops=3 * 2 * 256 * 256 * 512, bytes_accessed=2 << 20, transcendentals=256 * 512
        ),
        name="dense",
    )(message)


def backward_kernel(group, info, entries, counts, tiles, message, own_out, other_out, *scratch):
    total, grad, ring, sems = scratch
    core = info[0]
    lanes_in_all = LOCAL * len(GROUPS[group])

    def clear(i, carry):
        total[:, pl.ds(pl.multiple_of(i * 2048, 2048), 2048)] = jnp.zeros((PAIR, 2048), F32)
        return carry

    lax.fori_loop(0, lanes_in_all // 2048, clear, 0)
    for g in range(8):
        for i in range(4):
            grad[4 * g + i] = message[g, :, 128 * i : 128 * (i + 1)]
    grad[ROWS] = jnp.zeros((PAIR, 128), BF16)

    def work(i, slot):
        for t in range(CHUNK):
            entry = entries[i * CHUNK + t]
            lanes = lanes_of(lax.rem(entry, 256))
            total[:, lanes] += jnp.dot(
                grad[entry // 65536], ring[slot, t], preferred_element_type=F32
            )

    each_chunk(core, entries, counts[group], tiles, ring, sems, work)
    own = pl.ds(pl.multiple_of(HALF * core, HALF), HALF)
    other = pl.ds(pl.multiple_of(HALF * (1 - core), HALF), HALF)
    own_out[...] = total[own, :].astype(BF16)
    other_out[...] = total[other, :].astype(BF16)


def backward(group, info, entries, counts, tiles, message):
    nodes = LOCAL * len(GROUPS[group])
    return pl.pallas_call(
        functools.partial(backward_kernel, group),
        out_shape=[jax.ShapeDtypeStruct((HALF, nodes), BF16)] * 2,
        in_specs=[SMEM, SMEM, SMEM, ANY, VMEM],
        out_specs=[VMEM] * 2,
        scratch_shapes=[
            pltpu.VMEM((PAIR, nodes), F32),
            pltpu.VMEM((ROWS + 1, PAIR, 128), BF16),
            *RING_SCRATCH,
        ],
        compiler_params=pltpu.CompilerParams(vmem_limit_bytes=16 << 20),
        cost_estimate=pl.CostEstimate(flops=1 << 20, bytes_accessed=1 << 20, transcendentals=0),
        name="backward_" + ("corner", "middle", "near")[group],
    )(info, entries, counts, tiles, message)


def cut_kernel(across_up, across_down, far, total, up_half, down_half):
    up_half[...] = across_up[:, :4096]
    down_half[...] = across_down[:, 4096:]


def cut(across_up, across_down, far, total):
    return pl.pallas_call(
        cut_kernel,
        out_shape=[jax.ShapeDtypeStruct((HALF, 4096), BF16)] * 2,
        in_specs=[VMEM, VMEM, ANY, ANY],
        out_specs=[VMEM] * 2,
        compiler_params=pltpu.CompilerParams(vmem_limit_bytes=4 << 20),
        cost_estimate=pl.CostEstimate(flops=0, bytes_accessed=1 << 19, transcendentals=0),
        name="cut",
    )(across_up, across_down, far, total)


def sum_call(kernel, shapes, args, name, before=()):
    def body(*refs):
        kernel(*refs[: len(args)], *refs[len(args) + len(before) :])

    return pl.pallas_call(
        body,
        out_shape=[jax.ShapeDtypeStruct(s, t) for s, t in shapes],
        in_specs=[VMEM] * len(args) + [ANY] * len(before),
        out_specs=[VMEM] * len(shapes),
        compiler_params=pltpu.CompilerParams(vmem_limit_bytes=8 << 20),
        cost_estimate=pl.CostEstimate(flops=0, bytes_accessed=2 << 20, transcendentals=0),
        name=name,
    )(*args, *before)


def corner_kernel(own, other, low, high):
    total = own[...].astype(F32) + other[...].astype(F32)
    low[...] = total[:, :4096].astype(BF16)
    high[...] = total[:, 4096:].astype(BF16)


def middle_kernel(own, other, low, high, across_up, across_down, far):
    def mine(i, first, count):
        lanes = slice(LOCAL * i + first, LOCAL * i + first + count)
        return own[:, lanes].astype(F32) + other[:, lanes].astype(F32)

    across_up[:, :4096] = (mine(0, 0, 4096) + low[...].astype(F32)).astype(BF16)
    across_up[:, 4096:] = mine(0, 4096, 4096).astype(BF16)
    across_down[:, :4096] = mine(1, 0, 4096).astype(BF16)
    across_down[:, 4096:] = (mine(1, 4096, 4096) + high[...].astype(F32)).astype(BF16)
    far[...] = mine(2, 0, LOCAL).astype(BF16)


def near_kernel(own, other, from_across, from_up, from_down, up, across, down, base):
    def mine(i):
        lanes = slice(LOCAL * i, LOCAL * (i + 1))
        return own[:, lanes].astype(F32) + other[:, lanes].astype(F32)

    up[...] = (mine(0) + from_across[...].astype(F32) + from_down[...].astype(F32)).astype(BF16)
    across[...] = (mine(1) + from_up[...].astype(F32)).astype(BF16)
    down[...] = mine(2).astype(BF16)
    base[...] = mine(3)


def last_kernel(base, a, b, c, out):
    total = base[...] + a[...].astype(F32) + b[...].astype(F32) + c[...].astype(F32)
    out[...] = total.astype(BF16)


def per_device(node_feats, weight, tiles, block_cols, cotangent):
    core = lax.axis_index("feat") % 2
    slab = lax.axis_index("blk")
    x, y = slab // 4, slab % 4
    info = jnp.stack([core] + [(x ^ dx) * 4 + (y + dy) % 4 for dx, dy in STEPS]).astype(jnp.int32)
    cols = block_cols.T

    up, down, across = (receive(node_feats, s) for s in (UP, DOWN, ACROSS))
    lists, counts = make_lists(info, cols)
    feats_swapped, cot_swapped = swap(node_feats), swap(cotangent)
    up, down, across, lists, counts, feats_swapped, cot_swapped = lax.optimization_barrier(
        (up, down, across, lists, counts, feats_swapped, cot_swapped)
    )
    far = receive(up, UP)
    across_up = receive(up, ACROSS)
    across_down = receive(across, DOWN)
    pieces = [up, swap(up), across, swap(across), down, swap(down), node_feats, feats_swapped]
    total = forward(2, info, lists[2], counts, tiles, pieces)
    far, across_up, across_down, total = lax.optimization_barrier(
        (far, across_up, across_down, total)
    )
    up_half, down_half = cut(across_up, across_down, far, total)
    corner = (receive(up_half, UP), receive(down_half, DOWN))
    weight_swapped = swap(weight)
    pieces = [across_up, swap(across_up), across_down, swap(across_down), far, swap(far)]
    total = forward(1, info, lists[1], counts, tiles, pieces, total)
    *corner, total = lax.optimization_barrier((*corner, total))
    pieces = [corner[0], swap(corner[0]), corner[1], swap(corner[1])]
    sides = (cotangent, weight, cot_swapped, weight_swapped)
    message = forward(0, info, lists[0], counts, tiles, pieces, total, sides)

    message = lax.all_to_all(message, "feat", 0, 0, axis_index_groups=SAME_CORE, tiled=True)
    message = dense(message.reshape(256, WIDE)).reshape(8, PAIR, WIDE)
    message = lax.all_to_all(message, "feat", 0, 0, axis_index_groups=SAME_CORE, tiled=True)

    own_a, other_a = backward(0, info, lists[0], counts, tiles, message)
    half, whole = ((HALF, 4096), BF16), ((HALF, LOCAL), BF16)
    low, high = sum_call(corner_kernel, [half] * 2, (own_a, swap(other_a)), "sum_corner")
    corner_up, corner_down = send(low, UP), send(high, DOWN)
    own_b, other_b = backward(1, info, lists[1], counts, tiles, after(message, low, high))
    hidden, hidden_other, wgrad, wgrad_other = unpack(info, after(message, low, high))
    wgrad_other, hidden_other = swap(wgrad_other), swap(hidden_other)
    other_b, corner_up, corner_down = lax.optimization_barrier((other_b, corner_up, corner_down))
    across_up, across_down, far = sum_call(
        middle_kernel,
        [whole] * 3,
        (own_b, swap(other_b), corner_up, corner_down),
        "sum_middle",
        before=(wgrad_other, hidden_other),
    )
    from_across = send(across_up, ACROSS)
    from_up = send(across_down, DOWN)
    from_down = send(far, UP)
    own_c, other_c = backward(2, info, lists[2], counts, tiles, after(message, far))
    wgrad = wgrad + after(wgrad_other, far)
    wgrad = wgrad + receive(wgrad, ACROSS)
    other_c, from_across, from_up, from_down = lax.optimization_barrier(
        (other_c, from_across, from_up, from_down)
    )
    up, across, down, base = sum_call(
        near_kernel,
        [whole] * 3 + [((HALF, LOCAL), F32)],
        (own_c, swap(other_c), from_across, from_up, from_down),
        "sum_near",
        before=(wgrad,),
    )
    last = [send(up, UP), send(across, ACROSS), send(down, DOWN)]
    wgrad = after(wgrad, down)
    wgrad = wgrad + lax.ppermute(wgrad, "blk", [(b, b ^ 1) for b in range(8)])
    weight_grad = wgrad + lax.ppermute(wgrad, "blk", [(b, b ^ 2) for b in range(8)])
    hidden = join(info, after(hidden, down), hidden_other)
    (feats_grad,) = sum_call(last_kernel, [whole], (base, *last), "sum_last")
    return hidden, weight_grad, feats_grad


def solution(mesh):
    placed = (
        P("feat", "blk"),
        P("feat", None),
        P("blk", None, None, None),
        P("blk", None),
        P("feat", "blk"),
    )
    return jax.shard_map(
        per_device,
        mesh=mesh,
        in_specs=placed,
        out_specs=(P("feat", "blk"), P("feat", None), P("feat", "blk")),
        check_vma=False,
    )
```

time: 137 us -> 191 us (1.39)
  Pallas kernels: 42.5 us -> 106 us
  waiting for transfers between devices: 26.6 us -> 13.9 us
  local copies, waits for them, and re-layouts: 0.11 us -> 3.57 us
  starting transfers between devices: 29.8 us -> 27.8 us
    pallas_call x4 -> x7, Pallas kernels: 38.6 us -> 102 us  [the longest x3 45.8 us: forward(): pl.pallas_call(functools.partial(forward_kernel, group, places), out_shap...]
    ppermute x9, waiting for transfers between devices: 11.1 us -> 2.83 us  [receive(): return lax.ppermute(a, 'blk', _from_step(step))]
    ppermute x8, waiting for transfers between devices: 6.16 us -> 0.02 us  [send(): return lax.ppermute(a, 'blk', _to_step(step))]
    unnamed x8 -> x18, local copies, waits for them, and re-layouts: 0.03 us -> 2.92 us
    all_to_all x2, blocking collectives: 35.9 us -> 37.8 us  [per_device(): lax.all_to_all(message, 'feat', 0, 0, axis_index_groups=SAME_CORE, tiled=...]
  transfers between devices with their start and end apart: 35 -> 35, of which waited for: 16 -> 6; matrix products, arithmetic and copies ran while one was open for 1% -> 1% of each run, Pallas kernels for 11% -> 49%
where the time goes in v6:
time: 191 us
  Pallas kernels  106 us (55%)
  blocking collectives  37.8 us (20%)
  starting transfers between devices  27.8 us (15%)
  waiting for transfers between devices  13.9 us (7%)
  local copies, waits for them, and re-layouts  3.57 us (2%)
    pallas_call x3, Pallas kernels, forward(): pl.pallas_call(functools.partial(forward_kernel, group, places), out_shap...  45.8 us
    pallas_call x3, Pallas kernels, backward(): pl.pallas_call(functools.partial(backward_kernel, group), out_shape=[jax....  38.5 us
    all_to_all x2, blocking collectives, per_device(): lax.all_to_all(message, 'feat', 0, 0, axis_index_groups=SAME_CORE, tiled=...  37.8 us
    pallas_call x1, Pallas kernels, make_lists(): pl.pallas_call(list_kernel, out_shape=[jax.ShapeDtypeStruct((LIST,), jnp....  18.2 us
    ppermute x9, starting transfers between devices, receive(): return lax.ppermute(a, 'blk', _from_step(step))  11.7 us
    ppermute x8, starting transfers between devices, send(): return lax.ppermute(a, 'blk', _to_step(step))  9.71 us
    ppermute x1, waiting for transfers between devices, per_device(): wgrad = wgrad + lax.ppermute(wgrad, 'blk', [(b, b ^ 1) for b in range(8)])  5.43 us
    ppermute x16, waiting for transfers between devices, swap(): return lax.ppermute(a, 'feat', CORE_SWAP)  3.86 us
  transfers between devices with their start and end apart: 35, of which 6 were waited for; matrix products, arithmetic and copies ran while one was open for 1% of the time, Pallas kernels for 49%

profile of v6, /device:TPU:0, one launch (start us, length us, event | category | flops | bytes accessed | tf_op | source)
XLA Modules:
  0.0 191.1 jit_solution(9699779894634135276)
XLA Ops:
  0.7 1.7 collective-permute-start.2
  2.4 1.6 collective-permute-start.1
  4.0 1.7 collective-permute-start
  6.3 18.2 %lists.1 = (s32[1152]{0:T(1024)}, s32[1152]{0:T(1024)}, s32[1152]{0:T(1024)}, s32[3]{0:T(128)}) custom-call(s32[9]{0:T(128)} %stack.39.info, s32[32,64]{1,0:T(8,128)} %bitcast.14), custom_call_target="tpu_custom_call" | custom-call | bytes 25165824 | tf_op jit(solution)/shard_map/lists/pallas_call | solution.py:103
  26.5 2.8 %collective-permute-start.5 = (bf16[16,8192]{1,0:T(8,128)(2,1)S(1)}, bf16[16,8192]{1,0:T(8,128)(2,1)S(1)}, u32[]{:S(2)}, u32[]{:S(2)}) collective-permute-start(bf16[16,8192]{1,0:T(8,128)(2,1)S(1)} %collective-permute-done.refs_0_), channel_id=1, source_target_pairs={{16,0},{32,16},{48,32},{0,48},{80,64},{96,80},{112,96},{64,112},{1... | collective-permute-start | bytes 786440 | tf_op jit(solution)/shard_map/ppermute | solution.py:53
  29.3 0.9 copy-done
  30.9 0.7 copy-done.3
  32.2 22.1 %forward_near.1.total.refs_6_ = f32[33,32,128]{2,1,0:T(8,128)S(1)} custom-call(s32[9]{0:T(128)S(1)} %copy-done.2, s32[1152]{0:T(1024)S(1)} %copy-done.3, s32[3]{0:T(128)S(1)} %copy-done.7, bf16[64,32,128,128]{3,2,1,0:T(8,128)(2,1)} %tiles.11, bf16[16,8192]{1,0:T(8,128)(2,1)S(1)} %collective-permute-done.refs_0_, ...), custom_call_target="tpu_custom_call" | custom-call | flops 1048576 | bytes 1048576 | tf_op jit(solution)/shard_map/forward_near/pallas_call | solution.py:279
  55.1 0.9 collective-permute-start.11
  56.0 1.2 collective-permute-start.12
  57.2 17.3 %forward_middle.1.refs_4_ = f32[33,32,128]{2,1,0:T(8,128)S(1)} custom-call(s32[9]{0:T(128)S(1)} %copy-done.2, s32[1152]{0:T(1024)S(1)} %copy-done.5, s32[3]{0:T(128)S(1)} %copy-done.7, bf16[64,32,128,128]{3,2,1,0:T(8,128)(2,1)} %tiles.11, bf16[16,8192]{1,0:T(8,128)(2,1)S(1)} %collective-permute-done.6.across_up.refs_0_, ...), custom_call_target="tpu_custom_call" | custom-call | flops 1048576 | bytes 1048576 | tf_op jit(solution)/shard_map/forward_middle/pallas_call | solution.py:279
  75.2 1.1 collective-permute-done.18.refs_8_
  76.3 6.4 %forward_corner.1 = bf16[8,32,1280]{2,1,0:T(8,128)(2,1)S(1)} custom-call(s32[9]{0:T(128)S(1)} %copy-done.2, s32[1152]{0:T(1024)S(1)} %copy-done.6, s32[3]{0:T(128)S(1)} %copy-done.7, bf16[64,32,128,128]{3,2,1,0:T(8,128)(2,1)} %tiles.11, bf16[16,4096]{1,0:T(8,128)(2,1)S(1)} %collective-permute-done.11.refs_0_, ...), custom_call_target="tpu_custom_call" | custom-call | flops 1048576 | bytes 1048576 | tf_op jit(solution)/shard_map/forward_corner/pallas_call | solution.py:279
  82.8 21.5 %all_to_all.10 = bf16[8,32,1280]{2,1,0:T(8,128)(2,1)S(1)} all-to-all(bf16[8,32,1280]{2,1,0:T(8,128)(2,1)S(1)} %forward_corner.1), channel_id=1, replica_groups={{0,2,4,6,8,10,12,14},{1,3,5,7,9,11,13,15},{16,18,20,22,24,26,28,30},{17..., dimensions={0} | all-to-all | bytes 1310720 | tf_op jit(solution)/shard_map/all_to_all | solution.py:463
  104.9 16.3 %all_to_all.11.message = bf16[8,32,1280]{2,1,0:T(8,128)(2,1)S(1)} all-to-all(bf16[8,32,1280]{2,1,0:T(8,128)(2,1)S(1)} %bitcast.13), channel_id=1, replica_groups={{0,2,4,6,8,10,12,14},{1,3,5,7,9,11,13,15},{16,18,20,22,24,26,28,30},{17..., dimensions={0} | all-to-all | bytes 1310720 | tf_op jit(solution)/shard_map/all_to_all | solution.py:465
  121.3 5.2 %backward_corner.1 = (bf16[16,8192]{1,0:T(8,128)(2,1)S(1)}, bf16[16,8192]{1,0:T(8,128)(2,1)S(1)}) custom-call(s32[9]{0:T(128)S(1)} %copy-done.2, s32[1152]{0:T(1024)S(1)} %copy-done.6, s32[3]{0:T(128)S(1)} %copy-done.7, bf16[64,32,128,128]{3,2,1,0:T(8,128)(2,1)} %tiles.11, bf16[8,32,1280]{2,1,0:T(8,128)(2,1)S(1)} %all_to_all.11.message), custom_call_target="tpu_custom_call" | custom-call | flops 1048576 | bytes 1048576 | tf_op jit(solution)/shard_map/backward_corner/pallas_call | solution.py:350
  126.6 1.5 collective-permute-done.19.refs_1_
  128.3 3.2 %collective-permute-start.21 = (bf16[16,4096]{1,0:T(8,128)(2,1)S(1)}, bf16[16,4096]{1,0:T(8,128)(2,1)S(1)}, u32[]{:S(2)}, u32[]{:S(2)}) collective-permute-start(bf16[16,4096]{1,0:T(8,128)(2,1)S(1)} %get-tuple-element.81), channel_id=1, source_target_pairs={{0,48},{16,0},{32,16},{48,32},{64,112},{80,64},{96,80},{112,96},{1... | collective-permute-start | bytes 393224 | tf_op jit(solution)/shard_map/ppermute | solution.py:57
  131.5 15.0 %backward_middle.1 = (bf16[16,24576]{1,0:T(8,128)(2,1)S(1)}, bf16[16,24576]{1,0:T(8,128)(2,1)S(1)}) custom-call(s32[9]{0:T(128)S(1)} %copy-done.2, s32[1152]{0:T(1024)S(1)} %copy-done.5, s32[3]{0:T(128)S(1)} %copy-done.7, bf16[64,32,128,128]{3,2,1,0:T(8,128)(2,1)} %tiles.11, bf16[8,32,1280]{2,1,0:T(8,128)(2,1)S(1)} %all_to_all.11.message), custom_call_target="tpu_custom_call" | custom-call | flops 1048576 | bytes 1048576 | tf_op jit(solution)/shard_map/backward_middle/pallas_call | solution.py:350
  147.9 1.2 collective-permute-done.23.refs_4_
  149.5 2.0 %collective-permute-start.27 = (bf16[16,8192]{1,0:T(8,128)(2,1)S(1)}, bf16[16,8192]{1,0:T(8,128)(2,1)S(1)}, u32[]{:S(2)}, u32[]{:S(2)}) collective-permute-start(bf16[16,8192]{1,0:T(8,128)(2,1)S(1)} %get-tuple-element.91), channel_id=1, source_target_pairs={{0,16},{16,32},{32,48},{48,0},{64,80},{80,96},{96,112},{112,64},{1... | collective-permute-start | bytes 786440 | tf_op jit(solution)/shard_map/ppermute | solution.py:57
  151.5 18.2 %backward_near.1 = (bf16[16,32768]{1,0:T(8,128)(2,1)S(1)}, bf16[16,32768]{1,0:T(8,128)(2,1)S(1)}) custom-call(s32[9]{0:T(128)S(1)} %copy-done.2, s32[1152]{0:T(1024)S(1)} %copy-done.4, s32[3]{0:T(128)S(1)} %copy-done.7, bf16[64,32,128,128]{3,2,1,0:T(8,128)(2,1)} %tiles.11, bf16[8,32,1280]{2,1,0:T(8,128)(2,1)S(1)} %all_to_all.11.message), custom_call_target="tpu_custom_call" | custom-call | flops 1048576 | bytes 1048576 | tf_op jit(solution)/shard_map/backward_near/pallas_call | solution.py:350
  169.9 1.0 collective-permute-start.29
  170.9 2.8 %collective-permute-done.29 = f32[16,256]{1,0:T(8,128)S(1)} collective-permute-done((f32[16,256]{1,0:T(8,128)S(1)}, f32[16,256]{1,0:T(8,128)S(1)}, u32[]{:S(2)}, u32[]{:S(2)}) %collective-permute-start.29) | collective-permute-done | bytes 16416 | tf_op jit(solution)/shard_map/ppermute | solution.py:53
  174.0 0.9 collective-permute-start.32
  174.9 2.0 %collective-permute-start.33 = (bf16[16,8192]{1,0:T(8,128)(2,1)S(1)}, bf16[16,8192]{1,0:T(8,128)(2,1)S(1)}, u32[]{:S(2)}, u32[]{:S(2)}) collective-permute-start(bf16[16,8192]{1,0:T(8,128)(2,1)S(1)} %get-tuple-element.108), channel_id=1, source_target_pairs={{0,64},{16,80},{32,96},{48,112},{64,0},{80,16},{96,32},{112,48},{1... | collective-permute-start | bytes 786440 | tf_op jit(solution)/shard_map/ppermute | solution.py:57
  176.9 1.4 collective-permute-start.34
  178.9 5.4 %collective-permute-done.30 = f32[16,256]{1,0:T(8,128)S(1)} collective-permute-done((f32[16,256]{1,0:T(8,128)S(1)}, f32[16,256]{1,0:T(8,128)S(1)}, u32[]{:S(2)}, u32[]{:S(2)}) %collective-permute-start.30) | collective-permute-done | bytes 16416 | tf_op jit(solution)/shard_map/ppermute | solution.py:500
  184.4 2.3 %collective-permute-start.31 = (f32[16,256]{1,0:T(8,128)S(1)}, f32[16,256]{1,0:T(8,128)S(1)}, u32[]{:S(2)}, u32[]{:S(2)}) collective-permute-start(f32[16,256]{1,0:T(8,128)S(1)} %add.91), channel_id=1, source_target_pairs={{0,32},{16,48},{32,0},{48,16},{64,96},{80,112},{96,64},{112,80},{1... | collective-permute-start | bytes 49160 | tf_op jit(solution)/shard_map/ppermute | solution.py:501
  186.7 1.3 join.1
  187.9 1.7 collective-permute-done.31
  190.2 0.8 sum_last.1
  (78 shorter events, 9.7 us)
Async XLA Ops:
  0.6 23.8 %collective-permute-start.4 = (bf16[16,8192]{1,0:T(8,128)(2,1)}, bf16[16,8192]{1,0:T(8,128)(2,1)S(1)}, u32[]{:S(2)}, u32[]{:S(2)}) collective-permute-start(bf16[16,8192]{1,0:T(8,128)(2,1)} %refs_5_.1), channel_id=1, source_target_pairs={{0,1},{1,0},{2,3},{3,2},{4,5},{5,4},{6,7},{7,6},{8,9},{9,8},{10,11... | collective-permute-start | bytes 786440 | tf_op jit(solution)/shard_map/ppermute | solution.py:49
  0.7 23.8 %collective-permute-start.2 = (bf16[16,8192]{1,0:T(8,128)(2,1)}, bf16[16,8192]{1,0:T(8,128)(2,1)S(1)}, u32[]{:S(2)}, u32[]{:S(2)}) collective-permute-start(bf16[16,8192]{1,0:T(8,128)(2,1)} %refs_6_.2), channel_id=1, source_target_pairs={{64,0},{80,16},{96,32},{112,48},{0,64},{16,80},{32,96},{48,112},{6... | collective-permute-start | bytes 786440 | tf_op jit(solution)/shard_map/ppermute | solution.py:53
  2.4 22.1 %collective-permute-start.1 = (bf16[16,8192]{1,0:T(8,128)(2,1)}, bf16[16,8192]{1,0:T(8,128)(2,1)S(1)}, u32[]{:S(2)}, u32[]{:S(2)}) collective-permute-start(bf16[16,8192]{1,0:T(8,128)(2,1)} %refs_6_.2), channel_id=1, source_target_pairs={{48,0},{0,16},{16,32},{32,48},{112,64},{64,80},{80,96},{96,112},{4... | collective-permute-start | bytes 786440 | tf_op jit(solution)/shard_map/ppermute | solution.py:53
  4.0 20.5 %collective-permute-start = (bf16[16,8192]{1,0:T(8,128)(2,1)}, bf16[16,8192]{1,0:T(8,128)(2,1)S(1)}, u32[]{:S(2)}, u32[]{:S(2)}) collective-permute-start(bf16[16,8192]{1,0:T(8,128)(2,1)} %refs_6_.2), channel_id=1, source_target_pairs={{16,0},{32,16},{48,32},{0,48},{80,64},{96,80},{112,96},{64,112},{1... | collective-permute-start | bytes 786440 | tf_op jit(solution)/shard_map/ppermute | solution.py:53
  5.6 18.9 %collective-permute-start.3 = (bf16[16,8192]{1,0:T(8,128)(2,1)}, bf16[16,8192]{1,0:T(8,128)(2,1)S(1)}, u32[]{:S(2)}, u32[]{:S(2)}) collective-permute-start(bf16[16,8192]{1,0:T(8,128)(2,1)} %refs_6_.2), channel_id=1, source_target_pairs={{0,1},{1,0},{2,3},{3,2},{4,5},{5,4},{6,7},{7,6},{8,9},{9,8},{10,11... | collective-permute-start | bytes 786440 | tf_op jit(solution)/shard_map/ppermute | solution.py:49
  24.5 2.0 %collective-permute-start.10 = (bf16[16,8192]{1,0:T(8,128)(2,1)S(1)}, bf16[16,8192]{1,0:T(8,128)(2,1)S(1)}, u32[]{:S(2)}, u32[]{:S(2)}) collective-permute-start(bf16[16,8192]{1,0:T(8,128)(2,1)S(1)} %collective-permute-done.1.refs_4_), channel_id=1, source_target_pairs={{0,1},{1,0},{2,3},{3,2},{4,5},{5,4},{6,7},{7,6},{8,9},{9,8},{10,11... | collective-permute-start | bytes 786440 | tf_op jit(solution)/shard_map/ppermute | solution.py:49
  25.1 4.2 %collective-permute-start.9 = (bf16[16,8192]{1,0:T(8,128)(2,1)S(1)}, bf16[16,8192]{1,0:T(8,128)(2,1)S(1)}, u32[]{:S(2)}, u32[]{:S(2)}) collective-permute-start(bf16[16,8192]{1,0:T(8,128)(2,1)S(1)} %collective-permute-done.2.refs_2_), channel_id=1, source_target_pairs={{0,1},{1,0},{2,3},{3,2},{4,5},{5,4},{6,7},{7,6},{8,9},{9,8},{10,11... | collective-permute-start | bytes 786440 | tf_op jit(solution)/shard_map/ppermute | solution.py:49
  25.2 4.1 %collective-permute-start.8 = (bf16[16,8192]{1,0:T(8,128)(2,1)S(1)}, bf16[16,8192]{1,0:T(8,128)(2,1)S(1)}, u32[]{:S(2)}, u32[]{:S(2)}) collective-permute-start(bf16[16,8192]{1,0:T(8,128)(2,1)S(1)} %collective-permute-done.refs_0_), channel_id=1, source_target_pairs={{0,1},{1,0},{2,3},{3,2},{4,5},{5,4},{6,7},{7,6},{8,9},{9,8},{10,11... | collective-permute-start | bytes 786440 | tf_op jit(solution)/shard_map/ppermute | solution.py:49
  25.6 28.7 %collective-permute-start.7 = (bf16[16,8192]{1,0:T(8,128)(2,1)S(1)}, bf16[16,8192]{1,0:T(8,128)(2,1)S(1)}, u32[]{:S(2)}, u32[]{:S(2)}) collective-permute-start(bf16[16,8192]{1,0:T(8,128)(2,1)S(1)} %collective-permute-done.2.refs_2_), channel_id=1, source_target_pairs={{48,0},{0,16},{16,32},{32,48},{112,64},{64,80},{80,96},{96,112},{4... | collective-permute-start | bytes 786440 | tf_op jit(solution)/shard_map/ppermute | solution.py:53
  26.0 28.4 %collective-permute-start.6 = (bf16[16,8192]{1,0:T(8,128)(2,1)S(1)}, bf16[16,8192]{1,0:T(8,128)(2,1)S(1)}, u32[]{:S(2)}, u32[]{:S(2)}) collective-permute-start(bf16[16,8192]{1,0:T(8,128)(2,1)S(1)} %collective-permute-done.refs_0_), channel_id=1, source_target_pairs={{64,0},{80,16},{96,32},{112,48},{0,64},{16,80},{32,96},{48,112},{6... | collective-permute-start | bytes 786440 | tf_op jit(solution)/shard_map/ppermute | solution.py:53
  26.5 27.9 %collective-permute-start.5 = (bf16[16,8192]{1,0:T(8,128)(2,1)S(1)}, bf16[16,8192]{1,0:T(8,128)(2,1)S(1)}, u32[]{:S(2)}, u32[]{:S(2)}) collective-permute-start(bf16[16,8192]{1,0:T(8,128)(2,1)S(1)} %collective-permute-done.refs_0_), channel_id=1, source_target_pairs={{16,0},{32,16},{48,32},{0,48},{80,64},{96,80},{112,96},{64,112},{1... | collective-permute-start | bytes 786440 | tf_op jit(solution)/shard_map/ppermute | solution.py:53
  54.4 2.8 %collective-permute-start.13 = (bf16[16,8192]{1,0:T(8,128)(2,1)S(1)}, bf16[16,8192]{1,0:T(8,128)(2,1)S(1)}, u32[]{:S(2)}, u32[]{:S(2)}) collective-permute-start(bf16[16,8192]{1,0:T(8,128)(2,1)S(1)} %collective-permute-done.6.across_up.refs_0_), channel_id=1, source_target_pairs={{0,1},{1,0},{2,3},{3,2},{4,5},{5,4},{6,7},{7,6},{8,9},{9,8},{10,11... | collective-permute-start | bytes 786440 | tf_op jit(solution)/shard_map/ppermute | solution.py:49
  54.5 2.7 %collective-permute-start.14 = (bf16[16,8192]{1,0:T(8,128)(2,1)S(1)}, bf16[16,8192]{1,0:T(8,128)(2,1)S(1)}, u32[]{:S(2)}, u32[]{:S(2)}) collective-permute-start(bf16[16,8192]{1,0:T(8,128)(2,1)S(1)} %collective-permute-done.7.across_down.refs_2_), channel_id=1, source_target_pairs={{0,1},{1,0},{2,3},{3,2},{4,5},{5,4},{6,7},{7,6},{8,9},{9,8},{10,11... | collective-permute-start | bytes 786440 | tf_op jit(solution)/shard_map/ppermute | solution.py:49
  55.0 2.2 %collective-permute-start.15 = (bf16[16,8192]{1,0:T(8,128)(2,1)S(1)}, bf16[16,8192]{1,0:T(8,128)(2,1)S(1)}, u32[]{:S(2)}, u32[]{:S(2)}) collective-permute-start(bf16[16,8192]{1,0:T(8,128)(2,1)S(1)} %collective-permute-done.5.far.refs_4_), channel_id=1, source_target_pairs={{0,1},{1,0},{2,3},{3,2},{4,5},{5,4},{6,7},{7,6},{8,9},{9,8},{10,11... | collective-permute-start | bytes 786440 | tf_op jit(solution)/shard_map/ppermute | solution.py:49
  55.1 19.4 %collective-permute-start.11 = (bf16[16,4096]{1,0:T(8,128)(2,1)S(1)}, bf16[16,4096]{1,0:T(8,128)(2,1)S(1)}, u32[]{:S(2)}, u32[]{:S(2)}) collective-permute-start(bf16[16,4096]{1,0:T(8,128)(2,1)S(1)} %get-tuple-element.71), channel_id=1, source_target_pairs={{16,0},{32,16},{48,32},{0,48},{80,64},{96,80},{112,96},{64,112},{1... | collective-permute-start | bytes 393224 | tf_op jit(solution)/shard_map/ppermute | solution.py:53
  56.0 18.6 %collective-permute-start.12 = (bf16[16,4096]{1,0:T(8,128)(2,1)S(1)}, bf16[16,4096]{1,0:T(8,128)(2,1)S(1)}, u32[]{:S(2)}, u32[]{:S(2)}) collective-permute-start(bf16[16,4096]{1,0:T(8,128)(2,1)S(1)} %get-tuple-element.72), channel_id=1, source_target_pairs={{48,0},{0,16},{16,32},{32,48},{112,64},{64,80},{80,96},{96,112},{4... | collective-permute-start | bytes 393224 | tf_op jit(solution)/shard_map/ppermute | solution.py:53
  74.6 1.8 collective-permute-start.16
  74.6 1.7 collective-permute-start.17
  128.2 18.3 %collective-permute-start.20 = (bf16[16,4096]{1,0:T(8,128)(2,1)S(1)}, bf16[16,4096]{1,0:T(8,128)(2,1)S(1)}, u32[]{:S(2)}, u32[]{:S(2)}) collective-permute-start(bf16[16,4096]{1,0:T(8,128)(2,1)S(1)} %get-tuple-element.80), channel_id=1, source_target_pairs={{0,16},{16,32},{32,48},{48,0},{64,80},{80,96},{96,112},{112,64},{1... | collective-permute-start | bytes 393224 | tf_op jit(solution)/shard_map/ppermute | solution.py:57
  128.3 18.2 %collective-permute-start.21 = (bf16[16,4096]{1,0:T(8,128)(2,1)S(1)}, bf16[16,4096]{1,0:T(8,128)(2,1)S(1)}, u32[]{:S(2)}, u32[]{:S(2)}) collective-permute-start(bf16[16,4096]{1,0:T(8,128)(2,1)S(1)} %get-tuple-element.81), channel_id=1, source_target_pairs={{0,48},{16,0},{32,16},{48,32},{64,112},{80,64},{96,80},{112,96},{1... | collective-permute-start | bytes 393224 | tf_op jit(solution)/shard_map/ppermute | solution.py:57
  146.5 2.6 %collective-permute-start.22 = (bf16[16,24576]{1,0:T(8,128)(2,1)S(1)}, bf16[16,24576]{1,0:T(8,128)(2,1)S(1)}, u32[]{:S(2)}, u32[]{:S(2)}) collective-permute-start(bf16[16,24576]{1,0:T(8,128)(2,1)S(1)} %get-tuple-element.86), channel_id=1, source_target_pairs={{0,1},{1,0},{2,3},{3,2},{4,5},{5,4},{6,7},{7,6},{8,9},{9,8},{10,11... | collective-permute-start | bytes 2359304 | tf_op jit(solution)/shard_map/ppermute | solution.py:49
  147.2 1.9 collective-permute-start.24
  149.3 20.4 %collective-permute-start.25 = (bf16[16,8192]{1,0:T(8,128)(2,1)S(1)}, bf16[16,8192]{1,0:T(8,128)(2,1)S(1)}, u32[]{:S(2)}, u32[]{:S(2)}) collective-permute-start(bf16[16,8192]{1,0:T(8,128)(2,1)S(1)} %get-tuple-element.95), channel_id=1, source_target_pairs={{0,64},{16,80},{32,96},{48,112},{64,0},{80,16},{96,32},{112,48},{1... | collective-permute-start | bytes 786440 | tf_op jit(solution)/shard_map/ppermute | solution.py:57
  149.4 20.3 %collective-permute-start.26 = (bf16[16,8192]{1,0:T(8,128)(2,1)S(1)}, bf16[16,8192]{1,0:T(8,128)(2,1)S(1)}, u32[]{:S(2)}, u32[]{:S(2)}) collective-permute-start(bf16[16,8192]{1,0:T(8,128)(2,1)S(1)} %get-tuple-element.96), channel_id=1, source_target_pairs={{0,48},{16,0},{32,16},{48,32},{64,112},{80,64},{96,80},{112,96},{1... | collective-permute-start | bytes 786440 | tf_op jit(solution)/shard_map/ppermute | solution.py:57
  149.5 20.3 %collective-permute-start.27 = (bf16[16,8192]{1,0:T(8,128)(2,1)S(1)}, bf16[16,8192]{1,0:T(8,128)(2,1)S(1)}, u32[]{:S(2)}, u32[]{:S(2)}) collective-permute-start(bf16[16,8192]{1,0:T(8,128)(2,1)S(1)} %get-tuple-element.91), channel_id=1, source_target_pairs={{0,16},{16,32},{32,48},{48,0},{64,80},{80,96},{96,112},{112,64},{1... | collective-permute-start | bytes 786440 | tf_op jit(solution)/shard_map/ppermute | solution.py:57
  169.8 3.9 %collective-permute-start.28 = (bf16[16,32768]{1,0:T(8,128)(2,1)S(1)}, bf16[16,32768]{1,0:T(8,128)(2,1)S(1)}, u32[]{:S(2)}, u32[]{:S(2)}) collective-permute-start(bf16[16,32768]{1,0:T(8,128)(2,1)S(1)} %get-tuple-element.97), channel_id=1, source_target_pairs={{0,1},{1,0},{2,3},{3,2},{4,5},{5,4},{6,7},{7,6},{8,9},{9,8},{10,11... | collective-permute-start | bytes 3145736 | tf_op jit(solution)/shard_map/ppermute | solution.py:49
  169.9 3.8 %collective-permute-start.29 = (f32[16,256]{1,0:T(8,128)S(1)}, f32[16,256]{1,0:T(8,128)S(1)}, u32[]{:S(2)}, u32[]{:S(2)}) collective-permute-start(f32[16,256]{1,0:T(8,128)S(1)} %add.89), channel_id=1, source_target_pairs={{64,0},{80,16},{96,32},{112,48},{0,64},{16,80},{32,96},{48,112},{6... | collective-permute-start | bytes 49160 | tf_op jit(solution)/shard_map/ppermute | solution.py:53
  174.0 16.2 %collective-permute-start.32 = (bf16[16,8192]{1,0:T(8,128)(2,1)S(1)}, bf16[16,8192]{1,0:T(8,128)(2,1)S(1)}, u32[]{:S(2)}, u32[]{:S(2)}) collective-permute-start(bf16[16,8192]{1,0:T(8,128)(2,1)S(1)} %get-tuple-element.107), channel_id=1, source_target_pairs={{0,16},{16,32},{32,48},{48,0},{64,80},{80,96},{96,112},{112,64},{1... | collective-permute-start | bytes 786440 | tf_op jit(solution)/shard_map/ppermute | solution.py:57
  174.9 15.3 %collective-permute-start.33 = (bf16[16,8192]{1,0:T(8,128)(2,1)S(1)}, bf16[16,8192]{1,0:T(8,128)(2,1)S(1)}, u32[]{:S(2)}, u32[]{:S(2)}) collective-permute-start(bf16[16,8192]{1,0:T(8,128)(2,1)S(1)} %get-tuple-element.108), channel_id=1, source_target_pairs={{0,64},{16,80},{32,96},{48,112},{64,0},{80,16},{96,32},{112,48},{1... | collective-permute-start | bytes 786440 | tf_op jit(solution)/shard_map/ppermute | solution.py:57
  176.9 13.3 %collective-permute-start.34 = (bf16[16,8192]{1,0:T(8,128)(2,1)S(1)}, bf16[16,8192]{1,0:T(8,128)(2,1)S(1)}, u32[]{:S(2)}, u32[]{:S(2)}) collective-permute-start(bf16[16,8192]{1,0:T(8,128)(2,1)S(1)} %get-tuple-element.103), channel_id=1, source_target_pairs={{0,48},{16,0},{32,16},{48,32},{64,112},{80,64},{96,80},{112,96},{1... | collective-permute-start | bytes 786440 | tf_op jit(solution)/shard_map/ppermute | solution.py:57
  178.3 6.1 %collective-permute-start.30 = (f32[16,256]{1,0:T(8,128)S(1)}, f32[16,256]{1,0:T(8,128)S(1)}, u32[]{:S(2)}, u32[]{:S(2)}) collective-permute-start(f32[16,256]{1,0:T(8,128)S(1)} %add.90.refs_5_), channel_id=1, source_target_pairs={{0,16},{16,0},{32,48},{48,32},{64,80},{80,64},{96,112},{112,96},{1... | collective-permute-start | bytes 49160 | tf_op jit(solution)/shard_map/ppermute | solution.py:500
  184.4 5.2 %collective-permute-start.31 = (f32[16,256]{1,0:T(8,128)S(1)}, f32[16,256]{1,0:T(8,128)S(1)}, u32[]{:S(2)}, u32[]{:S(2)}) collective-permute-start(f32[16,256]{1,0:T(8,128)S(1)} %add.91), channel_id=1, source_target_pairs={{0,32},{16,48},{32,0},{48,16},{64,96},{80,112},{96,64},{112,80},{1... | collective-permute-start | bytes 49160 | tf_op jit(solution)/shard_map/ppermute | solution.py:501
  (12 other events, 193.4 us)

commit v7 on v5

--- a/solution.py
+++ b/solution.py
@@ -14,9 +14,8 @@
 SMEM = pl.BlockSpec(memory_space=pltpu.SMEM)
 
 STEPS = ((0, 0), (0, 1), (0, 3), (1, 0), (0, 2), (1, 1), (1, 3), (1, 2))
-UP, DOWN, ACROSS = (0, 1), (0, 3), (1, 0)
-GROUPS = ((7,), (5, 6, 4), (1, 3, 2, 0))
-PIECES = tuple((d, 0, 8192) for d in range(7)) + ((7, 0, 4096), (7, 4096, 4096))
+UP, DOWN, ACROSS, CORNER = (0, 1), (0, 3), (1, 0), (1, 2)
+GROUPS = ((5, 6, 4, 7), (1, 3, 2, 0))
 SLABS = 8
 HALF = 16
 PAIR = 32
@@ -24,7 +23,6 @@
 NODES = 65536
 SLOTS = 32
 ROWS = 32
-HELD = 16
 RING = 16
 
 
@@ -57,10 +55,6 @@
     return lax.ppermute(a, "blk", _to_step(step))
 
 
-def after(a, *others):
-    return lax.optimization_barrier((a, *others))[0]
-
-
 def row_of(core, local):
     return 8 * (local // 4) + 4 * core + local % 4
 
@@ -69,15 +63,14 @@
     return pl.ds(pl.multiple_of(block * 128, 128), 128)
 
 
-def load_kernel(first, info, tiles, out, token, sems):
+def load_kernel(info, tiles, low, high, token, sems):
     core = info[0]
     copies = []
-    for g in range(HELD // 4):
+    for g in range(8):
+        half = (low, high)[g // 4]
         copies.append(
             pltpu.make_async_copy(
-                tiles.at[pl.ds(8 * (first + g) + 4 * core, 4)],
-                out.at[pl.ds(4 * g, 4)],
-                sems.at[g],
+                tiles.at[pl.ds(8 * g + 4 * core, 4)], half.at[pl.ds(4 * (g % 4), 4)], sems.at[g]
             )
         )
     for c in copies:
@@ -87,27 +80,42 @@
         c.wait()
 
 
-def load_tiles(info, tiles, first):
-    held, token = pl.pallas_call(
-        functools.partial(load_kernel, first),
+def load_tiles(info, tiles):
+    *held, token = pl.pallas_call(
+        load_kernel,
         out_shape=(
-            pltpu.VMEM((HELD, SLOTS, 128, 128), BF16),
+            pltpu.VMEM((ROWS // 2, SLOTS, 128, 128), BF16),
+            pltpu.VMEM((ROWS // 2, SLOTS, 128, 128), BF16),
             jax.ShapeDtypeStruct((8, 128), F32),
         ),
         in_specs=[SMEM, ANY],
-        out_specs=(VMEM, VMEM),
-        scratch_shapes=[pltpu.SemaphoreType.DMA((HELD // 4,))],
+        out_specs=(VMEM, VMEM, VMEM),
+        scratch_shapes=[pltpu.SemaphoreType.DMA((8,))],
         compiler_params=pltpu.CompilerParams(vmem_limit_bytes=2 << 20),
-        cost_estimate=pl.CostEstimate(flops=0, bytes_accessed=32 << 20, transcendentals=0),
+        cost_estimate=pl.CostEstimate(flops=0, bytes_accessed=48 << 20, transcendentals=0),
         name="load_tiles",
     )(info, tiles)
-    return pltpu.with_memory_space_constraint(held, pltpu.VMEM), token
+    return [pltpu.with_memory_space_constraint(h, pltpu.VMEM) for h in held], token
+
+
+def gate(arrays, before):
+    n = len(arrays)
+    return pl.pallas_call(
+        lambda *refs: None,
+        out_shape=[jax.ShapeDtypeStruct(a.shape, a.dtype) for a in arrays],
+        in_specs=[ANY] * (n + len(before)),
+        out_specs=[ANY] * n,
+        input_output_aliases={i: i for i in range(n)},
+        compiler_params=pltpu.CompilerParams(vmem_limit_bytes=1 << 20),
+        cost_estimate=pl.CostEstimate(flops=0, bytes_accessed=1024, transcendentals=0),
+        name="gate",
+    )(*arrays, *before)
 
 
 WIDE = 1280
 
 
-def unpack_kernel(info, message, mine, other, wgrad_mine, wgrad_other):
+def unpack_kernel(info, message, before, mine, other, wgrad_mine, wgrad_other):
     core = info[0]
     own = pl.ds(pl.multiple_of(HALF * core, HALF), HALF)
     sibling = pl.ds(pl.multiple_of(HALF * (1 - core), HALF), HALF)
@@ -119,7 +127,7 @@
         wgrad[...] = total
 
 
-def unpack(info, message):
+def unpack(info, message, before):
     return pl.pallas_call(
         unpack_kernel,
         out_shape=(
@@ -128,15 +136,15 @@
             jax.ShapeDtypeStruct((HALF, 256), F32),
             jax.ShapeDtypeStruct((HALF, 256), F32),
         ),
-        in_specs=[SMEM, VMEM],
+        in_specs=[SMEM, VMEM, ANY],
         out_specs=(VMEM,) * 4,
         compiler_params=pltpu.CompilerParams(vmem_limit_bytes=4 << 20),
         cost_estimate=pl.CostEstimate(flops=0, bytes_accessed=1 << 20, transcendentals=0),
         name="unpack",
-    )(info, message)
-
-
-def join_kernel(info, mine, received, hidden):
+    )(info, message, before)
+
+
+def join_kernel(info, mine, received, before, hidden):
     core = info[0]
     for g in range(8):
         chunk = slice(512 * g, 512 * (g + 1))
@@ -145,29 +153,29 @@
         hidden[:, 1024 * g + 512 : 1024 * (g + 1)] = jnp.where(core == 0, b, a)
 
 
-def join(info, mine, received):
+def join(info, mine, received, before):
     return pl.pallas_call(
         join_kernel,
         out_shape=jax.ShapeDtypeStruct((HALF, LOCAL), BF16),
-        in_specs=[SMEM, VMEM, VMEM],
+        in_specs=[SMEM, VMEM, VMEM, ANY],
         out_specs=VMEM,
         compiler_params=pltpu.CompilerParams(vmem_limit_bytes=4 << 20),
         cost_estimate=pl.CostEstimate(flops=0, bytes_accessed=1 << 20, transcendentals=0),
         name="join",
-    )(info, mine, received)
+    )(info, mine, received, before)
 
 
 def forward_kernel(info, cols, low_tiles, high_tiles, *refs):
-    pieces, sides, (out, feats, sems) = refs[:18], refs[18:22], refs[22:]
+    pieces, sides, (out, feats, sems) = refs[:16], refs[16:20], refs[20:]
     core = info[0]
     copies = []
-    for i, (d, first, count) in enumerate(PIECES):
-        at = pl.multiple_of(info[1 + d] * LOCAL + first, 4096)
+    for i in range(SLABS):
+        at = pl.multiple_of(info[1 + i] * LOCAL, LOCAL)
         for h in range(2):
             rows = pl.ds(pl.multiple_of(jnp.where(core == h, 0, HALF), HALF), HALF)
             copies.append(
                 pltpu.make_async_copy(
-                    pieces[2 * i + h], feats.at[rows, pl.ds(at, count)], sems.at[2 * i + h]
+                    pieces[2 * i + h], feats.at[rows, pl.ds(at, LOCAL)], sems.at[2 * i + h]
                 )
             )
     for c in copies:
@@ -182,12 +190,12 @@
     for c in copies:
         c.wait()
 
-    def four_rows(first, source, offset, sums):
+    def four_rows(first, tiles, sums):
         rows = [row_of(core, first + k) for k in range(4)]
 
         def push(unit, p, register):
             right = [
-                jnp.concatenate([source[first - offset + k, p + e] for e in range(2)], axis=1)
+                jnp.concatenate([tiles[lax.rem(first, 16) + k, p + e] for e in range(2)], axis=1)
                 for k in (2 * unit, 2 * unit + 1)
             ]
             pltpu.matmul_push_rhs(
@@ -218,27 +226,27 @@
                 j = 2 * unit + k
                 out[first // 4, :, 128 * j : 128 * (j + 1)] = value.astype(BF16)
 
-    for source, offset in ((low_tiles, 0), (high_tiles, HELD)):
-
-        def step(i, carry, source=source, offset=offset):
+    for half, tiles in enumerate((low_tiles, high_tiles)):
+
+        def step(i, carry, tiles=tiles):
             pl.run_scoped(
-                lambda *sums: four_rows(offset + 4 * i, source, offset, sums),
+                lambda *sums: four_rows(4 * i, tiles, sums),
                 *[pltpu.ACC(unit)((2 * PAIR, 256), F32) for unit in range(2)],
             )
             return carry
 
-        lax.fori_loop(0, HELD // 4, step, 0)
+        lax.fori_loop(4 * half, 4 * half + 4, step, 0)
 
 
 def forward(info, cols, held, pieces, sides):
     return pl.pallas_call(
         forward_kernel,
         out_shape=jax.ShapeDtypeStruct((8, PAIR, WIDE), BF16),
-        in_specs=[SMEM, SMEM, VMEM, VMEM] + [ANY] * 18 + [VMEM] * 4,
+        in_specs=[SMEM, SMEM, VMEM, VMEM] + [ANY] * 16 + [VMEM] * 4,
         out_specs=VMEM,
         scratch_shapes=[
             pltpu.VMEM((PAIR, NODES), BF16),
-            pltpu.SemaphoreType.DMA((18,)),
+            pltpu.SemaphoreType.DMA((16,)),
         ],
         compiler_params=pltpu.CompilerParams(vmem_limit_bytes=8 << 20),
         cost_estimate=pl.CostEstimate(
@@ -276,7 +284,7 @@
 
 
 def backward_kernel(info, cols, tiles, grad, *refs):
-    outs, (total, ring, sems) = refs[:6], refs[6:]
+    outs, (total, ring, sems) = refs[:4], refs[4:]
     core = info[0]
 
     def copy(i):
@@ -329,7 +337,7 @@
             lanes = pl.ds(pl.multiple_of(info[1 + d] * LOCAL, LOCAL), LOCAL)
             place = slice(LOCAL * i, LOCAL * (i + 1))
             outs[phase][:, place] = total[own, lanes].astype(BF16)
-            outs[3 + phase][:, place] = total[other, lanes].astype(BF16)
+            outs[2 + phase][:, place] = total[other, lanes].astype(BF16)
 
 
 def backward(info, cols, tiles, grad):
@@ -337,7 +345,7 @@
         backward_kernel,
         out_shape=[jax.ShapeDtypeStruct((HALF, LOCAL * len(g)), BF16) for g in GROUPS] * 2,
         in_specs=[SMEM, SMEM, ANY, VMEM],
-        out_specs=[VMEM] * 6,
+        out_specs=[VMEM] * 4,
         scratch_shapes=[
             pltpu.VMEM((PAIR, NODES), F32),
             pltpu.VMEM((RING, SLOTS, 128, 128), BF16),
@@ -351,23 +359,6 @@
     )(info, cols, tiles, grad)
 
 
-def cut_kernel(across_up, across_down, far, token, up_half, down_half):
-    up_half[...] = across_up[:, :4096]
-    down_half[...] = across_down[:, 4096:]
-
-
-def cut(across_up, across_down, far, token):
-    return pl.pallas_call(
-        cut_kernel,
-        out_shape=[jax.ShapeDtypeStruct((HALF, 4096), BF16)] * 2,
-        in_specs=[VMEM, VMEM, ANY, ANY],
-        out_specs=[VMEM] * 2,
-        compiler_params=pltpu.CompilerParams(vmem_limit_bytes=4 << 20),
-        cost_estimate=pl.CostEstimate(flops=0, bytes_accessed=1 << 19, transcendentals=0),
-        name="cut",
-    )(across_up, across_down, far, token)
-
-
 def sum_call(kernel, shapes, args, name, before=()):
     def body(*refs):
         kernel(*refs[: len(args)], *refs[len(args) + len(before) :])
@@ -383,22 +374,11 @@
     )(*args, *before)
 
 
-def corner_kernel(own, other, low, high):
-    total = own[...].astype(F32) + other[...].astype(F32)
-    low[...] = total[:, :4096].astype(BF16)
-    high[...] = total[:, 4096:].astype(BF16)
-
-
-def middle_kernel(own, other, low, high, across_up, across_down, far):
-    def mine(i, first, count):
-        lanes = slice(LOCAL * i + first, LOCAL * i + first + count)
-        return own[:, lanes].astype(F32) + other[:, lanes].astype(F32)
-
-    across_up[:, :4096] = (mine(0, 0, 4096) + low[...].astype(F32)).astype(BF16)
-    across_up[:, 4096:] = mine(0, 4096, 4096).astype(BF16)
-    across_down[:, :4096] = mine(1, 0, 4096).astype(BF16)
-    across_down[:, 4096:] = (mine(1, 4096, 4096) + high[...].astype(F32)).astype(BF16)
-    far[...] = mine(2, 0, LOCAL).astype(BF16)
+def far_kernel(own, other, wgrad, wgrad_other, *outs):
+    for i, out in enumerate(outs[:4]):
+        lanes = slice(LOCAL * i, LOCAL * (i + 1))
+        out[...] = (own[:, lanes].astype(F32) + other[:, lanes].astype(F32)).astype(BF16)
+    outs[4][...] = wgrad[...] + wgrad_other[...]
 
 
 def near_kernel(own, other, from_across, from_up, from_down, up, across, down, base):
@@ -412,8 +392,11 @@
     base[...] = mine(3)
 
 
-def last_kernel(base, a, b, c, out):
-    total = base[...] + a[...].astype(F32) + b[...].astype(F32) + c[...].astype(F32)
+def last_kernel(base, *refs):
+    *received, out = refs
+    total = base[...]
+    for a in received:
+        total += a[...].astype(F32)
     out[...] = total.astype(BF16)
 
 
@@ -424,60 +407,53 @@
     info = jnp.stack([core] + [(x ^ dx) * 4 + (y + dy) % 4 for dx, dy in STEPS]).astype(jnp.int32)
     cols = block_cols.T
 
-    up, down, across = (receive(node_feats, s) for s in (UP, DOWN, ACROSS))
-    low_tiles, token = load_tiles(info, tiles, 0)
+    up, down, across, corner = (receive(node_feats, s) for s in (UP, DOWN, ACROSS, CORNER))
+    held, token = load_tiles(info, tiles)
     feats_swapped, cot_swapped = swap(node_feats), swap(cotangent)
-    up2, across2 = after(up, token, feats_swapped, cot_swapped), after(across, token, down)
-    far = receive(up2, UP)
-    across_up = receive(up2, ACROSS)
-    across_down = receive(across2, DOWN)
-    high_tiles, token = load_tiles(info, after(tiles, up2, across2), HELD // 4)
-    weight_swapped = swap(after(weight, up2))
-    up_half, down_half = cut(across_up, across_down, far, token)
-    corner = [receive(up_half, UP), receive(down_half, DOWN)]
+    up, down, across, corner = gate(
+        (up, down, across, corner), (token, feats_swapped, cot_swapped)
+    )
+    far = receive(up, UP)
+    across_up = receive(up, ACROSS)
+    across_down = receive(across, DOWN)
     pieces = [node_feats, feats_swapped]
-    for block in (up, down, across, far, across_up, across_down):
-        pieces += [block, swap(after(block, up_half, down_half))]
-    for block in corner:
+    for block in (up, down, across, far, across_up, across_down, corner):
         pieces += [block, swap(block)]
-    sides = [cotangent, weight, cot_swapped, weight_swapped]
-
-    message = forward(info, cols, (low_tiles, high_tiles), pieces, sides)
+    sides = [cotangent, weight, cot_swapped, swap(weight)]
+
+    message = forward(info, cols, held, pieces, sides)
     message = lax.all_to_all(message, "feat", 0, 0, axis_index_groups=SAME_CORE, tiled=True)
     message = dense(message.reshape(256, WIDE)).reshape(8, PAIR, WIDE)
     message = lax.all_to_all(message, "feat", 0, 0, axis_index_groups=SAME_CORE, tiled=True)
 
-    own_a, own_b, own_c, other_a, other_b, other_c = backward(info, cols, tiles, message)
-    half, whole = ((HALF, 4096), BF16), ((HALF, LOCAL), BF16)
-    low, high = sum_call(corner_kernel, [half] * 2, (own_a, swap(other_a)), "sum_corner")
-    corner_up, corner_down = send(low, UP), send(high, DOWN)
-    hidden, hidden_other, wgrad, wgrad_other = unpack(info, after(message, low, high))
-    wgrad_other, hidden_other = swap(wgrad_other), swap(hidden_other)
-    across_up, across_down, far = sum_call(
-        middle_kernel,
-        [whole] * 3,
-        (own_b, swap(after(other_b, low, high)), corner_up, corner_down),
-        "sum_middle",
-        before=(wgrad_other, hidden_other),
+    own_a, own_c, other_a, other_c = backward(info, cols, tiles, message)
+    whole = ((HALF, LOCAL), BF16)
+    hidden, hidden_other, wgrad, wgrad_other = unpack(info, message, own_a)
+    hidden_other, wgrad_other = swap(hidden_other), swap(wgrad_other)
+    across_up, across_down, far, corner, wgrad = sum_call(
+        far_kernel,
+        [whole] * 4 + [((HALF, 256), F32)],
+        (own_a, swap(other_a), wgrad, wgrad_other),
+        "sum_far",
+        (hidden_other,),
     )
     from_across = send(across_up, ACROSS)
     from_up = send(across_down, DOWN)
     from_down = send(far, UP)
-    wgrad = wgrad + after(wgrad_other, far)
+    from_corner = send(corner, CORNER)
+    (other_c,) = gate((other_c,), (far,))
     wgrad = wgrad + receive(wgrad, ACROSS)
     up, across, down, base = sum_call(
         near_kernel,
         [whole] * 3 + [((HALF, LOCAL), F32)],
-        (own_c, swap(after(other_c, far)), from_across, from_up, from_down),
+        (own_c, swap(other_c), from_across, from_up, from_down),
         "sum_near",
-        before=(wgrad,),
+        (wgrad,),
     )
     last = [send(up, UP), send(across, ACROSS), send(down, DOWN)]
-    wgrad = after(wgrad, down)
-    wgrad = wgrad + lax.ppermute(wgrad, "blk", [(b, b ^ 1) for b in range(8)])
-    weight_grad = wgrad + lax.ppermute(wgrad, "blk", [(b, b ^ 2) for b in range(8)])
-    hidden = join(info, after(hidden, down), hidden_other)
-    (feats_grad,) = sum_call(last_kernel, [whole], (base, *last), "sum_last")
+    weight_grad = wgrad + receive(wgrad, UP) + receive(wgrad, DOWN) + receive(wgrad, (0, 2))
+    hidden = join(info, hidden, hidden_other, down)
+    (feats_grad,) = sum_call(last_kernel, [whole], (base, from_corner, *last), "sum_last")
     return hidden, weight_grad, feats_grad
 
 

time: 137 us -> 133 us (0.971)
  Pallas kernels: 42.5 us -> 39.9 us
    ppermute x9 -> x11, waiting for transfers between devices: 11.1 us -> 23.5 us  [receive(): return lax.ppermute(a, 'blk', _from_step(step))]
    ppermute x8 -> x7, waiting for transfers between devices: 6.16 us -> 0.16 us  [send(): return lax.ppermute(a, 'blk', _to_step(step))]
    ppermute x9 -> x11, starting transfers between devices: 12 us -> 17.7 us  [receive(): return lax.ppermute(a, 'blk', _from_step(step))]
    ppermute x2 -> x0, waiting for transfers between devices: 5.42 us -> none  [the longest x1 4.17 us: per_device(): wgrad = wgrad + lax.ppermute(wgrad, 'blk', [(b, b ^ 1) for b in range(8)])]
    ppermute x8 -> x7, starting transfers between devices: 11.6 us -> 8.83 us  [send(): return lax.ppermute(a, 'blk', _to_step(step))]
    ppermute x2 -> x0, starting transfers between devices: 2.73 us -> none  [the longest x1 2.73 us: per_device(): lax.ppermute(wgrad, 'blk', [(b, b ^ 2) for b in range(8)])]
    pallas_call x3, Pallas kernels: 13.5 us -> 11.3 us  [the longest x1 11.3 us: load_tiles(): pl.pallas_call(load_kernel, out_shape=(pltpu.VMEM((ROWS // 2, SLOTS, 128,...]
    ppermute x16 -> x14, waiting for transfers between devices: 3.98 us -> 3.15 us  [swap(): return lax.ppermute(a, 'feat', CORE_SWAP)]
  transfers between devices with their start and end apart: 35 -> 32, of which waited for: 16 -> 11; matrix products, arithmetic and copies ran while one was open for 1% -> 1% of each run, Pallas kernels for 11% -> 10%
where the time goes in v7:
time: 133 us
  Pallas kernels  39.9 us (30%)
  blocking collectives  35.6 us (27%)
  starting transfers between devices  29.2 us (22%)
  waiting for transfers between devices  26.9 us (20%)
    all_to_all x2, blocking collectives, per_device(): lax.all_to_all(message, 'feat', 0, 0, axis_index_groups=SAME_CORE, tiled=...  35.6 us
    ppermute x11, waiting for transfers between devices, receive(): return lax.ppermute(a, 'blk', _from_step(step))  23.5 us
    ppermute x11, starting transfers between devices, receive(): return lax.ppermute(a, 'blk', _from_step(step))  17.7 us
    pallas_call x1, Pallas kernels, backward(): pl.pallas_call(backward_kernel, out_shape=[jax.ShapeDtypeStruct((HALF, LO...  12.6 us
    pallas_call x1, Pallas kernels, forward(): pl.pallas_call(forward_kernel, out_shape=jax.ShapeDtypeStruct((8, PAIR, W...  12.1 us
    pallas_call x1, Pallas kernels, load_tiles(): pl.pallas_call(load_kernel, out_shape=(pltpu.VMEM((ROWS // 2, SLOTS, 128,...  11.3 us
    ppermute x7, starting transfers between devices, send(): return lax.ppermute(a, 'blk', _to_step(step))  8.83 us
    ppermute x14, waiting for transfers between devices, swap(): return lax.ppermute(a, 'feat', CORE_SWAP)  3.15 us
  transfers between devices with their start and end apart: 32, of which 11 were waited for; matrix products, arithmetic and copies ran while one was open for 1% of the time, Pallas kernels for 10%

profile of v7, /device:TPU:0, one launch (start us, length us, event | category | flops | bytes accessed | tf_op | source)
XLA Modules:
  0.0 133.2 jit_solution(17486203404537821117)
XLA Ops:
  0.7 1.7 %collective-permute-start.3 = (bf16[16,8192]{1,0:T(8,128)(2,1)}, bf16[16,8192]{1,0:T(8,128)(2,1)S(1)}, u32[]{:S(2)}, u32[]{:S(2)}) collective-permute-start(bf16[16,8192]{1,0:T(8,128)(2,1)} %refs_0_.1), channel_id=1, source_target_pairs={{64,0},{80,16},{96,32},{112,48},{0,64},{16,80},{32,96},{48,112},{6... | collective-permute-start | bytes 786440 | tf_op jit(solution)/shard_map/ppermute | solution.py:51
  2.4 1.6 %collective-permute-start.2 = (bf16[16,8192]{1,0:T(8,128)(2,1)}, bf16[16,8192]{1,0:T(8,128)(2,1)S(1)}, u32[]{:S(2)}, u32[]{:S(2)}) collective-permute-start(bf16[16,8192]{1,0:T(8,128)(2,1)} %refs_0_.1), channel_id=1, source_target_pairs={{48,0},{0,16},{16,32},{32,48},{112,64},{64,80},{80,96},{96,112},{4... | collective-permute-start | bytes 786440 | tf_op jit(solution)/shard_map/ppermute | solution.py:51
  4.0 1.7 %collective-permute-start.1 = (bf16[16,8192]{1,0:T(8,128)(2,1)}, bf16[16,8192]{1,0:T(8,128)(2,1)S(1)}, u32[]{:S(2)}, u32[]{:S(2)}) collective-permute-start(bf16[16,8192]{1,0:T(8,128)(2,1)} %refs_0_.1), channel_id=1, source_target_pairs={{16,0},{32,16},{48,32},{0,48},{80,64},{96,80},{112,96},{64,112},{1... | collective-permute-start | bytes 786440 | tf_op jit(solution)/shard_map/ppermute | solution.py:51
  5.6 2.0 %collective-permute-start.4 = (bf16[16,8192]{1,0:T(8,128)(2,1)}, bf16[16,8192]{1,0:T(8,128)(2,1)S(1)}, u32[]{:S(2)}, u32[]{:S(2)}) collective-permute-start(bf16[16,8192]{1,0:T(8,128)(2,1)} %refs_0_.1), channel_id=1, source_target_pairs={{96,0},{112,16},{64,32},{80,48},{32,64},{48,80},{0,96},{16,112},{9... | collective-permute-start | bytes 786440 | tf_op jit(solution)/shard_map/ppermute | solution.py:51
  7.6 2.1 %collective-permute-done.3.refs_2_ = bf16[16,8192]{1,0:T(8,128)(2,1)S(1)} collective-permute-done((bf16[16,8192]{1,0:T(8,128)(2,1)}, bf16[16,8192]{1,0:T(8,128)(2,1)S(1)}, u32[]{:S(2)}, u32[]{:S(2)}) %collective-permute-start.3) | collective-permute-done | bytes 262176 | tf_op jit(solution)/shard_map/ppermute | solution.py:51
  9.8 11.3 %load_tiles.1 = (bf16[16,32,128,128]{3,2,1,0:T(8,128)(2,1)S(1)}, bf16[16,32,128,128]{3,2,1,0:T(8,128)(2,1)S(1)}, f32[8,128]{1,0:T(8,128)S(1)}) custom-call(s32[9]{0:T(128)S(1)} %stack.39.info, bf16[64,32,128,128]{3,2,1,0:T(8,128)(2,1)} %tiles.3), custom_call_target="tpu_custom_call" | custom-call | bytes 50331648 | tf_op jit(solution)/shard_map/load_tiles/pallas_call | solution.py:84
  21.8 1.9 %collective-permute-start.13 = (bf16[16,8192]{1,0:T(8,128)(2,1)S(1)}, bf16[16,8192]{1,0:T(8,128)(2,1)S(1)}, u32[]{:S(2)}, u32[]{:S(2)}) collective-permute-start(bf16[16,8192]{1,0:T(8,128)(2,1)S(1)} %get-tuple-element.32.refs_6_), channel_id=1, source_target_pairs={{48,0},{0,16},{16,32},{32,48},{112,64},{64,80},{80,96},{96,112},{4... | collective-permute-start | bytes 786440 | tf_op jit(solution)/shard_map/ppermute | solution.py:51
  23.6 1.7 %collective-permute-start.11 = (bf16[16,8192]{1,0:T(8,128)(2,1)S(1)}, bf16[16,8192]{1,0:T(8,128)(2,1)S(1)}, u32[]{:S(2)}, u32[]{:S(2)}) collective-permute-start(bf16[16,8192]{1,0:T(8,128)(2,1)S(1)} %get-tuple-element.30.refs_2_), channel_id=1, source_target_pairs={{64,0},{80,16},{96,32},{112,48},{0,64},{16,80},{32,96},{48,112},{6... | collective-permute-start | bytes 786440 | tf_op jit(solution)/shard_map/ppermute | solution.py:51
  25.4 1.5 %collective-permute-start.9 = (bf16[16,8192]{1,0:T(8,128)(2,1)S(1)}, bf16[16,8192]{1,0:T(8,128)(2,1)S(1)}, u32[]{:S(2)}, u32[]{:S(2)}) collective-permute-start(bf16[16,8192]{1,0:T(8,128)(2,1)S(1)} %get-tuple-element.30.refs_2_), channel_id=1, source_target_pairs={{16,0},{32,16},{48,32},{0,48},{80,64},{96,80},{112,96},{64,112},{1... | collective-permute-start | bytes 786440 | tf_op jit(solution)/shard_map/ppermute | solution.py:51
  27.4 4.8 %collective-permute-done.13.refs_12_ = bf16[16,8192]{1,0:T(8,128)(2,1)S(1)} collective-permute-done((bf16[16,8192]{1,0:T(8,128)(2,1)S(1)}, bf16[16,8192]{1,0:T(8,128)(2,1)S(1)}, u32[]{:S(2)}, u32[]{:S(2)}) %collective-permute-start.13) | collective-permute-done | bytes 262176 | tf_op jit(solution)/shard_map/ppermute | solution.py:51
  32.7 0.7 collective-permute-done.9.refs_8_
  34.1 0.9 collective-permute-done.10.refs_9_
  35.0 12.1 %forward.1 = bf16[8,32,1280]{2,1,0:T(8,128)(2,1)S(1)} custom-call(s32[9]{0:T(128)S(1)} %stack.39.info, s32[32,64]{1,0:T(8,128)S(1)} %bitcast.14, bf16[16,32,128,128]{3,2,1,0:T(8,128)(2,1)S(1)} %get-tuple-element.27.low_tiles, bf16[16,32,128,128]{3,2,1,0:T(8,128)(2,1)S(1)} %get-tuple-element.28.high_tiles, bf16[16,8192]{1,0:T(8,128)(2,1)S(1)} %copy-done, ...), custom_call_target="tpu_custom_call" | custom-call | flops 8589934592 | bytes 8388608 | tf_op jit(solution)/shard_map/forward/pallas_call | solution.py:242
  47.2 20.6 %all_to_all.10 = bf16[8,32,1280]{2,1,0:T(8,128)(2,1)S(1)} all-to-all(bf16[8,32,1280]{2,1,0:T(8,128)(2,1)S(1)} %forward.1), channel_id=1, replica_groups={{0,2,4,6,8,10,12,14},{1,3,5,7,9,11,13,15},{16,18,20,22,24,26,28,30},{17..., dimensions={0} | all-to-all | bytes 1310720 | tf_op jit(solution)/shard_map/all_to_all | solution.py:425
  67.7 0.6 dense.1
  68.4 15.0 %all_to_all.11.grad.message = bf16[8,32,1280]{2,1,0:T(8,128)(2,1)S(1)} all-to-all(bf16[8,32,1280]{2,1,0:T(8,128)(2,1)S(1)} %bitcast.13), channel_id=1, replica_groups={{0,2,4,6,8,10,12,14},{1,3,5,7,9,11,13,15},{16,18,20,22,24,26,28,30},{17..., dimensions={0} | all-to-all | bytes 1310720 | tf_op jit(solution)/shard_map/all_to_all | solution.py:427
  83.4 12.6 %backward.1 = (bf16[16,32768]{1,0:T(8,128)(2,1)S(1)}, bf16[16,32768]{1,0:T(8,128)(2,1)S(1)}, bf16[16,32768]{1,0:T(8,128)(2,1)S(1)}, bf16[16,32768]{1,0:T(8,128)(2,1)S(1)}) custom-call(s32[9]{0:T(128)S(1)} %stack.39.info, s32[32,64]{1,0:T(8,128)S(1)} %bitcast.15, bf16[64,32,128,128]{3,2,1,0:T(8,128)(2,1)} %tiles.3, ...), custom_call_target="tpu_custom_call" | custom-call | flops 8589934592 | bytes 8388608 | tf_op jit(solution)/shard_map/backward/pallas_call | solution.py:344
  96.1 0.6 unpack.1
  97.3 1.6 %collective-permute-done.19.refs_3_ = f32[16,256]{1,0:T(8,128)S(1)} collective-permute-done((f32[16,256]{1,0:T(8,128)S(1)}, f32[16,256]{1,0:T(8,128)S(1)}, u32[]{:S(2)}, u32[]{:S(2)}) %collective-permute-start.19) | collective-permute-done | bytes 16416 | tf_op jit(solution)/shard_map/ppermute | solution.py:47
  99.8 2.8 %collective-permute-start.22 = (bf16[16,8192]{1,0:T(8,128)(2,1)S(1)}, bf16[16,8192]{1,0:T(8,128)(2,1)S(1)}, u32[]{:S(2)}, u32[]{:S(2)}) collective-permute-start(bf16[16,8192]{1,0:T(8,128)(2,1)S(1)} %get-tuple-element.44), channel_id=1, source_target_pairs={{0,48},{16,0},{32,16},{48,32},{64,112},{80,64},{96,80},{112,96},{1... | collective-permute-start | bytes 786440 | tf_op jit(solution)/shard_map/ppermute | solution.py:55
  102.6 1.8 %collective-permute-start.24 = (f32[16,256]{1,0:T(8,128)S(1)}, f32[16,256]{1,0:T(8,128)S(1)}, u32[]{:S(2)}, u32[]{:S(2)}) collective-permute-start(f32[16,256]{1,0:T(8,128)S(1)} %get-tuple-element.45), channel_id=1, source_target_pairs={{64,0},{80,16},{96,32},{112,48},{0,64},{16,80},{32,96},{48,112},{6... | collective-permute-start | bytes 49160 | tf_op jit(solution)/shard_map/ppermute | solution.py:51
  104.4 4.0 %collective-permute-done.24 = f32[16,256]{1,0:T(8,128)S(1)} collective-permute-done((f32[16,256]{1,0:T(8,128)S(1)}, f32[16,256]{1,0:T(8,128)S(1)}, u32[]{:S(2)}, u32[]{:S(2)}) %collective-permute-start.24) | collective-permute-done | bytes 16416 | tf_op jit(solution)/shard_map/ppermute | solution.py:51
  108.4 2.9 %collective-permute-start.27 = (f32[16,256]{1,0:T(8,128)S(1)}, f32[16,256]{1,0:T(8,128)S(1)}, u32[]{:S(2)}, u32[]{:S(2)}) collective-permute-start(f32[16,256]{1,0:T(8,128)S(1)} %add.89.refs_5_), channel_id=1, source_target_pairs={{32,0},{48,16},{0,32},{16,48},{96,64},{112,80},{64,96},{80,112},{3... | collective-permute-start | bytes 49160 | tf_op jit(solution)/shard_map/ppermute | solution.py:51
  112.2 1.4 %collective-permute-start.29 = (bf16[16,8192]{1,0:T(8,128)(2,1)S(1)}, bf16[16,8192]{1,0:T(8,128)(2,1)S(1)}, u32[]{:S(2)}, u32[]{:S(2)}) collective-permute-start(bf16[16,8192]{1,0:T(8,128)(2,1)S(1)} %get-tuple-element.49), channel_id=1, source_target_pairs={{0,16},{16,32},{32,48},{48,0},{64,80},{80,96},{96,112},{112,64},{1... | collective-permute-start | bytes 786440 | tf_op jit(solution)/shard_map/ppermute | solution.py:55
  113.6 1.7 %collective-permute-start.30 = (bf16[16,8192]{1,0:T(8,128)(2,1)S(1)}, bf16[16,8192]{1,0:T(8,128)(2,1)S(1)}, u32[]{:S(2)}, u32[]{:S(2)}) collective-permute-start(bf16[16,8192]{1,0:T(8,128)(2,1)S(1)} %get-tuple-element.50), channel_id=1, source_target_pairs={{0,64},{16,80},{32,96},{48,112},{64,0},{80,16},{96,32},{112,48},{1... | collective-permute-start | bytes 786440 | tf_op jit(solution)/shard_map/ppermute | solution.py:55
  115.4 2.1 %collective-permute-start.31 = (bf16[16,8192]{1,0:T(8,128)(2,1)S(1)}, bf16[16,8192]{1,0:T(8,128)(2,1)S(1)}, u32[]{:S(2)}, u32[]{:S(2)}) collective-permute-start(bf16[16,8192]{1,0:T(8,128)(2,1)S(1)} %get-tuple-element.46.before), channel_id=1, source_target_pairs={{0,48},{16,0},{32,16},{48,32},{64,112},{80,64},{96,80},{112,96},{1... | collective-permute-start | bytes 786440 | tf_op jit(solution)/shard_map/ppermute | solution.py:55
  117.4 9.2 %collective-permute-done.26 = f32[16,256]{1,0:T(8,128)S(1)} collective-permute-done((f32[16,256]{1,0:T(8,128)S(1)}, f32[16,256]{1,0:T(8,128)S(1)}, u32[]{:S(2)}, u32[]{:S(2)}) %collective-permute-start.26) | collective-permute-done | bytes 16416 | tf_op jit(solution)/shard_map/ppermute | solution.py:51
  126.6 1.1 collective-permute-start.25
  127.7 2.7 %collective-permute-done.25 = f32[16,256]{1,0:T(8,128)S(1)} collective-permute-done((f32[16,256]{1,0:T(8,128)S(1)}, f32[16,256]{1,0:T(8,128)S(1)}, u32[]{:S(2)}, u32[]{:S(2)}) %collective-permute-start.25) | collective-permute-done | bytes 16416 | tf_op jit(solution)/shard_map/ppermute | solution.py:51
  130.4 0.6 add_add_fusion
  131.0 1.3 join.1
  132.3 0.9 sum_last.1
  (56 shorter events, 5.1 us)
Async XLA Ops:
  0.6 5.0 %collective-permute-start.5 = (bf16[16,8192]{1,0:T(8,128)(2,1)}, bf16[16,8192]{1,0:T(8,128)(2,1)S(1)}, u32[]{:S(2)}, u32[]{:S(2)}) collective-permute-start(bf16[16,8192]{1,0:T(8,128)(2,1)} %refs_16_.1), channel_id=1, source_target_pairs={{0,1},{1,0},{2,3},{3,2},{4,5},{5,4},{6,7},{7,6},{8,9},{9,8},{10,11... | collective-permute-start | bytes 786440 | tf_op jit(solution)/shard_map/ppermute | solution.py:47
  0.7 8.9 %collective-permute-start.3 = (bf16[16,8192]{1,0:T(8,128)(2,1)}, bf16[16,8192]{1,0:T(8,128)(2,1)S(1)}, u32[]{:S(2)}, u32[]{:S(2)}) collective-permute-start(bf16[16,8192]{1,0:T(8,128)(2,1)} %refs_0_.1), channel_id=1, source_target_pairs={{64,0},{80,16},{96,32},{112,48},{0,64},{16,80},{32,96},{48,112},{6... | collective-permute-start | bytes 786440 | tf_op jit(solution)/shard_map/ppermute | solution.py:51
  2.4 18.7 %collective-permute-start.2 = (bf16[16,8192]{1,0:T(8,128)(2,1)}, bf16[16,8192]{1,0:T(8,128)(2,1)S(1)}, u32[]{:S(2)}, u32[]{:S(2)}) collective-permute-start(bf16[16,8192]{1,0:T(8,128)(2,1)} %refs_0_.1), channel_id=1, source_target_pairs={{48,0},{0,16},{16,32},{32,48},{112,64},{64,80},{80,96},{96,112},{4... | collective-permute-start | bytes 786440 | tf_op jit(solution)/shard_map/ppermute | solution.py:51
  4.0 17.1 %collective-permute-start.1 = (bf16[16,8192]{1,0:T(8,128)(2,1)}, bf16[16,8192]{1,0:T(8,128)(2,1)S(1)}, u32[]{:S(2)}, u32[]{:S(2)}) collective-permute-start(bf16[16,8192]{1,0:T(8,128)(2,1)} %refs_0_.1), channel_id=1, source_target_pairs={{16,0},{32,16},{48,32},{0,48},{80,64},{96,80},{112,96},{64,112},{1... | collective-permute-start | bytes 786440 | tf_op jit(solution)/shard_map/ppermute | solution.py:51
  5.6 15.5 %collective-permute-start = (bf16[16,8192]{1,0:T(8,128)(2,1)}, bf16[16,8192]{1,0:T(8,128)(2,1)S(1)}, u32[]{:S(2)}, u32[]{:S(2)}) collective-permute-start(bf16[16,8192]{1,0:T(8,128)(2,1)} %refs_0_.1), channel_id=1, source_target_pairs={{0,1},{1,0},{2,3},{3,2},{4,5},{5,4},{6,7},{7,6},{8,9},{9,8},{10,11... | collective-permute-start | bytes 786440 | tf_op jit(solution)/shard_map/ppermute | solution.py:47
  5.6 15.5 %collective-permute-start.4 = (bf16[16,8192]{1,0:T(8,128)(2,1)}, bf16[16,8192]{1,0:T(8,128)(2,1)S(1)}, u32[]{:S(2)}, u32[]{:S(2)}) collective-permute-start(bf16[16,8192]{1,0:T(8,128)(2,1)} %refs_0_.1), channel_id=1, source_target_pairs={{96,0},{112,16},{64,32},{80,48},{32,64},{48,80},{0,96},{16,112},{9... | collective-permute-start | bytes 786440 | tf_op jit(solution)/shard_map/ppermute | solution.py:51
  9.7 15.7 %collective-permute-start.16 = (bf16[16,256]{1,0:T(8,128)(2,1)}, bf16[16,256]{1,0:T(8,128)(2,1)S(1)}, u32[]{:S(2)}, u32[]{:S(2)}) collective-permute-start(bf16[16,256]{1,0:T(8,128)(2,1)} %refs_17_.1), channel_id=1, source_target_pairs={{0,1},{1,0},{2,3},{3,2},{4,5},{5,4},{6,7},{7,6},{8,9},{9,8},{10,11... | collective-permute-start | bytes 24584 | tf_op jit(solution)/shard_map/ppermute | solution.py:47
  21.1 5.8 %collective-permute-start.7 = (bf16[16,8192]{1,0:T(8,128)(2,1)S(1)}, bf16[16,8192]{1,0:T(8,128)(2,1)S(1)}, u32[]{:S(2)}, u32[]{:S(2)}) collective-permute-start(bf16[16,8192]{1,0:T(8,128)(2,1)S(1)} %get-tuple-element.31.refs_4_), channel_id=1, source_target_pairs={{0,1},{1,0},{2,3},{3,2},{4,5},{5,4},{6,7},{7,6},{8,9},{9,8},{10,11... | collective-permute-start | bytes 786440 | tf_op jit(solution)/shard_map/ppermute | solution.py:47
  21.7 5.2 %collective-permute-start.15 = (bf16[16,8192]{1,0:T(8,128)(2,1)S(1)}, bf16[16,8192]{1,0:T(8,128)(2,1)S(1)}, u32[]{:S(2)}, u32[]{:S(2)}) collective-permute-start(bf16[16,8192]{1,0:T(8,128)(2,1)S(1)} %get-tuple-element.33.refs_14_), channel_id=1, source_target_pairs={{0,1},{1,0},{2,3},{3,2},{4,5},{5,4},{6,7},{7,6},{8,9},{9,8},{10,11... | collective-permute-start | bytes 786440 | tf_op jit(solution)/shard_map/ppermute | solution.py:47
  21.8 10.5 %collective-permute-start.13 = (bf16[16,8192]{1,0:T(8,128)(2,1)S(1)}, bf16[16,8192]{1,0:T(8,128)(2,1)S(1)}, u32[]{:S(2)}, u32[]{:S(2)}) collective-permute-start(bf16[16,8192]{1,0:T(8,128)(2,1)S(1)} %get-tuple-element.32.refs_6_), channel_id=1, source_target_pairs={{48,0},{0,16},{16,32},{32,48},{112,64},{64,80},{80,96},{96,112},{4... | collective-permute-start | bytes 786440 | tf_op jit(solution)/shard_map/ppermute | solution.py:51
  23.6 8.6 %collective-permute-start.11 = (bf16[16,8192]{1,0:T(8,128)(2,1)S(1)}, bf16[16,8192]{1,0:T(8,128)(2,1)S(1)}, u32[]{:S(2)}, u32[]{:S(2)}) collective-permute-start(bf16[16,8192]{1,0:T(8,128)(2,1)S(1)} %get-tuple-element.30.refs_2_), channel_id=1, source_target_pairs={{64,0},{80,16},{96,32},{112,48},{0,64},{16,80},{32,96},{48,112},{6... | collective-permute-start | bytes 786440 | tf_op jit(solution)/shard_map/ppermute | solution.py:51
  25.4 8.1 %collective-permute-start.9 = (bf16[16,8192]{1,0:T(8,128)(2,1)S(1)}, bf16[16,8192]{1,0:T(8,128)(2,1)S(1)}, u32[]{:S(2)}, u32[]{:S(2)}) collective-permute-start(bf16[16,8192]{1,0:T(8,128)(2,1)S(1)} %get-tuple-element.30.refs_2_), channel_id=1, source_target_pairs={{16,0},{32,16},{48,32},{0,48},{80,64},{96,80},{112,96},{64,112},{1... | collective-permute-start | bytes 786440 | tf_op jit(solution)/shard_map/ppermute | solution.py:51
  26.9 6.6 %collective-permute-start.8 = (bf16[16,8192]{1,0:T(8,128)(2,1)S(1)}, bf16[16,8192]{1,0:T(8,128)(2,1)S(1)}, u32[]{:S(2)}, u32[]{:S(2)}) collective-permute-start(bf16[16,8192]{1,0:T(8,128)(2,1)S(1)} %get-tuple-element.32.refs_6_), channel_id=1, source_target_pairs={{0,1},{1,0},{2,3},{3,2},{4,5},{5,4},{6,7},{7,6},{8,9},{9,8},{10,11... | collective-permute-start | bytes 786440 | tf_op jit(solution)/shard_map/ppermute | solution.py:47
  26.9 6.6 %collective-permute-start.6 = (bf16[16,8192]{1,0:T(8,128)(2,1)S(1)}, bf16[16,8192]{1,0:T(8,128)(2,1)S(1)}, u32[]{:S(2)}, u32[]{:S(2)}) collective-permute-start(bf16[16,8192]{1,0:T(8,128)(2,1)S(1)} %get-tuple-element.30.refs_2_), channel_id=1, source_target_pairs={{0,1},{1,0},{2,3},{3,2},{4,5},{5,4},{6,7},{7,6},{8,9},{9,8},{10,11... | collective-permute-start | bytes 786440 | tf_op jit(solution)/shard_map/ppermute | solution.py:47
  32.2 1.5 %collective-permute-start.14 = (bf16[16,8192]{1,0:T(8,128)(2,1)S(1)}, bf16[16,8192]{1,0:T(8,128)(2,1)S(1)}, u32[]{:S(2)}, u32[]{:S(2)}) collective-permute-start(bf16[16,8192]{1,0:T(8,128)(2,1)S(1)} %collective-permute-done.13.refs_12_), channel_id=1, source_target_pairs={{0,1},{1,0},{2,3},{3,2},{4,5},{5,4},{6,7},{7,6},{8,9},{9,8},{10,11... | collective-permute-start | bytes 786440 | tf_op jit(solution)/shard_map/ppermute | solution.py:47
  32.2 1.9 %collective-permute-start.12 = (bf16[16,8192]{1,0:T(8,128)(2,1)S(1)}, bf16[16,8192]{1,0:T(8,128)(2,1)S(1)}, u32[]{:S(2)}, u32[]{:S(2)}) collective-permute-start(bf16[16,8192]{1,0:T(8,128)(2,1)S(1)} %collective-permute-done.11.refs_10_), channel_id=1, source_target_pairs={{0,1},{1,0},{2,3},{3,2},{4,5},{5,4},{6,7},{7,6},{8,9},{9,8},{10,11... | collective-permute-start | bytes 786440 | tf_op jit(solution)/shard_map/ppermute | solution.py:47
  33.5 1.5 %collective-permute-start.10 = (bf16[16,8192]{1,0:T(8,128)(2,1)S(1)}, bf16[16,8192]{1,0:T(8,128)(2,1)S(1)}, u32[]{:S(2)}, u32[]{:S(2)}) collective-permute-start(bf16[16,8192]{1,0:T(8,128)(2,1)S(1)} %collective-permute-done.9.refs_8_), channel_id=1, source_target_pairs={{0,1},{1,0},{2,3},{3,2},{4,5},{5,4},{6,7},{7,6},{8,9},{9,8},{10,11... | collective-permute-start | bytes 786440 | tf_op jit(solution)/shard_map/ppermute | solution.py:47
  96.0 3.0 %collective-permute-start.18 = (bf16[16,32768]{1,0:T(8,128)(2,1)S(1)}, bf16[16,32768]{1,0:T(8,128)(2,1)S(1)}, u32[]{:S(2)}, u32[]{:S(2)}) collective-permute-start(bf16[16,32768]{1,0:T(8,128)(2,1)S(1)} %get-tuple-element.39), channel_id=1, source_target_pairs={{0,1},{1,0},{2,3},{3,2},{4,5},{5,4},{6,7},{7,6},{8,9},{9,8},{10,11... | collective-permute-start | bytes 3145736 | tf_op jit(solution)/shard_map/ppermute | solution.py:47
  96.7 2.3 %collective-permute-start.17 = (bf16[16,4096]{1,0:T(8,128)(2,1)S(1)}, bf16[16,4096]{1,0:T(8,128)(2,1)S(1)}, u32[]{:S(2)}, u32[]{:S(2)}) collective-permute-start(bf16[16,4096]{1,0:T(8,128)(2,1)S(1)} %get-tuple-element.36), channel_id=1, source_target_pairs={{0,1},{1,0},{2,3},{3,2},{4,5},{5,4},{6,7},{7,6},{8,9},{9,8},{10,11... | collective-permute-start | bytes 393224 | tf_op jit(solution)/shard_map/ppermute | solution.py:47
  97.3 1.7 %collective-permute-start.19 = (f32[16,256]{1,0:T(8,128)S(1)}, f32[16,256]{1,0:T(8,128)S(1)}, u32[]{:S(2)}, u32[]{:S(2)}) collective-permute-start(f32[16,256]{1,0:T(8,128)S(1)} %get-tuple-element.41), channel_id=1, source_target_pairs={{0,1},{1,0},{2,3},{3,2},{4,5},{5,4},{6,7},{7,6},{8,9},{9,8},{10,11... | collective-permute-start | bytes 49160 | tf_op jit(solution)/shard_map/ppermute | solution.py:47
  99.2 12.6 %collective-permute-start.20 = (bf16[16,32768]{1,0:T(8,128)(2,1)S(1)}, bf16[16,32768]{1,0:T(8,128)(2,1)S(1)}, u32[]{:S(2)}, u32[]{:S(2)}) collective-permute-start(bf16[16,32768]{1,0:T(8,128)(2,1)S(1)} %gate.3), channel_id=1, source_target_pairs={{0,1},{1,0},{2,3},{3,2},{4,5},{5,4},{6,7},{7,6},{8,9},{9,8},{10,11... | collective-permute-start | bytes 3145736 | tf_op jit(solution)/shard_map/ppermute | solution.py:47
  99.4 11.8 %collective-permute-start.21 = (bf16[16,8192]{1,0:T(8,128)(2,1)S(1)}, bf16[16,8192]{1,0:T(8,128)(2,1)S(1)}, u32[]{:S(2)}, u32[]{:S(2)}) collective-permute-start(bf16[16,8192]{1,0:T(8,128)(2,1)S(1)} %get-tuple-element.43), channel_id=1, source_target_pairs={{0,64},{16,80},{32,96},{48,112},{64,0},{80,16},{96,32},{112,48},{1... | collective-permute-start | bytes 786440 | tf_op jit(solution)/shard_map/ppermute | solution.py:55
  99.8 11.9 %collective-permute-start.22 = (bf16[16,8192]{1,0:T(8,128)(2,1)S(1)}, bf16[16,8192]{1,0:T(8,128)(2,1)S(1)}, u32[]{:S(2)}, u32[]{:S(2)}) collective-permute-start(bf16[16,8192]{1,0:T(8,128)(2,1)S(1)} %get-tuple-element.44), channel_id=1, source_target_pairs={{0,48},{16,0},{32,16},{48,32},{64,112},{80,64},{96,80},{112,96},{1... | collective-permute-start | bytes 786440 | tf_op jit(solution)/shard_map/ppermute | solution.py:55
  102.6 9.3 %collective-permute-start.23 = (bf16[16,8192]{1,0:T(8,128)(2,1)S(1)}, bf16[16,8192]{1,0:T(8,128)(2,1)S(1)}, u32[]{:S(2)}, u32[]{:S(2)}) collective-permute-start(bf16[16,8192]{1,0:T(8,128)(2,1)S(1)} %get-tuple-element.42.refs_1_), channel_id=1, source_target_pairs={{0,16},{16,32},{32,48},{48,0},{64,80},{80,96},{96,112},{112,64},{1... | collective-permute-start | bytes 786440 | tf_op jit(solution)/shard_map/ppermute | solution.py:55
  102.6 5.8 %collective-permute-start.24 = (f32[16,256]{1,0:T(8,128)S(1)}, f32[16,256]{1,0:T(8,128)S(1)}, u32[]{:S(2)}, u32[]{:S(2)}) collective-permute-start(f32[16,256]{1,0:T(8,128)S(1)} %get-tuple-element.45), channel_id=1, source_target_pairs={{64,0},{80,16},{96,32},{112,48},{0,64},{16,80},{32,96},{48,112},{6... | collective-permute-start | bytes 49160 | tf_op jit(solution)/shard_map/ppermute | solution.py:51
  108.4 9.1 %collective-permute-start.27 = (f32[16,256]{1,0:T(8,128)S(1)}, f32[16,256]{1,0:T(8,128)S(1)}, u32[]{:S(2)}, u32[]{:S(2)}) collective-permute-start(f32[16,256]{1,0:T(8,128)S(1)} %add.89.refs_5_), channel_id=1, source_target_pairs={{32,0},{48,16},{0,32},{16,48},{96,64},{112,80},{64,96},{80,112},{3... | collective-permute-start | bytes 49160 | tf_op jit(solution)/shard_map/ppermute | solution.py:51
  111.3 21.0 %collective-permute-start.28 = (bf16[16,8192]{1,0:T(8,128)(2,1)S(1)}, bf16[16,8192]{1,0:T(8,128)(2,1)S(1)}, u32[]{:S(2)}, u32[]{:S(2)}) collective-permute-start(bf16[16,8192]{1,0:T(8,128)(2,1)S(1)} %get-tuple-element.48), channel_id=1, source_target_pairs={{0,96},{16,112},{32,64},{48,80},{64,32},{80,48},{96,0},{112,16},{1... | collective-permute-start | bytes 786440 | tf_op jit(solution)/shard_map/ppermute | solution.py:55
  112.2 20.1 %collective-permute-start.29 = (bf16[16,8192]{1,0:T(8,128)(2,1)S(1)}, bf16[16,8192]{1,0:T(8,128)(2,1)S(1)}, u32[]{:S(2)}, u32[]{:S(2)}) collective-permute-start(bf16[16,8192]{1,0:T(8,128)(2,1)S(1)} %get-tuple-element.49), channel_id=1, source_target_pairs={{0,16},{16,32},{32,48},{48,0},{64,80},{80,96},{96,112},{112,64},{1... | collective-permute-start | bytes 786440 | tf_op jit(solution)/shard_map/ppermute | solution.py:55
  113.6 18.6 %collective-permute-start.30 = (bf16[16,8192]{1,0:T(8,128)(2,1)S(1)}, bf16[16,8192]{1,0:T(8,128)(2,1)S(1)}, u32[]{:S(2)}, u32[]{:S(2)}) collective-permute-start(bf16[16,8192]{1,0:T(8,128)(2,1)S(1)} %get-tuple-element.50), channel_id=1, source_target_pairs={{0,64},{16,80},{32,96},{48,112},{64,0},{80,16},{96,32},{112,48},{1... | collective-permute-start | bytes 786440 | tf_op jit(solution)/shard_map/ppermute | solution.py:55
  115.4 16.9 %collective-permute-start.31 = (bf16[16,8192]{1,0:T(8,128)(2,1)S(1)}, bf16[16,8192]{1,0:T(8,128)(2,1)S(1)}, u32[]{:S(2)}, u32[]{:S(2)}) collective-permute-start(bf16[16,8192]{1,0:T(8,128)(2,1)S(1)} %get-tuple-element.46.before), channel_id=1, source_target_pairs={{0,48},{16,0},{32,16},{48,32},{64,112},{80,64},{96,80},{112,96},{1... | collective-permute-start | bytes 786440 | tf_op jit(solution)/shard_map/ppermute | solution.py:55
  117.4 9.2 %collective-permute-start.26 = (f32[16,256]{1,0:T(8,128)S(1)}, f32[16,256]{1,0:T(8,128)S(1)}, u32[]{:S(2)}, u32[]{:S(2)}) collective-permute-start(f32[16,256]{1,0:T(8,128)S(1)} %add.89.refs_5_), channel_id=1, source_target_pairs={{48,0},{0,16},{16,32},{32,48},{112,64},{64,80},{80,96},{96,112},{4... | collective-permute-start | bytes 49160 | tf_op jit(solution)/shard_map/ppermute | solution.py:51
  126.6 3.7 %collective-permute-start.25 = (f32[16,256]{1,0:T(8,128)S(1)}, f32[16,256]{1,0:T(8,128)S(1)}, u32[]{:S(2)}, u32[]{:S(2)}) collective-permute-start(f32[16,256]{1,0:T(8,128)S(1)} %add.89.refs_5_), channel_id=1, source_target_pairs={{16,0},{32,16},{48,32},{0,48},{80,64},{96,80},{112,96},{64,112},{1... | collective-permute-start | bytes 49160 | tf_op jit(solution)/shard_map/ppermute | solution.py:51
  (4 other events, 101.0 us)

commit v8 on v7

--- a/solution.py
+++ b/solution.py
@@ -112,6 +112,30 @@
     )(*arrays, *before)
 
 
+def bundle_kernel(up, across, down, corner, feats, cot, weight, token, up_out, across_out, out):
+    for i, a in enumerate((up, across, down, corner, feats, cot)):
+        out[:, LOCAL * i : LOCAL * (i + 1)] = a[...]
+    out[:, 6 * LOCAL :] = weight[...]
+
+
+def bundle(up, across, down, corner, feats, cot, weight, token):
+    wide = 6 * LOCAL + 256
+    return pl.pallas_call(
+        bundle_kernel,
+        out_shape=[
+            jax.ShapeDtypeStruct(up.shape, BF16),
+            jax.ShapeDtypeStruct(across.shape, BF16),
+            jax.ShapeDtypeStruct((HALF, wide), BF16),
+        ],
+        in_specs=[VMEM] * 7 + [ANY],
+        out_specs=[ANY, ANY, VMEM],
+        input_output_aliases={0: 0, 1: 1},
+        compiler_params=pltpu.CompilerParams(vmem_limit_bytes=8 << 20),
+        cost_estimate=pl.CostEstimate(flops=0, bytes_accessed=3 << 20, transcendentals=0),
+        name="bundle",
+    )(up, across, down, corner, feats, cot, weight, token)
+
+
 WIDE = 1280
 
 
@@ -165,28 +189,29 @@
     )(info, mine, received, before)
 
 
-def forward_kernel(info, cols, low_tiles, high_tiles, *refs):
-    pieces, sides, (out, feats, sems) = refs[:16], refs[16:20], refs[20:]
+def forward_kernel(places, info, cols, low_tiles, high_tiles, *refs):
+    own, others, cot, weight, (out, feats, sems) = refs[:8], refs[8:12], refs[12], refs[13], refs[14:]
     core = info[0]
+    mine = pl.ds(pl.multiple_of(HALF * core, HALF), HALF)
+    sibling = pl.ds(pl.multiple_of(HALF * (1 - core), HALF), HALF)
     copies = []
-    for i in range(SLABS):
-        at = pl.multiple_of(info[1 + i] * LOCAL, LOCAL)
-        for h in range(2):
-            rows = pl.ds(pl.multiple_of(jnp.where(core == h, 0, HALF), HALF), HALF)
-            copies.append(
-                pltpu.make_async_copy(
-                    pieces[2 * i + h], feats.at[rows, pl.ds(at, LOCAL)], sems.at[2 * i + h]
-                )
-            )
+    for i, (which, first) in enumerate(places):
+        at = pl.ds(pl.multiple_of(info[1 + i] * LOCAL, LOCAL), LOCAL)
+        other = others[which].at[:, pl.ds(first, LOCAL)]
+        copies += [
+            pltpu.make_async_copy(own[i], feats.at[mine, at], sems.at[2 * i]),
+            pltpu.make_async_copy(other, feats.at[sibling, at], sems.at[2 * i + 1]),
+        ]
     for c in copies:
         c.start()
-    for h in range(2):
-        rows = pl.ds(pl.multiple_of(jnp.where(core == h, 0, HALF), HALF), HALF)
-        cot, weight = sides[2 * h], sides[2 * h + 1]
-        for g in range(8):
-            nodes = pl.ds(pl.multiple_of(1024 * g + 512 * core, 512), 512)
-            out[g, rows, 512:1024] = cot[:, nodes]
-            out[g, rows, 1024:] = weight[...]
+    near = others[0]
+    for g in range(8):
+        at = 1024 * g + 512 * core
+        out[g, mine, 512:1024] = cot[:, pl.ds(pl.multiple_of(at, 512), 512)]
+        out[g, mine, 1024:] = weight[...]
+        at = 5 * LOCAL + at
+        out[g, sibling, 512:1024] = near[:, pl.ds(pl.multiple_of(at, 512), 512)]
+        out[g, sibling, 1024:] = near[:, 6 * LOCAL :]
     for c in copies:
         c.wait()
 
@@ -238,22 +263,28 @@
         lax.fori_loop(4 * half, 4 * half + 4, step, 0)
 
 
-def forward(info, cols, held, pieces, sides):
-    return pl.pallas_call(
-        forward_kernel,
+def forward(info, cols, held, pieces, cot, weight):
+    own = [p[0] for p in pieces]
+    others = []
+    for _, other, _ in pieces:
+        if not any(other is o for o in others):
+            others.append(other)
+    places = tuple((next(k for k, o in enumerate(others) if o is p[1]), p[2]) for p in pieces)
+    return pl.pallas_call(
+        functools.partial(forward_kernel, places),
         out_shape=jax.ShapeDtypeStruct((8, PAIR, WIDE), BF16),
-        in_specs=[SMEM, SMEM, VMEM, VMEM] + [ANY] * 16 + [VMEM] * 4,
+        in_specs=[SMEM, SMEM, VMEM, VMEM] + [ANY] * 8 + [VMEM] + [ANY] * 3 + [VMEM] * 2,
         out_specs=VMEM,
         scratch_shapes=[
             pltpu.VMEM((PAIR, NODES), BF16),
             pltpu.SemaphoreType.DMA((16,)),
         ],
-        compiler_params=pltpu.CompilerParams(vmem_limit_bytes=8 << 20),
+        compiler_params=pltpu.CompilerParams(vmem_limit_bytes=10 << 20),
         cost_estimate=pl.CostEstimate(
             flops=8 * 2 * 1024 * 128 * 128 * 32, bytes_accessed=8 << 20, transcendentals=0
         ),
         name="forward",
-    )(info, cols, *held, *pieces, *sides)
+    )(info, cols, *held, *own, *others, cot, weight)
 
 
 def dense_kernel(message, out):
@@ -377,27 +408,34 @@
 def far_kernel(own, other, wgrad, wgrad_other, *outs):
     for i, out in enumerate(outs[:4]):
         lanes = slice(LOCAL * i, LOCAL * (i + 1))
-        out[...] = (own[:, lanes].astype(F32) + other[:, lanes].astype(F32)).astype(BF16)
+        out[:, :LOCAL] = (own[:, lanes].astype(F32) + other[:, lanes].astype(F32)).astype(BF16)
+        out[:, LOCAL:] = (wgrad[...] + wgrad_other[...]).astype(BF16)
     outs[4][...] = wgrad[...] + wgrad_other[...]
 
 
-def near_kernel(own, other, from_across, from_up, from_down, up, across, down, base):
+def near_kernel(own, other, wgrad, from_across, from_up, from_down, up, across, down, base):
     def mine(i):
         lanes = slice(LOCAL * i, LOCAL * (i + 1))
         return own[:, lanes].astype(F32) + other[:, lanes].astype(F32)
 
-    up[...] = (mine(0) + from_across[...].astype(F32) + from_down[...].astype(F32)).astype(BF16)
-    across[...] = (mine(1) + from_up[...].astype(F32)).astype(BF16)
-    down[...] = mine(2).astype(BF16)
-    base[...] = mine(3)
+    for i, (out, received) in enumerate(
+        ((up, (from_across, from_down)), (across, (from_up,)), (down, ()), (base, ()))
+    ):
+        piece, terms = mine(i), wgrad[...]
+        for r in received:
+            piece += r[:, :LOCAL].astype(F32)
+            terms += r[:, LOCAL:].astype(F32)
+        out[:, :LOCAL] = piece.astype(out.dtype)
+        out[:, LOCAL:] = terms.astype(out.dtype)
 
 
 def last_kernel(base, *refs):
-    *received, out = refs
+    *received, feats_grad, weight_grad = refs
     total = base[...]
     for a in received:
         total += a[...].astype(F32)
-    out[...] = total.astype(BF16)
+    feats_grad[...] = total[:, :LOCAL].astype(BF16)
+    weight_grad[...] = total[:, LOCAL:]
 
 
 def per_device(node_feats, weight, tiles, block_cols, cotangent):
@@ -409,51 +447,55 @@
 
     up, down, across, corner = (receive(node_feats, s) for s in (UP, DOWN, ACROSS, CORNER))
     held, token = load_tiles(info, tiles)
-    feats_swapped, cot_swapped = swap(node_feats), swap(cotangent)
-    up, down, across, corner = gate(
-        (up, down, across, corner), (token, feats_swapped, cot_swapped)
-    )
+    up, across, near = bundle(up, across, down, corner, node_feats, cotangent, weight, token)
     far = receive(up, UP)
     across_up = receive(up, ACROSS)
     across_down = receive(across, DOWN)
-    pieces = [node_feats, feats_swapped]
-    for block in (up, down, across, far, across_up, across_down, corner):
-        pieces += [block, swap(block)]
-    sides = [cotangent, weight, cot_swapped, swap(weight)]
-
-    message = forward(info, cols, held, pieces, sides)
+    near = swap(near)
+    pieces = [
+        (node_feats, near, 4 * LOCAL),
+        (up, near, 0),
+        (down, near, 2 * LOCAL),
+        (across, near, LOCAL),
+        (far, swap(far), 0),
+        (across_up, swap(across_up), 0),
+        (across_down, swap(across_down), 0),
+        (corner, near, 3 * LOCAL),
+    ]
+    message = forward(info, cols, held, pieces, cotangent, weight)
     message = lax.all_to_all(message, "feat", 0, 0, axis_index_groups=SAME_CORE, tiled=True)
     message = dense(message.reshape(256, WIDE)).reshape(8, PAIR, WIDE)
     message = lax.all_to_all(message, "feat", 0, 0, axis_index_groups=SAME_CORE, tiled=True)
 
     own_a, own_c, other_a, other_c = backward(info, cols, tiles, message)
-    whole = ((HALF, LOCAL), BF16)
+    piece = ((HALF, LOCAL + 256), BF16)
     hidden, hidden_other, wgrad, wgrad_other = unpack(info, message, own_a)
-    hidden_other, wgrad_other = swap(hidden_other), swap(wgrad_other)
+    hidden_other = swap(hidden_other)
     across_up, across_down, far, corner, wgrad = sum_call(
         far_kernel,
-        [whole] * 4 + [((HALF, 256), F32)],
-        (own_a, swap(other_a), wgrad, wgrad_other),
+        [piece] * 4 + [((HALF, 256), F32)],
+        (own_a, swap(other_a), wgrad, swap(wgrad_other)),
         "sum_far",
-        (hidden_other,),
     )
     from_across = send(across_up, ACROSS)
     from_up = send(across_down, DOWN)
     from_down = send(far, UP)
     from_corner = send(corner, CORNER)
     (other_c,) = gate((other_c,), (far,))
-    wgrad = wgrad + receive(wgrad, ACROSS)
     up, across, down, base = sum_call(
         near_kernel,
-        [whole] * 3 + [((HALF, LOCAL), F32)],
-        (own_c, swap(other_c), from_across, from_up, from_down),
+        [piece] * 3 + [((HALF, LOCAL + 256), F32)],
+        (own_c, swap(other_c), wgrad, from_across, from_up, from_down),
         "sum_near",
-        (wgrad,),
     )
+    hidden = join(info, hidden, hidden_other, down)
     last = [send(up, UP), send(across, ACROSS), send(down, DOWN)]
-    weight_grad = wgrad + receive(wgrad, UP) + receive(wgrad, DOWN) + receive(wgrad, (0, 2))
-    hidden = join(info, hidden, hidden_other, down)
-    (feats_grad,) = sum_call(last_kernel, [whole], (base, from_corner, *last), "sum_last")
+    feats_grad, weight_grad = sum_call(
+        last_kernel,
+        [((HALF, LOCAL), BF16), ((HALF, 256), F32)],
+        (base, from_corner, *last),
+        "sum_last",
+    )
     return hidden, weight_grad, feats_grad
 
 

time: 133 us -> 128 us (0.962); the launches traced: 133 us -> 127 us
  starting transfers between devices: 29.2 us -> 23.3 us
  waiting for transfers between devices: 26.9 us -> 25 us
  Pallas kernels: 39.9 us -> 41.7 us
    ppermute x11 -> x7, waiting for transfers between devices: 23.5 us -> 6.1 us  [receive(): return lax.ppermute(a, 'blk', _from_step(step))]
    ppermute x7, waiting for transfers between devices: 0.16 us -> 14.5 us  [send(): return lax.ppermute(a, 'blk', _to_step(step))]
    ppermute x11 -> x7, starting transfers between devices: 17.7 us -> 12.2 us  [receive(): return lax.ppermute(a, 'blk', _from_step(step))]
    pallas_call x1 -> x2, Pallas kernels: 12.1 us -> 13.9 us  [the longest x1 12.8 us: forward(): pl.pallas_call(functools.partial(forward_kernel, places), out_shape=jax.S...]
    ppermute x14 -> x8, starting transfers between devices: 2.74 us -> 1.48 us  [swap(): return lax.ppermute(a, 'feat', CORE_SWAP)]
    ppermute x14 -> x8, waiting for transfers between devices: 3.15 us -> 4.39 us  [swap(): return lax.ppermute(a, 'feat', CORE_SWAP)]
  transfers between devices with their start and end apart: 32 -> 22, of which waited for: 11 -> 12; matrix products, arithmetic and copies ran while one was open for 1% -> 0% of each run, Pallas kernels for 10% -> 11%
where the time goes in v8:
time: 128 us; the launch traced here: 127 us
  Pallas kernels  41.7 us (33%)
  blocking collectives  35.9 us (28%)
  waiting for transfers between devices  25 us (20%)
  starting transfers between devices  23.3 us (18%)
    all_to_all x2, blocking collectives, per_device(): lax.all_to_all(message, 'feat', 0, 0, axis_index_groups=SAME_CORE, tiled=...  35.9 us
    ppermute x7, waiting for transfers between devices, send(): return lax.ppermute(a, 'blk', _to_step(step))  14.5 us
    pallas_call x1, Pallas kernels, forward(): pl.pallas_call(functools.partial(forward_kernel, places), out_shape=jax.S...  12.8 us
    pallas_call x1, Pallas kernels, backward(): pl.pallas_call(backward_kernel, out_shape=[jax.ShapeDtypeStruct((HALF, LO...  12.6 us
    ppermute x7, starting transfers between devices, receive(): return lax.ppermute(a, 'blk', _from_step(step))  12.2 us
    pallas_call x1, Pallas kernels, load_tiles(): pl.pallas_call(load_kernel, out_shape=(pltpu.VMEM((ROWS // 2, SLOTS, 128,...  11.3 us
    ppermute x7, starting transfers between devices, send(): return lax.ppermute(a, 'blk', _to_step(step))  9.55 us
    ppermute x7, waiting for transfers between devices, receive(): return lax.ppermute(a, 'blk', _from_step(step))  6.1 us
  transfers between devices with their start and end apart: 22, of which 12 were waited for; matrix products, arithmetic and copies ran while one was open for 0% of the time, Pallas kernels for 11%

profile of v8, /device:TPU:0, one launch (start us, length us, event | category | flops | bytes accessed | tf_op | source)
XLA Modules:
  0.0 126.7 jit_solution(1873605395636586631)
XLA Ops:
  0.6 1.7 %collective-permute-start.2 = (bf16[16,8192]{1,0:T(8,128)(2,1)}, bf16[16,8192]{1,0:T(8,128)(2,1)S(1)}, u32[]{:S(2)}, u32[]{:S(2)}) collective-permute-start(bf16[16,8192]{1,0:T(8,128)(2,1)} %refs_0_.1), channel_id=1, source_target_pairs={{48,0},{0,16},{16,32},{32,48},{112,64},{64,80},{80,96},{96,112},{4... | collective-permute-start | bytes 786440 | tf_op jit(solution)/shard_map/ppermute | solution.py:51
  2.4 3.8 %collective-permute-start.3 = (bf16[16,8192]{1,0:T(8,128)(2,1)}, bf16[16,8192]{1,0:T(8,128)(2,1)S(1)}, u32[]{:S(2)}, u32[]{:S(2)}) collective-permute-start(bf16[16,8192]{1,0:T(8,128)(2,1)} %refs_0_.1), channel_id=1, source_target_pairs={{96,0},{112,16},{64,32},{80,48},{32,64},{48,80},{0,96},{16,112},{9... | collective-permute-start | bytes 786440 | tf_op jit(solution)/shard_map/ppermute | solution.py:51
  6.2 1.3 %collective-permute-start = (bf16[16,8192]{1,0:T(8,128)(2,1)}, bf16[16,8192]{1,0:T(8,128)(2,1)S(1)}, u32[]{:S(2)}, u32[]{:S(2)}) collective-permute-start(bf16[16,8192]{1,0:T(8,128)(2,1)} %refs_0_.1), channel_id=1, source_target_pairs={{16,0},{32,16},{48,32},{0,48},{80,64},{96,80},{112,96},{64,112},{1... | collective-permute-start | bytes 786440 | tf_op jit(solution)/shard_map/ppermute | solution.py:51
  7.5 0.5 collective-permute-start.1
  8.2 11.3 %load_tiles.1 = (bf16[16,32,128,128]{3,2,1,0:T(8,128)(2,1)S(1)}, bf16[16,32,128,128]{3,2,1,0:T(8,128)(2,1)S(1)}, f32[8,128]{1,0:T(8,128)S(1)}) custom-call(s32[9]{0:T(128)S(1)} %stack.39.info, bf16[64,32,128,128]{3,2,1,0:T(8,128)(2,1)} %tiles.3), custom_call_target="tpu_custom_call" | custom-call | bytes 50331648 | tf_op jit(solution)/shard_map/load_tiles/pallas_call | solution.py:84
  19.5 1.1 bundle.1
  20.7 0.7 collective-permute-start.6
  21.4 2.6 %collective-permute-start.4 = (bf16[16,8192]{1,0:T(8,128)(2,1)S(1)}, bf16[16,8192]{1,0:T(8,128)(2,1)S(1)}, u32[]{:S(2)}, u32[]{:S(2)}) collective-permute-start(bf16[16,8192]{1,0:T(8,128)(2,1)S(1)} %get-tuple-element.31.refs_1_), channel_id=1, source_target_pairs={{16,0},{32,16},{48,32},{0,48},{80,64},{96,80},{112,96},{64,112},{1... | collective-permute-start | bytes 786440 | tf_op jit(solution)/shard_map/ppermute | solution.py:51
  24.0 1.5 %collective-permute-start.5 = (bf16[16,8192]{1,0:T(8,128)(2,1)S(1)}, bf16[16,8192]{1,0:T(8,128)(2,1)S(1)}, u32[]{:S(2)}, u32[]{:S(2)}) collective-permute-start(bf16[16,8192]{1,0:T(8,128)(2,1)S(1)} %get-tuple-element.31.refs_1_), channel_id=1, source_target_pairs={{64,0},{80,16},{96,32},{112,48},{0,64},{16,80},{32,96},{48,112},{6... | collective-permute-start | bytes 786440 | tf_op jit(solution)/shard_map/ppermute | solution.py:51
  25.5 5.3 %collective-permute-done.6.refs_6_ = bf16[16,8192]{1,0:T(8,128)(2,1)S(1)} collective-permute-done((bf16[16,8192]{1,0:T(8,128)(2,1)}, bf16[16,8192]{1,0:T(8,128)(2,1)S(1)}, u32[]{:S(2)}, u32[]{:S(2)}) %collective-permute-start.6) | collective-permute-done | bytes 262176 | tf_op jit(solution)/shard_map/ppermute | solution.py:51
  31.3 0.7 collective-permute-done.5.refs_5_
  32.7 0.9 collective-permute-done.9.refs_10_
  33.6 12.8 %forward.1 = bf16[8,32,1280]{2,1,0:T(8,128)(2,1)S(1)} custom-call(s32[9]{0:T(128)S(1)} %stack.39.info, s32[32,64]{1,0:T(8,128)S(1)} %bitcast.14, bf16[16,32,128,128]{3,2,1,0:T(8,128)(2,1)S(1)} %get-tuple-element.28.low_tiles, bf16[16,32,128,128]{3,2,1,0:T(8,128)(2,1)S(1)} %get-tuple-element.29.high_tiles, bf16[16,8192]{1,0:T(8,128)(2,1)S(1)} %copy-done, ...), custom_call_target="tpu_custom_call" | custom-call | flops 8589934592 | bytes 8388608 | tf_op jit(solution)/shard_map/forward/pallas_call | solution.py:273
  46.5 20.9 %all_to_all.10 = bf16[8,32,1280]{2,1,0:T(8,128)(2,1)S(1)} all-to-all(bf16[8,32,1280]{2,1,0:T(8,128)(2,1)S(1)} %forward.1), channel_id=1, replica_groups={{0,2,4,6,8,10,12,14},{1,3,5,7,9,11,13,15},{16,18,20,22,24,26,28,30},{17..., dimensions={0} | all-to-all | bytes 1310720 | tf_op jit(solution)/shard_map/all_to_all | solution.py:466
  67.4 0.6 dense.1
  68.0 15.0 %all_to_all.11.grad.message = bf16[8,32,1280]{2,1,0:T(8,128)(2,1)S(1)} all-to-all(bf16[8,32,1280]{2,1,0:T(8,128)(2,1)S(1)} %bitcast.13), channel_id=1, replica_groups={{0,2,4,6,8,10,12,14},{1,3,5,7,9,11,13,15},{16,18,20,22,24,26,28,30},{17..., dimensions={0} | all-to-all | bytes 1310720 | tf_op jit(solution)/shard_map/all_to_all | solution.py:468
  83.0 12.6 %backward.1 = (bf16[16,32768]{1,0:T(8,128)(2,1)S(1)}, bf16[16,32768]{1,0:T(8,128)(2,1)S(1)}, bf16[16,32768]{1,0:T(8,128)(2,1)S(1)}, bf16[16,32768]{1,0:T(8,128)(2,1)S(1)}) custom-call(s32[9]{0:T(128)S(1)} %stack.39.info, s32[32,64]{1,0:T(8,128)S(1)} %bitcast.15, bf16[64,32,128,128]{3,2,1,0:T(8,128)(2,1)} %tiles.3, ...), custom_call_target="tpu_custom_call" | custom-call | flops 8589934592 | bytes 8388608 | tf_op jit(solution)/shard_map/backward/pallas_call | solution.py:375
  95.7 0.6 unpack.1
  96.3 0.6 collective-permute-start.13
  96.9 1.5 %collective-permute-done.13.refs_3_ = f32[16,256]{1,0:T(8,128)S(1)} collective-permute-done((f32[16,256]{1,0:T(8,128)S(1)}, f32[16,256]{1,0:T(8,128)S(1)}, u32[]{:S(2)}, u32[]{:S(2)}) %collective-permute-start.13) | collective-permute-done | bytes 16416 | tf_op jit(solution)/shard_map/ppermute | solution.py:47
  98.9 0.6 collective-permute-start.15
  99.5 1.8 %collective-permute-start.16 = (bf16[16,8448]{1,0:T(8,128)(2,1)S(1)}, bf16[16,8448]{1,0:T(8,128)(2,1)S(1)}, u32[]{:S(2)}, u32[]{:S(2)}) collective-permute-start(bf16[16,8448]{1,0:T(8,128)(2,1)S(1)} %get-tuple-element.45), channel_id=1, source_target_pairs={{0,48},{16,0},{32,16},{48,32},{64,112},{80,64},{96,80},{112,96},{1... | collective-permute-start | bytes 811016 | tf_op jit(solution)/shard_map/ppermute | solution.py:55
  101.5 2.2 %collective-permute-start.18 = (bf16[16,8448]{1,0:T(8,128)(2,1)S(1)}, bf16[16,8448]{1,0:T(8,128)(2,1)S(1)}, u32[]{:S(2)}, u32[]{:S(2)}) collective-permute-start(bf16[16,8448]{1,0:T(8,128)(2,1)S(1)} %get-tuple-element.48), channel_id=1, source_target_pairs={{0,96},{16,112},{32,64},{48,80},{64,32},{80,48},{96,0},{112,16},{1... | collective-permute-start | bytes 811016 | tf_op jit(solution)/shard_map/ppermute | solution.py:55
  103.7 4.5 %collective-permute-done.15.refs_3_ = bf16[16,8448]{1,0:T(8,128)(2,1)S(1)} collective-permute-done((bf16[16,8448]{1,0:T(8,128)(2,1)S(1)}, bf16[16,8448]{1,0:T(8,128)(2,1)S(1)}, u32[]{:S(2)}, u32[]{:S(2)}) %collective-permute-start.15) | collective-permute-done | bytes 270368 | tf_op jit(solution)/shard_map/ppermute | solution.py:55
  108.2 5.5 %collective-permute-done.16.refs_4_ = bf16[16,8448]{1,0:T(8,128)(2,1)S(1)} collective-permute-done((bf16[16,8448]{1,0:T(8,128)(2,1)S(1)}, bf16[16,8448]{1,0:T(8,128)(2,1)S(1)}, u32[]{:S(2)}, u32[]{:S(2)}) %collective-permute-start.16) | collective-permute-done | bytes 270368 | tf_op jit(solution)/shard_map/ppermute | solution.py:55
  113.7 2.8 %collective-permute-done.17.refs_5_ = bf16[16,8448]{1,0:T(8,128)(2,1)S(1)} collective-permute-done((bf16[16,8448]{1,0:T(8,128)(2,1)S(1)}, bf16[16,8448]{1,0:T(8,128)(2,1)S(1)}, u32[]{:S(2)}, u32[]{:S(2)}) %collective-permute-start.17) | collective-permute-done | bytes 270368 | tf_op jit(solution)/shard_map/ppermute | solution.py:55
  116.9 1.5 %collective-permute-start.20 = (bf16[16,8448]{1,0:T(8,128)(2,1)S(1)}, bf16[16,8448]{1,0:T(8,128)(2,1)S(1)}, u32[]{:S(2)}, u32[]{:S(2)}) collective-permute-start(bf16[16,8448]{1,0:T(8,128)(2,1)S(1)} %get-tuple-element.50), channel_id=1, source_target_pairs={{0,64},{16,80},{32,96},{48,112},{64,0},{80,16},{96,32},{112,48},{1... | collective-permute-start | bytes 811016 | tf_op jit(solution)/shard_map/ppermute | solution.py:55
  118.5 3.1 %collective-permute-start.21 = (bf16[16,8448]{1,0:T(8,128)(2,1)S(1)}, bf16[16,8448]{1,0:T(8,128)(2,1)S(1)}, u32[]{:S(2)}, u32[]{:S(2)}) collective-permute-start(bf16[16,8448]{1,0:T(8,128)(2,1)S(1)} %get-tuple-element.46.before), channel_id=1, source_target_pairs={{0,48},{16,0},{32,16},{48,32},{64,112},{80,64},{96,80},{112,96},{1... | collective-permute-start | bytes 811016 | tf_op jit(solution)/shard_map/ppermute | solution.py:55
  121.6 1.3 %collective-permute-done.11.received = bf16[16,4096]{1,0:T(8,128)(2,1)S(1)} collective-permute-done((bf16[16,4096]{1,0:T(8,128)(2,1)S(1)}, bf16[16,4096]{1,0:T(8,128)(2,1)S(1)}, u32[]{:S(2)}, u32[]{:S(2)}) %collective-permute-start.11) | collective-permute-done | bytes 131104 | tf_op jit(solution)/shard_map/ppermute | solution.py:47
  123.0 1.3 join.1
  124.2 1.2 collective-permute-done.19.refs_2_
  125.9 0.9 sum_last.1
  (34 shorter events, 3.0 us)
Async XLA Ops:
  0.6 18.8 %collective-permute-start.2 = (bf16[16,8192]{1,0:T(8,128)(2,1)}, bf16[16,8192]{1,0:T(8,128)(2,1)S(1)}, u32[]{:S(2)}, u32[]{:S(2)}) collective-permute-start(bf16[16,8192]{1,0:T(8,128)(2,1)} %refs_0_.1), channel_id=1, source_target_pairs={{48,0},{0,16},{16,32},{32,48},{112,64},{64,80},{80,96},{96,112},{4... | collective-permute-start | bytes 786440 | tf_op jit(solution)/shard_map/ppermute | solution.py:51
  2.4 17.1 %collective-permute-start.3 = (bf16[16,8192]{1,0:T(8,128)(2,1)}, bf16[16,8192]{1,0:T(8,128)(2,1)S(1)}, u32[]{:S(2)}, u32[]{:S(2)}) collective-permute-start(bf16[16,8192]{1,0:T(8,128)(2,1)} %refs_0_.1), channel_id=1, source_target_pairs={{96,0},{112,16},{64,32},{80,48},{32,64},{48,80},{0,96},{16,112},{9... | collective-permute-start | bytes 786440 | tf_op jit(solution)/shard_map/ppermute | solution.py:51
  6.2 13.3 %collective-permute-start = (bf16[16,8192]{1,0:T(8,128)(2,1)}, bf16[16,8192]{1,0:T(8,128)(2,1)S(1)}, u32[]{:S(2)}, u32[]{:S(2)}) collective-permute-start(bf16[16,8192]{1,0:T(8,128)(2,1)} %refs_0_.1), channel_id=1, source_target_pairs={{16,0},{32,16},{48,32},{0,48},{80,64},{96,80},{112,96},{64,112},{1... | collective-permute-start | bytes 786440 | tf_op jit(solution)/shard_map/ppermute | solution.py:51
  7.5 12.0 %collective-permute-start.1 = (bf16[16,8192]{1,0:T(8,128)(2,1)}, bf16[16,8192]{1,0:T(8,128)(2,1)}, u32[]{:S(2)}, u32[]{:S(2)}) collective-permute-start(bf16[16,8192]{1,0:T(8,128)(2,1)} %refs_0_.1), channel_id=1, source_target_pairs={{64,0},{80,16},{96,32},{112,48},{0,64},{16,80},{32,96},{48,112},{6... | collective-permute-start | bytes 786440 | tf_op jit(solution)/shard_map/ppermute | solution.py:51
  8.2 11.3 %copy-start = (bf16[16,8192]{1,0:T(8,128)(2,1)S(1)}, bf16[16,8192]{1,0:T(8,128)(2,1)}, u32[]{:S(2)}) copy-start(bf16[16,8192]{1,0:T(8,128)(2,1)} %refs_0_.1) | copy-start | bytes 786436
  8.2 11.4 %copy-start.1 = (bf16[16,8192]{1,0:T(8,128)(2,1)S(1)}, bf16[16,8192]{1,0:T(8,128)(2,1)}, u32[]{:S(2)}) copy-start(bf16[16,8192]{1,0:T(8,128)(2,1)} %refs_12_.1) | copy-start | bytes 786436
  8.2 11.4 %copy-start.3 = (bf16[16,256]{1,0:T(8,128)(2,1)S(1)}, bf16[16,256]{1,0:T(8,128)(2,1)}, u32[]{:S(2)}) copy-start(bf16[16,256]{1,0:T(8,128)(2,1)} %refs_13_.1) | copy-start | bytes 24580
  8.2 25.4 %copy-start.2 = (s32[64,32]{0,1:T(8,128)S(1)}, s32[64,32]{0,1:T(8,128)}, u32[]{:S(2)}) copy-start(s32[64,32]{0,1:T(8,128)} %param.8) | copy-start | bytes 24580
  20.6 13.0 %collective-permute-start.7 = (bf16[16,49408]{1,0:T(8,128)(2,1)S(1)}, bf16[16,49408]{1,0:T(8,128)(2,1)S(1)}, u32[]{:S(2)}, u32[]{:S(2)}) collective-permute-start(bf16[16,49408]{1,0:T(8,128)(2,1)S(1)} %get-tuple-element.33), channel_id=1, source_target_pairs={{0,1},{1,0},{2,3},{3,2},{4,5},{5,4},{6,7},{7,6},{8,9},{9,8},{10,11... | collective-permute-start | bytes 4743176 | tf_op jit(solution)/shard_map/ppermute | solution.py:47
  20.7 10.1 %collective-permute-start.6 = (bf16[16,8192]{1,0:T(8,128)(2,1)}, bf16[16,8192]{1,0:T(8,128)(2,1)S(1)}, u32[]{:S(2)}, u32[]{:S(2)}) collective-permute-start(bf16[16,8192]{1,0:T(8,128)(2,1)} %get-tuple-element.32.refs_3_), channel_id=1, source_target_pairs={{48,0},{0,16},{16,32},{32,48},{112,64},{64,80},{80,96},{96,112},{4... | collective-permute-start | bytes 786440 | tf_op jit(solution)/shard_map/ppermute | solution.py:51
  21.4 9.4 %collective-permute-start.4 = (bf16[16,8192]{1,0:T(8,128)(2,1)S(1)}, bf16[16,8192]{1,0:T(8,128)(2,1)S(1)}, u32[]{:S(2)}, u32[]{:S(2)}) collective-permute-start(bf16[16,8192]{1,0:T(8,128)(2,1)S(1)} %get-tuple-element.31.refs_1_), channel_id=1, source_target_pairs={{16,0},{32,16},{48,32},{0,48},{80,64},{96,80},{112,96},{64,112},{1... | collective-permute-start | bytes 786440 | tf_op jit(solution)/shard_map/ppermute | solution.py:51
  24.0 8.1 %collective-permute-start.5 = (bf16[16,8192]{1,0:T(8,128)(2,1)S(1)}, bf16[16,8192]{1,0:T(8,128)(2,1)S(1)}, u32[]{:S(2)}, u32[]{:S(2)}) collective-permute-start(bf16[16,8192]{1,0:T(8,128)(2,1)S(1)} %get-tuple-element.31.refs_1_), channel_id=1, source_target_pairs={{64,0},{80,16},{96,32},{112,48},{0,64},{16,80},{32,96},{48,112},{6... | collective-permute-start | bytes 786440 | tf_op jit(solution)/shard_map/ppermute | solution.py:51
  30.8 1.5 %collective-permute-start.10 = (bf16[16,8192]{1,0:T(8,128)(2,1)S(1)}, bf16[16,8192]{1,0:T(8,128)(2,1)S(1)}, u32[]{:S(2)}, u32[]{:S(2)}) collective-permute-start(bf16[16,8192]{1,0:T(8,128)(2,1)S(1)} %collective-permute-done.6.refs_6_), channel_id=1, source_target_pairs={{0,1},{1,0},{2,3},{3,2},{4,5},{5,4},{6,7},{7,6},{8,9},{9,8},{10,11... | collective-permute-start | bytes 786440 | tf_op jit(solution)/shard_map/ppermute | solution.py:47
  30.8 1.9 %collective-permute-start.8 = (bf16[16,8192]{1,0:T(8,128)(2,1)S(1)}, bf16[16,8192]{1,0:T(8,128)(2,1)S(1)}, u32[]{:S(2)}, u32[]{:S(2)}) collective-permute-start(bf16[16,8192]{1,0:T(8,128)(2,1)S(1)} %collective-permute-done.4.refs_4_), channel_id=1, source_target_pairs={{0,1},{1,0},{2,3},{3,2},{4,5},{5,4},{6,7},{7,6},{8,9},{9,8},{10,11... | collective-permute-start | bytes 786440 | tf_op jit(solution)/shard_map/ppermute | solution.py:47
  32.1 1.5 %collective-permute-start.9 = (bf16[16,8192]{1,0:T(8,128)(2,1)S(1)}, bf16[16,8192]{1,0:T(8,128)(2,1)S(1)}, u32[]{:S(2)}, u32[]{:S(2)}) collective-permute-start(bf16[16,8192]{1,0:T(8,128)(2,1)S(1)} %collective-permute-done.5.refs_5_), channel_id=1, source_target_pairs={{0,1},{1,0},{2,3},{3,2},{4,5},{5,4},{6,7},{7,6},{8,9},{9,8},{10,11... | collective-permute-start | bytes 786440 | tf_op jit(solution)/shard_map/ppermute | solution.py:47
  95.6 2.8 %collective-permute-start.12 = (bf16[16,32768]{1,0:T(8,128)(2,1)S(1)}, bf16[16,32768]{1,0:T(8,128)(2,1)S(1)}, u32[]{:S(2)}, u32[]{:S(2)}) collective-permute-start(bf16[16,32768]{1,0:T(8,128)(2,1)S(1)} %get-tuple-element.39), channel_id=1, source_target_pairs={{0,1},{1,0},{2,3},{3,2},{4,5},{5,4},{6,7},{7,6},{8,9},{9,8},{10,11... | collective-permute-start | bytes 3145736 | tf_op jit(solution)/shard_map/ppermute | solution.py:47
  96.3 2.1 %collective-permute-start.13 = (f32[16,256]{1,0:T(8,128)S(1)}, f32[16,256]{1,0:T(8,128)S(1)}, u32[]{:S(2)}, u32[]{:S(2)}) collective-permute-start(f32[16,256]{1,0:T(8,128)S(1)} %get-tuple-element.41), channel_id=1, source_target_pairs={{0,1},{1,0},{2,3},{3,2},{4,5},{5,4},{6,7},{7,6},{8,9},{9,8},{10,11... | collective-permute-start | bytes 49160 | tf_op jit(solution)/shard_map/ppermute | solution.py:47
  98.7 17.8 %collective-permute-start.14 = (bf16[16,32768]{1,0:T(8,128)(2,1)S(1)}, bf16[16,32768]{1,0:T(8,128)(2,1)S(1)}, u32[]{:S(2)}, u32[]{:S(2)}) collective-permute-start(bf16[16,32768]{1,0:T(8,128)(2,1)S(1)} %gate.1), channel_id=1, source_target_pairs={{0,1},{1,0},{2,3},{3,2},{4,5},{5,4},{6,7},{7,6},{8,9},{9,8},{10,11... | collective-permute-start | bytes 3145736 | tf_op jit(solution)/shard_map/ppermute | solution.py:47
  98.9 9.3 %collective-permute-start.15 = (bf16[16,8448]{1,0:T(8,128)(2,1)S(1)}, bf16[16,8448]{1,0:T(8,128)(2,1)S(1)}, u32[]{:S(2)}, u32[]{:S(2)}) collective-permute-start(bf16[16,8448]{1,0:T(8,128)(2,1)S(1)} %get-tuple-element.44), channel_id=1, source_target_pairs={{0,64},{16,80},{32,96},{48,112},{64,0},{80,16},{96,32},{112,48},{1... | collective-permute-start | bytes 811016 | tf_op jit(solution)/shard_map/ppermute | solution.py:55
  99.5 14.3 %collective-permute-start.16 = (bf16[16,8448]{1,0:T(8,128)(2,1)S(1)}, bf16[16,8448]{1,0:T(8,128)(2,1)S(1)}, u32[]{:S(2)}, u32[]{:S(2)}) collective-permute-start(bf16[16,8448]{1,0:T(8,128)(2,1)S(1)} %get-tuple-element.45), channel_id=1, source_target_pairs={{0,48},{16,0},{32,16},{48,32},{64,112},{80,64},{96,80},{112,96},{1... | collective-permute-start | bytes 811016 | tf_op jit(solution)/shard_map/ppermute | solution.py:55
  101.3 15.2 %collective-permute-start.17 = (bf16[16,8448]{1,0:T(8,128)(2,1)S(1)}, bf16[16,8448]{1,0:T(8,128)(2,1)S(1)}, u32[]{:S(2)}, u32[]{:S(2)}) collective-permute-start(bf16[16,8448]{1,0:T(8,128)(2,1)S(1)} %get-tuple-element.42.refs_1_), channel_id=1, source_target_pairs={{0,16},{16,32},{32,48},{48,0},{64,80},{80,96},{96,112},{112,64},{1... | collective-permute-start | bytes 811016 | tf_op jit(solution)/shard_map/ppermute | solution.py:55
  101.5 22.7 %collective-permute-start.18 = (bf16[16,8448]{1,0:T(8,128)(2,1)S(1)}, bf16[16,8448]{1,0:T(8,128)(2,1)S(1)}, u32[]{:S(2)}, u32[]{:S(2)}) collective-permute-start(bf16[16,8448]{1,0:T(8,128)(2,1)S(1)} %get-tuple-element.48), channel_id=1, source_target_pairs={{0,96},{16,112},{32,64},{48,80},{64,32},{80,48},{96,0},{112,16},{1... | collective-permute-start | bytes 811016 | tf_op jit(solution)/shard_map/ppermute | solution.py:55
  116.8 8.6 %collective-permute-start.19 = (bf16[16,8448]{1,0:T(8,128)(2,1)S(1)}, bf16[16,8448]{1,0:T(8,128)(2,1)S(1)}, u32[]{:S(2)}, u32[]{:S(2)}) collective-permute-start(bf16[16,8448]{1,0:T(8,128)(2,1)S(1)} %get-tuple-element.49), channel_id=1, source_target_pairs={{0,16},{16,32},{32,48},{48,0},{64,80},{80,96},{96,112},{112,64},{1... | collective-permute-start | bytes 811016 | tf_op jit(solution)/shard_map/ppermute | solution.py:55
  116.9 8.5 %collective-permute-start.20 = (bf16[16,8448]{1,0:T(8,128)(2,1)S(1)}, bf16[16,8448]{1,0:T(8,128)(2,1)S(1)}, u32[]{:S(2)}, u32[]{:S(2)}) collective-permute-start(bf16[16,8448]{1,0:T(8,128)(2,1)S(1)} %get-tuple-element.50), channel_id=1, source_target_pairs={{0,64},{16,80},{32,96},{48,112},{64,0},{80,16},{96,32},{112,48},{1... | collective-permute-start | bytes 811016 | tf_op jit(solution)/shard_map/ppermute | solution.py:55
  118.5 7.4 %collective-permute-start.21 = (bf16[16,8448]{1,0:T(8,128)(2,1)S(1)}, bf16[16,8448]{1,0:T(8,128)(2,1)S(1)}, u32[]{:S(2)}, u32[]{:S(2)}) collective-permute-start(bf16[16,8448]{1,0:T(8,128)(2,1)S(1)} %get-tuple-element.46.before), channel_id=1, source_target_pairs={{0,48},{16,0},{32,16},{48,32},{64,112},{80,64},{96,80},{112,96},{1... | collective-permute-start | bytes 811016 | tf_op jit(solution)/shard_map/ppermute | solution.py:55
  121.6 1.3 %collective-permute-start.11 = (bf16[16,4096]{1,0:T(8,128)(2,1)S(1)}, bf16[16,4096]{1,0:T(8,128)(2,1)S(1)}, u32[]{:S(2)}, u32[]{:S(2)}) collective-permute-start(bf16[16,4096]{1,0:T(8,128)(2,1)S(1)} %get-tuple-element.36), channel_id=1, source_target_pairs={{0,1},{1,0},{2,3},{3,2},{4,5},{5,4},{6,7},{7,6},{8,9},{9,8},{10,11... | collective-permute-start | bytes 393224 | tf_op jit(solution)/shard_map/ppermute | solution.py:47

commit v9 on v8

--- a/solution.py
+++ b/solution.py
@@ -23,7 +23,6 @@
 NODES = 65536
 SLOTS = 32
 ROWS = 32
-RING = 16
 
 
 def _index(x, y):
@@ -63,14 +62,13 @@
     return pl.ds(pl.multiple_of(block * 128, 128), 128)
 
 
-def load_kernel(info, tiles, low, high, token, sems):
+def load_kernel(info, tiles, held, token, sems):
     core = info[0]
     copies = []
-    for g in range(8):
-        half = (low, high)[g // 4]
+    for g in range(4):
         copies.append(
             pltpu.make_async_copy(
-                tiles.at[pl.ds(8 * g + 4 * core, 4)], half.at[pl.ds(4 * (g % 4), 4)], sems.at[g]
+                tiles.at[pl.ds(8 * g + 4 * core, 4)], held.at[pl.ds(4 * g, 4)], sems.at[g]
             )
         )
     for c in copies:
@@ -81,21 +79,20 @@
 
 
 def load_tiles(info, tiles):
-    *held, token = pl.pallas_call(
+    held, token = pl.pallas_call(
         load_kernel,
         out_shape=(
-            pltpu.VMEM((ROWS // 2, SLOTS, 128, 128), BF16),
             pltpu.VMEM((ROWS // 2, SLOTS, 128, 128), BF16),
             jax.ShapeDtypeStruct((8, 128), F32),
         ),
         in_specs=[SMEM, ANY],
-        out_specs=(VMEM, VMEM, VMEM),
-        scratch_shapes=[pltpu.SemaphoreType.DMA((8,))],
+        out_specs=(VMEM, VMEM),
+        scratch_shapes=[pltpu.SemaphoreType.DMA((4,))],
         compiler_params=pltpu.CompilerParams(vmem_limit_bytes=2 << 20),
         cost_estimate=pl.CostEstimate(flops=0, bytes_accessed=48 << 20, transcendentals=0),
         name="load_tiles",
     )(info, tiles)
-    return [pltpu.with_memory_space_constraint(h, pltpu.VMEM) for h in held], token
+    return pltpu.with_memory_space_constraint(held, pltpu.VMEM), token
 
 
 def gate(arrays, before):
@@ -189,8 +186,9 @@
     )(info, mine, received, before)
 
 
-def forward_kernel(places, info, cols, low_tiles, high_tiles, *refs):
-    own, others, cot, weight, (out, feats, sems) = refs[:8], refs[8:12], refs[12], refs[13], refs[14:]
+def forward_kernel(places, info, cols, low_tiles, tiles, *refs):
+    own, others, cot, weight = refs[:8], refs[8:12], refs[12], refs[13]
+    out, high_tiles, feats, sems, stream_sems = refs[14:]
     core = info[0]
     mine = pl.ds(pl.multiple_of(HALF * core, HALF), HALF)
     sibling = pl.ds(pl.multiple_of(HALF * (1 - core), HALF), HALF)
@@ -202,7 +200,15 @@
             pltpu.make_async_copy(own[i], feats.at[mine, at], sems.at[2 * i]),
             pltpu.make_async_copy(other, feats.at[sibling, at], sems.at[2 * i + 1]),
         ]
-    for c in copies:
+    stream = [
+        pltpu.make_async_copy(
+            tiles.at[pl.ds(8 * (4 + g) + 4 * core, 4)],
+            high_tiles.at[pl.ds(4 * g, 4)],
+            stream_sems.at[g],
+        )
+        for g in range(4)
+    ]
+    for c in copies + stream:
         c.start()
     near = others[0]
     for g in range(8):
@@ -260,31 +266,39 @@
             )
             return carry
 
+        if half:
+            for c in stream:
+                c.wait()
         lax.fori_loop(4 * half, 4 * half + 4, step, 0)
 
 
-def forward(info, cols, held, pieces, cot, weight):
+def forward(info, cols, held, tiles, pieces, cot, weight):
     own = [p[0] for p in pieces]
     others = []
     for _, other, _ in pieces:
         if not any(other is o for o in others):
             others.append(other)
     places = tuple((next(k for k, o in enumerate(others) if o is p[1]), p[2]) for p in pieces)
-    return pl.pallas_call(
+    message, streamed = pl.pallas_call(
         functools.partial(forward_kernel, places),
-        out_shape=jax.ShapeDtypeStruct((8, PAIR, WIDE), BF16),
-        in_specs=[SMEM, SMEM, VMEM, VMEM] + [ANY] * 8 + [VMEM] + [ANY] * 3 + [VMEM] * 2,
-        out_specs=VMEM,
+        out_shape=(
+            jax.ShapeDtypeStruct((8, PAIR, WIDE), BF16),
+            pltpu.VMEM((ROWS // 2, SLOTS, 128, 128), BF16),
+        ),
+        in_specs=[SMEM, SMEM, VMEM, ANY] + [ANY] * 8 + [VMEM] + [ANY] * 3 + [VMEM] * 2,
+        out_specs=(VMEM, VMEM),
         scratch_shapes=[
             pltpu.VMEM((PAIR, NODES), BF16),
             pltpu.SemaphoreType.DMA((16,)),
+            pltpu.SemaphoreType.DMA((4,)),
         ],
         compiler_params=pltpu.CompilerParams(vmem_limit_bytes=10 << 20),
         cost_estimate=pl.CostEstimate(
             flops=8 * 2 * 1024 * 128 * 128 * 32, bytes_accessed=8 << 20, transcendentals=0
         ),
         name="forward",
-    )(info, cols, *held, *own, *others, cot, weight)
+    )(info, cols, held, tiles, *own, *others, cot, weight)
+    return message, pltpu.with_memory_space_constraint(streamed, pltpu.VMEM)
 
 
 def dense_kernel(message, out):
@@ -314,16 +328,9 @@
     )(message)
 
 
-def backward_kernel(info, cols, tiles, grad, *refs):
-    outs, (total, ring, sems) = refs[:4], refs[4:]
+def backward_kernel(info, cols, low_tiles, high_tiles, grad, *refs):
+    outs, total = refs[:4], refs[4]
     core = info[0]
-
-    def copy(i):
-        slot = lax.rem(i, RING)
-        return pltpu.make_async_copy(tiles.at[row_of(core, i)], ring.at[slot], sems.at[slot])
-
-    for i in range(RING):
-        copy(jnp.int32(i)).start()
 
     def clear(i, carry):
         total[:, pl.ds(pl.multiple_of(i * 2048, 2048), 2048)] = jnp.zeros((PAIR, 2048), F32)
@@ -331,35 +338,29 @@
 
     lax.fori_loop(0, NODES // 2048, clear, 0)
 
-    def row(local):
+    def row(local, tiles):
         r = row_of(core, local)
-        slot = lax.rem(local, RING)
         g = grad[local // 4, :, lanes_of(lax.rem(local, 4))]
+        at = lax.rem(local, 16)
         for first in range(0, SLOTS, 8):
             blocks = [lanes_of(cols[first + i, r]) for i in range(8)]
             terms = []
             for i in range(first, first + 8, 2):
-                pair = jnp.concatenate([ring[slot, i], ring[slot, i + 1]], axis=1)
+                pair = jnp.concatenate([tiles[at, i], tiles[at, i + 1]], axis=1)
                 both = jnp.dot(g, pair, preferred_element_type=F32)
                 terms += [both[:, :128], both[:, 128:]]
             sums = [total[:, blocks[i]] + terms[i] for i in range(8)]
             for i in range(8):
                 total[:, blocks[i]] = sums[i]
 
-    def step(i, carry):
-        for k in range(2):
-            copy(2 * i + k).wait()
-        for k in range(2):
-            row(2 * i + k)
-
-        @pl.when(2 * i + RING < ROWS)
-        def _():
-            for k in range(2):
-                copy(2 * i + k + RING).start()
-
-        return carry
-
-    lax.fori_loop(0, ROWS // 2, step, 0)
+    for half, tiles in enumerate((low_tiles, high_tiles)):
+
+        def step(i, carry, tiles=tiles):
+            for k in range(4):
+                row(4 * i + k, tiles)
+            return carry
+
+        lax.fori_loop(4 * half, 4 * half + 4, step, 0)
 
     own = pl.ds(pl.multiple_of(HALF * core, HALF), HALF)
     other = pl.ds(pl.multiple_of(HALF * (1 - core), HALF), HALF)
@@ -371,23 +372,21 @@
             outs[2 + phase][:, place] = total[other, lanes].astype(BF16)
 
 
-def backward(info, cols, tiles, grad):
+def backward(info, cols, held, grad):
     return pl.pallas_call(
         backward_kernel,
         out_shape=[jax.ShapeDtypeStruct((HALF, LOCAL * len(g)), BF16) for g in GROUPS] * 2,
-        in_specs=[SMEM, SMEM, ANY, VMEM],
+        in_specs=[SMEM, SMEM, VMEM, VMEM, VMEM],
         out_specs=[VMEM] * 4,
         scratch_shapes=[
             pltpu.VMEM((PAIR, NODES), F32),
-            pltpu.VMEM((RING, SLOTS, 128, 128), BF16),
-            pltpu.SemaphoreType.DMA((RING,)),
         ],
-        compiler_params=pltpu.CompilerParams(vmem_limit_bytes=32 << 20),
+        compiler_params=pltpu.CompilerParams(vmem_limit_bytes=10 << 20),
         cost_estimate=pl.CostEstimate(
             flops=8 * 2 * 1024 * 128 * 128 * 32, bytes_accessed=8 << 20, transcendentals=0
         ),
         name="backward",
-    )(info, cols, tiles, grad)
+    )(info, cols, *held, grad)
 
 
 def sum_call(kernel, shapes, args, name, before=()):
@@ -462,12 +461,12 @@
         (across_down, swap(across_down), 0),
         (corner, near, 3 * LOCAL),
     ]
-    message = forward(info, cols, held, pieces, cotangent, weight)
+    message, streamed = forward(info, cols, held, tiles, pieces, cotangent, weight)
     message = lax.all_to_all(message, "feat", 0, 0, axis_index_groups=SAME_CORE, tiled=True)
     message = dense(message.reshape(256, WIDE)).reshape(8, PAIR, WIDE)
     message = lax.all_to_all(message, "feat", 0, 0, axis_index_groups=SAME_CORE, tiled=True)
 
-    own_a, own_c, other_a, other_c = backward(info, cols, tiles, message)
+    own_a, own_c, other_a, other_c = backward(info, cols, (held, streamed), message)
     piece = ((HALF, LOCAL + 256), BF16)
     hidden, hidden_other, wgrad, wgrad_other = unpack(info, message, own_a)
     hidden_other = swap(hidden_other)

time: 128 us -> 122 us (0.953)
  Pallas kernels: 41.7 us -> 33 us
  starting transfers between devices: 23.3 us -> 25.8 us
  waiting for transfers between devices: 25 us -> 26.3 us
    pallas_call x1, Pallas kernels: 11.3 us -> 6.43 us  [load_tiles(): pl.pallas_call(load_kernel, out_shape=(pltpu.VMEM((ROWS // 2, SLOTS, 128,...]
    pallas_call x1, Pallas kernels: 12.6 us -> 8.75 us  [backward(): pl.pallas_call(backward_kernel, out_shape=[jax.ShapeDtypeStruct((HALF, LO...]
    ppermute x7, starting transfers between devices: 9.55 us -> 11.5 us  [send(): return lax.ppermute(a, 'blk', _to_step(step))]
    ppermute x7, waiting for transfers between devices: 6.1 us -> 8.05 us  [receive(): return lax.ppermute(a, 'blk', _from_step(step))]
  transfers between devices with their start and end apart: 22 -> 22, of which waited for: 12 -> 15; matrix products, arithmetic and copies ran while one was open for 0% -> 0% of each run, Pallas kernels for 11% -> 7%
where the time goes in v9:
time: 122 us
  blocking collectives  35.6 us (29%)
  Pallas kernels  33 us (27%)
  waiting for transfers between devices  26.3 us (22%)
  starting transfers between devices  25.8 us (21%)
    all_to_all x2, blocking collectives, per_device(): lax.all_to_all(message, 'feat', 0, 0, axis_index_groups=SAME_CORE, tiled=...  35.6 us
    ppermute x7, waiting for transfers between devices, send(): return lax.ppermute(a, 'blk', _to_step(step))  13.9 us
    ppermute x7, starting transfers between devices, receive(): return lax.ppermute(a, 'blk', _from_step(step))  12.8 us
    pallas_call x1, Pallas kernels, forward(): pl.pallas_call(functools.partial(forward_kernel, places), out_shape=(jax....  12.8 us
    ppermute x7, starting transfers between devices, send(): return lax.ppermute(a, 'blk', _to_step(step))  11.5 us
    pallas_call x1, Pallas kernels, backward(): pl.pallas_call(backward_kernel, out_shape=[jax.ShapeDtypeStruct((HALF, LO...  8.75 us
    ppermute x7, waiting for transfers between devices, receive(): return lax.ppermute(a, 'blk', _from_step(step))  8.05 us
    pallas_call x1, Pallas kernels, load_tiles(): pl.pallas_call(load_kernel, out_shape=(pltpu.VMEM((ROWS // 2, SLOTS, 128,...  6.43 us
  transfers between devices with their start and end apart: 22, of which 15 were waited for; matrix products, arithmetic and copies ran while one was open for 0% of the time, Pallas kernels for 7%

profile of v9, /device:TPU:0, one launch (start us, length us, event | category | flops | bytes accessed | tf_op | source)
XLA Modules:
  0.0 121.6 jit_solution(7843747645957256580)
XLA Ops:
  0.6 4.3 %collective-permute-start.3 = (bf16[16,8192]{1,0:T(8,128)(2,1)}, bf16[16,8192]{1,0:T(8,128)(2,1)S(1)}, u32[]{:S(2)}, u32[]{:S(2)}) collective-permute-start(bf16[16,8192]{1,0:T(8,128)(2,1)} %refs_0_.1), channel_id=1, source_target_pairs={{96,0},{112,16},{64,32},{80,48},{32,64},{48,80},{0,96},{16,112},{9... | collective-permute-start | bytes 786440 | tf_op jit(solution)/shard_map/ppermute | solution.py:50
  4.9 0.7 collective-permute-start.2
  6.1 2.6 %collective-permute-start = (bf16[16,8192]{1,0:T(8,128)(2,1)}, bf16[16,8192]{1,0:T(8,128)(2,1)}, u32[]{:S(2)}, u32[]{:S(2)}) collective-permute-start(bf16[16,8192]{1,0:T(8,128)(2,1)} %refs_0_.1), channel_id=1, source_target_pairs={{16,0},{32,16},{48,32},{0,48},{80,64},{96,80},{112,96},{64,112},{1... | collective-permute-start | bytes 786440 | tf_op jit(solution)/shard_map/ppermute | solution.py:50
  8.8 6.4 %load_tiles.1 = (bf16[16,32,128,128]{3,2,1,0:T(8,128)(2,1)S(1)}, f32[8,128]{1,0:T(8,128)S(1)}) custom-call(s32[9]{0:T(128)S(1)} %stack.39.info, bf16[64,32,128,128]{3,2,1,0:T(8,128)(2,1)} %tiles.3), custom_call_target="tpu_custom_call" | custom-call | bytes 50331648 | tf_op jit(solution)/shard_map/load_tiles/pallas_call | solution.py:82
  15.3 1.9 %collective-permute-done.2.down.refs_2_ = bf16[16,8192]{1,0:T(8,128)(2,1)S(1)} collective-permute-done((bf16[16,8192]{1,0:T(8,128)(2,1)}, bf16[16,8192]{1,0:T(8,128)(2,1)S(1)}, u32[]{:S(2)}, u32[]{:S(2)}) %collective-permute-start.2) | collective-permute-done | bytes 262176 | tf_op jit(solution)/shard_map/ppermute | solution.py:50
  17.5 1.1 bundle.1
  18.7 1.4 %collective-permute-start.6 = (bf16[16,8192]{1,0:T(8,128)(2,1)S(1)}, bf16[16,8192]{1,0:T(8,128)(2,1)S(1)}, u32[]{:S(2)}, u32[]{:S(2)}) collective-permute-start(bf16[16,8192]{1,0:T(8,128)(2,1)S(1)} %get-tuple-element.32.refs_3_), channel_id=1, source_target_pairs={{48,0},{0,16},{16,32},{32,48},{112,64},{64,80},{80,96},{96,112},{4... | collective-permute-start | bytes 786440 | tf_op jit(solution)/shard_map/ppermute | solution.py:50
  20.0 1.4 %collective-permute-start.5 = (bf16[16,8192]{1,0:T(8,128)(2,1)}, bf16[16,8192]{1,0:T(8,128)(2,1)S(1)}, u32[]{:S(2)}, u32[]{:S(2)}) collective-permute-start(bf16[16,8192]{1,0:T(8,128)(2,1)} %get-tuple-element.31.refs_1_), channel_id=1, source_target_pairs={{64,0},{80,16},{96,32},{112,48},{0,64},{16,80},{32,96},{48,112},{6... | collective-permute-start | bytes 786440 | tf_op jit(solution)/shard_map/ppermute | solution.py:50
  21.5 2.0 %collective-permute-start.4 = (bf16[16,8192]{1,0:T(8,128)(2,1)}, bf16[16,8192]{1,0:T(8,128)(2,1)S(1)}, u32[]{:S(2)}, u32[]{:S(2)}) collective-permute-start(bf16[16,8192]{1,0:T(8,128)(2,1)} %get-tuple-element.31.refs_1_), channel_id=1, source_target_pairs={{16,0},{32,16},{48,32},{0,48},{80,64},{96,80},{112,96},{64,112},{1... | collective-permute-start | bytes 786440 | tf_op jit(solution)/shard_map/ppermute | solution.py:50
  23.5 5.1 %collective-permute-done.6.refs_6_ = bf16[16,8192]{1,0:T(8,128)(2,1)S(1)} collective-permute-done((bf16[16,8192]{1,0:T(8,128)(2,1)S(1)}, bf16[16,8192]{1,0:T(8,128)(2,1)S(1)}, u32[]{:S(2)}, u32[]{:S(2)}) %collective-permute-start.6) | collective-permute-done | bytes 262176 | tf_op jit(solution)/shard_map/ppermute | solution.py:50
  29.1 0.7 collective-permute-done.4.refs_4_
  30.5 0.8 collective-permute-done.8.refs_9_
  31.3 12.8 %forward.1 = (bf16[8,32,1280]{2,1,0:T(8,128)(2,1)S(1)}, bf16[16,32,128,128]{3,2,1,0:T(8,128)(2,1)S(1)}) custom-call(s32[9]{0:T(128)S(1)} %stack.39.info, s32[32,64]{1,0:T(8,128)S(1)} %bitcast.14, bf16[16,32,128,128]{3,2,1,0:T(8,128)(2,1)S(1)} %get-tuple-element.29.low_tiles, bf16[64,32,128,128]{3,2,1,0:T(8,128)(2,1)} %tiles.3, bf16[16,8192]{1,0:T(8,128)(2,1)S(1)} %copy-done, ...), custom_call_target="tpu_custom_call" | custom-call | flops 8589934592 | bytes 8388608 | tf_op jit(solution)/shard_map/forward/pallas_call | solution.py:282
  44.1 20.6 %all_to_all.10 = bf16[8,32,1280]{2,1,0:T(8,128)(2,1)S(1)} all-to-all(bf16[8,32,1280]{2,1,0:T(8,128)(2,1)S(1)} %get-tuple-element.34), channel_id=1, replica_groups={{0,2,4,6,8,10,12,14},{1,3,5,7,9,11,13,15},{16,18,20,22,24,26,28,30},{17..., dimensions={0} | all-to-all | bytes 1310720 | tf_op jit(solution)/shard_map/all_to_all | solution.py:465
  64.7 0.6 dense.1
  65.3 15.0 %all_to_all.11.grad.message = bf16[8,32,1280]{2,1,0:T(8,128)(2,1)S(1)} all-to-all(bf16[8,32,1280]{2,1,0:T(8,128)(2,1)S(1)} %bitcast.13), channel_id=1, replica_groups={{0,2,4,6,8,10,12,14},{1,3,5,7,9,11,13,15},{16,18,20,22,24,26,28,30},{17..., dimensions={0} | all-to-all | bytes 1310720 | tf_op jit(solution)/shard_map/all_to_all | solution.py:467
  80.4 8.7 %backward.1 = (bf16[16,32768]{1,0:T(8,128)(2,1)S(1)}, bf16[16,32768]{1,0:T(8,128)(2,1)S(1)}, bf16[16,32768]{1,0:T(8,128)(2,1)S(1)}, bf16[16,32768]{1,0:T(8,128)(2,1)S(1)}) custom-call(s32[9]{0:T(128)S(1)} %stack.39.info, s32[32,64]{1,0:T(8,128)S(1)} %bitcast.15, bf16[16,32,128,128]{3,2,1,0:T(8,128)(2,1)S(1)} %get-tuple-element.29.low_tiles, ...), custom_call_target="tpu_custom_call" | custom-call | flops 8589934592 | bytes 8388608 | tf_op jit(solution)/shard_map/backward/pallas_call | solution.py:376
  89.2 0.6 unpack.1
  89.8 0.6 collective-permute-start.13
  90.4 1.5 %collective-permute-done.13.refs_3_ = f32[16,256]{1,0:T(8,128)S(1)} collective-permute-done((f32[16,256]{1,0:T(8,128)S(1)}, f32[16,256]{1,0:T(8,128)S(1)}, u32[]{:S(2)}, u32[]{:S(2)}) %collective-permute-start.13) | collective-permute-done | bytes 16416 | tf_op jit(solution)/shard_map/ppermute | solution.py:46
  92.8 3.0 %collective-permute-start.16 = (bf16[16,8448]{1,0:T(8,128)(2,1)S(1)}, bf16[16,8448]{1,0:T(8,128)(2,1)S(1)}, u32[]{:S(2)}, u32[]{:S(2)}) collective-permute-start(bf16[16,8448]{1,0:T(8,128)(2,1)S(1)} %get-tuple-element.47), channel_id=1, source_target_pairs={{0,48},{16,0},{32,16},{48,32},{64,112},{80,64},{96,80},{112,96},{1... | collective-permute-start | bytes 811016 | tf_op jit(solution)/shard_map/ppermute | solution.py:54
  95.8 3.0 %collective-permute-start.18 = (bf16[16,8448]{1,0:T(8,128)(2,1)S(1)}, bf16[16,8448]{1,0:T(8,128)(2,1)S(1)}, u32[]{:S(2)}, u32[]{:S(2)}) collective-permute-start(bf16[16,8448]{1,0:T(8,128)(2,1)S(1)} %get-tuple-element.50), channel_id=1, source_target_pairs={{0,96},{16,112},{32,64},{48,80},{64,32},{80,48},{96,0},{112,16},{1... | collective-permute-start | bytes 811016 | tf_op jit(solution)/shard_map/ppermute | solution.py:54
  98.8 2.9 %collective-permute-done.15.refs_3_ = bf16[16,8448]{1,0:T(8,128)(2,1)S(1)} collective-permute-done((bf16[16,8448]{1,0:T(8,128)(2,1)S(1)}, bf16[16,8448]{1,0:T(8,128)(2,1)S(1)}, u32[]{:S(2)}, u32[]{:S(2)}) %collective-permute-start.15) | collective-permute-done | bytes 270368 | tf_op jit(solution)/shard_map/ppermute | solution.py:54
  101.7 6.0 %collective-permute-done.16.refs_4_ = bf16[16,8448]{1,0:T(8,128)(2,1)S(1)} collective-permute-done((bf16[16,8448]{1,0:T(8,128)(2,1)S(1)}, bf16[16,8448]{1,0:T(8,128)(2,1)S(1)}, u32[]{:S(2)}, u32[]{:S(2)}) %collective-permute-start.16) | collective-permute-done | bytes 270368 | tf_op jit(solution)/shard_map/ppermute | solution.py:54
  107.7 3.4 %collective-permute-done.17.refs_5_ = bf16[16,8448]{1,0:T(8,128)(2,1)S(1)} collective-permute-done((bf16[16,8448]{1,0:T(8,128)(2,1)S(1)}, bf16[16,8448]{1,0:T(8,128)(2,1)S(1)}, u32[]{:S(2)}, u32[]{:S(2)}) %collective-permute-start.17) | collective-permute-done | bytes 270368 | tf_op jit(solution)/shard_map/ppermute | solution.py:54
  111.5 1.8 %collective-permute-start.20 = (bf16[16,8448]{1,0:T(8,128)(2,1)S(1)}, bf16[16,8448]{1,0:T(8,128)(2,1)S(1)}, u32[]{:S(2)}, u32[]{:S(2)}) collective-permute-start(bf16[16,8448]{1,0:T(8,128)(2,1)S(1)} %get-tuple-element.52), channel_id=1, source_target_pairs={{0,64},{16,80},{32,96},{48,112},{64,0},{80,16},{96,32},{112,48},{1... | collective-permute-start | bytes 811016 | tf_op jit(solution)/shard_map/ppermute | solution.py:54
  113.3 3.1 %collective-permute-start.21 = (bf16[16,8448]{1,0:T(8,128)(2,1)S(1)}, bf16[16,8448]{1,0:T(8,128)(2,1)S(1)}, u32[]{:S(2)}, u32[]{:S(2)}) collective-permute-start(bf16[16,8448]{1,0:T(8,128)(2,1)S(1)} %get-tuple-element.48.before), channel_id=1, source_target_pairs={{0,48},{16,0},{32,16},{48,32},{64,112},{80,64},{96,80},{112,96},{1... | collective-permute-start | bytes 811016 | tf_op jit(solution)/shard_map/ppermute | solution.py:54
  116.5 1.3 %collective-permute-done.11.received = bf16[16,4096]{1,0:T(8,128)(2,1)S(1)} collective-permute-done((bf16[16,4096]{1,0:T(8,128)(2,1)S(1)}, bf16[16,4096]{1,0:T(8,128)(2,1)S(1)}, u32[]{:S(2)}, u32[]{:S(2)}) %collective-permute-start.11) | collective-permute-done | bytes 131104 | tf_op jit(solution)/shard_map/ppermute | solution.py:46
  117.8 1.3 %join.1 = bf16[16,8192]{1,0:T(8,128)(2,1)} custom-call(s32[9]{0:T(128)S(1)} %stack.39.info, bf16[16,4096]{1,0:T(8,128)(2,1)S(1)} %get-tuple-element.37.mine, bf16[16,4096]{1,0:T(8,128)(2,1)S(1)} %collective-permute-done.11.received, bf16[16,8448]{1,0:T(8,128)(2,1)S(1)} %get-tuple-element.48.before), custom_call_target="tpu_custom_call" | custom-call | bytes 1048576 | tf_op jit(solution)/shard_map/join/pallas_call | solution.py:178
  119.1 1.0 collective-permute-done.19.refs_2_
  120.1 0.6 collective-permute-done.21.refs_4_
  120.7 0.9 sum_last.1
  (34 shorter events, 3.8 us)
Async XLA Ops:
  0.6 14.6 %collective-permute-start.3 = (bf16[16,8192]{1,0:T(8,128)(2,1)}, bf16[16,8192]{1,0:T(8,128)(2,1)S(1)}, u32[]{:S(2)}, u32[]{:S(2)}) collective-permute-start(bf16[16,8192]{1,0:T(8,128)(2,1)} %refs_0_.1), channel_id=1, source_target_pairs={{96,0},{112,16},{64,32},{80,48},{32,64},{48,80},{0,96},{16,112},{9... | collective-permute-start | bytes 786440 | tf_op jit(solution)/shard_map/ppermute | solution.py:50
  4.9 12.2 %collective-permute-start.2 = (bf16[16,8192]{1,0:T(8,128)(2,1)}, bf16[16,8192]{1,0:T(8,128)(2,1)S(1)}, u32[]{:S(2)}, u32[]{:S(2)}) collective-permute-start(bf16[16,8192]{1,0:T(8,128)(2,1)} %refs_0_.1), channel_id=1, source_target_pairs={{48,0},{0,16},{16,32},{32,48},{112,64},{64,80},{80,96},{96,112},{4... | collective-permute-start | bytes 786440 | tf_op jit(solution)/shard_map/ppermute | solution.py:50
  5.6 11.7 %collective-permute-start.1 = (bf16[16,8192]{1,0:T(8,128)(2,1)}, bf16[16,8192]{1,0:T(8,128)(2,1)S(1)}, u32[]{:S(2)}, u32[]{:S(2)}) collective-permute-start(bf16[16,8192]{1,0:T(8,128)(2,1)} %refs_0_.1), channel_id=1, source_target_pairs={{64,0},{80,16},{96,32},{112,48},{0,64},{16,80},{32,96},{48,112},{6... | collective-permute-start | bytes 786440 | tf_op jit(solution)/shard_map/ppermute | solution.py:50
  6.1 11.4 %collective-permute-start = (bf16[16,8192]{1,0:T(8,128)(2,1)}, bf16[16,8192]{1,0:T(8,128)(2,1)}, u32[]{:S(2)}, u32[]{:S(2)}) collective-permute-start(bf16[16,8192]{1,0:T(8,128)(2,1)} %refs_0_.1), channel_id=1, source_target_pairs={{16,0},{32,16},{48,32},{0,48},{80,64},{96,80},{112,96},{64,112},{1... | collective-permute-start | bytes 786440 | tf_op jit(solution)/shard_map/ppermute | solution.py:50
  8.8 8.7 %copy-start = (bf16[16,8192]{1,0:T(8,128)(2,1)S(1)}, bf16[16,8192]{1,0:T(8,128)(2,1)}, u32[]{:S(2)}) copy-start(bf16[16,8192]{1,0:T(8,128)(2,1)} %refs_0_.1) | copy-start | bytes 786436
  8.8 8.7 %copy-start.1 = (bf16[16,8192]{1,0:T(8,128)(2,1)S(1)}, bf16[16,8192]{1,0:T(8,128)(2,1)}, u32[]{:S(2)}) copy-start(bf16[16,8192]{1,0:T(8,128)(2,1)} %refs_12_.1) | copy-start | bytes 786436
  8.8 8.7 %copy-start.3 = (bf16[16,256]{1,0:T(8,128)(2,1)S(1)}, bf16[16,256]{1,0:T(8,128)(2,1)}, u32[]{:S(2)}) copy-start(bf16[16,256]{1,0:T(8,128)(2,1)} %refs_13_.1) | copy-start | bytes 24580
  8.8 22.5 %copy-start.2 = (s32[64,32]{0,1:T(8,128)S(1)}, s32[64,32]{0,1:T(8,128)}, u32[]{:S(2)}) copy-start(s32[64,32]{0,1:T(8,128)} %param.8) | copy-start | bytes 24580
  18.6 12.7 %collective-permute-start.7 = (bf16[16,49408]{1,0:T(8,128)(2,1)S(1)}, bf16[16,49408]{1,0:T(8,128)(2,1)S(1)}, u32[]{:S(2)}, u32[]{:S(2)}) collective-permute-start(bf16[16,49408]{1,0:T(8,128)(2,1)S(1)} %get-tuple-element.33), channel_id=1, source_target_pairs={{0,1},{1,0},{2,3},{3,2},{4,5},{5,4},{6,7},{7,6},{8,9},{9,8},{10,11... | collective-permute-start | bytes 4743176 | tf_op jit(solution)/shard_map/ppermute | solution.py:46
  18.7 9.9 %collective-permute-start.6 = (bf16[16,8192]{1,0:T(8,128)(2,1)S(1)}, bf16[16,8192]{1,0:T(8,128)(2,1)S(1)}, u32[]{:S(2)}, u32[]{:S(2)}) collective-permute-start(bf16[16,8192]{1,0:T(8,128)(2,1)S(1)} %get-tuple-element.32.refs_3_), channel_id=1, source_target_pairs={{48,0},{0,16},{16,32},{32,48},{112,64},{64,80},{80,96},{96,112},{4... | collective-permute-start | bytes 786440 | tf_op jit(solution)/shard_map/ppermute | solution.py:50
  20.0 8.6 %collective-permute-start.5 = (bf16[16,8192]{1,0:T(8,128)(2,1)}, bf16[16,8192]{1,0:T(8,128)(2,1)S(1)}, u32[]{:S(2)}, u32[]{:S(2)}) collective-permute-start(bf16[16,8192]{1,0:T(8,128)(2,1)} %get-tuple-element.31.refs_1_), channel_id=1, source_target_pairs={{64,0},{80,16},{96,32},{112,48},{0,64},{16,80},{32,96},{48,112},{6... | collective-permute-start | bytes 786440 | tf_op jit(solution)/shard_map/ppermute | solution.py:50
  21.5 8.3 %collective-permute-start.4 = (bf16[16,8192]{1,0:T(8,128)(2,1)}, bf16[16,8192]{1,0:T(8,128)(2,1)S(1)}, u32[]{:S(2)}, u32[]{:S(2)}) collective-permute-start(bf16[16,8192]{1,0:T(8,128)(2,1)} %get-tuple-element.31.refs_1_), channel_id=1, source_target_pairs={{16,0},{32,16},{48,32},{0,48},{80,64},{96,80},{112,96},{64,112},{1... | collective-permute-start | bytes 786440 | tf_op jit(solution)/shard_map/ppermute | solution.py:50
  28.6 1.5 %collective-permute-start.10 = (bf16[16,8192]{1,0:T(8,128)(2,1)S(1)}, bf16[16,8192]{1,0:T(8,128)(2,1)S(1)}, u32[]{:S(2)}, u32[]{:S(2)}) collective-permute-start(bf16[16,8192]{1,0:T(8,128)(2,1)S(1)} %collective-permute-done.6.refs_6_), channel_id=1, source_target_pairs={{0,1},{1,0},{2,3},{3,2},{4,5},{5,4},{6,7},{7,6},{8,9},{9,8},{10,11... | collective-permute-start | bytes 786440 | tf_op jit(solution)/shard_map/ppermute | solution.py:46
  28.6 1.9 %collective-permute-start.9 = (bf16[16,8192]{1,0:T(8,128)(2,1)S(1)}, bf16[16,8192]{1,0:T(8,128)(2,1)S(1)}, u32[]{:S(2)}, u32[]{:S(2)}) collective-permute-start(bf16[16,8192]{1,0:T(8,128)(2,1)S(1)} %collective-permute-done.5.refs_5_), channel_id=1, source_target_pairs={{0,1},{1,0},{2,3},{3,2},{4,5},{5,4},{6,7},{7,6},{8,9},{9,8},{10,11... | collective-permute-start | bytes 786440 | tf_op jit(solution)/shard_map/ppermute | solution.py:46
  29.8 1.5 %collective-permute-start.8 = (bf16[16,8192]{1,0:T(8,128)(2,1)S(1)}, bf16[16,8192]{1,0:T(8,128)(2,1)S(1)}, u32[]{:S(2)}, u32[]{:S(2)}) collective-permute-start(bf16[16,8192]{1,0:T(8,128)(2,1)S(1)} %collective-permute-done.4.refs_4_), channel_id=1, source_target_pairs={{0,1},{1,0},{2,3},{3,2},{4,5},{5,4},{6,7},{7,6},{8,9},{9,8},{10,11... | collective-permute-start | bytes 786440 | tf_op jit(solution)/shard_map/ppermute | solution.py:46
  89.1 2.8 %collective-permute-start.12 = (bf16[16,32768]{1,0:T(8,128)(2,1)S(1)}, bf16[16,32768]{1,0:T(8,128)(2,1)S(1)}, u32[]{:S(2)}, u32[]{:S(2)}) collective-permute-start(bf16[16,32768]{1,0:T(8,128)(2,1)S(1)} %get-tuple-element.41), channel_id=1, source_target_pairs={{0,1},{1,0},{2,3},{3,2},{4,5},{5,4},{6,7},{7,6},{8,9},{9,8},{10,11... | collective-permute-start | bytes 3145736 | tf_op jit(solution)/shard_map/ppermute | solution.py:46
  89.8 2.1 %collective-permute-start.13 = (f32[16,256]{1,0:T(8,128)S(1)}, f32[16,256]{1,0:T(8,128)S(1)}, u32[]{:S(2)}, u32[]{:S(2)}) collective-permute-start(f32[16,256]{1,0:T(8,128)S(1)} %get-tuple-element.43), channel_id=1, source_target_pairs={{0,1},{1,0},{2,3},{3,2},{4,5},{5,4},{6,7},{7,6},{8,9},{9,8},{10,11... | collective-permute-start | bytes 49160 | tf_op jit(solution)/shard_map/ppermute | solution.py:46
  92.1 18.9 %collective-permute-start.14 = (bf16[16,32768]{1,0:T(8,128)(2,1)S(1)}, bf16[16,32768]{1,0:T(8,128)(2,1)S(1)}, u32[]{:S(2)}, u32[]{:S(2)}) collective-permute-start(bf16[16,32768]{1,0:T(8,128)(2,1)S(1)} %gate.1), channel_id=1, source_target_pairs={{0,1},{1,0},{2,3},{3,2},{4,5},{5,4},{6,7},{7,6},{8,9},{9,8},{10,11... | collective-permute-start | bytes 3145736 | tf_op jit(solution)/shard_map/ppermute | solution.py:46
  92.4 9.3 %collective-permute-start.15 = (bf16[16,8448]{1,0:T(8,128)(2,1)S(1)}, bf16[16,8448]{1,0:T(8,128)(2,1)S(1)}, u32[]{:S(2)}, u32[]{:S(2)}) collective-permute-start(bf16[16,8448]{1,0:T(8,128)(2,1)S(1)} %get-tuple-element.46), channel_id=1, source_target_pairs={{0,64},{16,80},{32,96},{48,112},{64,0},{80,16},{96,32},{112,48},{1... | collective-permute-start | bytes 811016 | tf_op jit(solution)/shard_map/ppermute | solution.py:54
  92.8 14.9 %collective-permute-start.16 = (bf16[16,8448]{1,0:T(8,128)(2,1)S(1)}, bf16[16,8448]{1,0:T(8,128)(2,1)S(1)}, u32[]{:S(2)}, u32[]{:S(2)}) collective-permute-start(bf16[16,8448]{1,0:T(8,128)(2,1)S(1)} %get-tuple-element.47), channel_id=1, source_target_pairs={{0,48},{16,0},{32,16},{48,32},{64,112},{80,64},{96,80},{112,96},{1... | collective-permute-start | bytes 811016 | tf_op jit(solution)/shard_map/ppermute | solution.py:54
  95.8 15.3 %collective-permute-start.17 = (bf16[16,8448]{1,0:T(8,128)(2,1)S(1)}, bf16[16,8448]{1,0:T(8,128)(2,1)S(1)}, u32[]{:S(2)}, u32[]{:S(2)}) collective-permute-start(bf16[16,8448]{1,0:T(8,128)(2,1)S(1)} %get-tuple-element.44.refs_1_), channel_id=1, source_target_pairs={{0,16},{16,32},{32,48},{48,0},{64,80},{80,96},{96,112},{112,64},{1... | collective-permute-start | bytes 811016 | tf_op jit(solution)/shard_map/ppermute | solution.py:54
  95.8 23.3 %collective-permute-start.18 = (bf16[16,8448]{1,0:T(8,128)(2,1)S(1)}, bf16[16,8448]{1,0:T(8,128)(2,1)S(1)}, u32[]{:S(2)}, u32[]{:S(2)}) collective-permute-start(bf16[16,8448]{1,0:T(8,128)(2,1)S(1)} %get-tuple-element.50), channel_id=1, source_target_pairs={{0,96},{16,112},{32,64},{48,80},{64,32},{80,48},{96,0},{112,16},{1... | collective-permute-start | bytes 811016 | tf_op jit(solution)/shard_map/ppermute | solution.py:54
  111.4 8.7 %collective-permute-start.19 = (bf16[16,8448]{1,0:T(8,128)(2,1)S(1)}, bf16[16,8448]{1,0:T(8,128)(2,1)S(1)}, u32[]{:S(2)}, u32[]{:S(2)}) collective-permute-start(bf16[16,8448]{1,0:T(8,128)(2,1)S(1)} %get-tuple-element.51), channel_id=1, source_target_pairs={{0,16},{16,32},{32,48},{48,0},{64,80},{80,96},{96,112},{112,64},{1... | collective-permute-start | bytes 811016 | tf_op jit(solution)/shard_map/ppermute | solution.py:54
  111.5 8.6 %collective-permute-start.20 = (bf16[16,8448]{1,0:T(8,128)(2,1)S(1)}, bf16[16,8448]{1,0:T(8,128)(2,1)S(1)}, u32[]{:S(2)}, u32[]{:S(2)}) collective-permute-start(bf16[16,8448]{1,0:T(8,128)(2,1)S(1)} %get-tuple-element.52), channel_id=1, source_target_pairs={{0,64},{16,80},{32,96},{48,112},{64,0},{80,16},{96,32},{112,48},{1... | collective-permute-start | bytes 811016 | tf_op jit(solution)/shard_map/ppermute | solution.py:54
  113.3 7.4 %collective-permute-start.21 = (bf16[16,8448]{1,0:T(8,128)(2,1)S(1)}, bf16[16,8448]{1,0:T(8,128)(2,1)S(1)}, u32[]{:S(2)}, u32[]{:S(2)}) collective-permute-start(bf16[16,8448]{1,0:T(8,128)(2,1)S(1)} %get-tuple-element.48.before), channel_id=1, source_target_pairs={{0,48},{16,0},{32,16},{48,32},{64,112},{80,64},{96,80},{112,96},{1... | collective-permute-start | bytes 811016 | tf_op jit(solution)/shard_map/ppermute | solution.py:54
  116.5 1.3 %collective-permute-start.11 = (bf16[16,4096]{1,0:T(8,128)(2,1)S(1)}, bf16[16,4096]{1,0:T(8,128)(2,1)S(1)}, u32[]{:S(2)}, u32[]{:S(2)}) collective-permute-start(bf16[16,4096]{1,0:T(8,128)(2,1)S(1)} %get-tuple-element.38), channel_id=1, source_target_pairs={{0,1},{1,0},{2,3},{3,2},{4,5},{5,4},{6,7},{7,6},{8,9},{9,8},{10,11... | collective-permute-start | bytes 393224 | tf_op jit(solution)/shard_map/ppermute | solution.py:46

commit v10 on v9

--- a/solution.py
+++ b/solution.py
@@ -109,56 +109,45 @@
     )(*arrays, *before)
 
 
-def bundle_kernel(up, across, down, corner, feats, cot, weight, token, up_out, across_out, out):
-    for i, a in enumerate((up, across, down, corner, feats, cot)):
-        out[:, LOCAL * i : LOCAL * (i + 1)] = a[...]
-    out[:, 6 * LOCAL :] = weight[...]
-
-
-def bundle(up, across, down, corner, feats, cot, weight, token):
-    wide = 6 * LOCAL + 256
+def bundle_kernel(feats, cot, weight, up, across, down, corner, token, local, first, second):
+    for out, parts in ((local, (feats, cot)), (first, (up, across)), (second, (down, corner))):
+        for i, a in enumerate(parts):
+            out[:, LOCAL * i : LOCAL * (i + 1)] = a[...]
+    local[:, 2 * LOCAL :] = weight[...]
+
+
+def bundle(*args):
     return pl.pallas_call(
         bundle_kernel,
         out_shape=[
-            jax.ShapeDtypeStruct(up.shape, BF16),
-            jax.ShapeDtypeStruct(across.shape, BF16),
-            jax.ShapeDtypeStruct((HALF, wide), BF16),
+            jax.ShapeDtypeStruct((HALF, 2 * LOCAL + n), BF16) for n in (256, 0, 0)
         ],
         in_specs=[VMEM] * 7 + [ANY],
-        out_specs=[ANY, ANY, VMEM],
-        input_output_aliases={0: 0, 1: 1},
+        out_specs=[VMEM] * 3,
         compiler_params=pltpu.CompilerParams(vmem_limit_bytes=8 << 20),
         cost_estimate=pl.CostEstimate(flops=0, bytes_accessed=3 << 20, transcendentals=0),
         name="bundle",
-    )(up, across, down, corner, feats, cot, weight, token)
+    )(*args)
 
 
 WIDE = 1280
 
 
-def unpack_kernel(info, message, before, mine, other, wgrad_mine, wgrad_other):
+def unpack_kernel(info, message, before, mine, other):
     core = info[0]
     own = pl.ds(pl.multiple_of(HALF * core, HALF), HALF)
     sibling = pl.ds(pl.multiple_of(HALF * (1 - core), HALF), HALF)
-    for rows, nodes, wgrad in ((own, mine, wgrad_mine), (sibling, other, wgrad_other)):
-        total = jnp.zeros((HALF, 256), F32)
+    for rows, nodes in ((own, mine), (sibling, other)):
         for g in range(8):
             nodes[:, 512 * g : 512 * (g + 1)] = message[g, rows, 512:1024]
-            total += message[g, rows, 1024:].astype(F32)
-        wgrad[...] = total
 
 
 def unpack(info, message, before):
     return pl.pallas_call(
         unpack_kernel,
-        out_shape=(
-            jax.ShapeDtypeStruct((HALF, 4096), BF16),
-            jax.ShapeDtypeStruct((HALF, 4096), BF16),
-            jax.ShapeDtypeStruct((HALF, 256), F32),
-            jax.ShapeDtypeStruct((HALF, 256), F32),
-        ),
+        out_shape=[jax.ShapeDtypeStruct((HALF, 4096), BF16)] * 2,
         in_specs=[SMEM, VMEM, ANY],
-        out_specs=(VMEM,) * 4,
+        out_specs=[VMEM] * 2,
         compiler_params=pltpu.CompilerParams(vmem_limit_bytes=4 << 20),
         cost_estimate=pl.CostEstimate(flops=0, bytes_accessed=1 << 20, transcendentals=0),
         name="unpack",
@@ -187,8 +176,8 @@
 
 
 def forward_kernel(places, info, cols, low_tiles, tiles, *refs):
-    own, others, cot, weight = refs[:8], refs[8:12], refs[12], refs[13]
-    out, high_tiles, feats, sems, stream_sems = refs[14:]
+    own, others, cot, weight = refs[:8], refs[8:14], refs[14], refs[15]
+    out, high_tiles, feats, sems, stream_sems = refs[16:]
     core = info[0]
     mine = pl.ds(pl.multiple_of(HALF * core, HALF), HALF)
     sibling = pl.ds(pl.multiple_of(HALF * (1 - core), HALF), HALF)
@@ -210,14 +199,14 @@
     ]
     for c in copies + stream:
         c.start()
-    near = others[0]
+    local = others[0]
     for g in range(8):
         at = 1024 * g + 512 * core
         out[g, mine, 512:1024] = cot[:, pl.ds(pl.multiple_of(at, 512), 512)]
         out[g, mine, 1024:] = weight[...]
-        at = 5 * LOCAL + at
-        out[g, sibling, 512:1024] = near[:, pl.ds(pl.multiple_of(at, 512), 512)]
-        out[g, sibling, 1024:] = near[:, 6 * LOCAL :]
+        at = LOCAL + at
+        out[g, sibling, 512:1024] = local[:, pl.ds(pl.multiple_of(at, 512), 512)]
+        out[g, sibling, 1024:] = local[:, 2 * LOCAL :]
     for c in copies:
         c.wait()
 
@@ -285,7 +274,7 @@
             jax.ShapeDtypeStruct((8, PAIR, WIDE), BF16),
             pltpu.VMEM((ROWS // 2, SLOTS, 128, 128), BF16),
         ),
-        in_specs=[SMEM, SMEM, VMEM, ANY] + [ANY] * 8 + [VMEM] + [ANY] * 3 + [VMEM] * 2,
+        in_specs=[SMEM, SMEM, VMEM, ANY] + [ANY] * 8 + [VMEM] + [ANY] * 5 + [VMEM] * 2,
         out_specs=(VMEM, VMEM),
         scratch_shapes=[
             pltpu.VMEM((PAIR, NODES), BF16),
@@ -329,7 +318,7 @@
 
 
 def backward_kernel(info, cols, low_tiles, high_tiles, grad, *refs):
-    outs, total = refs[:4], refs[4]
+    outs, wgrad, total = refs[:4], refs[4], refs[5]
     core = info[0]
 
     def clear(i, carry):
@@ -370,14 +359,26 @@
             place = slice(LOCAL * i, LOCAL * (i + 1))
             outs[phase][:, place] = total[own, lanes].astype(BF16)
             outs[2 + phase][:, place] = total[other, lanes].astype(BF16)
+    for rows, keep in ((own, True), (other, False)):
+        terms = grad[0, rows, 1024:].astype(F32)
+        for g in range(1, 8):
+            terms += grad[g, rows, 1024:].astype(F32)
+        if keep:
+            wgrad[...] = terms
+        else:
+            outs[2][:, LOCAL * len(GROUPS[0]) :] = terms.astype(BF16)
 
 
 def backward(info, cols, held, grad):
+    widths = [LOCAL * len(g) for g in GROUPS]
     return pl.pallas_call(
         backward_kernel,
-        out_shape=[jax.ShapeDtypeStruct((HALF, LOCAL * len(g)), BF16) for g in GROUPS] * 2,
+        out_shape=[
+            jax.ShapeDtypeStruct((HALF, n), BF16) for n in (*widths, widths[0] + 256, widths[1])
+        ]
+        + [jax.ShapeDtypeStruct((HALF, 256), F32)],
         in_specs=[SMEM, SMEM, VMEM, VMEM, VMEM],
-        out_specs=[VMEM] * 4,
+        out_specs=[VMEM] * 5,
         scratch_shapes=[
             pltpu.VMEM((PAIR, NODES), F32),
         ],
@@ -404,12 +405,13 @@
     )(*args, *before)
 
 
-def far_kernel(own, other, wgrad, wgrad_other, *outs):
+def far_kernel(own, other, wgrad, *outs):
+    terms = wgrad[...] + other[:, 4 * LOCAL :].astype(F32)
     for i, out in enumerate(outs[:4]):
         lanes = slice(LOCAL * i, LOCAL * (i + 1))
         out[:, :LOCAL] = (own[:, lanes].astype(F32) + other[:, lanes].astype(F32)).astype(BF16)
-        out[:, LOCAL:] = (wgrad[...] + wgrad_other[...]).astype(BF16)
-    outs[4][...] = wgrad[...] + wgrad_other[...]
+        out[:, LOCAL:] = terms.astype(BF16)
+    outs[4][...] = terms
 
 
 def near_kernel(own, other, wgrad, from_across, from_up, from_down, up, across, down, base):
@@ -446,34 +448,33 @@
 
     up, down, across, corner = (receive(node_feats, s) for s in (UP, DOWN, ACROSS, CORNER))
     held, token = load_tiles(info, tiles)
-    up, across, near = bundle(up, across, down, corner, node_feats, cotangent, weight, token)
+    up, across = gate((up, across), (token,))
     far = receive(up, UP)
     across_up = receive(up, ACROSS)
     across_down = receive(across, DOWN)
-    near = swap(near)
+    near = bundle(node_feats, cotangent, weight, up, across, down, corner, token)
+    local, first, second = (swap(n) for n in near)
     pieces = [
-        (node_feats, near, 4 * LOCAL),
-        (up, near, 0),
-        (down, near, 2 * LOCAL),
-        (across, near, LOCAL),
+        (node_feats, local, 0),
+        (up, first, 0),
+        (down, second, 0),
+        (across, first, LOCAL),
         (far, swap(far), 0),
         (across_up, swap(across_up), 0),
         (across_down, swap(across_down), 0),
-        (corner, near, 3 * LOCAL),
+        (corner, second, LOCAL),
     ]
     message, streamed = forward(info, cols, held, tiles, pieces, cotangent, weight)
     message = lax.all_to_all(message, "feat", 0, 0, axis_index_groups=SAME_CORE, tiled=True)
     message = dense(message.reshape(256, WIDE)).reshape(8, PAIR, WIDE)
     message = lax.all_to_all(message, "feat", 0, 0, axis_index_groups=SAME_CORE, tiled=True)
 
-    own_a, own_c, other_a, other_c = backward(info, cols, (held, streamed), message)
+    own_a, own_c, other_a, other_c, wgrad = backward(info, cols, (held, streamed), message)
     piece = ((HALF, LOCAL + 256), BF16)
-    hidden, hidden_other, wgrad, wgrad_other = unpack(info, message, own_a)
-    hidden_other = swap(hidden_other)
     across_up, across_down, far, corner, wgrad = sum_call(
         far_kernel,
         [piece] * 4 + [((HALF, 256), F32)],
-        (own_a, swap(other_a), wgrad, swap(wgrad_other)),
+        (own_a, swap(other_a), wgrad),
         "sum_far",
     )
     from_across = send(across_up, ACROSS)
@@ -487,7 +488,8 @@
         (own_c, swap(other_c), wgrad, from_across, from_up, from_down),
         "sum_near",
     )
-    hidden = join(info, hidden, hidden_other, down)
+    hidden, hidden_other = unpack(info, message, far)
+    hidden = join(info, hidden, swap(hidden_other), down)
     last = [send(up, UP), send(across, ACROSS), send(down, DOWN)]
     feats_grad, weight_grad = sum_call(
         last_kernel,

time: 122 us -> 124 us (1.016)
  starting transfers between devices: 25.8 us -> 17.6 us
  waiting for transfers between devices: 26.3 us -> 34.1 us
  blocking collectives: 35.6 us -> 37.3 us
    ppermute x7, waiting for transfers between devices: 8.05 us -> 14.8 us  [receive(): return lax.ppermute(a, 'blk', _from_step(step))]
    ppermute x7, starting transfers between devices: 12.8 us -> 6.94 us  [receive(): return lax.ppermute(a, 'blk', _from_step(step))]
    ppermute x7, starting transfers between devices: 11.5 us -> 9.17 us  [send(): return lax.ppermute(a, 'blk', _to_step(step))]
    all_to_all x2, blocking collectives: 35.6 us -> 37.3 us  [per_device(): lax.all_to_all(message, 'feat', 0, 0, axis_index_groups=SAME_CORE, tiled=...]
    ppermute x8 -> x9, waiting for transfers between devices: 4.39 us -> 5.4 us  [swap(): return lax.ppermute(a, 'feat', CORE_SWAP)]
  transfers between devices with their start and end apart: 22 -> 23, of which waited for: 15 -> 14; matrix products, arithmetic and copies ran while one was open for 0% -> 0% of each run, Pallas kernels for 7% -> 8%
where the time goes in v10:
time: 124 us; the launch traced here: 123 us
  blocking collectives  37.3 us (30%)
  waiting for transfers between devices  34.1 us (28%)
  Pallas kernels  33 us (27%)
  starting transfers between devices  17.6 us (14%)
    all_to_all x2, blocking collectives, per_device(): lax.all_to_all(message, 'feat', 0, 0, axis_index_groups=SAME_CORE, tiled=...  37.3 us
    ppermute x7, waiting for transfers between devices, receive(): return lax.ppermute(a, 'blk', _from_step(step))  14.8 us
    ppermute x7, waiting for transfers between devices, send(): return lax.ppermute(a, 'blk', _to_step(step))  13.9 us
    pallas_call x1, Pallas kernels, forward(): pl.pallas_call(functools.partial(forward_kernel, places), out_shape=(jax....  12.8 us
    ppermute x7, starting transfers between devices, send(): return lax.ppermute(a, 'blk', _to_step(step))  9.17 us
    pallas_call x1, Pallas kernels, backward(): pl.pallas_call(backward_kernel, out_shape=[jax.ShapeDtypeStruct((HALF, n)...  8.79 us
    ppermute x7, starting transfers between devices, receive(): return lax.ppermute(a, 'blk', _from_step(step))  6.94 us
    pallas_call x1, Pallas kernels, load_tiles(): pl.pallas_call(load_kernel, out_shape=(pltpu.VMEM((ROWS // 2, SLOTS, 128,...  6.43 us
  transfers between devices with their start and end apart: 23, of which 14 were waited for; matrix products, arithmetic and copies ran while one was open for 0% of the time, Pallas kernels for 8%

profile of v10, /device:TPU:0, one launch (start us, length us, event | category | flops | bytes accessed | tf_op | source)
XLA Modules:
  0.0 122.9 jit_solution(15048183366210155255)
XLA Ops:
  0.6 1.7 %collective-permute-start.1 = (bf16[16,8192]{1,0:T(8,128)(2,1)}, bf16[16,8192]{1,0:T(8,128)(2,1)S(1)}, u32[]{:S(2)}, u32[]{:S(2)}) collective-permute-start(bf16[16,8192]{1,0:T(8,128)(2,1)} %refs_0_.1), channel_id=1, source_target_pairs={{64,0},{80,16},{96,32},{112,48},{0,64},{16,80},{32,96},{48,112},{6... | collective-permute-start | bytes 786440 | tf_op jit(solution)/shard_map/ppermute | solution.py:50
  2.3 3.0 %collective-permute-start = (bf16[16,8192]{1,0:T(8,128)(2,1)}, bf16[16,8192]{1,0:T(8,128)(2,1)S(1)}, u32[]{:S(2)}, u32[]{:S(2)}) collective-permute-start(bf16[16,8192]{1,0:T(8,128)(2,1)} %refs_0_.1), channel_id=1, source_target_pairs={{16,0},{32,16},{48,32},{0,48},{80,64},{96,80},{112,96},{64,112},{1... | collective-permute-start | bytes 786440 | tf_op jit(solution)/shard_map/ppermute | solution.py:50
  5.3 0.6 collective-permute-start.6
  5.9 1.0 collective-permute-start.2
  7.0 6.4 %load_tiles.1 = (bf16[16,32,128,128]{3,2,1,0:T(8,128)(2,1)S(1)}, f32[8,128]{1,0:T(8,128)S(1)}) custom-call(s32[9]{0:T(128)S(1)} %stack.39.info, bf16[64,32,128,128]{3,2,1,0:T(8,128)(2,1)} %tiles.3), custom_call_target="tpu_custom_call" | custom-call | bytes 50331648 | tf_op jit(solution)/shard_map/load_tiles/pallas_call | solution.py:82
  13.4 3.1 %collective-permute-done.refs_0_ = bf16[16,8192]{1,0:T(8,128)(2,1)S(1)} collective-permute-done((bf16[16,8192]{1,0:T(8,128)(2,1)}, bf16[16,8192]{1,0:T(8,128)(2,1)S(1)}, u32[]{:S(2)}, u32[]{:S(2)}) %collective-permute-start) | collective-permute-done | bytes 262176 | tf_op jit(solution)/shard_map/ppermute | solution.py:50
  16.5 0.6 collective-permute-start.4
  17.5 3.3 %collective-permute-done.2.down.refs_2_ = bf16[16,8192]{1,0:T(8,128)(2,1)} collective-permute-done((bf16[16,8192]{1,0:T(8,128)(2,1)}, bf16[16,8192]{1,0:T(8,128)(2,1)}, u32[]{:S(2)}, u32[]{:S(2)}) %collective-permute-start.2) | collective-permute-done | bytes 262176 | tf_op jit(solution)/shard_map/ppermute | solution.py:50
  20.7 1.1 bundle.1
  22.0 3.7 %collective-permute-done.5.refs_6_ = bf16[16,8192]{1,0:T(8,128)(2,1)S(1)} collective-permute-done((bf16[16,8192]{1,0:T(8,128)(2,1)S(1)}, bf16[16,8192]{1,0:T(8,128)(2,1)S(1)}, u32[]{:S(2)}, u32[]{:S(2)}) %collective-permute-start.5) | collective-permute-done | bytes 262176 | tf_op jit(solution)/shard_map/ppermute | solution.py:50
  26.3 4.3 %collective-permute-done.3.refs_4_ = bf16[16,8192]{1,0:T(8,128)(2,1)S(1)} collective-permute-done((bf16[16,8192]{1,0:T(8,128)(2,1)S(1)}, bf16[16,8192]{1,0:T(8,128)(2,1)S(1)}, u32[]{:S(2)}, u32[]{:S(2)}) %collective-permute-start.3) | collective-permute-done | bytes 262176 | tf_op jit(solution)/shard_map/ppermute | solution.py:50
  30.6 0.5 collective-permute-start.10
  31.1 1.0 collective-permute-done.11.refs_12_
  32.5 12.8 %forward.1 = (bf16[8,32,1280]{2,1,0:T(8,128)(2,1)S(1)}, bf16[16,32,128,128]{3,2,1,0:T(8,128)(2,1)S(1)}) custom-call(s32[9]{0:T(128)S(1)} %stack.39.info, s32[32,64]{1,0:T(8,128)S(1)} %bitcast.14, bf16[16,32,128,128]{3,2,1,0:T(8,128)(2,1)S(1)} %get-tuple-element.30.low_tiles, bf16[64,32,128,128]{3,2,1,0:T(8,128)(2,1)} %tiles.3, bf16[16,8192]{1,0:T(8,128)(2,1)S(1)} %copy-done, ...), custom_call_target="tpu_custom_call" | custom-call | flops 8589934592 | bytes 8388608 | tf_op jit(solution)/shard_map/forward/pallas_call | solution.py:271
  45.4 22.3 %all_to_all.10 = bf16[8,32,1280]{2,1,0:T(8,128)(2,1)S(1)} all-to-all(bf16[8,32,1280]{2,1,0:T(8,128)(2,1)S(1)} %get-tuple-element.37), channel_id=1, replica_groups={{0,2,4,6,8,10,12,14},{1,3,5,7,9,11,13,15},{16,18,20,22,24,26,28,30},{17..., dimensions={0} | all-to-all | bytes 1310720 | tf_op jit(solution)/shard_map/all_to_all | solution.py:468
  67.7 0.6 dense.1
  68.3 15.0 %all_to_all.11.grad.message = bf16[8,32,1280]{2,1,0:T(8,128)(2,1)S(1)} all-to-all(bf16[8,32,1280]{2,1,0:T(8,128)(2,1)S(1)} %bitcast.13), channel_id=1, replica_groups={{0,2,4,6,8,10,12,14},{1,3,5,7,9,11,13,15},{16,18,20,22,24,26,28,30},{17..., dimensions={0} | all-to-all | bytes 1310720 | tf_op jit(solution)/shard_map/all_to_all | solution.py:470
  83.3 8.8 %backward.1 = (bf16[16,32768]{1,0:T(8,128)(2,1)S(1)}, bf16[16,32768]{1,0:T(8,128)(2,1)S(1)}, bf16[16,33024]{1,0:T(8,128)(2,1)S(1)}, bf16[16,32768]{1,0:T(8,128)(2,1)S(1)}, f32[16,256]{1,0:T(8,128)S(1)}) custom-call(s32[9]{0:T(128)S(1)} %stack.39.info, s32[32,64]{1,0:T(8,128)S(1)} %bitcast.15, bf16[16,32,128,128]{3,2,1,0:T(8,128)(2,1)S(1)} %get-tuple-element.30.low_tiles, ...), custom_call_target="tpu_custom_call" | custom-call | flops 8589934592 | bytes 8388608 | tf_op jit(solution)/shard_map/backward/pallas_call | solution.py:374
  92.2 2.7 %collective-permute-done.13.refs_1_ = bf16[16,33024]{1,0:T(8,128)(2,1)S(1)} collective-permute-done((bf16[16,33024]{1,0:T(8,128)(2,1)S(1)}, bf16[16,33024]{1,0:T(8,128)(2,1)S(1)}, u32[]{:S(2)}, u32[]{:S(2)}) %collective-permute-start.13) | collective-permute-done | bytes 1056800 | tf_op jit(solution)/shard_map/ppermute | solution.py:46
  95.4 0.6 collective-permute-start.16
  96.0 1.6 %collective-permute-start.17 = (bf16[16,8448]{1,0:T(8,128)(2,1)S(1)}, bf16[16,8448]{1,0:T(8,128)(2,1)S(1)}, u32[]{:S(2)}, u32[]{:S(2)}) collective-permute-start(bf16[16,8448]{1,0:T(8,128)(2,1)S(1)} %get-tuple-element.49), channel_id=1, source_target_pairs={{0,48},{16,0},{32,16},{48,32},{64,112},{80,64},{96,80},{112,96},{1... | collective-permute-start | bytes 811016 | tf_op jit(solution)/shard_map/ppermute | solution.py:54
  98.0 1.9 %collective-permute-start.19 = (bf16[16,8448]{1,0:T(8,128)(2,1)S(1)}, bf16[16,8448]{1,0:T(8,128)(2,1)S(1)}, u32[]{:S(2)}, u32[]{:S(2)}) collective-permute-start(bf16[16,8448]{1,0:T(8,128)(2,1)S(1)} %get-tuple-element.52), channel_id=1, source_target_pairs={{0,96},{16,112},{32,64},{48,80},{64,32},{80,48},{96,0},{112,16},{1... | collective-permute-start | bytes 811016 | tf_op jit(solution)/shard_map/ppermute | solution.py:54
  99.9 4.8 %collective-permute-done.16.refs_3_ = bf16[16,8448]{1,0:T(8,128)(2,1)S(1)} collective-permute-done((bf16[16,8448]{1,0:T(8,128)(2,1)S(1)}, bf16[16,8448]{1,0:T(8,128)(2,1)S(1)}, u32[]{:S(2)}, u32[]{:S(2)}) %collective-permute-start.16) | collective-permute-done | bytes 270368 | tf_op jit(solution)/shard_map/ppermute | solution.py:54
  104.7 5.5 %collective-permute-done.17.refs_4_ = bf16[16,8448]{1,0:T(8,128)(2,1)S(1)} collective-permute-done((bf16[16,8448]{1,0:T(8,128)(2,1)S(1)}, bf16[16,8448]{1,0:T(8,128)(2,1)S(1)}, u32[]{:S(2)}, u32[]{:S(2)}) %collective-permute-start.17) | collective-permute-done | bytes 270368 | tf_op jit(solution)/shard_map/ppermute | solution.py:54
  110.2 2.6 %collective-permute-done.18.refs_5_ = bf16[16,8448]{1,0:T(8,128)(2,1)S(1)} collective-permute-done((bf16[16,8448]{1,0:T(8,128)(2,1)S(1)}, bf16[16,8448]{1,0:T(8,128)(2,1)S(1)}, u32[]{:S(2)}, u32[]{:S(2)}) %collective-permute-start.18) | collective-permute-done | bytes 270368 | tf_op jit(solution)/shard_map/ppermute | solution.py:54
  113.2 1.5 %collective-permute-start.21 = (bf16[16,8448]{1,0:T(8,128)(2,1)S(1)}, bf16[16,8448]{1,0:T(8,128)(2,1)S(1)}, u32[]{:S(2)}, u32[]{:S(2)}) collective-permute-start(bf16[16,8448]{1,0:T(8,128)(2,1)S(1)} %get-tuple-element.54), channel_id=1, source_target_pairs={{0,64},{16,80},{32,96},{48,112},{64,0},{80,16},{96,32},{112,48},{1... | collective-permute-start | bytes 811016 | tf_op jit(solution)/shard_map/ppermute | solution.py:54
  114.7 3.1 %collective-permute-start.22 = (bf16[16,8448]{1,0:T(8,128)(2,1)S(1)}, bf16[16,8448]{1,0:T(8,128)(2,1)S(1)}, u32[]{:S(2)}, u32[]{:S(2)}) collective-permute-start(bf16[16,8448]{1,0:T(8,128)(2,1)S(1)} %get-tuple-element.50.before), channel_id=1, source_target_pairs={{0,48},{16,0},{32,16},{48,32},{64,112},{80,64},{96,80},{112,96},{1... | collective-permute-start | bytes 811016 | tf_op jit(solution)/shard_map/ppermute | solution.py:54
  117.8 0.6 unpack.1
  118.5 1.3 %collective-permute-done.14.received = bf16[16,4096]{1,0:T(8,128)(2,1)S(1)} collective-permute-done((bf16[16,4096]{1,0:T(8,128)(2,1)S(1)}, bf16[16,4096]{1,0:T(8,128)(2,1)S(1)}, u32[]{:S(2)}, u32[]{:S(2)}) %collective-permute-start.14) | collective-permute-done | bytes 131104 | tf_op jit(solution)/shard_map/ppermute | solution.py:46
  119.8 1.3 %join.1 = bf16[16,8192]{1,0:T(8,128)(2,1)} custom-call(s32[9]{0:T(128)S(1)} %stack.39.info, bf16[16,4096]{1,0:T(8,128)(2,1)S(1)} %get-tuple-element.43.mine, bf16[16,4096]{1,0:T(8,128)(2,1)S(1)} %collective-permute-done.14.received, bf16[16,8448]{1,0:T(8,128)(2,1)S(1)} %get-tuple-element.50.before), custom_call_target="tpu_custom_call" | custom-call | bytes 1048576 | tf_op jit(solution)/shard_map/join/pallas_call | solution.py:167
  121.1 0.6 collective-permute-done.20.refs_2_
  122.1 0.9 sum_last.1
  (37 shorter events, 3.4 us)
Async XLA Ops:
  0.6 12.8 %collective-permute-start.1 = (bf16[16,8192]{1,0:T(8,128)(2,1)}, bf16[16,8192]{1,0:T(8,128)(2,1)S(1)}, u32[]{:S(2)}, u32[]{:S(2)}) collective-permute-start(bf16[16,8192]{1,0:T(8,128)(2,1)} %refs_0_.1), channel_id=1, source_target_pairs={{64,0},{80,16},{96,32},{112,48},{0,64},{16,80},{32,96},{48,112},{6... | collective-permute-start | bytes 786440 | tf_op jit(solution)/shard_map/ppermute | solution.py:50
  2.3 14.2 %collective-permute-start = (bf16[16,8192]{1,0:T(8,128)(2,1)}, bf16[16,8192]{1,0:T(8,128)(2,1)S(1)}, u32[]{:S(2)}, u32[]{:S(2)}) collective-permute-start(bf16[16,8192]{1,0:T(8,128)(2,1)} %refs_0_.1), channel_id=1, source_target_pairs={{16,0},{32,16},{48,32},{0,48},{80,64},{96,80},{112,96},{64,112},{1... | collective-permute-start | bytes 786440 | tf_op jit(solution)/shard_map/ppermute | solution.py:50
  5.3 12.2 %collective-permute-start.6 = (bf16[16,8192]{1,0:T(8,128)(2,1)}, bf16[16,8192]{1,0:T(8,128)(2,1)S(1)}, u32[]{:S(2)}, u32[]{:S(2)}) collective-permute-start(bf16[16,8192]{1,0:T(8,128)(2,1)} %refs_0_.1), channel_id=1, source_target_pairs={{96,0},{112,16},{64,32},{80,48},{32,64},{48,80},{0,96},{16,112},{9... | collective-permute-start | bytes 786440 | tf_op jit(solution)/shard_map/ppermute | solution.py:50
  5.9 14.8 %collective-permute-start.2 = (bf16[16,8192]{1,0:T(8,128)(2,1)}, bf16[16,8192]{1,0:T(8,128)(2,1)}, u32[]{:S(2)}, u32[]{:S(2)}) collective-permute-start(bf16[16,8192]{1,0:T(8,128)(2,1)} %refs_0_.1), channel_id=1, source_target_pairs={{48,0},{0,16},{16,32},{32,48},{112,64},{64,80},{80,96},{96,112},{4... | collective-permute-start | bytes 786440 | tf_op jit(solution)/shard_map/ppermute | solution.py:50
  7.0 13.8 %copy-start = (bf16[16,8192]{1,0:T(8,128)(2,1)S(1)}, bf16[16,8192]{1,0:T(8,128)(2,1)}, u32[]{:S(2)}) copy-start(bf16[16,8192]{1,0:T(8,128)(2,1)} %refs_0_.1) | copy-start | bytes 786436
  7.0 13.8 %copy-start.1 = (bf16[16,8192]{1,0:T(8,128)(2,1)S(1)}, bf16[16,8192]{1,0:T(8,128)(2,1)}, u32[]{:S(2)}) copy-start(bf16[16,8192]{1,0:T(8,128)(2,1)} %refs_14_.1) | copy-start | bytes 786436
  7.0 13.8 %copy-start.3 = (bf16[16,256]{1,0:T(8,128)(2,1)S(1)}, bf16[16,256]{1,0:T(8,128)(2,1)}, u32[]{:S(2)}) copy-start(bf16[16,256]{1,0:T(8,128)(2,1)} %refs_15_.1) | copy-start | bytes 24580
  7.0 25.6 %copy-start.2 = (s32[64,32]{0,1:T(8,128)S(1)}, s32[64,32]{0,1:T(8,128)}, u32[]{:S(2)}) copy-start(s32[64,32]{0,1:T(8,128)} %param.8) | copy-start | bytes 24580
  16.5 9.2 %collective-permute-start.5 = (bf16[16,8192]{1,0:T(8,128)(2,1)S(1)}, bf16[16,8192]{1,0:T(8,128)(2,1)S(1)}, u32[]{:S(2)}, u32[]{:S(2)}) collective-permute-start(bf16[16,8192]{1,0:T(8,128)(2,1)S(1)} %get-tuple-element.33.across.refs_3_), channel_id=1, source_target_pairs={{48,0},{0,16},{16,32},{32,48},{112,64},{64,80},{80,96},{96,112},{4... | collective-permute-start | bytes 786440 | tf_op jit(solution)/shard_map/ppermute | solution.py:50
  16.5 9.8 %collective-permute-start.4 = (bf16[16,8192]{1,0:T(8,128)(2,1)S(1)}, bf16[16,8192]{1,0:T(8,128)(2,1)S(1)}, u32[]{:S(2)}, u32[]{:S(2)}) collective-permute-start(bf16[16,8192]{1,0:T(8,128)(2,1)S(1)} %get-tuple-element.32.up.refs_1_), channel_id=1, source_target_pairs={{64,0},{80,16},{96,32},{112,48},{0,64},{16,80},{32,96},{48,112},{6... | collective-permute-start | bytes 786440 | tf_op jit(solution)/shard_map/ppermute | solution.py:50
  21.8 10.7 %collective-permute-start.7 = (bf16[16,16640]{1,0:T(8,128)(2,1)S(1)}, bf16[16,16640]{1,0:T(8,128)(2,1)S(1)}, u32[]{:S(2)}, u32[]{:S(2)}) collective-permute-start(bf16[16,16640]{1,0:T(8,128)(2,1)S(1)} %get-tuple-element.34), channel_id=1, source_target_pairs={{0,1},{1,0},{2,3},{3,2},{4,5},{5,4},{6,7},{7,6},{8,9},{9,8},{10,11... | collective-permute-start | bytes 1597448 | tf_op jit(solution)/shard_map/ppermute | solution.py:46
  21.9 8.7 %collective-permute-start.3 = (bf16[16,8192]{1,0:T(8,128)(2,1)S(1)}, bf16[16,8192]{1,0:T(8,128)(2,1)S(1)}, u32[]{:S(2)}, u32[]{:S(2)}) collective-permute-start(bf16[16,8192]{1,0:T(8,128)(2,1)S(1)} %get-tuple-element.32.up.refs_1_), channel_id=1, source_target_pairs={{16,0},{32,16},{48,32},{0,48},{80,64},{96,80},{112,96},{64,112},{1... | collective-permute-start | bytes 786440 | tf_op jit(solution)/shard_map/ppermute | solution.py:50
  25.8 4.9 %collective-permute-start.12 = (bf16[16,8192]{1,0:T(8,128)(2,1)S(1)}, bf16[16,8192]{1,0:T(8,128)(2,1)S(1)}, u32[]{:S(2)}, u32[]{:S(2)}) collective-permute-start(bf16[16,8192]{1,0:T(8,128)(2,1)S(1)} %collective-permute-done.5.refs_6_), channel_id=1, source_target_pairs={{0,1},{1,0},{2,3},{3,2},{4,5},{5,4},{6,7},{7,6},{8,9},{9,8},{10,11... | collective-permute-start | bytes 786440 | tf_op jit(solution)/shard_map/ppermute | solution.py:46
  25.8 6.8 %collective-permute-start.8 = (bf16[16,16384]{1,0:T(8,128)(2,1)S(1)}, bf16[16,16384]{1,0:T(8,128)(2,1)S(1)}, u32[]{:S(2)}, u32[]{:S(2)}) collective-permute-start(bf16[16,16384]{1,0:T(8,128)(2,1)S(1)} %get-tuple-element.35), channel_id=1, source_target_pairs={{0,1},{1,0},{2,3},{3,2},{4,5},{5,4},{6,7},{7,6},{8,9},{9,8},{10,11... | collective-permute-start | bytes 1572872 | tf_op jit(solution)/shard_map/ppermute | solution.py:46
  26.3 6.3 %collective-permute-start.9 = (bf16[16,16384]{1,0:T(8,128)(2,1)S(1)}, bf16[16,16384]{1,0:T(8,128)(2,1)S(1)}, u32[]{:S(2)}, u32[]{:S(2)}) collective-permute-start(bf16[16,16384]{1,0:T(8,128)(2,1)S(1)} %get-tuple-element.36), channel_id=1, source_target_pairs={{0,1},{1,0},{2,3},{3,2},{4,5},{5,4},{6,7},{7,6},{8,9},{9,8},{10,11... | collective-permute-start | bytes 1572872 | tf_op jit(solution)/shard_map/ppermute | solution.py:46
  30.6 1.5 %collective-permute-start.11 = (bf16[16,8192]{1,0:T(8,128)(2,1)S(1)}, bf16[16,8192]{1,0:T(8,128)(2,1)S(1)}, u32[]{:S(2)}, u32[]{:S(2)}) collective-permute-start(bf16[16,8192]{1,0:T(8,128)(2,1)S(1)} %collective-permute-done.4.refs_5_), channel_id=1, source_target_pairs={{0,1},{1,0},{2,3},{3,2},{4,5},{5,4},{6,7},{7,6},{8,9},{9,8},{10,11... | collective-permute-start | bytes 786440 | tf_op jit(solution)/shard_map/ppermute | solution.py:46
  30.6 1.9 %collective-permute-start.10 = (bf16[16,8192]{1,0:T(8,128)(2,1)S(1)}, bf16[16,8192]{1,0:T(8,128)(2,1)S(1)}, u32[]{:S(2)}, u32[]{:S(2)}) collective-permute-start(bf16[16,8192]{1,0:T(8,128)(2,1)S(1)} %collective-permute-done.3.refs_4_), channel_id=1, source_target_pairs={{0,1},{1,0},{2,3},{3,2},{4,5},{5,4},{6,7},{7,6},{8,9},{9,8},{10,11... | collective-permute-start | bytes 786440 | tf_op jit(solution)/shard_map/ppermute | solution.py:46
  92.1 2.8 %collective-permute-start.13 = (bf16[16,33024]{1,0:T(8,128)(2,1)S(1)}, bf16[16,33024]{1,0:T(8,128)(2,1)S(1)}, u32[]{:S(2)}, u32[]{:S(2)}) collective-permute-start(bf16[16,33024]{1,0:T(8,128)(2,1)S(1)} %get-tuple-element.40), channel_id=1, source_target_pairs={{0,1},{1,0},{2,3},{3,2},{4,5},{5,4},{6,7},{7,6},{8,9},{9,8},{10,11... | collective-permute-start | bytes 3170312 | tf_op jit(solution)/shard_map/ppermute | solution.py:46
  95.1 17.6 %collective-permute-start.15 = (bf16[16,32768]{1,0:T(8,128)(2,1)S(1)}, bf16[16,32768]{1,0:T(8,128)(2,1)S(1)}, u32[]{:S(2)}, u32[]{:S(2)}) collective-permute-start(bf16[16,32768]{1,0:T(8,128)(2,1)S(1)} %gate.3), channel_id=1, source_target_pairs={{0,1},{1,0},{2,3},{3,2},{4,5},{5,4},{6,7},{7,6},{8,9},{9,8},{10,11... | collective-permute-start | bytes 3145736 | tf_op jit(solution)/shard_map/ppermute | solution.py:46
  95.4 9.3 %collective-permute-start.16 = (bf16[16,8448]{1,0:T(8,128)(2,1)S(1)}, bf16[16,8448]{1,0:T(8,128)(2,1)S(1)}, u32[]{:S(2)}, u32[]{:S(2)}) collective-permute-start(bf16[16,8448]{1,0:T(8,128)(2,1)S(1)} %get-tuple-element.48), channel_id=1, source_target_pairs={{0,64},{16,80},{32,96},{48,112},{64,0},{80,16},{96,32},{112,48},{1... | collective-permute-start | bytes 811016 | tf_op jit(solution)/shard_map/ppermute | solution.py:54
  96.0 14.3 %collective-permute-start.17 = (bf16[16,8448]{1,0:T(8,128)(2,1)S(1)}, bf16[16,8448]{1,0:T(8,128)(2,1)S(1)}, u32[]{:S(2)}, u32[]{:S(2)}) collective-permute-start(bf16[16,8448]{1,0:T(8,128)(2,1)S(1)} %get-tuple-element.49), channel_id=1, source_target_pairs={{0,48},{16,0},{32,16},{48,32},{64,112},{80,64},{96,80},{112,96},{1... | collective-permute-start | bytes 811016 | tf_op jit(solution)/shard_map/ppermute | solution.py:54
  97.6 15.2 %collective-permute-start.18 = (bf16[16,8448]{1,0:T(8,128)(2,1)S(1)}, bf16[16,8448]{1,0:T(8,128)(2,1)S(1)}, u32[]{:S(2)}, u32[]{:S(2)}) collective-permute-start(bf16[16,8448]{1,0:T(8,128)(2,1)S(1)} %get-tuple-element.42.before.refs_1_), channel_id=1, source_target_pairs={{0,16},{16,32},{32,48},{48,0},{64,80},{80,96},{96,112},{112,64},{1... | collective-permute-start | bytes 811016 | tf_op jit(solution)/shard_map/ppermute | solution.py:54
  98.0 23.1 %collective-permute-start.19 = (bf16[16,8448]{1,0:T(8,128)(2,1)S(1)}, bf16[16,8448]{1,0:T(8,128)(2,1)S(1)}, u32[]{:S(2)}, u32[]{:S(2)}) collective-permute-start(bf16[16,8448]{1,0:T(8,128)(2,1)S(1)} %get-tuple-element.52), channel_id=1, source_target_pairs={{0,96},{16,112},{32,64},{48,80},{64,32},{80,48},{96,0},{112,16},{1... | collective-permute-start | bytes 811016 | tf_op jit(solution)/shard_map/ppermute | solution.py:54
  113.1 8.6 %collective-permute-start.20 = (bf16[16,8448]{1,0:T(8,128)(2,1)S(1)}, bf16[16,8448]{1,0:T(8,128)(2,1)S(1)}, u32[]{:S(2)}, u32[]{:S(2)}) collective-permute-start(bf16[16,8448]{1,0:T(8,128)(2,1)S(1)} %get-tuple-element.53), channel_id=1, source_target_pairs={{0,16},{16,32},{32,48},{48,0},{64,80},{80,96},{96,112},{112,64},{1... | collective-permute-start | bytes 811016 | tf_op jit(solution)/shard_map/ppermute | solution.py:54
  113.2 8.5 %collective-permute-start.21 = (bf16[16,8448]{1,0:T(8,128)(2,1)S(1)}, bf16[16,8448]{1,0:T(8,128)(2,1)S(1)}, u32[]{:S(2)}, u32[]{:S(2)}) collective-permute-start(bf16[16,8448]{1,0:T(8,128)(2,1)S(1)} %get-tuple-element.54), channel_id=1, source_target_pairs={{0,64},{16,80},{32,96},{48,112},{64,0},{80,16},{96,32},{112,48},{1... | collective-permute-start | bytes 811016 | tf_op jit(solution)/shard_map/ppermute | solution.py:54
  114.7 7.4 %collective-permute-start.22 = (bf16[16,8448]{1,0:T(8,128)(2,1)S(1)}, bf16[16,8448]{1,0:T(8,128)(2,1)S(1)}, u32[]{:S(2)}, u32[]{:S(2)}) collective-permute-start(bf16[16,8448]{1,0:T(8,128)(2,1)S(1)} %get-tuple-element.50.before), channel_id=1, source_target_pairs={{0,48},{16,0},{32,16},{48,32},{64,112},{80,64},{96,80},{112,96},{1... | collective-permute-start | bytes 811016 | tf_op jit(solution)/shard_map/ppermute | solution.py:54
  118.4 1.4 %collective-permute-start.14 = (bf16[16,4096]{1,0:T(8,128)(2,1)S(1)}, bf16[16,4096]{1,0:T(8,128)(2,1)S(1)}, u32[]{:S(2)}, u32[]{:S(2)}) collective-permute-start(bf16[16,4096]{1,0:T(8,128)(2,1)S(1)} %get-tuple-element.44), channel_id=1, source_target_pairs={{0,1},{1,0},{2,3},{3,2},{4,5},{5,4},{6,7},{7,6},{8,9},{9,8},{10,11... | collective-permute-start | bytes 393224 | tf_op jit(solution)/shard_map/ppermute | solution.py:46

commit v11 on v10

--- a/solution.py
+++ b/solution.py
@@ -109,25 +109,28 @@
     )(*arrays, *before)
 
 
-def bundle_kernel(feats, cot, weight, up, across, down, corner, token, local, first, second):
-    for out, parts in ((local, (feats, cot)), (first, (up, across)), (second, (down, corner))):
-        for i, a in enumerate(parts):
-            out[:, LOCAL * i : LOCAL * (i + 1)] = a[...]
-    local[:, 2 * LOCAL :] = weight[...]
-
-
-def bundle(*args):
-    return pl.pallas_call(
-        bundle_kernel,
-        out_shape=[
-            jax.ShapeDtypeStruct((HALF, 2 * LOCAL + n), BF16) for n in (256, 0, 0)
-        ],
-        in_specs=[VMEM] * 7 + [ANY],
-        out_specs=[VMEM] * 3,
+def bundle_kernel(widths, before, *refs):
+    parts, outs = refs[: sum(widths)], refs[sum(widths) + before :]
+    parts = list(parts)
+    for count, out in zip(widths, outs):
+        at = 0
+        for a in parts[:count]:
+            out[:, at : at + a.shape[1]] = a[...]
+            at += a.shape[1]
+        parts = parts[count:]
+
+
+def bundle(groups, before=()):
+    arrays = [a for g in groups for a in g]
+    return pl.pallas_call(
+        functools.partial(bundle_kernel, [len(g) for g in groups], len(before)),
+        out_shape=[jax.ShapeDtypeStruct((HALF, sum(a.shape[1] for a in g)), BF16) for g in groups],
+        in_specs=[VMEM] * len(arrays) + [ANY] * len(before),
+        out_specs=[VMEM] * len(groups),
         compiler_params=pltpu.CompilerParams(vmem_limit_bytes=8 << 20),
-        cost_estimate=pl.CostEstimate(flops=0, bytes_accessed=3 << 20, transcendentals=0),
+        cost_estimate=pl.CostEstimate(flops=0, bytes_accessed=2 << 20, transcendentals=0),
         name="bundle",
-    )(*args)
+    )(*arrays, *before)
 
 
 WIDE = 1280
@@ -448,12 +451,14 @@
 
     up, down, across, corner = (receive(node_feats, s) for s in (UP, DOWN, ACROSS, CORNER))
     held, token = load_tiles(info, tiles)
-    up, across = gate((up, across), (token,))
+    (local,) = bundle(((node_feats, cotangent, weight),), (token,))
+    local = swap(local)
+    up, across = gate((up, across), (token, local))
     far = receive(up, UP)
     across_up = receive(up, ACROSS)
     across_down = receive(across, DOWN)
-    near = bundle(node_feats, cotangent, weight, up, across, down, corner, token)
-    local, first, second = (swap(n) for n in near)
+    first, second = bundle(((up, across), (down, corner)))
+    first, second = swap(first), swap(second)
     pieces = [
         (node_feats, local, 0),
         (up, first, 0),

time: 124 us -> 125 us (level)
  starting transfers between devices: 17.6 us -> 23.7 us
  blocking collectives: 37.3 us -> 35.3 us
    ppermute x7, starting transfers between devices: 6.94 us -> 11.1 us  [receive(): return lax.ppermute(a, 'blk', _from_step(step))]
    all_to_all x2, blocking collectives: 37.3 us -> 35.3 us  [per_device(): lax.all_to_all(message, 'feat', 0, 0, axis_index_groups=SAME_CORE, tiled=...]
    ppermute x7, starting transfers between devices: 9.17 us -> 10.9 us  [send(): return lax.ppermute(a, 'blk', _to_step(step))]
  transfers between devices with their start and end apart: 23 -> 23, of which waited for: 14 -> 13; matrix products, arithmetic and copies ran while one was open for 0% -> 0% of each run, Pallas kernels for 8% -> 2%
where the time goes in v11:
time: 125 us
  blocking collectives  35.3 us (28%)
  waiting for transfers between devices  32.9 us (26%)
  Pallas kernels  31.8 us (25%)
  starting transfers between devices  23.7 us (19%)
    all_to_all x2, blocking collectives, per_device(): lax.all_to_all(message, 'feat', 0, 0, axis_index_groups=SAME_CORE, tiled=...  35.3 us
    ppermute x7, waiting for transfers between devices, receive(): return lax.ppermute(a, 'blk', _from_step(step))  13.8 us
    ppermute x7, waiting for transfers between devices, send(): return lax.ppermute(a, 'blk', _to_step(step))  13.4 us
    pallas_call x1, Pallas kernels, forward(): pl.pallas_call(functools.partial(forward_kernel, places), out_shape=(jax....  12.6 us
    ppermute x7, starting transfers between devices, receive(): return lax.ppermute(a, 'blk', _from_step(step))  11.1 us
    ppermute x7, starting transfers between devices, send(): return lax.ppermute(a, 'blk', _to_step(step))  10.9 us
    pallas_call x1, Pallas kernels, backward(): pl.pallas_call(backward_kernel, out_shape=[jax.ShapeDtypeStruct((HALF, n)...  8.77 us
    pallas_call x1, Pallas kernels, load_tiles(): pl.pallas_call(load_kernel, out_shape=(pltpu.VMEM((ROWS // 2, SLOTS, 128,...  6.43 us
  transfers between devices with their start and end apart: 23, of which 13 were waited for; matrix products, arithmetic and copies ran while one was open for 0% of the time, Pallas kernels for 2%

profile of v11, /device:TPU:0, one launch (start us, length us, event | category | flops | bytes accessed | tf_op | source)
XLA Modules:
  0.0 124.6 jit_solution(10616502716584568916)
XLA Ops:
  0.8 6.4 %load_tiles.1 = (bf16[16,32,128,128]{3,2,1,0:T(8,128)(2,1)S(1)}, f32[8,128]{1,0:T(8,128)S(1)}) custom-call(s32[9]{0:T(128)S(1)} %stack.39.info, bf16[64,32,128,128]{3,2,1,0:T(8,128)(2,1)} %tiles.3), custom_call_target="tpu_custom_call" | custom-call | bytes 50331648 | tf_op jit(solution)/shard_map/load_tiles/pallas_call | solution.py:82
  7.4 1.7 %collective-permute-start.1 = (bf16[16,8192]{1,0:T(8,128)(2,1)S(1)}, bf16[16,8192]{1,0:T(8,128)(2,1)S(1)}, u32[]{:S(2)}, u32[]{:S(2)}) collective-permute-start(bf16[16,8192]{1,0:T(8,128)(2,1)S(1)} %copy-done), channel_id=1, source_target_pairs={{64,0},{80,16},{96,32},{112,48},{0,64},{16,80},{32,96},{48,112},{6... | collective-permute-start | bytes 786440 | tf_op jit(solution)/shard_map/ppermute | solution.py:50
  9.1 3.0 %collective-permute-start = (bf16[16,8192]{1,0:T(8,128)(2,1)S(1)}, bf16[16,8192]{1,0:T(8,128)(2,1)S(1)}, u32[]{:S(2)}, u32[]{:S(2)}) collective-permute-start(bf16[16,8192]{1,0:T(8,128)(2,1)S(1)} %copy-done), channel_id=1, source_target_pairs={{16,0},{32,16},{48,32},{0,48},{80,64},{96,80},{112,96},{64,112},{1... | collective-permute-start | bytes 786440 | tf_op jit(solution)/shard_map/ppermute | solution.py:50
  12.1 2.2 %collective-permute-start.7 = (bf16[16,8192]{1,0:T(8,128)(2,1)S(1)}, bf16[16,8192]{1,0:T(8,128)(2,1)S(1)}, u32[]{:S(2)}, u32[]{:S(2)}) collective-permute-start(bf16[16,8192]{1,0:T(8,128)(2,1)S(1)} %copy-done), channel_id=1, source_target_pairs={{96,0},{112,16},{64,32},{80,48},{32,64},{48,80},{0,96},{16,112},{9... | collective-permute-start | bytes 786440 | tf_op jit(solution)/shard_map/ppermute | solution.py:50
  14.3 2.0 %collective-permute-done.1.refs_1_ = bf16[16,8192]{1,0:T(8,128)(2,1)S(1)} collective-permute-done((bf16[16,8192]{1,0:T(8,128)(2,1)S(1)}, bf16[16,8192]{1,0:T(8,128)(2,1)S(1)}, u32[]{:S(2)}, u32[]{:S(2)}) %collective-permute-start.1) | collective-permute-done | bytes 262176 | tf_op jit(solution)/shard_map/ppermute | solution.py:50
  16.3 7.3 %collective-permute-done.refs_0_ = bf16[16,8192]{1,0:T(8,128)(2,1)S(1)} collective-permute-done((bf16[16,8192]{1,0:T(8,128)(2,1)S(1)}, bf16[16,8192]{1,0:T(8,128)(2,1)S(1)}, u32[]{:S(2)}, u32[]{:S(2)}) %collective-permute-start) | collective-permute-done | bytes 262176 | tf_op jit(solution)/shard_map/ppermute | solution.py:50
  23.7 0.5 collective-permute-start.5
  24.2 3.7 %collective-permute-start.4 = (bf16[16,8192]{1,0:T(8,128)(2,1)S(1)}, bf16[16,8192]{1,0:T(8,128)(2,1)S(1)}, u32[]{:S(2)}, u32[]{:S(2)}) collective-permute-start(bf16[16,8192]{1,0:T(8,128)(2,1)S(1)} %get-tuple-element.31.refs_0_.refs_1_), channel_id=1, source_target_pairs={{16,0},{32,16},{48,32},{0,48},{80,64},{96,80},{112,96},{64,112},{1... | collective-permute-start | bytes 786440 | tf_op jit(solution)/shard_map/ppermute | solution.py:50
  28.1 0.5 collective-permute-start.9
  28.6 4.4 %collective-permute-done.6.refs_6_ = bf16[16,8192]{1,0:T(8,128)(2,1)S(1)} collective-permute-done((bf16[16,8192]{1,0:T(8,128)(2,1)S(1)}, bf16[16,8192]{1,0:T(8,128)(2,1)S(1)}, u32[]{:S(2)}, u32[]{:S(2)}) %collective-permute-start.6) | collective-permute-done | bytes 262176 | tf_op jit(solution)/shard_map/ppermute | solution.py:50
  33.0 0.5 collective-permute-start.11
  33.6 0.9 collective-permute-done.12.refs_13_
  34.9 0.4 collective-permute-done.10.refs_11_
  35.3 12.6 %forward.1 = (bf16[8,32,1280]{2,1,0:T(8,128)(2,1)S(1)}, bf16[16,32,128,128]{3,2,1,0:T(8,128)(2,1)S(1)}) custom-call(s32[9]{0:T(128)S(1)} %stack.39.info, s32[32,64]{1,0:T(8,128)S(1)} %bitcast.14, bf16[16,32,128,128]{3,2,1,0:T(8,128)(2,1)S(1)} %get-tuple-element.29.low_tiles, bf16[64,32,128,128]{3,2,1,0:T(8,128)(2,1)} %tiles.3, bf16[16,8192]{1,0:T(8,128)(2,1)S(1)} %copy-done, ...), custom_call_target="tpu_custom_call" | custom-call | flops 8589934592 | bytes 8388608 | tf_op jit(solution)/shard_map/forward/pallas_call | solution.py:274
  47.9 20.2 %all_to_all.10 = bf16[8,32,1280]{2,1,0:T(8,128)(2,1)S(1)} all-to-all(bf16[8,32,1280]{2,1,0:T(8,128)(2,1)S(1)} %get-tuple-element.35), channel_id=1, replica_groups={{0,2,4,6,8,10,12,14},{1,3,5,7,9,11,13,15},{16,18,20,22,24,26,28,30},{17..., dimensions={0} | all-to-all | bytes 1310720 | tf_op jit(solution)/shard_map/all_to_all | solution.py:473
  68.1 0.6 dense.1
  68.8 15.0 %all_to_all.11.grad.message = bf16[8,32,1280]{2,1,0:T(8,128)(2,1)S(1)} all-to-all(bf16[8,32,1280]{2,1,0:T(8,128)(2,1)S(1)} %bitcast.13), channel_id=1, replica_groups={{0,2,4,6,8,10,12,14},{1,3,5,7,9,11,13,15},{16,18,20,22,24,26,28,30},{17..., dimensions={0} | all-to-all | bytes 1310720 | tf_op jit(solution)/shard_map/all_to_all | solution.py:475
  83.8 8.8 %backward.1 = (bf16[16,32768]{1,0:T(8,128)(2,1)S(1)}, bf16[16,32768]{1,0:T(8,128)(2,1)S(1)}, bf16[16,33024]{1,0:T(8,128)(2,1)S(1)}, bf16[16,32768]{1,0:T(8,128)(2,1)S(1)}, f32[16,256]{1,0:T(8,128)S(1)}) custom-call(s32[9]{0:T(128)S(1)} %stack.39.info, s32[32,64]{1,0:T(8,128)S(1)} %bitcast.15, bf16[16,32,128,128]{3,2,1,0:T(8,128)(2,1)S(1)} %get-tuple-element.29.low_tiles, ...), custom_call_target="tpu_custom_call" | custom-call | flops 8589934592 | bytes 8388608 | tf_op jit(solution)/shard_map/backward/pallas_call | solution.py:377
  92.7 2.7 %collective-permute-done.13.refs_1_ = bf16[16,33024]{1,0:T(8,128)(2,1)S(1)} collective-permute-done((bf16[16,33024]{1,0:T(8,128)(2,1)S(1)}, bf16[16,33024]{1,0:T(8,128)(2,1)S(1)}, u32[]{:S(2)}, u32[]{:S(2)}) %collective-permute-start.13) | collective-permute-done | bytes 1056800 | tf_op jit(solution)/shard_map/ppermute | solution.py:46
  96.0 3.2 %collective-permute-start.17 = (bf16[16,8448]{1,0:T(8,128)(2,1)S(1)}, bf16[16,8448]{1,0:T(8,128)(2,1)S(1)}, u32[]{:S(2)}, u32[]{:S(2)}) collective-permute-start(bf16[16,8448]{1,0:T(8,128)(2,1)S(1)} %get-tuple-element.47), channel_id=1, source_target_pairs={{0,48},{16,0},{32,16},{48,32},{64,112},{80,64},{96,80},{112,96},{1... | collective-permute-start | bytes 811016 | tf_op jit(solution)/shard_map/ppermute | solution.py:54
  99.2 2.8 %collective-permute-start.19 = (bf16[16,8448]{1,0:T(8,128)(2,1)S(1)}, bf16[16,8448]{1,0:T(8,128)(2,1)S(1)}, u32[]{:S(2)}, u32[]{:S(2)}) collective-permute-start(bf16[16,8448]{1,0:T(8,128)(2,1)S(1)} %get-tuple-element.50), channel_id=1, source_target_pairs={{0,96},{16,112},{32,64},{48,80},{64,32},{80,48},{96,0},{112,16},{1... | collective-permute-start | bytes 811016 | tf_op jit(solution)/shard_map/ppermute | solution.py:54
  102.0 3.2 %collective-permute-done.16.refs_3_ = bf16[16,8448]{1,0:T(8,128)(2,1)S(1)} collective-permute-done((bf16[16,8448]{1,0:T(8,128)(2,1)S(1)}, bf16[16,8448]{1,0:T(8,128)(2,1)S(1)}, u32[]{:S(2)}, u32[]{:S(2)}) %collective-permute-start.16) | collective-permute-done | bytes 270368 | tf_op jit(solution)/shard_map/ppermute | solution.py:54
  105.1 5.8 %collective-permute-done.17.refs_4_ = bf16[16,8448]{1,0:T(8,128)(2,1)S(1)} collective-permute-done((bf16[16,8448]{1,0:T(8,128)(2,1)S(1)}, bf16[16,8448]{1,0:T(8,128)(2,1)S(1)}, u32[]{:S(2)}, u32[]{:S(2)}) %collective-permute-start.17) | collective-permute-done | bytes 270368 | tf_op jit(solution)/shard_map/ppermute | solution.py:54
  111.0 3.4 %collective-permute-done.18.refs_5_ = bf16[16,8448]{1,0:T(8,128)(2,1)S(1)} collective-permute-done((bf16[16,8448]{1,0:T(8,128)(2,1)S(1)}, bf16[16,8448]{1,0:T(8,128)(2,1)S(1)}, u32[]{:S(2)}, u32[]{:S(2)}) %collective-permute-start.18) | collective-permute-done | bytes 270368 | tf_op jit(solution)/shard_map/ppermute | solution.py:54
  114.8 1.5 %collective-permute-start.21 = (bf16[16,8448]{1,0:T(8,128)(2,1)S(1)}, bf16[16,8448]{1,0:T(8,128)(2,1)S(1)}, u32[]{:S(2)}, u32[]{:S(2)}) collective-permute-start(bf16[16,8448]{1,0:T(8,128)(2,1)S(1)} %get-tuple-element.52), channel_id=1, source_target_pairs={{0,64},{16,80},{32,96},{48,112},{64,0},{80,16},{96,32},{112,48},{1... | collective-permute-start | bytes 811016 | tf_op jit(solution)/shard_map/ppermute | solution.py:54
  116.4 3.1 %collective-permute-start.22 = (bf16[16,8448]{1,0:T(8,128)(2,1)S(1)}, bf16[16,8448]{1,0:T(8,128)(2,1)S(1)}, u32[]{:S(2)}, u32[]{:S(2)}) collective-permute-start(bf16[16,8448]{1,0:T(8,128)(2,1)S(1)} %get-tuple-element.48.before), channel_id=1, source_target_pairs={{0,48},{16,0},{32,16},{48,32},{64,112},{80,64},{96,80},{112,96},{1... | collective-permute-start | bytes 811016 | tf_op jit(solution)/shard_map/ppermute | solution.py:54
  119.5 0.6 unpack.1
  120.2 1.3 %collective-permute-done.14.received = bf16[16,4096]{1,0:T(8,128)(2,1)S(1)} collective-permute-done((bf16[16,4096]{1,0:T(8,128)(2,1)S(1)}, bf16[16,4096]{1,0:T(8,128)(2,1)S(1)}, u32[]{:S(2)}, u32[]{:S(2)}) %collective-permute-start.14) | collective-permute-done | bytes 131104 | tf_op jit(solution)/shard_map/ppermute | solution.py:46
  121.5 1.3 %join.1 = bf16[16,8192]{1,0:T(8,128)(2,1)} custom-call(s32[9]{0:T(128)S(1)} %stack.39.info, bf16[16,4096]{1,0:T(8,128)(2,1)S(1)} %get-tuple-element.41.mine, bf16[16,4096]{1,0:T(8,128)(2,1)S(1)} %collective-permute-done.14.received, bf16[16,8448]{1,0:T(8,128)(2,1)S(1)} %get-tuple-element.48.before), custom_call_target="tpu_custom_call" | custom-call | bytes 1048576 | tf_op jit(solution)/shard_map/join/pallas_call | solution.py:170
  122.8 0.6 collective-permute-done.20.refs_2_
  123.3 0.4 collective-permute-done.22.refs_4_
  123.8 0.9 sum_last.1
  (38 shorter events, 2.1 us)
Async XLA Ops:
  0.8 6.5 %copy-start = (bf16[16,8192]{1,0:T(8,128)(2,1)S(1)}, bf16[16,8192]{1,0:T(8,128)(2,1)}, u32[]{:S(2)}) copy-start(bf16[16,8192]{1,0:T(8,128)(2,1)} %refs_0_.3) | copy-start | bytes 786436
  0.8 6.5 %copy-start.1 = (bf16[16,8192]{1,0:T(8,128)(2,1)S(1)}, bf16[16,8192]{1,0:T(8,128)(2,1)}, u32[]{:S(2)}) copy-start(bf16[16,8192]{1,0:T(8,128)(2,1)} %refs_14_.1) | copy-start | bytes 786436
  0.8 6.5 %copy-start.3 = (bf16[16,256]{1,0:T(8,128)(2,1)S(1)}, bf16[16,256]{1,0:T(8,128)(2,1)}, u32[]{:S(2)}) copy-start(bf16[16,256]{1,0:T(8,128)(2,1)} %refs_15_.1) | copy-start | bytes 24580
  0.8 34.5 %copy-start.2 = (s32[64,32]{0,1:T(8,128)S(1)}, s32[64,32]{0,1:T(8,128)}, u32[]{:S(2)}) copy-start(s32[64,32]{0,1:T(8,128)} %param.8) | copy-start | bytes 24580
  7.4 16.3 %collective-permute-start.2 = (bf16[16,16640]{1,0:T(8,128)(2,1)S(1)}, bf16[16,16640]{1,0:T(8,128)(2,1)S(1)}, u32[]{:S(2)}, u32[]{:S(2)}) collective-permute-start(bf16[16,16640]{1,0:T(8,128)(2,1)S(1)} %bundle.2), channel_id=1, source_target_pairs={{0,1},{1,0},{2,3},{3,2},{4,5},{5,4},{6,7},{7,6},{8,9},{9,8},{10,11... | collective-permute-start | bytes 1597448 | tf_op jit(solution)/shard_map/ppermute | solution.py:46
  7.4 8.9 %collective-permute-start.1 = (bf16[16,8192]{1,0:T(8,128)(2,1)S(1)}, bf16[16,8192]{1,0:T(8,128)(2,1)S(1)}, u32[]{:S(2)}, u32[]{:S(2)}) collective-permute-start(bf16[16,8192]{1,0:T(8,128)(2,1)S(1)} %copy-done), channel_id=1, source_target_pairs={{64,0},{80,16},{96,32},{112,48},{0,64},{16,80},{32,96},{48,112},{6... | collective-permute-start | bytes 786440 | tf_op jit(solution)/shard_map/ppermute | solution.py:50
  9.1 14.5 %collective-permute-start = (bf16[16,8192]{1,0:T(8,128)(2,1)S(1)}, bf16[16,8192]{1,0:T(8,128)(2,1)S(1)}, u32[]{:S(2)}, u32[]{:S(2)}) collective-permute-start(bf16[16,8192]{1,0:T(8,128)(2,1)S(1)} %copy-done), channel_id=1, source_target_pairs={{16,0},{32,16},{48,32},{0,48},{80,64},{96,80},{112,96},{64,112},{1... | collective-permute-start | bytes 786440 | tf_op jit(solution)/shard_map/ppermute | solution.py:50
  12.1 15.8 %collective-permute-start.3 = (bf16[16,8192]{1,0:T(8,128)(2,1)S(1)}, bf16[16,8192]{1,0:T(8,128)(2,1)S(1)}, u32[]{:S(2)}, u32[]{:S(2)}) collective-permute-start(bf16[16,8192]{1,0:T(8,128)(2,1)S(1)} %copy-done), channel_id=1, source_target_pairs={{48,0},{0,16},{16,32},{32,48},{112,64},{64,80},{80,96},{96,112},{4... | collective-permute-start | bytes 786440 | tf_op jit(solution)/shard_map/ppermute | solution.py:50
  12.1 15.8 %collective-permute-start.7 = (bf16[16,8192]{1,0:T(8,128)(2,1)S(1)}, bf16[16,8192]{1,0:T(8,128)(2,1)S(1)}, u32[]{:S(2)}, u32[]{:S(2)}) collective-permute-start(bf16[16,8192]{1,0:T(8,128)(2,1)S(1)} %copy-done), channel_id=1, source_target_pairs={{96,0},{112,16},{64,32},{80,48},{32,64},{48,80},{0,96},{16,112},{9... | collective-permute-start | bytes 786440 | tf_op jit(solution)/shard_map/ppermute | solution.py:50
  23.6 9.3 %collective-permute-start.6 = (bf16[16,8192]{1,0:T(8,128)(2,1)S(1)}, bf16[16,8192]{1,0:T(8,128)(2,1)S(1)}, u32[]{:S(2)}, u32[]{:S(2)}) collective-permute-start(bf16[16,8192]{1,0:T(8,128)(2,1)S(1)} %get-tuple-element.32.refs_1_.refs_3_), channel_id=1, source_target_pairs={{48,0},{0,16},{16,32},{32,48},{112,64},{64,80},{80,96},{96,112},{4... | collective-permute-start | bytes 786440 | tf_op jit(solution)/shard_map/ppermute | solution.py:50
  23.7 9.3 %collective-permute-start.5 = (bf16[16,8192]{1,0:T(8,128)(2,1)S(1)}, bf16[16,8192]{1,0:T(8,128)(2,1)S(1)}, u32[]{:S(2)}, u32[]{:S(2)}) collective-permute-start(bf16[16,8192]{1,0:T(8,128)(2,1)S(1)} %get-tuple-element.31.refs_0_.refs_1_), channel_id=1, source_target_pairs={{64,0},{80,16},{96,32},{112,48},{0,64},{16,80},{32,96},{48,112},{6... | collective-permute-start | bytes 786440 | tf_op jit(solution)/shard_map/ppermute | solution.py:50
  24.2 9.3 %collective-permute-start.4 = (bf16[16,8192]{1,0:T(8,128)(2,1)S(1)}, bf16[16,8192]{1,0:T(8,128)(2,1)S(1)}, u32[]{:S(2)}, u32[]{:S(2)}) collective-permute-start(bf16[16,8192]{1,0:T(8,128)(2,1)S(1)} %get-tuple-element.31.refs_0_.refs_1_), channel_id=1, source_target_pairs={{16,0},{32,16},{48,32},{0,48},{80,64},{96,80},{112,96},{64,112},{1... | collective-permute-start | bytes 786440 | tf_op jit(solution)/shard_map/ppermute | solution.py:50
  28.0 7.3 %collective-permute-start.8 = (bf16[16,16384]{1,0:T(8,128)(2,1)S(1)}, bf16[16,16384]{1,0:T(8,128)(2,1)S(1)}, u32[]{:S(2)}, u32[]{:S(2)}) collective-permute-start(bf16[16,16384]{1,0:T(8,128)(2,1)S(1)} %get-tuple-element.33), channel_id=1, source_target_pairs={{0,1},{1,0},{2,3},{3,2},{4,5},{5,4},{6,7},{7,6},{8,9},{9,8},{10,11... | collective-permute-start | bytes 1572872 | tf_op jit(solution)/shard_map/ppermute | solution.py:46
  28.1 7.2 %collective-permute-start.9 = (bf16[16,16384]{1,0:T(8,128)(2,1)S(1)}, bf16[16,16384]{1,0:T(8,128)(2,1)S(1)}, u32[]{:S(2)}, u32[]{:S(2)}) collective-permute-start(bf16[16,16384]{1,0:T(8,128)(2,1)S(1)} %get-tuple-element.34), channel_id=1, source_target_pairs={{0,1},{1,0},{2,3},{3,2},{4,5},{5,4},{6,7},{7,6},{8,9},{9,8},{10,11... | collective-permute-start | bytes 1572872 | tf_op jit(solution)/shard_map/ppermute | solution.py:46
  33.0 1.5 %collective-permute-start.12 = (bf16[16,8192]{1,0:T(8,128)(2,1)S(1)}, bf16[16,8192]{1,0:T(8,128)(2,1)S(1)}, u32[]{:S(2)}, u32[]{:S(2)}) collective-permute-start(bf16[16,8192]{1,0:T(8,128)(2,1)S(1)} %collective-permute-done.6.refs_6_), channel_id=1, source_target_pairs={{0,1},{1,0},{2,3},{3,2},{4,5},{5,4},{6,7},{7,6},{8,9},{9,8},{10,11... | collective-permute-start | bytes 786440 | tf_op jit(solution)/shard_map/ppermute | solution.py:46
  33.0 1.9 %collective-permute-start.11 = (bf16[16,8192]{1,0:T(8,128)(2,1)S(1)}, bf16[16,8192]{1,0:T(8,128)(2,1)S(1)}, u32[]{:S(2)}, u32[]{:S(2)}) collective-permute-start(bf16[16,8192]{1,0:T(8,128)(2,1)S(1)} %collective-permute-done.5.refs_5_), channel_id=1, source_target_pairs={{0,1},{1,0},{2,3},{3,2},{4,5},{5,4},{6,7},{7,6},{8,9},{9,8},{10,11... | collective-permute-start | bytes 786440 | tf_op jit(solution)/shard_map/ppermute | solution.py:46
  33.5 1.8 %collective-permute-start.10 = (bf16[16,8192]{1,0:T(8,128)(2,1)S(1)}, bf16[16,8192]{1,0:T(8,128)(2,1)S(1)}, u32[]{:S(2)}, u32[]{:S(2)}) collective-permute-start(bf16[16,8192]{1,0:T(8,128)(2,1)S(1)} %collective-permute-done.4.refs_4_), channel_id=1, source_target_pairs={{0,1},{1,0},{2,3},{3,2},{4,5},{5,4},{6,7},{7,6},{8,9},{9,8},{10,11... | collective-permute-start | bytes 786440 | tf_op jit(solution)/shard_map/ppermute | solution.py:46
  92.6 2.8 %collective-permute-start.13 = (bf16[16,33024]{1,0:T(8,128)(2,1)S(1)}, bf16[16,33024]{1,0:T(8,128)(2,1)S(1)}, u32[]{:S(2)}, u32[]{:S(2)}) collective-permute-start(bf16[16,33024]{1,0:T(8,128)(2,1)S(1)} %get-tuple-element.38), channel_id=1, source_target_pairs={{0,1},{1,0},{2,3},{3,2},{4,5},{5,4},{6,7},{7,6},{8,9},{9,8},{10,11... | collective-permute-start | bytes 3170312 | tf_op jit(solution)/shard_map/ppermute | solution.py:46
  95.6 18.8 %collective-permute-start.15 = (bf16[16,32768]{1,0:T(8,128)(2,1)S(1)}, bf16[16,32768]{1,0:T(8,128)(2,1)S(1)}, u32[]{:S(2)}, u32[]{:S(2)}) collective-permute-start(bf16[16,32768]{1,0:T(8,128)(2,1)S(1)} %gate.3), channel_id=1, source_target_pairs={{0,1},{1,0},{2,3},{3,2},{4,5},{5,4},{6,7},{7,6},{8,9},{9,8},{10,11... | collective-permute-start | bytes 3145736 | tf_op jit(solution)/shard_map/ppermute | solution.py:46
  95.8 9.3 %collective-permute-start.16 = (bf16[16,8448]{1,0:T(8,128)(2,1)S(1)}, bf16[16,8448]{1,0:T(8,128)(2,1)S(1)}, u32[]{:S(2)}, u32[]{:S(2)}) collective-permute-start(bf16[16,8448]{1,0:T(8,128)(2,1)S(1)} %get-tuple-element.46), channel_id=1, source_target_pairs={{0,64},{16,80},{32,96},{48,112},{64,0},{80,16},{96,32},{112,48},{1... | collective-permute-start | bytes 811016 | tf_op jit(solution)/shard_map/ppermute | solution.py:54
  96.0 15.0 %collective-permute-start.17 = (bf16[16,8448]{1,0:T(8,128)(2,1)S(1)}, bf16[16,8448]{1,0:T(8,128)(2,1)S(1)}, u32[]{:S(2)}, u32[]{:S(2)}) collective-permute-start(bf16[16,8448]{1,0:T(8,128)(2,1)S(1)} %get-tuple-element.47), channel_id=1, source_target_pairs={{0,48},{16,0},{32,16},{48,32},{64,112},{80,64},{96,80},{112,96},{1... | collective-permute-start | bytes 811016 | tf_op jit(solution)/shard_map/ppermute | solution.py:54
  99.2 15.2 %collective-permute-start.18 = (bf16[16,8448]{1,0:T(8,128)(2,1)S(1)}, bf16[16,8448]{1,0:T(8,128)(2,1)S(1)}, u32[]{:S(2)}, u32[]{:S(2)}) collective-permute-start(bf16[16,8448]{1,0:T(8,128)(2,1)S(1)} %get-tuple-element.40.before.refs_1_), channel_id=1, source_target_pairs={{0,16},{16,32},{32,48},{48,0},{64,80},{80,96},{96,112},{112,64},{1... | collective-permute-start | bytes 811016 | tf_op jit(solution)/shard_map/ppermute | solution.py:54
  99.2 23.6 %collective-permute-start.19 = (bf16[16,8448]{1,0:T(8,128)(2,1)S(1)}, bf16[16,8448]{1,0:T(8,128)(2,1)S(1)}, u32[]{:S(2)}, u32[]{:S(2)}) collective-permute-start(bf16[16,8448]{1,0:T(8,128)(2,1)S(1)} %get-tuple-element.50), channel_id=1, source_target_pairs={{0,96},{16,112},{32,64},{48,80},{64,32},{80,48},{96,0},{112,16},{1... | collective-permute-start | bytes 811016 | tf_op jit(solution)/shard_map/ppermute | solution.py:54
  114.7 8.6 %collective-permute-start.20 = (bf16[16,8448]{1,0:T(8,128)(2,1)S(1)}, bf16[16,8448]{1,0:T(8,128)(2,1)S(1)}, u32[]{:S(2)}, u32[]{:S(2)}) collective-permute-start(bf16[16,8448]{1,0:T(8,128)(2,1)S(1)} %get-tuple-element.51), channel_id=1, source_target_pairs={{0,16},{16,32},{32,48},{48,0},{64,80},{80,96},{96,112},{112,64},{1... | collective-permute-start | bytes 811016 | tf_op jit(solution)/shard_map/ppermute | solution.py:54
  114.8 8.5 %collective-permute-start.21 = (bf16[16,8448]{1,0:T(8,128)(2,1)S(1)}, bf16[16,8448]{1,0:T(8,128)(2,1)S(1)}, u32[]{:S(2)}, u32[]{:S(2)}) collective-permute-start(bf16[16,8448]{1,0:T(8,128)(2,1)S(1)} %get-tuple-element.52), channel_id=1, source_target_pairs={{0,64},{16,80},{32,96},{48,112},{64,0},{80,16},{96,32},{112,48},{1... | collective-permute-start | bytes 811016 | tf_op jit(solution)/shard_map/ppermute | solution.py:54
  116.4 7.4 %collective-permute-start.22 = (bf16[16,8448]{1,0:T(8,128)(2,1)S(1)}, bf16[16,8448]{1,0:T(8,128)(2,1)S(1)}, u32[]{:S(2)}, u32[]{:S(2)}) collective-permute-start(bf16[16,8448]{1,0:T(8,128)(2,1)S(1)} %get-tuple-element.48.before), channel_id=1, source_target_pairs={{0,48},{16,0},{32,16},{48,32},{64,112},{80,64},{96,80},{112,96},{1... | collective-permute-start | bytes 811016 | tf_op jit(solution)/shard_map/ppermute | solution.py:54
  120.1 1.4 %collective-permute-start.14 = (bf16[16,4096]{1,0:T(8,128)(2,1)S(1)}, bf16[16,4096]{1,0:T(8,128)(2,1)S(1)}, u32[]{:S(2)}, u32[]{:S(2)}) collective-permute-start(bf16[16,4096]{1,0:T(8,128)(2,1)S(1)} %get-tuple-element.42), channel_id=1, source_target_pairs={{0,1},{1,0},{2,3},{3,2},{4,5},{5,4},{6,7},{7,6},{8,9},{9,8},{10,11... | collective-permute-start | bytes 393224 | tf_op jit(solution)/shard_map/ppermute | solution.py:46

commit v12 on v11

--- a/solution.py
+++ b/solution.py
@@ -179,8 +179,8 @@
 
 
 def forward_kernel(places, info, cols, low_tiles, tiles, *refs):
-    own, others, cot, weight = refs[:8], refs[8:14], refs[14], refs[15]
-    out, high_tiles, feats, sems, stream_sems = refs[16:]
+    own, others, (cot, weight, sides) = refs[:8], refs[8:14], refs[14:17]
+    out, high_tiles, feats, sems, stream_sems = refs[17:]
     core = info[0]
     mine = pl.ds(pl.multiple_of(HALF * core, HALF), HALF)
     sibling = pl.ds(pl.multiple_of(HALF * (1 - core), HALF), HALF)
@@ -202,14 +202,12 @@
     ]
     for c in copies + stream:
         c.start()
-    local = others[0]
     for g in range(8):
         at = 1024 * g + 512 * core
         out[g, mine, 512:1024] = cot[:, pl.ds(pl.multiple_of(at, 512), 512)]
         out[g, mine, 1024:] = weight[...]
-        at = LOCAL + at
-        out[g, sibling, 512:1024] = local[:, pl.ds(pl.multiple_of(at, 512), 512)]
-        out[g, sibling, 1024:] = local[:, 2 * LOCAL :]
+        out[g, sibling, 512:1024] = sides[:, pl.ds(pl.multiple_of(at, 512), 512)]
+        out[g, sibling, 1024:] = sides[:, LOCAL:]
     for c in copies:
         c.wait()
 
@@ -264,7 +262,7 @@
         lax.fori_loop(4 * half, 4 * half + 4, step, 0)
 
 
-def forward(info, cols, held, tiles, pieces, cot, weight):
+def forward(info, cols, held, tiles, pieces, sides):
     own = [p[0] for p in pieces]
     others = []
     for _, other, _ in pieces:
@@ -277,7 +275,7 @@
             jax.ShapeDtypeStruct((8, PAIR, WIDE), BF16),
             pltpu.VMEM((ROWS // 2, SLOTS, 128, 128), BF16),
         ),
-        in_specs=[SMEM, SMEM, VMEM, ANY] + [ANY] * 8 + [VMEM] + [ANY] * 5 + [VMEM] * 2,
+        in_specs=[SMEM, SMEM, VMEM, ANY] + [ANY] * 14 + [VMEM] * 3,
         out_specs=(VMEM, VMEM),
         scratch_shapes=[
             pltpu.VMEM((PAIR, NODES), BF16),
@@ -289,7 +287,7 @@
             flops=8 * 2 * 1024 * 128 * 128 * 32, bytes_accessed=8 << 20, transcendentals=0
         ),
         name="forward",
-    )(info, cols, held, tiles, *own, *others, cot, weight)
+    )(info, cols, held, tiles, *own, *others, *sides)
     return message, pltpu.with_memory_space_constraint(streamed, pltpu.VMEM)
 
 
@@ -451,14 +449,15 @@
 
     up, down, across, corner = (receive(node_feats, s) for s in (UP, DOWN, ACROSS, CORNER))
     held, token = load_tiles(info, tiles)
-    (local,) = bundle(((node_feats, cotangent, weight),), (token,))
-    local = swap(local)
+    local = swap(node_feats)
     up, across = gate((up, across), (token, local))
     far = receive(up, UP)
     across_up = receive(up, ACROSS)
     across_down = receive(across, DOWN)
     first, second = bundle(((up, across), (down, corner)))
     first, second = swap(first), swap(second)
+    (sides,) = bundle(((cotangent, weight),), (far,))
+    sides = swap(sides)
     pieces = [
         (node_feats, local, 0),
         (up, first, 0),
@@ -469,7 +468,9 @@
         (across_down, swap(across_down), 0),
         (corner, second, LOCAL),
     ]
-    message, streamed = forward(info, cols, held, tiles, pieces, cotangent, weight)
+    message, streamed = forward(
+        info, cols, held, tiles, pieces, (cotangent, weight, sides)
+    )
     message = lax.all_to_all(message, "feat", 0, 0, axis_index_groups=SAME_CORE, tiled=True)
     message = dense(message.reshape(256, WIDE)).reshape(8, PAIR, WIDE)
     message = lax.all_to_all(message, "feat", 0, 0, axis_index_groups=SAME_CORE, tiled=True)

time: 125 us -> 121 us (0.968)
  waiting for transfers between devices: 32.9 us -> 27.3 us
  Pallas kernels: 31.8 us -> 33.3 us
    ppermute x7, waiting for transfers between devices: 13.8 us -> 7.53 us  [receive(): return lax.ppermute(a, 'blk', _from_step(step))]
    ppermute x9 -> x10, waiting for transfers between devices: 5.69 us -> 6.26 us  [swap(): return lax.ppermute(a, 'feat', CORE_SWAP)]
  transfers between devices with their start and end apart: 23 -> 24, of which waited for: 13 -> 13; matrix products, arithmetic and copies ran while one was open for 0% -> 0% of each run, Pallas kernels for 2% -> 8%
where the time goes in v12:
time: 121 us; the launch traced here: 120 us
  blocking collectives  35.6 us (29%)
  Pallas kernels  33.3 us (28%)
  waiting for transfers between devices  27.3 us (23%)
  starting transfers between devices  22.7 us (19%)
    all_to_all x2, blocking collectives, per_device(): lax.all_to_all(message, 'feat', 0, 0, axis_index_groups=SAME_CORE, tiled=...  35.6 us
    ppermute x7, waiting for transfers between devices, send(): return lax.ppermute(a, 'blk', _to_step(step))  13.5 us
    pallas_call x1, Pallas kernels, forward(): pl.pallas_call(functools.partial(forward_kernel, places), out_shape=(jax....  13 us
    ppermute x7, starting transfers between devices, receive(): return lax.ppermute(a, 'blk', _from_step(step))  11 us
    ppermute x7, starting transfers between devices, send(): return lax.ppermute(a, 'blk', _to_step(step))  9.71 us
    pallas_call x1, Pallas kernels, backward(): pl.pallas_call(backward_kernel, out_shape=[jax.ShapeDtypeStruct((HALF, n)...  8.76 us
    ppermute x7, waiting for transfers between devices, receive(): return lax.ppermute(a, 'blk', _from_step(step))  7.53 us
    pallas_call x1, Pallas kernels, load_tiles(): pl.pallas_call(load_kernel, out_shape=(pltpu.VMEM((ROWS // 2, SLOTS, 128,...  6.43 us
  transfers between devices with their start and end apart: 24, of which 13 were waited for; matrix products, arithmetic and copies ran while one was open for 0% of the time, Pallas kernels for 8%

profile of v12, /device:TPU:0, one launch (start us, length us, event | category | flops | bytes accessed | tf_op | source)
XLA Modules:
  0.0 119.8 jit_solution(4839331786329927623)
XLA Ops:
  0.7 1.7 %collective-permute-start.1 = (bf16[16,8192]{1,0:T(8,128)(2,1)}, bf16[16,8192]{1,0:T(8,128)(2,1)S(1)}, u32[]{:S(2)}, u32[]{:S(2)}) collective-permute-start(bf16[16,8192]{1,0:T(8,128)(2,1)} %refs_0_.3), channel_id=1, source_target_pairs={{64,0},{80,16},{96,32},{112,48},{0,64},{16,80},{32,96},{48,112},{6... | collective-permute-start | bytes 786440 | tf_op jit(solution)/shard_map/ppermute | solution.py:50
  2.4 3.0 %collective-permute-start = (bf16[16,8192]{1,0:T(8,128)(2,1)}, bf16[16,8192]{1,0:T(8,128)(2,1)S(1)}, u32[]{:S(2)}, u32[]{:S(2)}) collective-permute-start(bf16[16,8192]{1,0:T(8,128)(2,1)} %refs_0_.3), channel_id=1, source_target_pairs={{16,0},{32,16},{48,32},{0,48},{80,64},{96,80},{112,96},{64,112},{1... | collective-permute-start | bytes 786440 | tf_op jit(solution)/shard_map/ppermute | solution.py:50
  5.4 2.2 %collective-permute-start.7 = (bf16[16,8192]{1,0:T(8,128)(2,1)}, bf16[16,8192]{1,0:T(8,128)(2,1)}, u32[]{:S(2)}, u32[]{:S(2)}) collective-permute-start(bf16[16,8192]{1,0:T(8,128)(2,1)} %refs_0_.3), channel_id=1, source_target_pairs={{96,0},{112,16},{64,32},{80,48},{32,64},{48,80},{0,96},{16,112},{9... | collective-permute-start | bytes 786440 | tf_op jit(solution)/shard_map/ppermute | solution.py:50
  7.7 6.4 %load_tiles.1 = (bf16[16,32,128,128]{3,2,1,0:T(8,128)(2,1)S(1)}, f32[8,128]{1,0:T(8,128)S(1)}) custom-call(s32[9]{0:T(128)S(1)} %stack.39.info, bf16[64,32,128,128]{3,2,1,0:T(8,128)(2,1)} %tiles.3), custom_call_target="tpu_custom_call" | custom-call | bytes 50331648 | tf_op jit(solution)/shard_map/load_tiles/pallas_call | solution.py:82
  14.1 3.1 %collective-permute-done.refs_0_ = bf16[16,8192]{1,0:T(8,128)(2,1)S(1)} collective-permute-done((bf16[16,8192]{1,0:T(8,128)(2,1)}, bf16[16,8192]{1,0:T(8,128)(2,1)S(1)}, u32[]{:S(2)}, u32[]{:S(2)}) %collective-permute-start) | collective-permute-done | bytes 262176 | tf_op jit(solution)/shard_map/ppermute | solution.py:50
  17.2 3.6 %collective-permute-start.4 = (bf16[16,8192]{1,0:T(8,128)(2,1)S(1)}, bf16[16,8192]{1,0:T(8,128)(2,1)S(1)}, u32[]{:S(2)}, u32[]{:S(2)}) collective-permute-start(bf16[16,8192]{1,0:T(8,128)(2,1)S(1)} %get-tuple-element.31.refs_0_.refs_1_), channel_id=1, source_target_pairs={{16,0},{32,16},{48,32},{0,48},{80,64},{96,80},{112,96},{64,112},{1... | collective-permute-start | bytes 786440 | tf_op jit(solution)/shard_map/ppermute | solution.py:50
  20.8 0.5 collective-permute-start.5
  21.3 1.1 bundle.2
  22.4 4.1 %collective-permute-done.6.refs_6_ = bf16[16,8192]{1,0:T(8,128)(2,1)S(1)} collective-permute-done((bf16[16,8192]{1,0:T(8,128)(2,1)S(1)}, bf16[16,8192]{1,0:T(8,128)(2,1)S(1)}, u32[]{:S(2)}, u32[]{:S(2)}) %collective-permute-start.6) | collective-permute-done | bytes 262176 | tf_op jit(solution)/shard_map/ppermute | solution.py:50
  26.6 0.5 collective-permute-start.8
  27.1 0.6 collective-permute-start.13
  28.1 0.4 collective-permute-start.10
  28.6 1.8 %collective-permute-done.11.refs_12_ = bf16[16,8192]{1,0:T(8,128)(2,1)S(1)} collective-permute-done((bf16[16,8192]{1,0:T(8,128)(2,1)S(1)}, bf16[16,8192]{1,0:T(8,128)(2,1)S(1)}, u32[]{:S(2)}, u32[]{:S(2)}) %collective-permute-start.11) | collective-permute-done | bytes 262176 | tf_op jit(solution)/shard_map/ppermute | solution.py:46
  30.4 0.4 collective-permute-done.10.refs_11_
  30.8 13.0 %forward.1 = (bf16[8,32,1280]{2,1,0:T(8,128)(2,1)S(1)}, bf16[16,32,128,128]{3,2,1,0:T(8,128)(2,1)S(1)}) custom-call(s32[9]{0:T(128)S(1)} %stack.39.info, s32[32,64]{1,0:T(8,128)S(1)} %bitcast.14, bf16[16,32,128,128]{3,2,1,0:T(8,128)(2,1)S(1)} %get-tuple-element.29.low_tiles, bf16[64,32,128,128]{3,2,1,0:T(8,128)(2,1)} %tiles.3, ...), custom_call_target="tpu_custom_call" | custom-call | flops 8589934592 | bytes 8388608 | tf_op jit(solution)/shard_map/forward/pallas_call | solution.py:272
  43.8 20.6 %all_to_all.10 = bf16[8,32,1280]{2,1,0:T(8,128)(2,1)S(1)} all-to-all(bf16[8,32,1280]{2,1,0:T(8,128)(2,1)S(1)} %get-tuple-element.35), channel_id=1, replica_groups={{0,2,4,6,8,10,12,14},{1,3,5,7,9,11,13,15},{16,18,20,22,24,26,28,30},{17..., dimensions={0} | all-to-all | bytes 1310720 | tf_op jit(solution)/shard_map/all_to_all | solution.py:474
  64.4 0.6 dense.1
  65.1 15.0 %all_to_all.11.grad.message = bf16[8,32,1280]{2,1,0:T(8,128)(2,1)S(1)} all-to-all(bf16[8,32,1280]{2,1,0:T(8,128)(2,1)S(1)} %bitcast.13), channel_id=1, replica_groups={{0,2,4,6,8,10,12,14},{1,3,5,7,9,11,13,15},{16,18,20,22,24,26,28,30},{17..., dimensions={0} | all-to-all | bytes 1310720 | tf_op jit(solution)/shard_map/all_to_all | solution.py:476
  80.1 8.8 %backward.1 = (bf16[16,32768]{1,0:T(8,128)(2,1)S(1)}, bf16[16,32768]{1,0:T(8,128)(2,1)S(1)}, bf16[16,33024]{1,0:T(8,128)(2,1)S(1)}, bf16[16,32768]{1,0:T(8,128)(2,1)S(1)}, f32[16,256]{1,0:T(8,128)S(1)}) custom-call(s32[9]{0:T(128)S(1)} %stack.39.info, s32[32,64]{1,0:T(8,128)S(1)} %bitcast.15, bf16[16,32,128,128]{3,2,1,0:T(8,128)(2,1)S(1)} %get-tuple-element.29.low_tiles, ...), custom_call_target="tpu_custom_call" | custom-call | flops 8589934592 | bytes 8388608 | tf_op jit(solution)/shard_map/backward/pallas_call | solution.py:375
  88.9 2.7 %collective-permute-done.14.refs_1_ = bf16[16,33024]{1,0:T(8,128)(2,1)S(1)} collective-permute-done((bf16[16,33024]{1,0:T(8,128)(2,1)S(1)}, bf16[16,33024]{1,0:T(8,128)(2,1)S(1)}, u32[]{:S(2)}, u32[]{:S(2)}) %collective-permute-start.14) | collective-permute-done | bytes 1056800 | tf_op jit(solution)/shard_map/ppermute | solution.py:46
  92.3 1.7 %collective-permute-start.18 = (bf16[16,8448]{1,0:T(8,128)(2,1)S(1)}, bf16[16,8448]{1,0:T(8,128)(2,1)S(1)}, u32[]{:S(2)}, u32[]{:S(2)}) collective-permute-start(bf16[16,8448]{1,0:T(8,128)(2,1)S(1)} %get-tuple-element.47), channel_id=1, source_target_pairs={{0,48},{16,0},{32,16},{48,32},{64,112},{80,64},{96,80},{112,96},{1... | collective-permute-start | bytes 811016 | tf_op jit(solution)/shard_map/ppermute | solution.py:54
  94.4 2.4 %collective-permute-start.20 = (bf16[16,8448]{1,0:T(8,128)(2,1)S(1)}, bf16[16,8448]{1,0:T(8,128)(2,1)S(1)}, u32[]{:S(2)}, u32[]{:S(2)}) collective-permute-start(bf16[16,8448]{1,0:T(8,128)(2,1)S(1)} %get-tuple-element.50), channel_id=1, source_target_pairs={{0,96},{16,112},{32,64},{48,80},{64,32},{80,48},{96,0},{112,16},{1... | collective-permute-start | bytes 811016 | tf_op jit(solution)/shard_map/ppermute | solution.py:54
  96.7 4.6 %collective-permute-done.17.refs_3_ = bf16[16,8448]{1,0:T(8,128)(2,1)S(1)} collective-permute-done((bf16[16,8448]{1,0:T(8,128)(2,1)S(1)}, bf16[16,8448]{1,0:T(8,128)(2,1)S(1)}, u32[]{:S(2)}, u32[]{:S(2)}) %collective-permute-start.17) | collective-permute-done | bytes 270368 | tf_op jit(solution)/shard_map/ppermute | solution.py:54
  101.4 5.2 %collective-permute-done.18.refs_4_ = bf16[16,8448]{1,0:T(8,128)(2,1)S(1)} collective-permute-done((bf16[16,8448]{1,0:T(8,128)(2,1)S(1)}, bf16[16,8448]{1,0:T(8,128)(2,1)S(1)}, u32[]{:S(2)}, u32[]{:S(2)}) %collective-permute-start.18) | collective-permute-done | bytes 270368 | tf_op jit(solution)/shard_map/ppermute | solution.py:54
  106.6 2.7 %collective-permute-done.19.refs_5_ = bf16[16,8448]{1,0:T(8,128)(2,1)S(1)} collective-permute-done((bf16[16,8448]{1,0:T(8,128)(2,1)S(1)}, bf16[16,8448]{1,0:T(8,128)(2,1)S(1)}, u32[]{:S(2)}, u32[]{:S(2)}) %collective-permute-start.19) | collective-permute-done | bytes 270368 | tf_op jit(solution)/shard_map/ppermute | solution.py:54
  109.7 1.8 %collective-permute-start.22 = (bf16[16,8448]{1,0:T(8,128)(2,1)S(1)}, bf16[16,8448]{1,0:T(8,128)(2,1)S(1)}, u32[]{:S(2)}, u32[]{:S(2)}) collective-permute-start(bf16[16,8448]{1,0:T(8,128)(2,1)S(1)} %get-tuple-element.52), channel_id=1, source_target_pairs={{0,64},{16,80},{32,96},{48,112},{64,0},{80,16},{96,32},{112,48},{1... | collective-permute-start | bytes 811016 | tf_op jit(solution)/shard_map/ppermute | solution.py:54
  111.5 3.1 %collective-permute-start.23 = (bf16[16,8448]{1,0:T(8,128)(2,1)S(1)}, bf16[16,8448]{1,0:T(8,128)(2,1)S(1)}, u32[]{:S(2)}, u32[]{:S(2)}) collective-permute-start(bf16[16,8448]{1,0:T(8,128)(2,1)S(1)} %get-tuple-element.48.before), channel_id=1, source_target_pairs={{0,48},{16,0},{32,16},{48,32},{64,112},{80,64},{96,80},{112,96},{1... | collective-permute-start | bytes 811016 | tf_op jit(solution)/shard_map/ppermute | solution.py:54
  114.7 0.6 unpack.1
  115.3 1.3 %collective-permute-done.15.received = bf16[16,4096]{1,0:T(8,128)(2,1)S(1)} collective-permute-done((bf16[16,4096]{1,0:T(8,128)(2,1)S(1)}, bf16[16,4096]{1,0:T(8,128)(2,1)S(1)}, u32[]{:S(2)}, u32[]{:S(2)}) %collective-permute-start.15) | collective-permute-done | bytes 131104 | tf_op jit(solution)/shard_map/ppermute | solution.py:46
  116.7 1.3 %join.1 = bf16[16,8192]{1,0:T(8,128)(2,1)} custom-call(s32[9]{0:T(128)S(1)} %stack.39.info, bf16[16,4096]{1,0:T(8,128)(2,1)S(1)} %get-tuple-element.41.mine, bf16[16,4096]{1,0:T(8,128)(2,1)S(1)} %collective-permute-done.15.received, bf16[16,8448]{1,0:T(8,128)(2,1)S(1)} %get-tuple-element.48.before), custom_call_target="tpu_custom_call" | custom-call | bytes 1048576 | tf_op jit(solution)/shard_map/join/pallas_call | solution.py:170
  118.3 0.7 collective-permute-done.23.refs_4_
  118.9 0.9 sum_last.1
  (40 shorter events, 2.6 us)
Async XLA Ops:
  0.6 13.5 %collective-permute-start.2 = (bf16[16,8192]{1,0:T(8,128)(2,1)}, bf16[16,8192]{1,0:T(8,128)(2,1)S(1)}, u32[]{:S(2)}, u32[]{:S(2)}) collective-permute-start(bf16[16,8192]{1,0:T(8,128)(2,1)} %refs_0_.3), channel_id=1, source_target_pairs={{0,1},{1,0},{2,3},{3,2},{4,5},{5,4},{6,7},{7,6},{8,9},{9,8},{10,11... | collective-permute-start | bytes 786440 | tf_op jit(solution)/shard_map/ppermute | solution.py:46
  0.7 13.4 %collective-permute-start.1 = (bf16[16,8192]{1,0:T(8,128)(2,1)}, bf16[16,8192]{1,0:T(8,128)(2,1)S(1)}, u32[]{:S(2)}, u32[]{:S(2)}) collective-permute-start(bf16[16,8192]{1,0:T(8,128)(2,1)} %refs_0_.3), channel_id=1, source_target_pairs={{64,0},{80,16},{96,32},{112,48},{0,64},{16,80},{32,96},{48,112},{6... | collective-permute-start | bytes 786440 | tf_op jit(solution)/shard_map/ppermute | solution.py:50
  2.4 14.8 %collective-permute-start = (bf16[16,8192]{1,0:T(8,128)(2,1)}, bf16[16,8192]{1,0:T(8,128)(2,1)S(1)}, u32[]{:S(2)}, u32[]{:S(2)}) collective-permute-start(bf16[16,8192]{1,0:T(8,128)(2,1)} %refs_0_.3), channel_id=1, source_target_pairs={{16,0},{32,16},{48,32},{0,48},{80,64},{96,80},{112,96},{64,112},{1... | collective-permute-start | bytes 786440 | tf_op jit(solution)/shard_map/ppermute | solution.py:50
  5.4 15.9 %collective-permute-start.3 = (bf16[16,8192]{1,0:T(8,128)(2,1)}, bf16[16,8192]{1,0:T(8,128)(2,1)}, u32[]{:S(2)}, u32[]{:S(2)}) collective-permute-start(bf16[16,8192]{1,0:T(8,128)(2,1)} %refs_0_.3), channel_id=1, source_target_pairs={{48,0},{0,16},{16,32},{32,48},{112,64},{64,80},{80,96},{96,112},{4... | collective-permute-start | bytes 786440 | tf_op jit(solution)/shard_map/ppermute | solution.py:50
  5.4 15.9 %collective-permute-start.7 = (bf16[16,8192]{1,0:T(8,128)(2,1)}, bf16[16,8192]{1,0:T(8,128)(2,1)}, u32[]{:S(2)}, u32[]{:S(2)}) collective-permute-start(bf16[16,8192]{1,0:T(8,128)(2,1)} %refs_0_.3), channel_id=1, source_target_pairs={{96,0},{112,16},{64,32},{80,48},{32,64},{48,80},{0,96},{16,112},{9... | collective-permute-start | bytes 786440 | tf_op jit(solution)/shard_map/ppermute | solution.py:50
  7.7 19.4 %copy-start = (bf16[16,8192]{1,0:T(8,128)(2,1)S(1)}, bf16[16,8192]{1,0:T(8,128)(2,1)}, u32[]{:S(2)}) copy-start(bf16[16,8192]{1,0:T(8,128)(2,1)} %refs_14_.1) | copy-start | bytes 786436
  7.7 19.4 %copy-start.3 = (bf16[16,256]{1,0:T(8,128)(2,1)S(1)}, bf16[16,256]{1,0:T(8,128)(2,1)}, u32[]{:S(2)}) copy-start(bf16[16,256]{1,0:T(8,128)(2,1)} %refs_15_.1) | copy-start | bytes 24580
  7.7 23.1 %copy-start.1 = (bf16[16,8192]{1,0:T(8,128)(2,1)S(1)}, bf16[16,8192]{1,0:T(8,128)(2,1)}, u32[]{:S(2)}) copy-start(bf16[16,8192]{1,0:T(8,128)(2,1)} %refs_0_.3) | copy-start | bytes 786436
  7.7 23.1 %copy-start.2 = (s32[64,32]{0,1:T(8,128)S(1)}, s32[64,32]{0,1:T(8,128)}, u32[]{:S(2)}) copy-start(s32[64,32]{0,1:T(8,128)} %param.8) | copy-start | bytes 24580
  17.2 9.4 %collective-permute-start.6 = (bf16[16,8192]{1,0:T(8,128)(2,1)S(1)}, bf16[16,8192]{1,0:T(8,128)(2,1)S(1)}, u32[]{:S(2)}, u32[]{:S(2)}) collective-permute-start(bf16[16,8192]{1,0:T(8,128)(2,1)S(1)} %get-tuple-element.32.refs_1_.refs_3_), channel_id=1, source_target_pairs={{48,0},{0,16},{16,32},{32,48},{112,64},{64,80},{80,96},{96,112},{4... | collective-permute-start | bytes 786440 | tf_op jit(solution)/shard_map/ppermute | solution.py:50
  17.2 9.9 %collective-permute-start.4 = (bf16[16,8192]{1,0:T(8,128)(2,1)S(1)}, bf16[16,8192]{1,0:T(8,128)(2,1)S(1)}, u32[]{:S(2)}, u32[]{:S(2)}) collective-permute-start(bf16[16,8192]{1,0:T(8,128)(2,1)S(1)} %get-tuple-element.31.refs_0_.refs_1_), channel_id=1, source_target_pairs={{16,0},{32,16},{48,32},{0,48},{80,64},{96,80},{112,96},{64,112},{1... | collective-permute-start | bytes 786440 | tf_op jit(solution)/shard_map/ppermute | solution.py:50
  20.8 7.3 %collective-permute-start.5 = (bf16[16,8192]{1,0:T(8,128)(2,1)S(1)}, bf16[16,8192]{1,0:T(8,128)(2,1)S(1)}, u32[]{:S(2)}, u32[]{:S(2)}) collective-permute-start(bf16[16,8192]{1,0:T(8,128)(2,1)S(1)} %get-tuple-element.31.refs_0_.refs_1_), channel_id=1, source_target_pairs={{64,0},{80,16},{96,32},{112,48},{0,64},{16,80},{32,96},{48,112},{6... | collective-permute-start | bytes 786440 | tf_op jit(solution)/shard_map/ppermute | solution.py:50
  26.6 1.5 %collective-permute-start.12 = (bf16[16,8192]{1,0:T(8,128)(2,1)S(1)}, bf16[16,8192]{1,0:T(8,128)(2,1)S(1)}, u32[]{:S(2)}, u32[]{:S(2)}) collective-permute-start(bf16[16,8192]{1,0:T(8,128)(2,1)S(1)} %collective-permute-done.6.refs_6_), channel_id=1, source_target_pairs={{0,1},{1,0},{2,3},{3,2},{4,5},{5,4},{6,7},{7,6},{8,9},{9,8},{10,11... | collective-permute-start | bytes 786440 | tf_op jit(solution)/shard_map/ppermute | solution.py:46
  26.6 4.2 %collective-permute-start.8 = (bf16[16,16384]{1,0:T(8,128)(2,1)S(1)}, bf16[16,16384]{1,0:T(8,128)(2,1)S(1)}, u32[]{:S(2)}, u32[]{:S(2)}) collective-permute-start(bf16[16,16384]{1,0:T(8,128)(2,1)S(1)} %get-tuple-element.33), channel_id=1, source_target_pairs={{0,1},{1,0},{2,3},{3,2},{4,5},{5,4},{6,7},{7,6},{8,9},{9,8},{10,11... | collective-permute-start | bytes 1572872 | tf_op jit(solution)/shard_map/ppermute | solution.py:46
  27.1 3.7 %collective-permute-start.9 = (bf16[16,16384]{1,0:T(8,128)(2,1)S(1)}, bf16[16,16384]{1,0:T(8,128)(2,1)S(1)}, u32[]{:S(2)}, u32[]{:S(2)}) collective-permute-start(bf16[16,16384]{1,0:T(8,128)(2,1)S(1)} %get-tuple-element.34), channel_id=1, source_target_pairs={{0,1},{1,0},{2,3},{3,2},{4,5},{5,4},{6,7},{7,6},{8,9},{9,8},{10,11... | collective-permute-start | bytes 1572872 | tf_op jit(solution)/shard_map/ppermute | solution.py:46
  27.1 3.6 %collective-permute-start.13 = (bf16[16,8448]{1,0:T(8,128)(2,1)S(1)}, bf16[16,8448]{1,0:T(8,128)(2,1)S(1)}, u32[]{:S(2)}, u32[]{:S(2)}) collective-permute-start(bf16[16,8448]{1,0:T(8,128)(2,1)S(1)} %bundle.3), channel_id=1, source_target_pairs={{0,1},{1,0},{2,3},{3,2},{4,5},{5,4},{6,7},{7,6},{8,9},{9,8},{10,11... | collective-permute-start | bytes 811016 | tf_op jit(solution)/shard_map/ppermute | solution.py:46
  28.0 2.3 %collective-permute-start.11 = (bf16[16,8192]{1,0:T(8,128)(2,1)S(1)}, bf16[16,8192]{1,0:T(8,128)(2,1)S(1)}, u32[]{:S(2)}, u32[]{:S(2)}) collective-permute-start(bf16[16,8192]{1,0:T(8,128)(2,1)S(1)} %collective-permute-done.5.refs_5_), channel_id=1, source_target_pairs={{0,1},{1,0},{2,3},{3,2},{4,5},{5,4},{6,7},{7,6},{8,9},{9,8},{10,11... | collective-permute-start | bytes 786440 | tf_op jit(solution)/shard_map/ppermute | solution.py:46
  28.1 2.6 %collective-permute-start.10 = (bf16[16,8192]{1,0:T(8,128)(2,1)S(1)}, bf16[16,8192]{1,0:T(8,128)(2,1)S(1)}, u32[]{:S(2)}, u32[]{:S(2)}) collective-permute-start(bf16[16,8192]{1,0:T(8,128)(2,1)S(1)} %collective-permute-done.4.refs_2_.refs_4_), channel_id=1, source_target_pairs={{0,1},{1,0},{2,3},{3,2},{4,5},{5,4},{6,7},{7,6},{8,9},{9,8},{10,11... | collective-permute-start | bytes 786440 | tf_op jit(solution)/shard_map/ppermute | solution.py:46
  88.8 2.8 %collective-permute-start.14 = (bf16[16,33024]{1,0:T(8,128)(2,1)S(1)}, bf16[16,33024]{1,0:T(8,128)(2,1)S(1)}, u32[]{:S(2)}, u32[]{:S(2)}) collective-permute-start(bf16[16,33024]{1,0:T(8,128)(2,1)S(1)} %get-tuple-element.38), channel_id=1, source_target_pairs={{0,1},{1,0},{2,3},{3,2},{4,5},{5,4},{6,7},{7,6},{8,9},{9,8},{10,11... | collective-permute-start | bytes 3170312 | tf_op jit(solution)/shard_map/ppermute | solution.py:46
  91.8 17.4 %collective-permute-start.16 = (bf16[16,32768]{1,0:T(8,128)(2,1)S(1)}, bf16[16,32768]{1,0:T(8,128)(2,1)S(1)}, u32[]{:S(2)}, u32[]{:S(2)}) collective-permute-start(bf16[16,32768]{1,0:T(8,128)(2,1)S(1)} %gate.3), channel_id=1, source_target_pairs={{0,1},{1,0},{2,3},{3,2},{4,5},{5,4},{6,7},{7,6},{8,9},{9,8},{10,11... | collective-permute-start | bytes 3145736 | tf_op jit(solution)/shard_map/ppermute | solution.py:46
  92.1 9.3 %collective-permute-start.17 = (bf16[16,8448]{1,0:T(8,128)(2,1)S(1)}, bf16[16,8448]{1,0:T(8,128)(2,1)S(1)}, u32[]{:S(2)}, u32[]{:S(2)}) collective-permute-start(bf16[16,8448]{1,0:T(8,128)(2,1)S(1)} %get-tuple-element.46), channel_id=1, source_target_pairs={{0,64},{16,80},{32,96},{48,112},{64,0},{80,16},{96,32},{112,48},{1... | collective-permute-start | bytes 811016 | tf_op jit(solution)/shard_map/ppermute | solution.py:54
  92.3 14.3 %collective-permute-start.18 = (bf16[16,8448]{1,0:T(8,128)(2,1)S(1)}, bf16[16,8448]{1,0:T(8,128)(2,1)S(1)}, u32[]{:S(2)}, u32[]{:S(2)}) collective-permute-start(bf16[16,8448]{1,0:T(8,128)(2,1)S(1)} %get-tuple-element.47), channel_id=1, source_target_pairs={{0,48},{16,0},{32,16},{48,32},{64,112},{80,64},{96,80},{112,96},{1... | collective-permute-start | bytes 811016 | tf_op jit(solution)/shard_map/ppermute | solution.py:54
  94.0 15.3 %collective-permute-start.19 = (bf16[16,8448]{1,0:T(8,128)(2,1)S(1)}, bf16[16,8448]{1,0:T(8,128)(2,1)S(1)}, u32[]{:S(2)}, u32[]{:S(2)}) collective-permute-start(bf16[16,8448]{1,0:T(8,128)(2,1)S(1)} %get-tuple-element.40.before.refs_1_), channel_id=1, source_target_pairs={{0,16},{16,32},{32,48},{48,0},{64,80},{80,96},{96,112},{112,64},{1... | collective-permute-start | bytes 811016 | tf_op jit(solution)/shard_map/ppermute | solution.py:54
  94.4 23.6 %collective-permute-start.20 = (bf16[16,8448]{1,0:T(8,128)(2,1)S(1)}, bf16[16,8448]{1,0:T(8,128)(2,1)S(1)}, u32[]{:S(2)}, u32[]{:S(2)}) collective-permute-start(bf16[16,8448]{1,0:T(8,128)(2,1)S(1)} %get-tuple-element.50), channel_id=1, source_target_pairs={{0,96},{16,112},{32,64},{48,80},{64,32},{80,48},{96,0},{112,16},{1... | collective-permute-start | bytes 811016 | tf_op jit(solution)/shard_map/ppermute | solution.py:54
  109.6 8.7 %collective-permute-start.21 = (bf16[16,8448]{1,0:T(8,128)(2,1)S(1)}, bf16[16,8448]{1,0:T(8,128)(2,1)S(1)}, u32[]{:S(2)}, u32[]{:S(2)}) collective-permute-start(bf16[16,8448]{1,0:T(8,128)(2,1)S(1)} %get-tuple-element.51), channel_id=1, source_target_pairs={{0,16},{16,32},{32,48},{48,0},{64,80},{80,96},{96,112},{112,64},{1... | collective-permute-start | bytes 811016 | tf_op jit(solution)/shard_map/ppermute | solution.py:54
  109.7 8.6 %collective-permute-start.22 = (bf16[16,8448]{1,0:T(8,128)(2,1)S(1)}, bf16[16,8448]{1,0:T(8,128)(2,1)S(1)}, u32[]{:S(2)}, u32[]{:S(2)}) collective-permute-start(bf16[16,8448]{1,0:T(8,128)(2,1)S(1)} %get-tuple-element.52), channel_id=1, source_target_pairs={{0,64},{16,80},{32,96},{48,112},{64,0},{80,16},{96,32},{112,48},{1... | collective-permute-start | bytes 811016 | tf_op jit(solution)/shard_map/ppermute | solution.py:54
  111.5 7.4 %collective-permute-start.23 = (bf16[16,8448]{1,0:T(8,128)(2,1)S(1)}, bf16[16,8448]{1,0:T(8,128)(2,1)S(1)}, u32[]{:S(2)}, u32[]{:S(2)}) collective-permute-start(bf16[16,8448]{1,0:T(8,128)(2,1)S(1)} %get-tuple-element.48.before), channel_id=1, source_target_pairs={{0,48},{16,0},{32,16},{48,32},{64,112},{80,64},{96,80},{112,96},{1... | collective-permute-start | bytes 811016 | tf_op jit(solution)/shard_map/ppermute | solution.py:54
  115.3 1.4 %collective-permute-start.15 = (bf16[16,4096]{1,0:T(8,128)(2,1)S(1)}, bf16[16,4096]{1,0:T(8,128)(2,1)S(1)}, u32[]{:S(2)}, u32[]{:S(2)}) collective-permute-start(bf16[16,4096]{1,0:T(8,128)(2,1)S(1)} %get-tuple-element.42), channel_id=1, source_target_pairs={{0,1},{1,0},{2,3},{3,2},{4,5},{5,4},{6,7},{7,6},{8,9},{9,8},{10,11... | collective-permute-start | bytes 393224 | tf_op jit(solution)/shard_map/ppermute | solution.py:46
